TPU v7x, 128 devices: a whole 4x4x4 slice. The times are simulated.
128 devices in a mesh: dp: 16 (over y, x_hi, core), tensor: 8 (over z, x_lo).
Axes of the slice: x: 4 (x_hi: 2, x_lo: 2; x = x_hi * 2 + x_lo), y: 4, z: 4, core: 2. Of those that a mesh axis runs over, the one named last changes fastest.
Arguments:
- hidden_acts: bfloat16 [16384, 14336], P('dp', 'tensor'), may hold values from -6 to 6
- act_basis: bfloat16 [14336, 1024], P('tensor'), may hold values from -0.046875 to 0.046875
- out_grads: bfloat16 [16384, 4096], P('dp', 'tensor'), may hold values from -6 to 6
- grad_basis: bfloat16 [4096, 1024], P('tensor'), may hold values from -0.09375 to 0.09375
- routed: int32 [16384], P('dp'), may hold values 0 or 1
Outputs:
- act_gram: float32 [1024, 1024], P('dp', 'tensor')
- grad_gram: float32 [1024, 1024], P('dp', 'tensor')
- correction: float32 [1024, 1024], P('dp', 'tensor')
All inputs are finite; a program needn't handle non-finite values. No bound on the sum of `routed` on one device may be relied on, other than what follows from the above.
Results may differ from a plain program's by a relative error of at most 0.0014.
Values may be sent and summed in bfloat16 or wider, within the bound.
No kernel may reach another device: no remote copies, remote signals or barrier semaphores. Data moves between devices by JAX's collectives and lax.ppermute only.
A program may use at most 64 MiB of HBM per device.

v0:
```python
import jax
import jax.numpy as jnp
from jax import lax
from jax.sharding import PartitionSpec as P


def shards(hidden_acts, act_basis, out_grads, grad_basis, routed):
    act_part = jnp.dot(hidden_acts, act_basis, preferred_element_type=jnp.float32)
    grad_part = jnp.dot(out_grads, grad_basis, preferred_element_type=jnp.float32)
    act_sum, grad_sum = lax.psum((act_part, grad_part), "tensor")
    rot_acts = act_sum.astype(jnp.bfloat16)
    rot_grads = grad_sum.astype(jnp.bfloat16)
    tok_rows = rot_acts.shape[0]
    total_tokens = tok_rows * lax.axis_size("dp")
    weights = routed.astype(jnp.float32)[:, None]
    acts_f = rot_acts.astype(jnp.float32)
    grads_f = rot_grads.astype(jnp.float32)
    masked_acts = (acts_f * weights).astype(jnp.bfloat16)
    masked_grads = (grads_f * weights).astype(jnp.bfloat16)
    sq_acts = (acts_f * acts_f * weights).astype(jnp.bfloat16)
    sq_grads = (grads_f * grads_f).astype(jnp.bfloat16)
    directions = rot_acts.shape[1]
    col_width = directions // lax.axis_size("tensor")
    col_start = lax.axis_index("tensor") * col_width
    act_cols = lax.dynamic_slice_in_dim(rot_acts, col_start, col_width, 1)
    grad_cols = lax.dynamic_slice_in_dim(rot_grads, col_start, col_width, 1)
    sqg_cols = lax.dynamic_slice_in_dim(sq_grads, col_start, col_width, 1)
    scale = 1.0 / total_tokens
    contract = (((0,), (0,)), ((), ()))
    own_rows = directions // lax.axis_size("dp")
    term_a = lax.dot_general(masked_acts, act_cols, contract, preferred_element_type=jnp.float32)
    term_g = lax.dot_general(masked_grads, grad_cols, contract, preferred_element_type=jnp.float32)
    term_s = lax.dot_general(sq_acts, sqg_cols, contract, preferred_element_type=jnp.float32)
    summed = lax.psum(jnp.concatenate([term_a, term_g, term_s], axis=1) * scale, "dp")
    owned = lax.dynamic_slice_in_dim(summed, lax.axis_index("dp") * own_rows, own_rows, 0)
    act_gram = owned[:, :col_width]
    grad_gram = owned[:, col_width : 2 * col_width]
    correction = owned[:, 2 * col_width :]
    return (act_gram, grad_gram, correction)


def solution(mesh):
    return jax.shard_map(
        shards,
        mesh=mesh,
        in_specs=(
            P("dp", "tensor"),
            P("tensor", None),
            P("dp", "tensor"),
            P("tensor", None),
            P("dp"),
        ),
        out_specs=(P("dp", "tensor"), P("dp", "tensor"), P("dp", "tensor")),
        check_vma=False,
    )
```

profile of v0, /device:TPU:0, one launch (start us, length us, event | category | flops | bytes accessed | tf_op | source)
XLA Modules:
  0.0 508.9 jit_solution(411253529704498492)
XLA Ops:
  7.2 0.0 copy-start
  7.2 0.0 all-reduce.4.cloned.1.call-start
  7.2 0.0 copy-start.3
  7.2 9.2 %fusion.20 = f32[1024,1024]{1,0:T(8,128)} fusion(bf16[1024,1792]{1,0:T(8,128)(2,1)} %param.5, bf16[1792,1024]{1,0:T(8,128)(2,1)} %param.6), kind=kOutput, calls=%fused_computation.23 | convolution fusion | flops 3758096384 | bytes 11534336 | tf_op jit(solution)/shard_map/dot_general | solution.py:8
  16.4 0.0 copy-done
  16.4 0.0 copy-done.3
  16.4 0.0 copy-start.1
  16.4 3.2 fusion.21
  19.7 0.0 copy-done.1
  19.7 328.8 %all-reduce.5 = (bf16[1024,1024]{1,0:T(8,128)(2,1)}, bf16[1024,1024]{1,0:T(8,128)(2,1)S(1)}) all-reduce(f32[1024,1024]{1,0:T(8,128)} %fusion.20, f32[1024,1024]{1,0:T(8,128)} %fusion.21), channel_id=1, replica_groups=mesh['dp'=16,'tensor'=8] {'tensor'}, use_global_device_ids=true, to_apply=%region_0.0 | all-reduce | flops 2097152 | bytes 12582912 | tf_op jit(solution)/shard_map/psum | solution.py:10
  348.5 2.4 convert_element_type.32
  350.9 0.0 copy-start.2
  350.9 0.6 fusion.3
  351.5 0.9 copy-done.2
  352.5 0.6 fusion.6
  353.1 1.8 fusion.4
  354.9 1.3 maximum_multiply_fusion
  356.2 0.0 all-reduce.4.cloned.1.call-update
  356.2 142.7 %all-reduce.4.cloned.1.call-done = f32[1024,384]{0,1:T(8,128)} async-done(((f32[1024,384]{0,1:T(8,128)}), f32[1024,384]{0,1:T(8,128)}) %all-reduce.4.cloned.1.call-update) | async-done | bytes 1572880 | tf_op jit(solution)/shard_map/psum | solution.py:34
  498.9 1.0 fusion.19
  500.0 0.7 copy.8
  500.7 0.7 copy.9
  501.4 0.7 copy.10
  (1 shorter events, 0.0 us)
Async XLA Ops:
  7.2 9.2 %copy-start = (bf16[1024,512]{1,0:T(8,128)(2,1)S(1)}, bf16[1024,512]{1,0:T(8,128)(2,1)}, u32[]{:S(2)}) copy-start(bf16[1024,512]{1,0:T(8,128)(2,1)} %param.7) | copy-start | bytes 3145732
  7.2 491.8 %all-reduce.4.cloned.1.call-start = ((), (), s32[]{:S(2)}) async-start(), calls=%async_computation | async-start | bytes 3145728 | tf_op jit(solution)/shard_map/psum | solution.py:34
  7.2 9.2 %copy-start.3 = (bf16[512,1024]{1,0:T(8,128)(2,1)S(1)}, bf16[512,1024]{1,0:T(8,128)(2,1)}, u32[]{:S(2)}) copy-start(bf16[512,1024]{1,0:T(8,128)(2,1)} %param.8) | copy-start | bytes 3145732
  16.4 3.3 copy-start.1
  350.9 1.6 copy-start.2
Sparse Core Ops, SparseCore 0:
  356.3 142.5 all-reduce.3
where the time goes:
time: 509 us
  blocking collectives  329 us (65%)
  waiting for transfers between devices  143 us (28%)
  matrix products  15.4 us (3%)
  between operations  14.1 us (3%)
    psum x1, blocking collectives, shards(): act_sum, grad_sum = lax.psum((act_part, grad_part), 'tensor')  329 us
    psum x1, waiting for transfers between devices, shards(): lax.psum(jnp.concatenate([term_a, term_g, term_s], axis=1) * scale, 'dp')  143 us
  transfers between devices with their start and end apart: 1, of which 1 were waited for; matrix products, arithmetic and copies ran while one was open for 0% of the time, Pallas kernels for 0%

commit v1 on v0

v1 whole, which is shorter than its diff:
```python
import jax
import jax.numpy as jnp
from jax import lax
from jax.experimental import pallas as pl
from jax.experimental.pallas import tpu as pltpu
from jax.sharding import Mesh
from jax.sharding import PartitionSpec as P

BF = jnp.bfloat16
F32 = jnp.float32
I16 = jnp.int16

SLOT = 72
KEEP = SLOT - 1
BLOCKS = 8
ROWS = SLOT * BLOCKS
CAP = KEEP * BLOCKS
TOP = 32767.0
HOPS = (1, 3, 2)
VMEM = pltpu.CompilerParams(vmem_limit_bytes=56 * 1024 * 1024)


def ring(dist):
    return [(i, (i + dist) % 4) for i in range(4)]


SWAP = [(0, 1), (1, 0)]


def last_row(shape):
    return lax.broadcasted_iota(jnp.int32, shape, len(shape) - 2) % SLOT == KEEP


def exponent_of(top):
    return jnp.clip(jnp.ceil(jnp.log2(jnp.maximum(top, 1e-37))), -100.0, 100.0)


def encode(x, k):
    y = x * jnp.exp2(-k)
    mag = jnp.abs(y)
    root = y * lax.rsqrt(jnp.maximum(mag, 1e-30))
    q = jnp.round(jnp.clip(root * TOP, -TOP, TOP))
    q = jnp.where(last_row(x.shape), k, q)
    return q.astype(jnp.int32).astype(I16)


def decode(q):
    q = q.astype(F32)
    unit = jnp.exp2(q[KEEP:SLOT, :]) * (1.0 / (TOP * TOP))
    x = q * jnp.abs(q) * unit
    return jnp.where(last_row(x.shape), 0.0, x)


def top_of(x):
    return jnp.max(jnp.max(jnp.abs(x), axis=1, keepdims=True), axis=0, keepdims=True)


def ranks(routed):
    r = routed.astype(F32).astype(BF)
    i = lax.broadcasted_iota(jnp.int32, (128, 128), 0)
    j = lax.broadcasted_iota(jnp.int32, (128, 128), 1)
    within = jnp.dot(r, (i <= j).astype(F32).astype(BF), preferred_element_type=F32)
    totals = jnp.dot(r, jnp.ones((128, 128), BF), preferred_element_type=F32)
    before = jnp.zeros((1, 128), F32)
    offs = []
    for row in range(8):
        offs.append(before)
        before = before + totals[row : row + 1, :]
    pos = within + jnp.concatenate(offs, axis=0) - 1.0
    return jnp.where(routed > 0, pos, -1.0), before


def build_select(sel_ref, pos, blocks):
    row = lax.broadcasted_iota(jnp.int32, (ROWS, 128), 0)
    base = jnp.zeros((ROWS, 128), jnp.int32)
    for b, q in enumerate(blocks):
        inside = (row >= b * SLOT) & (row < (b + 1) * SLOT)
        base = jnp.where(inside, q * KEEP - b * SLOT, base)
    want = jnp.where(row % SLOT == KEEP, -2, base + row).astype(F32)
    for c in range(8):
        sel_ref[:, c * 128 : (c + 1) * 128] = (want == pos[c : c + 1, :]).astype(F32).astype(BF)


def grads_kernel(routed_ref, g_ref, b_ref, send_ref, keep_ref, sel_ref, out_ref):
    z, xl = lax.axis_index("z"), lax.axis_index("xl")
    pos, _ = ranks(routed_ref[...])
    zs = [lax.rem(z + d, 4) for d in (0,) + HOPS]
    build_select(sel_ref, pos, [zz * 2 + (1 - xl) for zz in zs] + [zz * 2 + xl for zz in zs])
    picked = jnp.dot(sel_ref[...], g_ref[...], preferred_element_type=F32).astype(BF)
    out_ref[...] = jnp.dot(picked, b_ref[...], preferred_element_type=F32)
    k = exponent_of(top_of(out_ref[: 4 * SLOT, :]))
    for b in range(4):
        send_ref[b] = encode(out_ref[b * SLOT : (b + 1) * SLOT, :], k)
        keep_ref[b] = out_ref[(4 + b) * SLOT : (5 + b) * SLOT, :]


def acts_kernel(routed_ref, h_ref, b_ref, s1_ref, s2_ref, s3_ref, keep_ref, bad_ref, sel_ref, out_ref):
    step = pl.program_id(0)

    @pl.when(step == 0)
    def _():
        z, xl = lax.axis_index("z"), lax.axis_index("xl")
        pos, total = ranks(routed_ref[...])
        bad_ref[...] = jnp.broadcast_to(jnp.where(total > CAP, jnp.nan, 0.0), (8, 128))
        blocks = []
        for d in HOPS + (0,):
            zz = lax.rem(z + d, 4)
            blocks += [zz * 2 + xl, zz * 2 + (1 - xl)]
        build_select(sel_ref, pos, blocks)

    picked = jnp.dot(sel_ref[...], h_ref[...], preferred_element_type=F32).astype(BF)
    part = jnp.dot(picked, b_ref[...], preferred_element_type=F32)

    @pl.when(step == 0)
    def _():
        out_ref[...] = part

    @pl.when(step > 0)
    def _():
        out_ref[...] += part

    @pl.when(step == pl.num_programs(0) - 1)
    def _():
        k = exponent_of(top_of(out_ref[: 6 * SLOT, :]))
        for b in range(2):
            for n, s_ref in enumerate((s1_ref, s2_ref, s3_ref)):
                at = (2 * n + b) * SLOT
                s_ref[b] = encode(out_ref[at : at + SLOT, :], k)
            keep_ref[b] = out_ref[(6 + b) * SLOT : (7 + b) * SLOT, :]


def grads_mid_kernel(keep_ref, got_ref, own_ref, s1_ref, s2_ref, s3_ref, tmp_ref):
    own_ref[...] = keep_ref[0] + decode(got_ref[0])
    for b in range(3):
        tmp_ref[b] = keep_ref[b + 1] + decode(got_ref[b + 1])
    top = top_of(tmp_ref[0])
    for b in (1, 2):
        top = jnp.maximum(top, top_of(tmp_ref[b]))
    k = exponent_of(top)
    for b, s_ref in enumerate((s1_ref, s2_ref, s3_ref)):
        s_ref[...] = encode(tmp_ref[b], k)


def acts_mid_kernel(keep_ref, r1_ref, r2_ref, r3_ref, own_ref, send_ref):
    own_ref[...] = keep_ref[0] + decode(r1_ref[0]) + decode(r2_ref[0]) + decode(r3_ref[0])
    other = keep_ref[1] + decode(r1_ref[1]) + decode(r2_ref[1]) + decode(r3_ref[1])
    send_ref[...] = encode(other, exponent_of(top_of(other)))


def grads_end_kernel(own_ref, r1_ref, r2_ref, r3_ref, rot_ref):
    x = own_ref[...] + decode(r1_ref[...]) + decode(r2_ref[...]) + decode(r3_ref[...])
    rot_ref[...] = x.astype(BF)


def acts_end_kernel(own_ref, got_ref, bad_ref, rot_ref):
    x = own_ref[...] + decode(got_ref[...]) + bad_ref[0:1, 0:1]
    rot_ref[...] = x.astype(BF)


PAD = 80


def gram_kernel(scale, a0, a1, a2, a3, g0, g1, g2, g3, out_ref, a_s, g_s):
    for s, refs in ((a_s, (a0, a1, a2, a3)), (g_s, (g0, g1, g2, g3))):
        for n, ref in enumerate(refs):
            s[n * PAD : n * PAD + SLOT, :] = ref[...]
            s[n * PAD + SLOT : (n + 1) * PAD, :] = jnp.zeros((PAD - SLOT, s.shape[1]), BF)
    y = lax.axis_index("y")
    rows = pl.ds(pl.multiple_of(y * 256, 256), 256)
    contract = (((0,), (0,)), ((), ()))

    def put(n, lhs, rhs):
        t = lax.dot_general(lhs, rhs, contract, preferred_element_type=F32) * scale
        t = t.astype(BF)
        for rb in range(4):
            for cb in range(8):
                out_ref[rb * 8 + cb, :, n * 128 : (n + 1) * 128] = t[rb * 64 : (rb + 1) * 64, cb * 128 : (cb + 1) * 128]

    def square(v):
        v = v.astype(F32)
        return (v * v).astype(BF)

    put(1, g_s[:, rows], g_s[...])
    put(0, a_s[:, rows], a_s[...])
    put(2, square(a_s[:, rows]), square(g_s[...]))


def final_kernel(in_ref, a_ref, g_ref, c_ref):
    t = in_ref[0].astype(F32)
    for n in range(1, 32):
        t = t + in_ref[n].astype(F32)
    a_ref[...] = t[:, :128]
    g_ref[...] = t[:, 128:256]
    c_ref[...] = t[:, 256:]


def sds(shape, dtype):
    return jax.ShapeDtypeStruct(shape, dtype)


def cost(flops, nbytes):
    return pl.CostEstimate(flops=flops, bytes_accessed=nbytes, transcendentals=0)


def fast(hidden_acts, act_basis, out_grads, grad_basis, routed):
    width = act_basis.shape[1]
    feats = hidden_acts.shape[1]
    tokens = hidden_acts.shape[0] * 16
    slots = routed.reshape(8, 128)
    blk = (SLOT, width)
    vmem = pl.BlockSpec(memory_space=pltpu.VMEM)

    g_send, g_keep = pl.pallas_call(
        grads_kernel,
        out_shape=(sds((4,) + blk, I16), sds((4,) + blk, F32)),
        in_specs=[vmem] * 3,
        out_specs=(vmem, vmem),
        scratch_shapes=[pltpu.VMEM((ROWS, 1024), BF), pltpu.VMEM((ROWS, width), F32)],
        compiler_params=VMEM,
        cost_estimate=cost(1_300_000_000, 4_000_000),
        name="grads",
    )(slots, out_grads, grad_basis)
    g_got = lax.ppermute(g_send, "xl", SWAP)

    step = 256
    *a_send, a_keep, bad = pl.pallas_call(
        acts_kernel,
        grid=(feats // step,),
        out_shape=(sds((2,) + blk, I16),) * 3 + (sds((2,) + blk, F32), sds((8, 128), F32)),
        in_specs=[
            pl.BlockSpec((8, 128), lambda i: (0, 0)),
            pl.BlockSpec((1024, step), lambda i: (0, i)),
            pl.BlockSpec((step, width), lambda i: (i, 0)),
        ],
        out_specs=(pl.BlockSpec((2,) + blk, lambda i: (0, 0, 0)),) * 4 + (pl.BlockSpec((8, 128), lambda i: (0, 0)),),
        scratch_shapes=[pltpu.VMEM((ROWS, 1024), BF), pltpu.VMEM((ROWS, width), F32)],
        compiler_params=VMEM,
        cost_estimate=cost(4_300_000_000, 9_000_000),
        name="acts",
    )(slots, hidden_acts, act_basis)
    a_got = [lax.ppermute(s, "z", ring(d)) for s, d in zip(a_send, HOPS)]

    g_own, *g_next = pl.pallas_call(
        grads_mid_kernel,
        out_shape=(sds(blk, F32),) + (sds(blk, I16),) * 3,
        in_specs=[vmem] * 2,
        out_specs=(vmem,) * 4,
        scratch_shapes=[pltpu.VMEM((3,) + blk, F32)],
        compiler_params=VMEM,
        name="grads_mid",
    )(g_keep, g_got)
    g_last = [lax.ppermute(s, "z", ring(d)) for s, d in zip(g_next, HOPS)]

    a_own, a_next = pl.pallas_call(
        acts_mid_kernel,
        out_shape=(sds(blk, F32), sds(blk, I16)),
        in_specs=[vmem] * 4,
        out_specs=(vmem,) * 2,
        compiler_params=VMEM,
        name="acts_mid",
    )(a_keep, *a_got)
    a_last = lax.ppermute(a_next, "xl", SWAP)

    rot_g = pl.pallas_call(
        grads_end_kernel,
        out_shape=sds(blk, BF),
        in_specs=[vmem] * 4,
        out_specs=vmem,
        compiler_params=VMEM,
        name="grads_end",
    )(g_own, *g_last)
    all_g = [rot_g] + [lax.ppermute(rot_g, "y", ring(d)) for d in HOPS]

    rot_a = pl.pallas_call(
        acts_end_kernel,
        out_shape=sds(blk, BF),
        in_specs=[vmem] * 3,
        out_specs=vmem,
        compiler_params=VMEM,
        name="acts_end",
    )(a_own, a_last, bad)
    all_a = [rot_a] + [lax.ppermute(rot_a, "y", ring(d)) for d in HOPS]

    parts = pl.pallas_call(
        lambda *refs: gram_kernel(1.0 / tokens, *refs),
        out_shape=sds((32, 64, 384), BF),
        in_specs=[vmem] * 8,
        out_specs=vmem,
        scratch_shapes=[pltpu.VMEM((4 * PAD, width), BF)] * 2,
        compiler_params=VMEM,
        name="gram",
    )(*all_a, *all_g)
    got = lax.all_to_all(parts, ("xh", "core", "z", "xl"), 0, 0, tiled=True)

    return pl.pallas_call(
        final_kernel,
        out_shape=(sds((64, 128), F32),) * 3,
        in_specs=[vmem],
        out_specs=(vmem,) * 3,
        compiler_params=VMEM,
        name="final",
    )(got)


DP = ("y", "xh", "core")
TENSOR = ("z", "xl")


def general(hidden_acts, act_basis, out_grads, grad_basis, routed):
    act_part = jnp.dot(hidden_acts, act_basis, preferred_element_type=F32)
    grad_part = jnp.dot(out_grads, grad_basis, preferred_element_type=F32)
    act_sum, grad_sum = lax.psum((act_part, grad_part), TENSOR)
    rot_acts = act_sum.astype(BF)
    rot_grads = grad_sum.astype(BF)
    total_tokens = rot_acts.shape[0] * 16
    weights = routed.astype(F32)[:, None]
    acts_f = rot_acts.astype(F32)
    grads_f = rot_grads.astype(F32)
    masked_acts = (acts_f * weights).astype(BF)
    masked_grads = (grads_f * weights).astype(BF)
    sq_acts = (acts_f * acts_f * weights).astype(BF)
    sq_grads = (grads_f * grads_f).astype(BF)
    col_width = rot_acts.shape[1] // 8
    col_start = (lax.axis_index("z") * 2 + lax.axis_index("xl")) * col_width
    own_rows = rot_acts.shape[1] // 16
    row_start = ((lax.axis_index("y") * 2 + lax.axis_index("xh")) * 2 + lax.axis_index("core")) * own_rows
    contract = (((0,), (0,)), ((), ()))
    terms = []
    for left, right in ((masked_acts, rot_acts), (masked_grads, rot_grads), (sq_acts, sq_grads)):
        cols = lax.dynamic_slice_in_dim(right, col_start, col_width, 1)
        terms.append(lax.dot_general(left, cols, contract, preferred_element_type=F32))
    summed = lax.psum(jnp.concatenate(terms, axis=1) * (1.0 / total_tokens), DP)
    owned = lax.dynamic_slice_in_dim(summed, row_start, own_rows, 0)
    return tuple(owned[:, n * col_width : (n + 1) * col_width] for n in range(3))


def shards(*args):
    act_gram, grad_gram, correction = fast(*args)
    whole = jnp.abs(act_gram[0, 0]) < 1e30
    return lax.cond(whole, lambda *_: (act_gram, grad_gram, correction), general, *args)


def solution(mesh):
    fine = Mesh(mesh.devices.reshape(4, 2, 2, 4, 2), ("y", "xh", "core", "z", "xl"))
    return jax.shard_map(
        shards,
        mesh=fine,
        in_specs=(P(DP, TENSOR), P(TENSOR, None), P(DP, TENSOR), P(TENSOR, None), P(DP)),
        out_specs=(P(DP, TENSOR),) * 3,
        check_vma=False,
    )
```

time: 509 us -> 127 us (0.25)
  blocking collectives: 329 us -> 0 us
  waiting for transfers between devices: 143 us -> 39.9 us
  Pallas kernels: 0 us -> 34.9 us
  starting transfers between devices: 0.04 us -> 28.4 us
  matrix products: 15.4 us -> 0 us
    psum x1 -> x0, blocking collectives: 329 us -> none  [shards(): act_sum, grad_sum = lax.psum((act_part, grad_part), 'tensor')]
    psum x1 -> x0, waiting for transfers between devices: 143 us -> none  [shards(): lax.psum(jnp.concatenate([term_a, term_g, term_s], axis=1) * scale, 'dp')]
    pallas_call x0 -> x8, Pallas kernels: none -> 34.9 us  [the longest x1 15.2 us: fast(): pl.pallas_call(acts_kernel, grid=(feats // step,), out_shape=(sds((2,) +...]
    all_to_all x0 -> x1, waiting for transfers between devices: none -> 21.4 us  [fast(): got = lax.all_to_all(parts, ('xh', 'core', 'z', 'xl'), 0, 0, tiled=True)]
    ppermute x0 -> x14, starting transfers between devices: none -> 20.8 us  [the longest x3 5.91 us: fast(): a_got = [lax.ppermute(s, 'z', ring(d)) for s, d in zip(a_send, HOPS)]]
    ppermute x0 -> x14, waiting for transfers between devices: none -> 18.5 us  [the longest x3 12.6 us: fast(): a_got = [lax.ppermute(s, 'z', ring(d)) for s, d in zip(a_send, HOPS)]]
    dot_general x5 -> x0, matrix products: 15.4 us -> none  [the longest x1 9.17 us: shards(): jnp.dot(hidden_acts, act_basis, preferred_element_type=jnp.float32)]
    all_to_all x0 -> x1, starting transfers between devices: none -> 7.62 us  [fast(): got = lax.all_to_all(parts, ('xh', 'core', 'z', 'xl'), 0, 0, tiled=True)]
  transfers between devices with their start and end apart: 1 -> 15, of which waited for: 1 -> 7; matrix products, arithmetic and copies ran while one was open for 0% -> 0% of each run, Pallas kernels for 0% -> 20%
where the time goes in v1:
time: 127 us; the launch traced here: 125 us
  waiting for transfers between devices  39.9 us (31%)
  Pallas kernels  34.9 us (27%)
  starting transfers between devices  28.4 us (22%)
  between operations  14.8 us (12%)
  local copies, waits for them, and re-layouts  7.09 us (6%)
    all_to_all x1, waiting for transfers between devices, fast(): got = lax.all_to_all(parts, ('xh', 'core', 'z', 'xl'), 0, 0, tiled=True)  21.4 us
    pallas_call x1, Pallas kernels, fast(): pl.pallas_call(acts_kernel, grid=(feats // step,), out_shape=(sds((2,) +...  15.2 us
    ppermute x3, waiting for transfers between devices, fast(): a_got = [lax.ppermute(s, 'z', ring(d)) for s, d in zip(a_send, HOPS)]  12.6 us
    all_to_all x1, starting transfers between devices, fast(): got = lax.all_to_all(parts, ('xh', 'core', 'z', 'xl'), 0, 0, tiled=True)  7.62 us
    unnamed x42, local copies, waits for them, and re-layouts  6.58 us
    ppermute x3, waiting for transfers between devices, fast(): all_g = [rot_g] + [lax.ppermute(rot_g, 'y', ring(d)) for d in HOPS]  5.91 us
    ppermute x3, starting transfers between devices, fast(): a_got = [lax.ppermute(s, 'z', ring(d)) for s, d in zip(a_send, HOPS)]  5.91 us
    ppermute x3, starting transfers between devices, fast(): all_a = [rot_a] + [lax.ppermute(rot_a, 'y', ring(d)) for d in HOPS]  5.22 us
  transfers between devices with their start and end apart: 15, of which 7 were waited for; matrix products, arithmetic and copies ran while one was open for 0% of the time, Pallas kernels for 20%

profile of v1, /device:TPU:0, one launch (start us, length us, event | category | flops | bytes accessed | tf_op | source)
XLA Modules:
  0.0 125.0 jit_solution(15649218799704795936)
XLA Ops:
  7.2 4.7 %grads.1 = (s16[4,72,1024]{2,1,0:T(8,128)(2,1)}, f32[4,72,1024]{2,1,0:T(8,128)}) custom-call(s32[8,128]{1,0:T(8,128)} %bitcast.6, bf16[1024,512]{1,0:T(8,128)(2,1)} %g_ref.1, bf16[512,1024]{1,0:T(8,128)(2,1)} %b_ref.3), custom_call_target="tpu_custom_call" | custom-call | flops 1300000000 | bytes 4000000 | tf_op jit(solution)/shard_map/grads/pallas_call | solution.py:213
  11.9 1.6 %collective-permute-start.7 = (s16[4,72,1024]{2,1,0:T(8,128)(2,1)}, s16[4,72,1024]{2,1,0:T(8,128)(2,1)S(1)}, u32[]{:S(2)}, u32[]{:S(2)}) collective-permute-start(s16[4,72,1024]{2,1,0:T(8,128)(2,1)} %get-tuple-element.46), channel_id=1, source_target_pairs={{0,1},{1,0},{2,3},{3,2},{4,5},{5,4},{6,7},{7,6},{8,9},{9,8},{10,11... | collective-permute-start | bytes 1769480 | tf_op jit(solution)/shard_map/ppermute | solution.py:223
  13.4 15.2 %acts.1 = (s16[2,72,1024]{2,1,0:T(8,128)(2,1)}, s16[2,72,1024]{2,1,0:T(8,128)(2,1)}, s16[2,72,1024]{2,1,0:T(8,128)(2,1)}, f32[2,72,1024]{2,1,0:T(8,128)}, f32[8,128]{1,0:T(8,128)}) custom-call(s32[8,128]{1,0:T(8,128)S(1)} %bitcast.7, bf16[1024,1792]{1,0:T(8,128)(2,1)S(1)} %copy-done.16, bf16[1792,1024]{1,0:T(8,128)(2,1)} %b_ref.2), custom_call_target="tpu_custom_call" | custom-call | flops 4300000256 | bytes 9000000 | tf_op jit(solution)/shard_map/acts/pallas_call | solution.py:226
  28.7 1.9 %collective-permute-start = (s16[2,72,1024]{2,1,0:T(8,128)(2,1)}, s16[2,72,1024]{2,1,0:T(8,128)(2,1)S(1)}, u32[]{:S(2)}, u32[]{:S(2)}) collective-permute-start(s16[2,72,1024]{2,1,0:T(8,128)(2,1)} %get-tuple-element.39), channel_id=1, source_target_pairs={{0,2},{2,4},{4,6},{6,0},{1,3},{3,5},{5,7},{7,1},{8,10},{10,12},{12... | collective-permute-start | bytes 884744 | tf_op jit(solution)/shard_map/ppermute | solution.py:241
  30.6 2.2 %collective-permute-start.1 = (s16[2,72,1024]{2,1,0:T(8,128)(2,1)}, s16[2,72,1024]{2,1,0:T(8,128)(2,1)S(1)}, u32[]{:S(2)}, u32[]{:S(2)}) collective-permute-start(s16[2,72,1024]{2,1,0:T(8,128)(2,1)} %get-tuple-element.40), channel_id=1, source_target_pairs={{0,6},{2,0},{4,2},{6,4},{1,7},{3,1},{5,3},{7,5},{8,14},{10,8},{12,... | collective-permute-start | bytes 884744 | tf_op jit(solution)/shard_map/ppermute | solution.py:241
  32.8 1.8 %collective-permute-start.2 = (s16[2,72,1024]{2,1,0:T(8,128)(2,1)}, s16[2,72,1024]{2,1,0:T(8,128)(2,1)S(1)}, u32[]{:S(2)}, u32[]{:S(2)}) collective-permute-start(s16[2,72,1024]{2,1,0:T(8,128)(2,1)} %get-tuple-element.41), channel_id=1, source_target_pairs={{0,4},{2,6},{4,0},{6,2},{1,5},{3,7},{5,1},{7,3},{8,12},{10,14},{12... | collective-permute-start | bytes 884744 | tf_op jit(solution)/shard_map/ppermute | solution.py:241
  34.6 5.4 %collective-permute-done.r1_ref = s16[2,72,1024]{2,1,0:T(8,128)(2,1)S(1)} collective-permute-done((s16[2,72,1024]{2,1,0:T(8,128)(2,1)}, s16[2,72,1024]{2,1,0:T(8,128)(2,1)S(1)}, u32[]{:S(2)}, u32[]{:S(2)}) %collective-permute-start) | collective-permute-done | bytes 294944 | tf_op jit(solution)/shard_map/ppermute | solution.py:241
  39.9 5.5 %collective-permute-done.1.r2_ref = s16[2,72,1024]{2,1,0:T(8,128)(2,1)S(1)} collective-permute-done((s16[2,72,1024]{2,1,0:T(8,128)(2,1)}, s16[2,72,1024]{2,1,0:T(8,128)(2,1)S(1)}, u32[]{:S(2)}, u32[]{:S(2)}) %collective-permute-start.1) | collective-permute-done | bytes 294944 | tf_op jit(solution)/shard_map/ppermute | solution.py:241
  45.4 1.7 %collective-permute-done.2.r3_ref = s16[2,72,1024]{2,1,0:T(8,128)(2,1)S(1)} collective-permute-done((s16[2,72,1024]{2,1,0:T(8,128)(2,1)}, s16[2,72,1024]{2,1,0:T(8,128)(2,1)S(1)}, u32[]{:S(2)}, u32[]{:S(2)}) %collective-permute-start.2) | collective-permute-done | bytes 294944 | tf_op jit(solution)/shard_map/ppermute | solution.py:241
  47.2 0.7 copy-done.4
  47.9 2.8 %acts_mid.1 = (f32[72,1024]{1,0:T(8,128)}, s16[72,1024]{1,0:T(8,128)(2,1)}) custom-call(f32[2,72,1024]{2,1,0:T(8,128)} %get-tuple-element.38.keep_ref, s16[2,72,1024]{2,1,0:T(8,128)(2,1)} %copy-done.2, s16[2,72,1024]{2,1,0:T(8,128)(2,1)} %copy-done.3, s16[2,72,1024]{2,1,0:T(8,128)(2,1)} %copy-done.4), custom_call_target="tpu_custom_call" | custom-call | tf_op jit(solution)/shard_map/acts_mid/pallas_call | solution.py:254
  51.2 0.8 copy-done.1
  52.0 3.0 %grads_mid.1 = (f32[72,1024]{1,0:T(8,128)}, s16[72,1024]{1,0:T(8,128)(2,1)}, s16[72,1024]{1,0:T(8,128)(2,1)}, s16[72,1024]{1,0:T(8,128)(2,1)}) custom-call(f32[4,72,1024]{2,1,0:T(8,128)} %get-tuple-element.45.keep_ref, s16[4,72,1024]{2,1,0:T(8,128)(2,1)} %copy-done.1), custom_call_target="tpu_custom_call" | custom-call | tf_op jit(solution)/shard_map/grads_mid/pallas_call | solution.py:243
  55.0 1.1 collective-permute-start.8
  56.1 2.1 %collective-permute-start.9 = (s16[72,1024]{1,0:T(8,128)(2,1)}, s16[72,1024]{1,0:T(8,128)(2,1)S(1)}, u32[]{:S(2)}, u32[]{:S(2)}) collective-permute-start(s16[72,1024]{1,0:T(8,128)(2,1)} %get-tuple-element.49), channel_id=1, source_target_pairs={{0,6},{2,0},{4,2},{6,4},{1,7},{3,1},{5,3},{7,5},{8,14},{10,8},{12,... | collective-permute-start | bytes 442376 | tf_op jit(solution)/shard_map/ppermute | solution.py:252
  59.1 1.8 %acts_end.1.refs_0_ = bf16[72,1024]{1,0:T(8,128)(2,1)} custom-call(f32[72,1024]{1,0:T(8,128)} %get-tuple-element.42.own_ref, s16[72,1024]{1,0:T(8,128)(2,1)} %copy-done.8, f32[8,128]{1,0:T(8,128)} %get-tuple-element.44.bad_ref), custom_call_target="tpu_custom_call" | custom-call | tf_op jit(solution)/shard_map/acts_end/pallas_call | solution.py:274
  60.9 1.6 %collective-permute-start.4 = (bf16[72,1024]{1,0:T(8,128)(2,1)}, bf16[72,1024]{1,0:T(8,128)(2,1)S(1)}, u32[]{:S(2)}, u32[]{:S(2)}) collective-permute-start(bf16[72,1024]{1,0:T(8,128)(2,1)} %acts_end.1.refs_0_), channel_id=1, source_target_pairs={{0,32},{32,64},{64,96},{96,0},{1,33},{33,65},{65,97},{97,1},{2,34}... | collective-permute-start | bytes 442376 | tf_op jit(solution)/shard_map/ppermute | solution.py:282
  62.5 1.7 %collective-permute-start.5 = (bf16[72,1024]{1,0:T(8,128)(2,1)}, bf16[72,1024]{1,0:T(8,128)(2,1)S(1)}, u32[]{:S(2)}, u32[]{:S(2)}) collective-permute-start(bf16[72,1024]{1,0:T(8,128)(2,1)} %acts_end.1.refs_0_), channel_id=1, source_target_pairs={{0,96},{32,0},{64,32},{96,64},{1,97},{33,1},{65,33},{97,65},{2,98}... | collective-permute-start | bytes 442376 | tf_op jit(solution)/shard_map/ppermute | solution.py:282
  64.1 2.0 %collective-permute-start.6 = (bf16[72,1024]{1,0:T(8,128)(2,1)}, bf16[72,1024]{1,0:T(8,128)(2,1)S(1)}, u32[]{:S(2)}, u32[]{:S(2)}) collective-permute-start(bf16[72,1024]{1,0:T(8,128)(2,1)} %acts_end.1.refs_0_), channel_id=1, source_target_pairs={{0,64},{32,96},{64,0},{96,32},{1,65},{33,97},{65,1},{97,33},{2,66}... | collective-permute-start | bytes 442376 | tf_op jit(solution)/shard_map/ppermute | solution.py:282
  66.8 2.0 %grads_end.1.refs_4_ = bf16[72,1024]{1,0:T(8,128)(2,1)} custom-call(f32[72,1024]{1,0:T(8,128)} %get-tuple-element.47.own_ref, s16[72,1024]{1,0:T(8,128)(2,1)} %copy-done.5, s16[72,1024]{1,0:T(8,128)(2,1)} %copy-done.6, s16[72,1024]{1,0:T(8,128)(2,1)} %copy-done.7), custom_call_target="tpu_custom_call" | custom-call | tf_op jit(solution)/shard_map/grads_end/pallas_call | solution.py:264
  68.9 0.7 collective-permute-start.11
  69.5 2.6 %collective-permute-start.12 = (bf16[72,1024]{1,0:T(8,128)(2,1)}, bf16[72,1024]{1,0:T(8,128)(2,1)S(1)}, u32[]{:S(2)}, u32[]{:S(2)}) collective-permute-start(bf16[72,1024]{1,0:T(8,128)(2,1)} %grads_end.1.refs_4_), channel_id=1, source_target_pairs={{0,96},{32,0},{64,32},{96,64},{1,97},{33,1},{65,33},{97,65},{2,98}... | collective-permute-start | bytes 442376 | tf_op jit(solution)/shard_map/ppermute | solution.py:272
  72.1 0.9 collective-permute-start.13
  73.0 3.0 %collective-permute-done.11.refs_5_ = bf16[72,1024]{1,0:T(8,128)(2,1)S(1)} collective-permute-done((bf16[72,1024]{1,0:T(8,128)(2,1)}, bf16[72,1024]{1,0:T(8,128)(2,1)S(1)}, u32[]{:S(2)}, u32[]{:S(2)}) %collective-permute-start.11) | collective-permute-done | bytes 147488 | tf_op jit(solution)/shard_map/ppermute | solution.py:272
  76.0 0.7 collective-permute-done.12.refs_6_
  76.7 2.3 %collective-permute-done.13.refs_7_ = bf16[72,1024]{1,0:T(8,128)(2,1)S(1)} collective-permute-done((bf16[72,1024]{1,0:T(8,128)(2,1)}, bf16[72,1024]{1,0:T(8,128)(2,1)S(1)}, u32[]{:S(2)}, u32[]{:S(2)}) %collective-permute-start.13) | collective-permute-done | bytes 147488 | tf_op jit(solution)/shard_map/ppermute | solution.py:272
  79.0 0.7 copy-done.14
  79.7 3.7 %gram.1 = bf16[32,64,384]{2,1,0:T(8,128)(2,1)} custom-call(bf16[72,1024]{1,0:T(8,128)(2,1)} %acts_end.1.refs_0_, bf16[72,1024]{1,0:T(8,128)(2,1)} %copy-done.9, bf16[72,1024]{1,0:T(8,128)(2,1)} %copy-done.10, bf16[72,1024]{1,0:T(8,128)(2,1)} %copy-done.11, bf16[72,1024]{1,0:T(8,128)(2,1)} %grads_end.1.refs_4_, bf16[72,1024]{1,0:T(8,128)(2,1)} %copy-done.12, ...), custom_call_target="tpu_custom_call" | custom-call | tf_op jit(solution)/shard_map/gram/pallas_call | solution.py:284
  83.3 7.6 %all-to-all-start = ((bf16[32,64,384]{2,1,0:T(8,128)(2,1)}), bf16[32,64,384]{2,1,0:T(8,128)(2,1)S(1)}, u32[]{:S(2)}, u32[]{:S(2)}) async-start(bf16[32,64,384]{2,1,0:T(8,128)(2,1)} %gram.1), calls=%async_computation | async-start | bytes 3145728 | tf_op jit(solution)/shard_map/all_to_all | solution.py:293
  91.0 21.4 %all-to-all-done.in_ref = bf16[32,64,384]{2,1,0:T(8,128)(2,1)S(1)} async-done(((bf16[32,64,384]{2,1,0:T(8,128)(2,1)}), bf16[32,64,384]{2,1,0:T(8,128)(2,1)S(1)}, u32[]{:S(2)}, u32[]{:S(2)}) %all-to-all-start) | async-done | bytes 1572896 | tf_op jit(solution)/shard_map/all_to_all | solution.py:293
  112.3 1.2 copy-done
  113.5 1.6 %final.1 = (f32[64,128]{1,0:T(8,128)S(1)}, f32[64,128]{1,0:T(8,128)S(1)}, f32[64,128]{1,0:T(8,128)S(1)}) custom-call(bf16[32,64,384]{2,1,0:T(8,128)(2,1)} %copy-done), custom_call_target="tpu_custom_call" | custom-call | tf_op jit(solution)/shard_map/final/pallas_call | solution.py:295
  (50 shorter events, 4.5 us)
Async XLA Ops:
  7.2 6.3 %copy-start.15 = (s32[1024]{0:T(1024)S(1)}, s32[1024]{0:T(1024)}, u32[]{:S(2)}) copy-start(s32[1024]{0:T(1024)} %param.11) | copy-start | bytes 12292
  7.2 6.3 %copy-start.16 = (bf16[1024,1792]{1,0:T(8,128)(2,1)S(1)}, bf16[1024,1792]{1,0:T(8,128)(2,1)}, u32[]{:S(2)}) copy-start(bf16[1024,1792]{1,0:T(8,128)(2,1)} %h_ref.1) | copy-start | bytes 11010052
  11.9 39.4 %collective-permute-start.7 = (s16[4,72,1024]{2,1,0:T(8,128)(2,1)}, s16[4,72,1024]{2,1,0:T(8,128)(2,1)S(1)}, u32[]{:S(2)}, u32[]{:S(2)}) collective-permute-start(s16[4,72,1024]{2,1,0:T(8,128)(2,1)} %get-tuple-element.46), channel_id=1, source_target_pairs={{0,1},{1,0},{2,3},{3,2},{4,5},{5,4},{6,7},{7,6},{8,9},{9,8},{10,11... | collective-permute-start | bytes 1769480 | tf_op jit(solution)/shard_map/ppermute | solution.py:223
  28.7 11.3 %collective-permute-start = (s16[2,72,1024]{2,1,0:T(8,128)(2,1)}, s16[2,72,1024]{2,1,0:T(8,128)(2,1)S(1)}, u32[]{:S(2)}, u32[]{:S(2)}) collective-permute-start(s16[2,72,1024]{2,1,0:T(8,128)(2,1)} %get-tuple-element.39), channel_id=1, source_target_pairs={{0,2},{2,4},{4,6},{6,0},{1,3},{3,5},{5,7},{7,1},{8,10},{10,12},{12... | collective-permute-start | bytes 884744 | tf_op jit(solution)/shard_map/ppermute | solution.py:241
  30.6 14.8 %collective-permute-start.1 = (s16[2,72,1024]{2,1,0:T(8,128)(2,1)}, s16[2,72,1024]{2,1,0:T(8,128)(2,1)S(1)}, u32[]{:S(2)}, u32[]{:S(2)}) collective-permute-start(s16[2,72,1024]{2,1,0:T(8,128)(2,1)} %get-tuple-element.40), channel_id=1, source_target_pairs={{0,6},{2,0},{4,2},{6,4},{1,7},{3,1},{5,3},{7,5},{8,14},{10,8},{12,... | collective-permute-start | bytes 884744 | tf_op jit(solution)/shard_map/ppermute | solution.py:241
  32.8 14.4 %collective-permute-start.2 = (s16[2,72,1024]{2,1,0:T(8,128)(2,1)}, s16[2,72,1024]{2,1,0:T(8,128)(2,1)S(1)}, u32[]{:S(2)}, u32[]{:S(2)}) collective-permute-start(s16[2,72,1024]{2,1,0:T(8,128)(2,1)} %get-tuple-element.41), channel_id=1, source_target_pairs={{0,4},{2,6},{4,0},{6,2},{1,5},{3,7},{5,1},{7,3},{8,12},{10,14},{12... | collective-permute-start | bytes 884744 | tf_op jit(solution)/shard_map/ppermute | solution.py:241
  39.9 7.2 %copy-start.2 = (s16[2,72,1024]{2,1,0:T(8,128)(2,1)}, s16[2,72,1024]{2,1,0:T(8,128)(2,1)S(1)}, u32[]{:S(2)}) copy-start(s16[2,72,1024]{2,1,0:T(8,128)(2,1)S(1)} %collective-permute-done.r1_ref) | copy-start | bytes 884740
  45.4 1.7 %copy-start.3 = (s16[2,72,1024]{2,1,0:T(8,128)(2,1)}, s16[2,72,1024]{2,1,0:T(8,128)(2,1)S(1)}, u32[]{:S(2)}) copy-start(s16[2,72,1024]{2,1,0:T(8,128)(2,1)S(1)} %collective-permute-done.1.r2_ref) | copy-start | bytes 884740
  47.2 0.7 copy-start.4
  50.7 7.7 %collective-permute-start.3 = (s16[72,1024]{1,0:T(8,128)(2,1)}, s16[72,1024]{1,0:T(8,128)(2,1)S(1)}, u32[]{:S(2)}, u32[]{:S(2)}) collective-permute-start(s16[72,1024]{1,0:T(8,128)(2,1)} %get-tuple-element.43), channel_id=1, source_target_pairs={{0,1},{1,0},{2,3},{3,2},{4,5},{5,4},{6,7},{7,6},{8,9},{9,8},{10,11... | collective-permute-start | bytes 442376 | tf_op jit(solution)/shard_map/ppermute | solution.py:262
  51.2 0.8 copy-start.1
  55.0 9.1 %collective-permute-start.8 = (s16[72,1024]{1,0:T(8,128)(2,1)}, s16[72,1024]{1,0:T(8,128)(2,1)S(1)}, u32[]{:S(2)}, u32[]{:S(2)}) collective-permute-start(s16[72,1024]{1,0:T(8,128)(2,1)} %get-tuple-element.48), channel_id=1, source_target_pairs={{0,2},{2,4},{4,6},{6,0},{1,3},{3,5},{5,7},{7,1},{8,10},{10,12},{12... | collective-permute-start | bytes 442376 | tf_op jit(solution)/shard_map/ppermute | solution.py:252
  56.1 10.0 %collective-permute-start.9 = (s16[72,1024]{1,0:T(8,128)(2,1)}, s16[72,1024]{1,0:T(8,128)(2,1)S(1)}, u32[]{:S(2)}, u32[]{:S(2)}) collective-permute-start(s16[72,1024]{1,0:T(8,128)(2,1)} %get-tuple-element.49), channel_id=1, source_target_pairs={{0,6},{2,0},{4,2},{6,4},{1,7},{3,1},{5,3},{7,5},{8,14},{10,8},{12,... | collective-permute-start | bytes 442376 | tf_op jit(solution)/shard_map/ppermute | solution.py:252
  58.2 7.9 %collective-permute-start.10 = (s16[72,1024]{1,0:T(8,128)(2,1)}, s16[72,1024]{1,0:T(8,128)(2,1)S(1)}, u32[]{:S(2)}, u32[]{:S(2)}) collective-permute-start(s16[72,1024]{1,0:T(8,128)(2,1)} %get-tuple-element.50), channel_id=1, source_target_pairs={{0,4},{2,6},{4,0},{6,2},{1,5},{3,7},{5,1},{7,3},{8,12},{10,14},{12... | collective-permute-start | bytes 442376 | tf_op jit(solution)/shard_map/ppermute | solution.py:252
  60.9 11.2 %collective-permute-start.4 = (bf16[72,1024]{1,0:T(8,128)(2,1)}, bf16[72,1024]{1,0:T(8,128)(2,1)S(1)}, u32[]{:S(2)}, u32[]{:S(2)}) collective-permute-start(bf16[72,1024]{1,0:T(8,128)(2,1)} %acts_end.1.refs_0_), channel_id=1, source_target_pairs={{0,32},{32,64},{64,96},{96,0},{1,33},{33,65},{65,97},{97,1},{2,34}... | collective-permute-start | bytes 442376 | tf_op jit(solution)/shard_map/ppermute | solution.py:282
  62.5 10.6 %collective-permute-start.5 = (bf16[72,1024]{1,0:T(8,128)(2,1)}, bf16[72,1024]{1,0:T(8,128)(2,1)S(1)}, u32[]{:S(2)}, u32[]{:S(2)}) collective-permute-start(bf16[72,1024]{1,0:T(8,128)(2,1)} %acts_end.1.refs_0_), channel_id=1, source_target_pairs={{0,96},{32,0},{64,32},{96,64},{1,97},{33,1},{65,33},{97,65},{2,98}... | collective-permute-start | bytes 442376 | tf_op jit(solution)/shard_map/ppermute | solution.py:282
  64.1 2.0 %copy-start.5 = (s16[72,1024]{1,0:T(8,128)(2,1)}, s16[72,1024]{1,0:T(8,128)(2,1)S(1)}, u32[]{:S(2)}) copy-start(s16[72,1024]{1,0:T(8,128)(2,1)S(1)} %collective-permute-done.8.r1_ref) | copy-start | bytes 442372
  64.1 8.9 %collective-permute-start.6 = (bf16[72,1024]{1,0:T(8,128)(2,1)}, bf16[72,1024]{1,0:T(8,128)(2,1)S(1)}, u32[]{:S(2)}, u32[]{:S(2)}) collective-permute-start(bf16[72,1024]{1,0:T(8,128)(2,1)} %acts_end.1.refs_0_), channel_id=1, source_target_pairs={{0,64},{32,96},{64,0},{96,32},{1,65},{33,97},{65,1},{97,33},{2,66}... | collective-permute-start | bytes 442376 | tf_op jit(solution)/shard_map/ppermute | solution.py:282
  66.1 0.7 copy-start.6
  66.1 0.7 copy-start.7
  68.9 7.2 %collective-permute-start.11 = (bf16[72,1024]{1,0:T(8,128)(2,1)}, bf16[72,1024]{1,0:T(8,128)(2,1)S(1)}, u32[]{:S(2)}, u32[]{:S(2)}) collective-permute-start(bf16[72,1024]{1,0:T(8,128)(2,1)} %grads_end.1.refs_4_), channel_id=1, source_target_pairs={{0,32},{32,64},{64,96},{96,0},{1,33},{33,65},{65,97},{97,1},{2,34}... | collective-permute-start | bytes 442376 | tf_op jit(solution)/shard_map/ppermute | solution.py:272
  69.5 7.2 %collective-permute-start.12 = (bf16[72,1024]{1,0:T(8,128)(2,1)}, bf16[72,1024]{1,0:T(8,128)(2,1)S(1)}, u32[]{:S(2)}, u32[]{:S(2)}) collective-permute-start(bf16[72,1024]{1,0:T(8,128)(2,1)} %grads_end.1.refs_4_), channel_id=1, source_target_pairs={{0,96},{32,0},{64,32},{96,64},{1,97},{33,1},{65,33},{97,65},{2,98}... | collective-permute-start | bytes 442376 | tf_op jit(solution)/shard_map/ppermute | solution.py:272
  72.1 6.9 %copy-start.9 = (bf16[72,1024]{1,0:T(8,128)(2,1)}, bf16[72,1024]{1,0:T(8,128)(2,1)S(1)}, u32[]{:S(2)}) copy-start(bf16[72,1024]{1,0:T(8,128)(2,1)S(1)} %collective-permute-done.4.refs_1_) | copy-start | bytes 442372
  72.1 6.9 %collective-permute-start.13 = (bf16[72,1024]{1,0:T(8,128)(2,1)}, bf16[72,1024]{1,0:T(8,128)(2,1)S(1)}, u32[]{:S(2)}, u32[]{:S(2)}) collective-permute-start(bf16[72,1024]{1,0:T(8,128)(2,1)} %grads_end.1.refs_4_), channel_id=1, source_target_pairs={{0,64},{32,96},{64,0},{96,32},{1,65},{33,97},{65,1},{97,33},{2,66}... | collective-permute-start | bytes 442376 | tf_op jit(solution)/shard_map/ppermute | solution.py:272
  73.0 5.9 %copy-start.10 = (bf16[72,1024]{1,0:T(8,128)(2,1)}, bf16[72,1024]{1,0:T(8,128)(2,1)S(1)}, u32[]{:S(2)}) copy-start(bf16[72,1024]{1,0:T(8,128)(2,1)S(1)} %collective-permute-done.5.refs_2_) | copy-start | bytes 442372
  73.0 5.9 %copy-start.11 = (bf16[72,1024]{1,0:T(8,128)(2,1)}, bf16[72,1024]{1,0:T(8,128)(2,1)S(1)}, u32[]{:S(2)}) copy-start(bf16[72,1024]{1,0:T(8,128)(2,1)S(1)} %collective-permute-done.6.refs_3_) | copy-start | bytes 442372
  76.0 2.9 %copy-start.12 = (bf16[72,1024]{1,0:T(8,128)(2,1)}, bf16[72,1024]{1,0:T(8,128)(2,1)S(1)}, u32[]{:S(2)}) copy-start(bf16[72,1024]{1,0:T(8,128)(2,1)S(1)} %collective-permute-done.11.refs_5_) | copy-start | bytes 442372
  76.7 2.3 %copy-start.13 = (bf16[72,1024]{1,0:T(8,128)(2,1)}, bf16[72,1024]{1,0:T(8,128)(2,1)S(1)}, u32[]{:S(2)}) copy-start(bf16[72,1024]{1,0:T(8,128)(2,1)S(1)} %collective-permute-done.12.refs_6_) | copy-start | bytes 442372
  79.0 0.7 copy-start.14
  83.3 33.0 %copy-start.18 = (bf16[1024,512]{1,0:T(8,128)(2,1)S(1)}, bf16[1024,512]{1,0:T(8,128)(2,1)}, u32[]{:S(2)}) copy-start(bf16[1024,512]{1,0:T(8,128)(2,1)} %g_ref.1) | copy-start | bytes 3145732
  83.3 29.0 %all-to-all-start = ((bf16[32,64,384]{2,1,0:T(8,128)(2,1)}), bf16[32,64,384]{2,1,0:T(8,128)(2,1)S(1)}, u32[]{:S(2)}, u32[]{:S(2)}) async-start(bf16[32,64,384]{2,1,0:T(8,128)(2,1)} %gram.1), calls=%async_computation | async-start | bytes 3145728 | tf_op jit(solution)/shard_map/all_to_all | solution.py:293
  112.3 1.2 copy-start
  (4 other events, 2.5 us)

commit v2 on v1

v2 whole, which is shorter than its diff:
```python
import jax
import jax.numpy as jnp
from jax import lax
from jax.experimental import pallas as pl
from jax.experimental.pallas import tpu as pltpu
from jax.sharding import Mesh
from jax.sharding import PartitionSpec as P

BF = jnp.bfloat16
F32 = jnp.float32
I16 = jnp.int16

SLOT = 72
KEEP = SLOT - 1
BLOCKS = 8
CAP = KEEP * BLOCKS
TOP = 32767.0
HOPS = (1, 3, 2)


def ring(dist):
    return [(i, (i + dist) % 4) for i in range(4)]


SWAP = [(0, 1), (1, 0)]


def last_row(shape):
    return lax.broadcasted_iota(jnp.int32, shape, len(shape) - 2) % SLOT == KEEP


def exponent_of(top):
    return jnp.clip(jnp.ceil(jnp.log2(jnp.maximum(top, 1e-37))), -100.0, 100.0)


def encode(x, k):
    y = x * jnp.exp2(-k)
    mag = jnp.abs(y)
    root = y * lax.rsqrt(jnp.maximum(mag, 1e-30))
    q = jnp.round(jnp.clip(root * TOP, -TOP, TOP))
    q = jnp.where(last_row(x.shape), k, q)
    return q.astype(jnp.int32).astype(I16)


def decode(q):
    q = q.astype(F32)
    unit = jnp.exp2(q[KEEP:SLOT, :]) * (1.0 / (TOP * TOP))
    x = q * jnp.abs(q) * unit
    return jnp.where(last_row(x.shape), 0.0, x)


def top_of(x):
    return jnp.max(jnp.max(jnp.abs(x), axis=1, keepdims=True), axis=0, keepdims=True)


def ranks(routed):
    r = routed.astype(F32).astype(BF)
    i = lax.broadcasted_iota(jnp.int32, (128, 128), 0)
    j = lax.broadcasted_iota(jnp.int32, (128, 128), 1)
    within = jnp.dot(r, (i <= j).astype(F32).astype(BF), preferred_element_type=F32)
    totals = jnp.dot(r, jnp.ones((128, 128), BF), preferred_element_type=F32)
    before = jnp.zeros((1, 128), F32)
    offs = []
    for row in range(8):
        offs.append(before)
        before = before + totals[row : row + 1, :]
    pos = within + jnp.concatenate(offs, axis=0) - 1.0
    return jnp.where(routed > 0, pos, -1.0), before


def build_select(sel_ref, pos, blocks):
    rows = len(blocks) * SLOT
    row = lax.broadcasted_iota(jnp.int32, (rows, 128), 0)
    base = jnp.zeros((rows, 128), jnp.int32)
    for b, q in enumerate(blocks):
        inside = (row >= b * SLOT) & (row < (b + 1) * SLOT)
        base = jnp.where(inside, q * KEEP - b * SLOT, base)
    want = jnp.where(row % SLOT == KEEP, -2, base + row).astype(F32)
    for c in range(8):
        sel_ref[:, c * 128 : (c + 1) * 128] = (want == pos[c : c + 1, :]).astype(F32).astype(BF)


def grads_send_kernel(routed_ref, g_ref, b_ref, send_ref, sel_ref, out_ref):
    z, xl = lax.axis_index("z"), lax.axis_index("xl")
    pos, _ = ranks(routed_ref[...])
    build_select(sel_ref, pos, [lax.rem(z + d, 4) * 2 + (1 - xl) for d in (0,) + HOPS])
    picked = jnp.dot(sel_ref[...], g_ref[...], preferred_element_type=F32).astype(BF)
    out_ref[...] = jnp.dot(picked, b_ref[...], preferred_element_type=F32)
    k = exponent_of(top_of(out_ref[...]))
    for b in range(4):
        send_ref[b] = encode(out_ref[b * SLOT : (b + 1) * SLOT, :], k)


def grads_keep_kernel(routed_ref, g_ref, b_ref, after_ref, keep_ref, sel_ref):
    z, xl = lax.axis_index("z"), lax.axis_index("xl")
    pos, _ = ranks(routed_ref[...])
    build_select(sel_ref, pos, [lax.rem(z + d, 4) * 2 + xl for d in (0,) + HOPS])
    picked = jnp.dot(sel_ref[...], g_ref[...], preferred_element_type=F32).astype(BF)
    keep_ref[...] = jnp.dot(picked, b_ref[...], preferred_element_type=F32)


def acts_send_kernel(routed_ref, h_ref, b_ref, s1_ref, s2_ref, s3_ref, bad_ref, sel_ref, out_ref):
    z, xl = lax.axis_index("z"), lax.axis_index("xl")
    pos, total = ranks(routed_ref[...])
    bad_ref[...] = jnp.broadcast_to(jnp.where(total > CAP, jnp.nan, 0.0), (8, 128))
    blocks = []
    for d in HOPS:
        zz = lax.rem(z + d, 4)
        blocks += [zz * 2 + xl, zz * 2 + (1 - xl)]
    build_select(sel_ref, pos, blocks)
    picked = jnp.dot(sel_ref[...], h_ref[...], preferred_element_type=F32).astype(BF)
    out_ref[...] = jnp.dot(picked, b_ref[...], preferred_element_type=F32)
    k = exponent_of(top_of(out_ref[...]))
    for n, s_ref in enumerate((s1_ref, s2_ref, s3_ref)):
        for b in range(2):
            at = (2 * n + b) * SLOT
            s_ref[b] = encode(out_ref[at : at + SLOT, :], k)


def acts_keep_kernel(routed_ref, h_ref, b_ref, after_ref, keep_ref, sel_ref):
    z, xl = lax.axis_index("z"), lax.axis_index("xl")
    pos, _ = ranks(routed_ref[...])
    build_select(sel_ref, pos, [z * 2 + xl, z * 2 + (1 - xl)])
    picked = jnp.dot(sel_ref[...], h_ref[...], preferred_element_type=F32).astype(BF)
    keep_ref[...] = jnp.dot(picked, b_ref[...], preferred_element_type=F32)


def grads_mid_kernel(keep_ref, got_ref, own_ref, s1_ref, s2_ref, s3_ref, tmp_ref):
    own_ref[...] = keep_ref[:SLOT, :] + decode(got_ref[0])
    for b in range(3):
        tmp_ref[b] = keep_ref[(b + 1) * SLOT : (b + 2) * SLOT, :] + decode(got_ref[b + 1])
    top = top_of(tmp_ref[0])
    for b in (1, 2):
        top = jnp.maximum(top, top_of(tmp_ref[b]))
    k = exponent_of(top)
    for b, s_ref in enumerate((s1_ref, s2_ref, s3_ref)):
        s_ref[...] = encode(tmp_ref[b], k)


def acts_mid_kernel(keep_ref, r1_ref, r2_ref, r3_ref, after_ref, own_ref, send_ref):
    own_ref[...] = keep_ref[:SLOT, :] + decode(r1_ref[0]) + decode(r2_ref[0]) + decode(r3_ref[0])
    other = keep_ref[SLOT:, :] + decode(r1_ref[1]) + decode(r2_ref[1]) + decode(r3_ref[1])
    send_ref[...] = encode(other, exponent_of(top_of(other)))


def grads_end_kernel(own_ref, r1_ref, r2_ref, r3_ref, rot_ref):
    x = own_ref[...] + decode(r1_ref[...]) + decode(r2_ref[...]) + decode(r3_ref[...])
    rot_ref[...] = x.astype(BF)


def acts_end_kernel(own_ref, got_ref, bad_ref, rot_ref):
    x = own_ref[...] + decode(got_ref[...]) + bad_ref[0:1, 0:1]
    rot_ref[...] = x.astype(BF)


PAD = 80
GATHERED = 8
CONTRACT = (((0,), (0,)), ((), ()))


def gather_rows(dst_ref, refs):
    for n, ref in enumerate(refs):
        dst_ref[n * PAD : n * PAD + SLOT, :] = ref[...]
        dst_ref[n * PAD + SLOT : (n + 1) * PAD, :] = jnp.zeros((PAD - SLOT, dst_ref.shape[1]), BF)


def square(v):
    v = v.astype(F32)
    return (v * v).astype(BF)


def own_columns(x_ref):
    y, core = lax.axis_index("y"), lax.axis_index("core")
    i = lax.broadcasted_iota(jnp.int32, (256, 128), 0)
    j = lax.broadcasted_iota(jnp.int32, (256, 128), 1)
    pick = (i == j + jnp.where(j >= 64, 64, 0) + core * 64).astype(F32).astype(BF)
    x = x_ref[:, pl.ds(pl.multiple_of(y * 256, 256), 256)]
    return jnp.dot(x, pick, preferred_element_type=F32).astype(BF)


def put(out_ref, n, t):
    for xh in range(2):
        for cb in range(8):
            out_ref[xh * 8 + cb, :, n * 128 : (n + 1) * 128] = t[xh * 64 : (xh + 1) * 64, cb * 128 : (cb + 1) * 128]


def grads_gram_kernel(scale, *refs):
    *g_refs, out_ref, g_s = refs
    gather_rows(g_s, g_refs)
    t = lax.dot_general(own_columns(g_s), g_s[...], CONTRACT, preferred_element_type=F32) * scale
    put(out_ref, 0, t.astype(BF))


def acts_gram_kernel(scale, *refs):
    *in_refs, gram_ref, out_ref, a_s, g_s = refs
    gather_rows(a_s, in_refs[:GATHERED])
    gather_rows(g_s, in_refs[GATHERED:])
    own = own_columns(a_s)
    t = lax.dot_general(own, a_s[...], CONTRACT, preferred_element_type=F32) * scale
    put(out_ref, 0, t.astype(BF))
    t = lax.dot_general(square(own), square(g_s[...]), CONTRACT, preferred_element_type=F32) * scale
    put(out_ref, 2, t.astype(BF))
    out_ref[:, :, 128:256] = gram_ref[...]


def final_kernel(in_ref, a_ref, g_ref, c_ref):
    t = in_ref[0].astype(F32)
    for n in range(1, 16):
        t = t + in_ref[n].astype(F32)
    a_ref[...] = t[:, :128]
    g_ref[...] = t[:, 128:256]
    c_ref[...] = t[:, 256:]


def sds(shape, dtype):
    return jax.ShapeDtypeStruct(shape, dtype)


def call(kernel, name, out_shape, args, scratch=(), mib=16, flops=0, behind=0):
    vmem = pl.BlockSpec(memory_space=pltpu.VMEM)
    anywhere = pl.BlockSpec(memory_space=pl.ANY)
    outs = out_shape if isinstance(out_shape, tuple) else (out_shape,)
    size = sum(a.size * a.dtype.itemsize for a in args + tuple(outs))
    return pl.pallas_call(
        kernel,
        out_shape=out_shape,
        in_specs=[vmem] * (len(args) - behind) + [anywhere] * behind,
        out_specs=(vmem,) * len(out_shape) if isinstance(out_shape, tuple) else vmem,
        scratch_shapes=list(scratch),
        compiler_params=pltpu.CompilerParams(vmem_limit_bytes=mib * 1024 * 1024),
        cost_estimate=pl.CostEstimate(flops=flops, bytes_accessed=size, transcendentals=0),
        name=name,
    )(*args)


def fast(hidden_acts, act_basis, out_grads, grad_basis, routed):
    width = act_basis.shape[1]
    tokens = hidden_acts.shape[0] * 16
    slots = routed.reshape(8, 128)
    blk = (SLOT, width)
    scale = 1.0 / tokens

    def sel(n):
        return pltpu.VMEM((n * SLOT, 1024), BF)

    def wide(n):
        return pltpu.VMEM((n * SLOT, width), F32)

    g_send = call(
        grads_send_kernel, "grads_send", sds((4,) + blk, I16), (slots, out_grads, grad_basis), (sel(4), wide(4)), 16, 600_000_000
    )
    g_got = lax.ppermute(g_send, "xl", SWAP)

    *a_send, bad = call(
        acts_send_kernel,
        "acts_send",
        (sds((2,) + blk, I16),) * 3 + (sds((8, 128), F32),),
        (slots, hidden_acts, act_basis),
        (sel(6), wide(6)),
        24,
        3_200_000_000,
    )
    a_got = [lax.ppermute(s, "z", ring(d)) for s, d in zip(a_send, HOPS)]

    g_keep = call(
        grads_keep_kernel,
        "grads_keep",
        sds((4 * SLOT, width), F32),
        (slots, out_grads, grad_basis, bad),
        (sel(4),),
        16,
        600_000_000,
        behind=1,
    )
    a_keep = call(
        acts_keep_kernel,
        "acts_keep",
        sds((2 * SLOT, width), F32),
        (slots, hidden_acts, act_basis, bad),
        (sel(2),),
        24,
        1_100_000_000,
        behind=1,
    )

    g_own, *g_next = call(
        grads_mid_kernel,
        "grads_mid",
        (sds(blk, F32),) + (sds(blk, I16),) * 3,
        (g_keep, g_got),
        (pltpu.VMEM((3,) + blk, F32),),
    )
    g_last = [lax.ppermute(s, "z", ring(d)) for s, d in zip(g_next, HOPS)]

    a_own, a_next = call(
        acts_mid_kernel, "acts_mid", (sds(blk, F32), sds(blk, I16)), (a_keep, *a_got, g_own), behind=1
    )
    a_last = lax.ppermute(a_next, "xl", SWAP)

    def gathered(rot):
        near = [rot] + [lax.ppermute(rot, "y", ring(d)) for d in HOPS]
        return near + [lax.ppermute(r, "core", SWAP) for r in near]

    rot_g = call(grads_end_kernel, "grads_end", sds(blk, BF), (g_own, *g_last))
    all_g = gathered(rot_g)
    rot_a = call(acts_end_kernel, "acts_end", sds(blk, BF), (a_own, a_last, bad))
    all_a = gathered(rot_a)

    def rows():
        return pltpu.VMEM((GATHERED * PAD, width), BF)

    gram = call(
        lambda *refs: grads_gram_kernel(scale, *refs), "grads_gram", sds((16, 64, 128), BF), tuple(all_g), (rows(),), 16, 200_000_000
    )
    parts = call(
        lambda *refs: acts_gram_kernel(scale, *refs),
        "acts_gram",
        sds((16, 64, 384), BF),
        (*all_a, *all_g, gram),
        (rows(), rows()),
        16,
        400_000_000,
    )
    got = lax.all_to_all(parts, ("xh", "z", "xl"), 0, 0, tiled=True)
    return call(final_kernel, "final", (sds((64, 128), F32),) * 3, (got,))


DP = ("y", "xh", "core")
TENSOR = ("z", "xl")


def general(hidden_acts, act_basis, out_grads, grad_basis, routed):
    act_part = jnp.dot(hidden_acts, act_basis, preferred_element_type=F32)
    grad_part = jnp.dot(out_grads, grad_basis, preferred_element_type=F32)
    act_sum, grad_sum = lax.psum((act_part, grad_part), TENSOR)
    rot_acts = act_sum.astype(BF)
    rot_grads = grad_sum.astype(BF)
    total_tokens = rot_acts.shape[0] * 16
    weights = routed.astype(F32)[:, None]
    acts_f = rot_acts.astype(F32)
    grads_f = rot_grads.astype(F32)
    masked_acts = (acts_f * weights).astype(BF)
    masked_grads = (grads_f * weights).astype(BF)
    sq_acts = (acts_f * acts_f * weights).astype(BF)
    sq_grads = (grads_f * grads_f).astype(BF)
    col_width = rot_acts.shape[1] // 8
    col_start = (lax.axis_index("z") * 2 + lax.axis_index("xl")) * col_width
    own_rows = rot_acts.shape[1] // 16
    row_start = ((lax.axis_index("y") * 2 + lax.axis_index("xh")) * 2 + lax.axis_index("core")) * own_rows
    contract = (((0,), (0,)), ((), ()))
    terms = []
    for left, right in ((masked_acts, rot_acts), (masked_grads, rot_grads), (sq_acts, sq_grads)):
        cols = lax.dynamic_slice_in_dim(right, col_start, col_width, 1)
        terms.append(lax.dot_general(left, cols, contract, preferred_element_type=F32))
    summed = lax.psum(jnp.concatenate(terms, axis=1) * (1.0 / total_tokens), DP)
    owned = lax.dynamic_slice_in_dim(summed, row_start, own_rows, 0)
    return tuple(owned[:, n * col_width : (n + 1) * col_width] for n in range(3))


def shards(*args):
    act_gram, grad_gram, correction = fast(*args)
    whole = jnp.abs(act_gram[0, 0]) < 1e30
    return lax.cond(whole, lambda *_: (act_gram, grad_gram, correction), general, *args)


def solution(mesh):
    fine = Mesh(mesh.devices.reshape(4, 2, 2, 4, 2), ("y", "xh", "core", "z", "xl"))
    return jax.shard_map(
        shards,
        mesh=fine,
        in_specs=(P(DP, TENSOR), P(TENSOR, None), P(DP, TENSOR), P(TENSOR, None), P(DP)),
        out_specs=(P(DP, TENSOR),) * 3,
        check_vma=False,
    )
```

time: 127 us -> 97 us (0.76); the launches traced: 125 us -> 96.7 us
  Pallas kernels: 34.9 us -> 18.3 us
  waiting for transfers between devices: 39.9 us -> 32.6 us
  local copies, waits for them, and re-layouts: 7.09 us -> 2.37 us
    pallas_call x8 -> x11, Pallas kernels: 34.9 us -> 18.3 us  [call(): pl.pallas_call(kernel, out_shape=out_shape, in_specs=[vmem] * (len(args)...]
    all_to_all x1, waiting for transfers between devices: 21.4 us -> 14.8 us  [fast(): got = lax.all_to_all(parts, ('xh', 'z', 'xl'), 0, 0, tiled=True)]
    unnamed x42 -> x16, local copies, waits for them, and re-layouts: 6.58 us -> 1.86 us
    ppermute x3, waiting for transfers between devices: 12.6 us -> 9.09 us  [fast(): a_got = [lax.ppermute(s, 'z', ring(d)) for s, d in zip(a_send, HOPS)]]
    all_to_all x1, starting transfers between devices: 7.62 us -> 4.9 us  [fast(): got = lax.all_to_all(parts, ('xh', 'z', 'xl'), 0, 0, tiled=True)]
    ppermute x6 -> x14, starting transfers between devices: 9.38 us -> 11.9 us  [the longest x6 10.3 us: gathered(): near = [rot] + [lax.ppermute(rot, 'y', ring(d)) for d in HOPS]]
    ppermute x3, waiting for transfers between devices: 0.01 us -> 1.65 us  [fast(): g_last = [lax.ppermute(s, 'z', ring(d)) for s, d in zip(g_next, HOPS)]]
    ppermute x6 -> x14, waiting for transfers between devices: 5.92 us -> 5.8 us  [the longest x6 5.54 us: gathered(): near = [rot] + [lax.ppermute(rot, 'y', ring(d)) for d in HOPS]]
  transfers between devices with their start and end apart: 15 -> 23, of which waited for: 7 -> 10; matrix products, arithmetic and copies ran while one was open for 0% -> 0% of each run, Pallas kernels for 20% -> 13%
where the time goes in v2:
time: 97 us; the launch traced here: 96.7 us
  waiting for transfers between devices  32.6 us (34%)
  starting transfers between devices  28.3 us (29%)
  Pallas kernels  18.3 us (19%)
  between operations  14.8 us (15%)
  local copies, waits for them, and re-layouts  2.37 us (2%)
    pallas_call x11, Pallas kernels, call(): pl.pallas_call(kernel, out_shape=out_shape, in_specs=[vmem] * (len(args)...  18.3 us
    all_to_all x1, waiting for transfers between devices, fast(): got = lax.all_to_all(parts, ('xh', 'z', 'xl'), 0, 0, tiled=True)  14.8 us
    ppermute x6, starting transfers between devices, gathered(): near = [rot] + [lax.ppermute(rot, 'y', ring(d)) for d in HOPS]  10.3 us
    ppermute x3, waiting for transfers between devices, fast(): a_got = [lax.ppermute(s, 'z', ring(d)) for s, d in zip(a_send, HOPS)]  9.09 us
    ppermute x3, starting transfers between devices, fast(): a_got = [lax.ppermute(s, 'z', ring(d)) for s, d in zip(a_send, HOPS)]  5.95 us
    ppermute x6, waiting for transfers between devices, gathered(): near = [rot] + [lax.ppermute(rot, 'y', ring(d)) for d in HOPS]  5.54 us
    all_to_all x1, starting transfers between devices, fast(): got = lax.all_to_all(parts, ('xh', 'z', 'xl'), 0, 0, tiled=True)  4.9 us
    ppermute x3, starting transfers between devices, fast(): g_last = [lax.ppermute(s, 'z', ring(d)) for s, d in zip(g_next, HOPS)]  3.33 us
  transfers between devices with their start and end apart: 23, of which 10 were waited for; matrix products, arithmetic and copies ran while one was open for 0% of the time, Pallas kernels for 13%

profile of v2, /device:TPU:0, one launch (start us, length us, event | category | flops | bytes accessed | tf_op | source)
XLA Modules:
  0.0 96.7 jit_solution(13288310166845642206)
XLA Ops:
  7.2 3.3 %grads_send.1 = s16[4,72,1024]{2,1,0:T(8,128)(2,1)S(1)} custom-call(s32[8,128]{1,0:T(8,128)} %bitcast.6, bf16[1024,512]{1,0:T(8,128)(2,1)} %g_ref.3, bf16[512,1024]{1,0:T(8,128)(2,1)} %b_ref.7), custom_call_target="tpu_custom_call" | custom-call | flops 600000000 | bytes 2691072 | tf_op jit(solution)/shard_map/grads_send/pallas_call | solution.py:224
  10.5 1.7 %collective-permute-start.3 = (s16[4,72,1024]{2,1,0:T(8,128)(2,1)S(1)}, s16[4,72,1024]{2,1,0:T(8,128)(2,1)S(1)}, u32[]{:S(2)}, u32[]{:S(2)}) collective-permute-start(s16[4,72,1024]{2,1,0:T(8,128)(2,1)S(1)} %grads_send.1), channel_id=1, source_target_pairs={{0,1},{1,0},{2,3},{3,2},{4,5},{5,4},{6,7},{7,6},{8,9},{9,8},{10,11... | collective-permute-start | bytes 1769480 | tf_op jit(solution)/shard_map/ppermute | solution.py:252
  12.1 7.8 %acts_send.1 = (s16[2,72,1024]{2,1,0:T(8,128)(2,1)S(1)}, s16[2,72,1024]{2,1,0:T(8,128)(2,1)S(1)}, s16[2,72,1024]{2,1,0:T(8,128)(2,1)S(1)}, f32[8,128]{1,0:T(8,128)S(1)}) custom-call(s32[8,128]{1,0:T(8,128)S(1)} %bitcast.7, bf16[1024,1792]{1,0:T(8,128)(2,1)} %h_ref.3, bf16[1792,1024]{1,0:T(8,128)(2,1)} %b_ref.5), custom_call_target="tpu_custom_call" | custom-call | flops 3200000000 | bytes 8232960 | tf_op jit(solution)/shard_map/acts_send/pallas_call | solution.py:224
  20.0 2.0 %collective-permute-start = (s16[2,72,1024]{2,1,0:T(8,128)(2,1)S(1)}, s16[2,72,1024]{2,1,0:T(8,128)(2,1)S(1)}, u32[]{:S(2)}, u32[]{:S(2)}) collective-permute-start(s16[2,72,1024]{2,1,0:T(8,128)(2,1)S(1)} %get-tuple-element.36), channel_id=1, source_target_pairs={{0,2},{2,4},{4,6},{6,0},{1,3},{3,5},{5,7},{7,1},{8,10},{10,12},{12... | collective-permute-start | bytes 884744 | tf_op jit(solution)/shard_map/ppermute | solution.py:263
  21.9 2.2 %collective-permute-start.1 = (s16[2,72,1024]{2,1,0:T(8,128)(2,1)S(1)}, s16[2,72,1024]{2,1,0:T(8,128)(2,1)S(1)}, u32[]{:S(2)}, u32[]{:S(2)}) collective-permute-start(s16[2,72,1024]{2,1,0:T(8,128)(2,1)S(1)} %get-tuple-element.37), channel_id=1, source_target_pairs={{0,6},{2,0},{4,2},{6,4},{1,7},{3,1},{5,3},{7,5},{8,14},{10,8},{12,... | collective-permute-start | bytes 884744 | tf_op jit(solution)/shard_map/ppermute | solution.py:263
  24.1 1.8 %collective-permute-start.2 = (s16[2,72,1024]{2,1,0:T(8,128)(2,1)S(1)}, s16[2,72,1024]{2,1,0:T(8,128)(2,1)S(1)}, u32[]{:S(2)}, u32[]{:S(2)}) collective-permute-start(s16[2,72,1024]{2,1,0:T(8,128)(2,1)S(1)} %get-tuple-element.38), channel_id=1, source_target_pairs={{0,4},{2,6},{4,0},{6,2},{1,5},{3,7},{5,1},{7,3},{8,12},{10,14},{12... | collective-permute-start | bytes 884744 | tf_op jit(solution)/shard_map/ppermute | solution.py:263
  25.9 1.0 %grads_keep.1.keep_ref = f32[288,1024]{1,0:T(8,128)S(1)} custom-call(s32[8,128]{1,0:T(8,128)S(1)} %bitcast.8, bf16[1024,512]{1,0:T(8,128)(2,1)S(1)} %copy-done, bf16[512,1024]{1,0:T(8,128)(2,1)S(1)} %copy-done.1, f32[8,128]{1,0:T(8,128)S(1)} %get-tuple-element.35.after_ref.bad_ref), custom_call_target="tpu_custom_call" | custom-call | flops 600000000 | bytes 3284992 | tf_op jit(solution)/shard_map/grads_keep/pallas_call | solution.py:224
  26.9 1.4 %acts_keep.1.keep_ref = f32[144,1024]{1,0:T(8,128)S(1)} custom-call(s32[8,128]{1,0:T(8,128)S(1)} %bitcast.9, bf16[1024,1792]{1,0:T(8,128)(2,1)S(1)} %copy-done.2, bf16[1792,1024]{1,0:T(8,128)(2,1)S(1)} %copy-done.3, f32[8,128]{1,0:T(8,128)S(1)} %get-tuple-element.35.after_ref.bad_ref), custom_call_target="tpu_custom_call" | custom-call | flops 1100000000 | bytes 7938048 | tf_op jit(solution)/shard_map/acts_keep/pallas_call | solution.py:224
  28.4 0.8 grads_mid.1
  29.2 1.9 %collective-permute-done.r1_ref = s16[2,72,1024]{2,1,0:T(8,128)(2,1)S(1)} collective-permute-done((s16[2,72,1024]{2,1,0:T(8,128)(2,1)S(1)}, s16[2,72,1024]{2,1,0:T(8,128)(2,1)S(1)}, u32[]{:S(2)}, u32[]{:S(2)}) %collective-permute-start) | collective-permute-done | bytes 294944 | tf_op jit(solution)/shard_map/ppermute | solution.py:263
  31.1 5.4 %collective-permute-done.1.r2_ref = s16[2,72,1024]{2,1,0:T(8,128)(2,1)S(1)} collective-permute-done((s16[2,72,1024]{2,1,0:T(8,128)(2,1)S(1)}, s16[2,72,1024]{2,1,0:T(8,128)(2,1)S(1)}, u32[]{:S(2)}, u32[]{:S(2)}) %collective-permute-start.1) | collective-permute-done | bytes 294944 | tf_op jit(solution)/shard_map/ppermute | solution.py:263
  36.5 1.8 %collective-permute-done.2.r3_ref = s16[2,72,1024]{2,1,0:T(8,128)(2,1)S(1)} collective-permute-done((s16[2,72,1024]{2,1,0:T(8,128)(2,1)S(1)}, s16[2,72,1024]{2,1,0:T(8,128)(2,1)S(1)}, u32[]{:S(2)}, u32[]{:S(2)}) %collective-permute-start.2) | collective-permute-done | bytes 294944 | tf_op jit(solution)/shard_map/ppermute | solution.py:263
  38.3 0.8 acts_mid.1
  39.1 0.6 collective-permute-start.4
  39.8 1.1 %collective-permute-start.12 = (s16[72,1024]{1,0:T(8,128)(2,1)S(1)}, s16[72,1024]{1,0:T(8,128)(2,1)S(1)}, u32[]{:S(2)}, u32[]{:S(2)}) collective-permute-start(s16[72,1024]{1,0:T(8,128)(2,1)S(1)} %get-tuple-element.42), channel_id=1, source_target_pairs={{0,2},{2,4},{4,6},{6,0},{1,3},{3,5},{5,7},{7,1},{8,10},{10,12},{12... | collective-permute-start | bytes 442376 | tf_op jit(solution)/shard_map/ppermute | solution.py:293
  40.9 2.1 %collective-permute-start.13 = (s16[72,1024]{1,0:T(8,128)(2,1)S(1)}, s16[72,1024]{1,0:T(8,128)(2,1)S(1)}, u32[]{:S(2)}, u32[]{:S(2)}) collective-permute-start(s16[72,1024]{1,0:T(8,128)(2,1)S(1)} %get-tuple-element.43), channel_id=1, source_target_pairs={{0,6},{2,0},{4,2},{6,4},{1,7},{3,1},{5,3},{7,5},{8,14},{10,8},{12,... | collective-permute-start | bytes 442376 | tf_op jit(solution)/shard_map/ppermute | solution.py:293
  43.1 1.3 %collective-permute-done.4.got_ref = s16[72,1024]{1,0:T(8,128)(2,1)S(1)} collective-permute-done((s16[72,1024]{1,0:T(8,128)(2,1)S(1)}, s16[72,1024]{1,0:T(8,128)(2,1)S(1)}, u32[]{:S(2)}, u32[]{:S(2)}) %collective-permute-start.4) | collective-permute-done | bytes 147488 | tf_op jit(solution)/shard_map/ppermute | solution.py:298
  44.5 1.8 %collective-permute-start.5 = (bf16[72,1024]{1,0:T(8,128)(2,1)S(1)}, bf16[72,1024]{1,0:T(8,128)(2,1)S(1)}, u32[]{:S(2)}, u32[]{:S(2)}) collective-permute-start(bf16[72,1024]{1,0:T(8,128)(2,1)S(1)} %acts_end.1.refs_0_), channel_id=1, source_target_pairs={{0,32},{32,64},{64,96},{96,0},{1,33},{33,65},{65,97},{97,1},{2,34}... | collective-permute-start | bytes 442376 | tf_op jit(solution)/shard_map/ppermute | solution.py:301
  46.3 1.7 %collective-permute-start.6 = (bf16[72,1024]{1,0:T(8,128)(2,1)S(1)}, bf16[72,1024]{1,0:T(8,128)(2,1)S(1)}, u32[]{:S(2)}, u32[]{:S(2)}) collective-permute-start(bf16[72,1024]{1,0:T(8,128)(2,1)S(1)} %acts_end.1.refs_0_), channel_id=1, source_target_pairs={{0,96},{32,0},{64,32},{96,64},{1,97},{33,1},{65,33},{97,65},{2,98}... | collective-permute-start | bytes 442376 | tf_op jit(solution)/shard_map/ppermute | solution.py:301
  48.0 1.6 %collective-permute-done.14.r3_ref = s16[72,1024]{1,0:T(8,128)(2,1)S(1)} collective-permute-done((s16[72,1024]{1,0:T(8,128)(2,1)S(1)}, s16[72,1024]{1,0:T(8,128)(2,1)S(1)}, u32[]{:S(2)}, u32[]{:S(2)}) %collective-permute-start.14) | collective-permute-done | bytes 147488 | tf_op jit(solution)/shard_map/ppermute | solution.py:293
  49.9 1.6 %collective-permute-start.15 = (bf16[72,1024]{1,0:T(8,128)(2,1)S(1)}, bf16[72,1024]{1,0:T(8,128)(2,1)S(1)}, u32[]{:S(2)}, u32[]{:S(2)}) collective-permute-start(bf16[72,1024]{1,0:T(8,128)(2,1)S(1)} %grads_end.1.refs_0_.refs_8_), channel_id=1, source_target_pairs={{0,32},{32,64},{64,96},{96,0},{1,33},{33,65},{65,97},{97,1},{2,34}... | collective-permute-start | bytes 442376 | tf_op jit(solution)/shard_map/ppermute | solution.py:301
  51.5 1.7 %collective-permute-start.16 = (bf16[72,1024]{1,0:T(8,128)(2,1)S(1)}, bf16[72,1024]{1,0:T(8,128)(2,1)S(1)}, u32[]{:S(2)}, u32[]{:S(2)}) collective-permute-start(bf16[72,1024]{1,0:T(8,128)(2,1)S(1)} %grads_end.1.refs_0_.refs_8_), channel_id=1, source_target_pairs={{0,96},{32,0},{64,32},{96,64},{1,97},{33,1},{65,33},{97,65},{2,98}... | collective-permute-start | bytes 442376 | tf_op jit(solution)/shard_map/ppermute | solution.py:301
  53.2 2.0 %collective-permute-start.17 = (bf16[72,1024]{1,0:T(8,128)(2,1)S(1)}, bf16[72,1024]{1,0:T(8,128)(2,1)S(1)}, u32[]{:S(2)}, u32[]{:S(2)}) collective-permute-start(bf16[72,1024]{1,0:T(8,128)(2,1)S(1)} %grads_end.1.refs_0_.refs_8_), channel_id=1, source_target_pairs={{0,64},{32,96},{64,0},{96,32},{1,65},{33,97},{65,1},{97,33},{2,66}... | collective-permute-start | bytes 442376 | tf_op jit(solution)/shard_map/ppermute | solution.py:301
  55.2 1.5 %collective-permute-start.7 = (bf16[72,1024]{1,0:T(8,128)(2,1)S(1)}, bf16[72,1024]{1,0:T(8,128)(2,1)S(1)}, u32[]{:S(2)}, u32[]{:S(2)}) collective-permute-start(bf16[72,1024]{1,0:T(8,128)(2,1)S(1)} %acts_end.1.refs_0_), channel_id=1, source_target_pairs={{0,64},{32,96},{64,0},{96,32},{1,65},{33,97},{65,1},{97,33},{2,66}... | collective-permute-start | bytes 442376 | tf_op jit(solution)/shard_map/ppermute | solution.py:301
  56.7 2.1 %collective-permute-done.15.refs_1_.refs_9_ = bf16[72,1024]{1,0:T(8,128)(2,1)S(1)} collective-permute-done((bf16[72,1024]{1,0:T(8,128)(2,1)S(1)}, bf16[72,1024]{1,0:T(8,128)(2,1)S(1)}, u32[]{:S(2)}, u32[]{:S(2)}) %collective-permute-start.15) | collective-permute-done | bytes 147488 | tf_op jit(solution)/shard_map/ppermute | solution.py:301
  59.4 1.8 %collective-permute-done.17.refs_3_.refs_11_ = bf16[72,1024]{1,0:T(8,128)(2,1)S(1)} collective-permute-done((bf16[72,1024]{1,0:T(8,128)(2,1)S(1)}, bf16[72,1024]{1,0:T(8,128)(2,1)S(1)}, u32[]{:S(2)}, u32[]{:S(2)}) %collective-permute-start.17) | collective-permute-done | bytes 147488 | tf_op jit(solution)/shard_map/ppermute | solution.py:301
  61.2 1.6 %collective-permute-done.7.refs_3_ = bf16[72,1024]{1,0:T(8,128)(2,1)S(1)} collective-permute-done((bf16[72,1024]{1,0:T(8,128)(2,1)S(1)}, bf16[72,1024]{1,0:T(8,128)(2,1)S(1)}, u32[]{:S(2)}, u32[]{:S(2)}) %collective-permute-start.7) | collective-permute-done | bytes 147488 | tf_op jit(solution)/shard_map/ppermute | solution.py:301
  63.8 0.8 grads_gram.1.refs_16_
  64.9 1.9 %acts_gram.1 = bf16[16,64,384]{2,1,0:T(8,128)(2,1)} custom-call(bf16[72,1024]{1,0:T(8,128)(2,1)S(1)} %acts_end.1.refs_0_, bf16[72,1024]{1,0:T(8,128)(2,1)S(1)} %collective-permute-done.5.refs_1_, bf16[72,1024]{1,0:T(8,128)(2,1)S(1)} %collective-permute-done.6.refs_2_, bf16[72,1024]{1,0:T(8,128)(2,1)S(1)} %collective-permute-done.7.refs_3_, ...), custom_call_target="tpu_custom_call" | custom-call | flops 400000000 | bytes 3407872 | tf_op jit(solution)/shard_map/acts_gram/pallas_call | solution.py:224
  66.8 4.9 %all-to-all-start = ((bf16[16,64,384]{2,1,0:T(8,128)(2,1)}), bf16[16,64,384]{2,1,0:T(8,128)(2,1)S(1)}, u32[]{:S(2)}, u32[]{:S(2)}) async-start(bf16[16,64,384]{2,1,0:T(8,128)(2,1)} %acts_gram.1), calls=%async_computation | async-start | bytes 1572864 | tf_op jit(solution)/shard_map/all_to_all | solution.py:324
  71.7 14.8 %all-to-all-done.in_ref = bf16[16,64,384]{2,1,0:T(8,128)(2,1)S(1)} async-done(((bf16[16,64,384]{2,1,0:T(8,128)(2,1)}), bf16[16,64,384]{2,1,0:T(8,128)(2,1)S(1)}, u32[]{:S(2)}, u32[]{:S(2)}) %all-to-all-start) | async-done | bytes 786464 | tf_op jit(solution)/shard_map/all_to_all | solution.py:324
  88.7 0.6 copy-done.7
  (43 shorter events, 4.4 us)
Async XLA Ops:
  7.2 5.0 %copy-start.4 = (s32[1024]{0:T(1024)S(1)}, s32[1024]{0:T(1024)}, u32[]{:S(2)}) copy-start(s32[1024]{0:T(1024)} %param.11) | copy-start | bytes 12292
  10.4 15.5 %copy-start = (bf16[1024,512]{1,0:T(8,128)(2,1)S(1)}, bf16[1024,512]{1,0:T(8,128)(2,1)}, u32[]{:S(2)}) copy-start(bf16[1024,512]{1,0:T(8,128)(2,1)} %g_ref.3) | copy-start | bytes 3145732
  10.5 15.5 %copy-start.1 = (bf16[512,1024]{1,0:T(8,128)(2,1)S(1)}, bf16[512,1024]{1,0:T(8,128)(2,1)}, u32[]{:S(2)}) copy-start(bf16[512,1024]{1,0:T(8,128)(2,1)} %b_ref.7) | copy-start | bytes 3145732
  10.5 17.9 %collective-permute-start.3 = (s16[4,72,1024]{2,1,0:T(8,128)(2,1)S(1)}, s16[4,72,1024]{2,1,0:T(8,128)(2,1)S(1)}, u32[]{:S(2)}, u32[]{:S(2)}) collective-permute-start(s16[4,72,1024]{2,1,0:T(8,128)(2,1)S(1)} %grads_send.1), channel_id=1, source_target_pairs={{0,1},{1,0},{2,3},{3,2},{4,5},{5,4},{6,7},{7,6},{8,9},{9,8},{10,11... | collective-permute-start | bytes 1769480 | tf_op jit(solution)/shard_map/ppermute | solution.py:252
  12.1 14.8 %copy-start.2 = (bf16[1024,1792]{1,0:T(8,128)(2,1)S(1)}, bf16[1024,1792]{1,0:T(8,128)(2,1)}, u32[]{:S(2)}) copy-start(bf16[1024,1792]{1,0:T(8,128)(2,1)} %h_ref.3) | copy-start | bytes 11010052
  12.1 14.8 %copy-start.3 = (bf16[1792,1024]{1,0:T(8,128)(2,1)S(1)}, bf16[1792,1024]{1,0:T(8,128)(2,1)}, u32[]{:S(2)}) copy-start(bf16[1792,1024]{1,0:T(8,128)(2,1)} %b_ref.5) | copy-start | bytes 11010052
  20.0 11.1 %collective-permute-start = (s16[2,72,1024]{2,1,0:T(8,128)(2,1)S(1)}, s16[2,72,1024]{2,1,0:T(8,128)(2,1)S(1)}, u32[]{:S(2)}, u32[]{:S(2)}) collective-permute-start(s16[2,72,1024]{2,1,0:T(8,128)(2,1)S(1)} %get-tuple-element.36), channel_id=1, source_target_pairs={{0,2},{2,4},{4,6},{6,0},{1,3},{3,5},{5,7},{7,1},{8,10},{10,12},{12... | collective-permute-start | bytes 884744 | tf_op jit(solution)/shard_map/ppermute | solution.py:263
  21.9 14.5 %collective-permute-start.1 = (s16[2,72,1024]{2,1,0:T(8,128)(2,1)S(1)}, s16[2,72,1024]{2,1,0:T(8,128)(2,1)S(1)}, u32[]{:S(2)}, u32[]{:S(2)}) collective-permute-start(s16[2,72,1024]{2,1,0:T(8,128)(2,1)S(1)} %get-tuple-element.37), channel_id=1, source_target_pairs={{0,6},{2,0},{4,2},{6,4},{1,7},{3,1},{5,3},{7,5},{8,14},{10,8},{12,... | collective-permute-start | bytes 884744 | tf_op jit(solution)/shard_map/ppermute | solution.py:263
  24.1 14.1 %collective-permute-start.2 = (s16[2,72,1024]{2,1,0:T(8,128)(2,1)S(1)}, s16[2,72,1024]{2,1,0:T(8,128)(2,1)S(1)}, u32[]{:S(2)}, u32[]{:S(2)}) collective-permute-start(s16[2,72,1024]{2,1,0:T(8,128)(2,1)S(1)} %get-tuple-element.38), channel_id=1, source_target_pairs={{0,4},{2,6},{4,0},{6,2},{1,5},{3,7},{5,1},{7,3},{8,12},{10,14},{12... | collective-permute-start | bytes 884744 | tf_op jit(solution)/shard_map/ppermute | solution.py:263
  39.1 5.2 %collective-permute-start.4 = (s16[72,1024]{1,0:T(8,128)(2,1)S(1)}, s16[72,1024]{1,0:T(8,128)(2,1)S(1)}, u32[]{:S(2)}, u32[]{:S(2)}) collective-permute-start(s16[72,1024]{1,0:T(8,128)(2,1)S(1)} %get-tuple-element.41), channel_id=1, source_target_pairs={{0,1},{1,0},{2,3},{3,2},{4,5},{5,4},{6,7},{7,6},{8,9},{9,8},{10,11... | collective-permute-start | bytes 442376 | tf_op jit(solution)/shard_map/ppermute | solution.py:298
  39.8 8.2 %collective-permute-start.12 = (s16[72,1024]{1,0:T(8,128)(2,1)S(1)}, s16[72,1024]{1,0:T(8,128)(2,1)S(1)}, u32[]{:S(2)}, u32[]{:S(2)}) collective-permute-start(s16[72,1024]{1,0:T(8,128)(2,1)S(1)} %get-tuple-element.42), channel_id=1, source_target_pairs={{0,2},{2,4},{4,6},{6,0},{1,3},{3,5},{5,7},{7,1},{8,10},{10,12},{12... | collective-permute-start | bytes 442376 | tf_op jit(solution)/shard_map/ppermute | solution.py:293
  40.9 7.1 %collective-permute-start.13 = (s16[72,1024]{1,0:T(8,128)(2,1)S(1)}, s16[72,1024]{1,0:T(8,128)(2,1)S(1)}, u32[]{:S(2)}, u32[]{:S(2)}) collective-permute-start(s16[72,1024]{1,0:T(8,128)(2,1)S(1)} %get-tuple-element.43), channel_id=1, source_target_pairs={{0,6},{2,0},{4,2},{6,4},{1,7},{3,1},{5,3},{7,5},{8,14},{10,8},{12,... | collective-permute-start | bytes 442376 | tf_op jit(solution)/shard_map/ppermute | solution.py:293
  43.0 6.6 %collective-permute-start.14 = (s16[72,1024]{1,0:T(8,128)(2,1)S(1)}, s16[72,1024]{1,0:T(8,128)(2,1)S(1)}, u32[]{:S(2)}, u32[]{:S(2)}) collective-permute-start(s16[72,1024]{1,0:T(8,128)(2,1)S(1)} %get-tuple-element.44), channel_id=1, source_target_pairs={{0,4},{2,6},{4,0},{6,2},{1,5},{3,7},{5,1},{7,3},{8,12},{10,14},{12... | collective-permute-start | bytes 442376 | tf_op jit(solution)/shard_map/ppermute | solution.py:293
  44.5 10.7 %collective-permute-start.5 = (bf16[72,1024]{1,0:T(8,128)(2,1)S(1)}, bf16[72,1024]{1,0:T(8,128)(2,1)S(1)}, u32[]{:S(2)}, u32[]{:S(2)}) collective-permute-start(bf16[72,1024]{1,0:T(8,128)(2,1)S(1)} %acts_end.1.refs_0_), channel_id=1, source_target_pairs={{0,32},{32,64},{64,96},{96,0},{1,33},{33,65},{65,97},{97,1},{2,34}... | collective-permute-start | bytes 442376 | tf_op jit(solution)/shard_map/ppermute | solution.py:301
  46.3 10.4 %collective-permute-start.6 = (bf16[72,1024]{1,0:T(8,128)(2,1)S(1)}, bf16[72,1024]{1,0:T(8,128)(2,1)S(1)}, u32[]{:S(2)}, u32[]{:S(2)}) collective-permute-start(bf16[72,1024]{1,0:T(8,128)(2,1)S(1)} %acts_end.1.refs_0_), channel_id=1, source_target_pairs={{0,96},{32,0},{64,32},{96,64},{1,97},{33,1},{65,33},{97,65},{2,98}... | collective-permute-start | bytes 442376 | tf_op jit(solution)/shard_map/ppermute | solution.py:301
  49.9 9.0 %collective-permute-start.15 = (bf16[72,1024]{1,0:T(8,128)(2,1)S(1)}, bf16[72,1024]{1,0:T(8,128)(2,1)S(1)}, u32[]{:S(2)}, u32[]{:S(2)}) collective-permute-start(bf16[72,1024]{1,0:T(8,128)(2,1)S(1)} %grads_end.1.refs_0_.refs_8_), channel_id=1, source_target_pairs={{0,32},{32,64},{64,96},{96,0},{1,33},{33,65},{65,97},{97,1},{2,34}... | collective-permute-start | bytes 442376 | tf_op jit(solution)/shard_map/ppermute | solution.py:301
  51.5 7.3 %collective-permute-start.16 = (bf16[72,1024]{1,0:T(8,128)(2,1)S(1)}, bf16[72,1024]{1,0:T(8,128)(2,1)S(1)}, u32[]{:S(2)}, u32[]{:S(2)}) collective-permute-start(bf16[72,1024]{1,0:T(8,128)(2,1)S(1)} %grads_end.1.refs_0_.refs_8_), channel_id=1, source_target_pairs={{0,96},{32,0},{64,32},{96,64},{1,97},{33,1},{65,33},{97,65},{2,98}... | collective-permute-start | bytes 442376 | tf_op jit(solution)/shard_map/ppermute | solution.py:301
  53.2 8.0 %collective-permute-start.17 = (bf16[72,1024]{1,0:T(8,128)(2,1)S(1)}, bf16[72,1024]{1,0:T(8,128)(2,1)S(1)}, u32[]{:S(2)}, u32[]{:S(2)}) collective-permute-start(bf16[72,1024]{1,0:T(8,128)(2,1)S(1)} %grads_end.1.refs_0_.refs_8_), channel_id=1, source_target_pairs={{0,64},{32,96},{64,0},{96,32},{1,65},{33,97},{65,1},{97,33},{2,66}... | collective-permute-start | bytes 442376 | tf_op jit(solution)/shard_map/ppermute | solution.py:301
  55.2 7.6 %collective-permute-start.7 = (bf16[72,1024]{1,0:T(8,128)(2,1)S(1)}, bf16[72,1024]{1,0:T(8,128)(2,1)S(1)}, u32[]{:S(2)}, u32[]{:S(2)}) collective-permute-start(bf16[72,1024]{1,0:T(8,128)(2,1)S(1)} %acts_end.1.refs_0_), channel_id=1, source_target_pairs={{0,64},{32,96},{64,0},{96,32},{1,65},{33,97},{65,1},{97,33},{2,66}... | collective-permute-start | bytes 442376 | tf_op jit(solution)/shard_map/ppermute | solution.py:301
  56.7 6.1 %collective-permute-start.18 = (bf16[72,1024]{1,0:T(8,128)(2,1)S(1)}, bf16[72,1024]{1,0:T(8,128)(2,1)S(1)}, u32[]{:S(2)}, u32[]{:S(2)}) collective-permute-start(bf16[72,1024]{1,0:T(8,128)(2,1)S(1)} %grads_end.1.refs_0_.refs_8_), channel_id=1, source_target_pairs={{0,8},{8,0},{1,9},{9,1},{2,10},{10,2},{3,11},{11,3},{4,12},{12,4},... | collective-permute-start | bytes 442376 | tf_op jit(solution)/shard_map/ppermute | solution.py:302
  58.8 4.5 %collective-permute-start.19 = (bf16[72,1024]{1,0:T(8,128)(2,1)S(1)}, bf16[72,1024]{1,0:T(8,128)(2,1)S(1)}, u32[]{:S(2)}, u32[]{:S(2)}) collective-permute-start(bf16[72,1024]{1,0:T(8,128)(2,1)S(1)} %collective-permute-done.15.refs_1_.refs_9_), channel_id=1, source_target_pairs={{0,8},{8,0},{1,9},{9,1},{2,10},{10,2},{3,11},{11,3},{4,12},{12,4},... | collective-permute-start | bytes 442376 | tf_op jit(solution)/shard_map/ppermute | solution.py:302
  58.8 4.5 %collective-permute-start.20 = (bf16[72,1024]{1,0:T(8,128)(2,1)S(1)}, bf16[72,1024]{1,0:T(8,128)(2,1)S(1)}, u32[]{:S(2)}, u32[]{:S(2)}) collective-permute-start(bf16[72,1024]{1,0:T(8,128)(2,1)S(1)} %collective-permute-done.16.refs_2_.refs_10_), channel_id=1, source_target_pairs={{0,8},{8,0},{1,9},{9,1},{2,10},{10,2},{3,11},{11,3},{4,12},{12,4},... | collective-permute-start | bytes 442376 | tf_op jit(solution)/shard_map/ppermute | solution.py:302
  61.2 2.6 %collective-permute-start.21 = (bf16[72,1024]{1,0:T(8,128)(2,1)S(1)}, bf16[72,1024]{1,0:T(8,128)(2,1)S(1)}, u32[]{:S(2)}, u32[]{:S(2)}) collective-permute-start(bf16[72,1024]{1,0:T(8,128)(2,1)S(1)} %collective-permute-done.17.refs_3_.refs_11_), channel_id=1, source_target_pairs={{0,8},{8,0},{1,9},{9,1},{2,10},{10,2},{3,11},{11,3},{4,12},{12,4},... | collective-permute-start | bytes 442376 | tf_op jit(solution)/shard_map/ppermute | solution.py:302
  62.8 1.8 %collective-permute-start.8 = (bf16[72,1024]{1,0:T(8,128)(2,1)S(1)}, bf16[72,1024]{1,0:T(8,128)(2,1)S(1)}, u32[]{:S(2)}, u32[]{:S(2)}) collective-permute-start(bf16[72,1024]{1,0:T(8,128)(2,1)S(1)} %acts_end.1.refs_0_), channel_id=1, source_target_pairs={{0,8},{8,0},{1,9},{9,1},{2,10},{10,2},{3,11},{11,3},{4,12},{12,4},... | collective-permute-start | bytes 442376 | tf_op jit(solution)/shard_map/ppermute | solution.py:302
  62.8 1.8 %collective-permute-start.9 = (bf16[72,1024]{1,0:T(8,128)(2,1)S(1)}, bf16[72,1024]{1,0:T(8,128)(2,1)S(1)}, u32[]{:S(2)}, u32[]{:S(2)}) collective-permute-start(bf16[72,1024]{1,0:T(8,128)(2,1)S(1)} %collective-permute-done.5.refs_1_), channel_id=1, source_target_pairs={{0,8},{8,0},{1,9},{9,1},{2,10},{10,2},{3,11},{11,3},{4,12},{12,4},... | collective-permute-start | bytes 442376 | tf_op jit(solution)/shard_map/ppermute | solution.py:302
  63.3 1.4 %collective-permute-start.10 = (bf16[72,1024]{1,0:T(8,128)(2,1)S(1)}, bf16[72,1024]{1,0:T(8,128)(2,1)S(1)}, u32[]{:S(2)}, u32[]{:S(2)}) collective-permute-start(bf16[72,1024]{1,0:T(8,128)(2,1)S(1)} %collective-permute-done.6.refs_2_), channel_id=1, source_target_pairs={{0,8},{8,0},{1,9},{9,1},{2,10},{10,2},{3,11},{11,3},{4,12},{12,4},... | collective-permute-start | bytes 442376 | tf_op jit(solution)/shard_map/ppermute | solution.py:302
  63.4 1.5 %collective-permute-start.11 = (bf16[72,1024]{1,0:T(8,128)(2,1)S(1)}, bf16[72,1024]{1,0:T(8,128)(2,1)S(1)}, u32[]{:S(2)}, u32[]{:S(2)}) collective-permute-start(bf16[72,1024]{1,0:T(8,128)(2,1)S(1)} %collective-permute-done.7.refs_3_), channel_id=1, source_target_pairs={{0,8},{8,0},{1,9},{9,1},{2,10},{10,2},{3,11},{11,3},{4,12},{12,4},... | collective-permute-start | bytes 442376 | tf_op jit(solution)/shard_map/ppermute | solution.py:302
  66.8 19.7 %all-to-all-start = ((bf16[16,64,384]{2,1,0:T(8,128)(2,1)}), bf16[16,64,384]{2,1,0:T(8,128)(2,1)S(1)}, u32[]{:S(2)}, u32[]{:S(2)}) async-start(bf16[16,64,384]{2,1,0:T(8,128)(2,1)} %acts_gram.1), calls=%async_computation | async-start | bytes 1572864 | tf_op jit(solution)/shard_map/all_to_all | solution.py:324
  88.1 0.6 copy-start.6
  88.7 0.6 copy-start.7
  89.3 0.6 copy-start.8

commit v3 on v2

--- a/solution.py
+++ b/solution.py
@@ -23,6 +23,9 @@
 
 
 SWAP = [(0, 1), (1, 0)]
+WIDTH = 1024
+AX = 256
+AZ = WIDTH - AX
 
 
 def last_row(shape):
@@ -99,58 +102,63 @@
     keep_ref[...] = jnp.dot(picked, b_ref[...], preferred_element_type=F32)
 
 
-def acts_send_kernel(routed_ref, h_ref, b_ref, s1_ref, s2_ref, s3_ref, bad_ref, sel_ref, out_ref):
+def acts_send_kernel(routed_ref, h_ref, b_ref, s1_ref, s2_ref, s3_ref, x_ref, keep_ref, picked_ref, bad_ref, sel_ref, z_ref):
     z, xl = lax.axis_index("z"), lax.axis_index("xl")
     pos, total = ranks(routed_ref[...])
     bad_ref[...] = jnp.broadcast_to(jnp.where(total > CAP, jnp.nan, 0.0), (8, 128))
-    blocks = []
-    for d in HOPS:
-        zz = lax.rem(z + d, 4)
-        blocks += [zz * 2 + xl, zz * 2 + (1 - xl)]
-    build_select(sel_ref, pos, blocks)
-    picked = jnp.dot(sel_ref[...], h_ref[...], preferred_element_type=F32).astype(BF)
-    out_ref[...] = jnp.dot(picked, b_ref[...], preferred_element_type=F32)
-    k = exponent_of(top_of(out_ref[...]))
+    zs = [lax.rem(z + d, 4) * 2 for d in (0,) + HOPS]
+    build_select(sel_ref, pos, [zz + xl for zz in zs] + [zz + (1 - xl) for zz in zs])
+    picked_ref[...] = jnp.dot(sel_ref[...], h_ref[...], preferred_element_type=F32).astype(BF)
+    z_ref[...] = jnp.dot(picked_ref[...], b_ref[:, :AZ], preferred_element_type=F32)
+    k = exponent_of(jnp.maximum(top_of(z_ref[SLOT : 4 * SLOT, :]), top_of(z_ref[5 * SLOT :, :])))
     for n, s_ref in enumerate((s1_ref, s2_ref, s3_ref)):
         for b in range(2):
-            at = (2 * n + b) * SLOT
-            s_ref[b] = encode(out_ref[at : at + SLOT, :], k)
-
-
-def acts_keep_kernel(routed_ref, h_ref, b_ref, after_ref, keep_ref, sel_ref):
-    z, xl = lax.axis_index("z"), lax.axis_index("xl")
-    pos, _ = ranks(routed_ref[...])
-    build_select(sel_ref, pos, [z * 2 + xl, z * 2 + (1 - xl)])
-    picked = jnp.dot(sel_ref[...], h_ref[...], preferred_element_type=F32).astype(BF)
-    keep_ref[...] = jnp.dot(picked, b_ref[...], preferred_element_type=F32)
-
-
-def grads_mid_kernel(keep_ref, got_ref, own_ref, s1_ref, s2_ref, s3_ref, tmp_ref):
-    own_ref[...] = keep_ref[:SLOT, :] + decode(got_ref[0])
+            at = (1 + n + 4 * b) * SLOT
+            s_ref[b] = encode(z_ref[at : at + SLOT, :], k)
+    for b in range(2):
+        keep_ref[b] = z_ref[4 * b * SLOT : (4 * b + 1) * SLOT, :]
+    x = jnp.dot(picked_ref[4 * SLOT :, :], b_ref[:, AZ:], preferred_element_type=F32)
+    k = exponent_of(top_of(x))
+    for b in range(4):
+        x_ref[b] = encode(x[b * SLOT : (b + 1) * SLOT, :], k)
+
+
+def acts_keep_kernel(picked_ref, b_ref, keep_ref):
+    keep_ref[...] = jnp.dot(picked_ref[: 4 * SLOT, :], b_ref[:, AZ:], preferred_element_type=F32)
+
+
+def x_mid_kernel(g_keep, g_got, a_keep, a_got, own_ref, s1_ref, s2_ref, s3_ref, tmp_ref):
+    def total(b):
+        rows = slice(b * SLOT, (b + 1) * SLOT)
+        return g_keep[rows, :] + decode(g_got[b]), a_keep[rows, :] + decode(a_got[b])
+
+    g, a = total(0)
+    own_ref[:, :WIDTH] = g
+    own_ref[:, WIDTH:] = a
+    top = jnp.zeros((1, 1), F32)
     for b in range(3):
-        tmp_ref[b] = keep_ref[(b + 1) * SLOT : (b + 2) * SLOT, :] + decode(got_ref[b + 1])
-    top = top_of(tmp_ref[0])
-    for b in (1, 2):
-        top = jnp.maximum(top, top_of(tmp_ref[b]))
+        g, a = total(b + 1)
+        tmp_ref[b, :, :WIDTH] = g
+        tmp_ref[b, :, WIDTH:] = a
+        top = jnp.maximum(top, jnp.maximum(top_of(g), top_of(a)))
     k = exponent_of(top)
     for b, s_ref in enumerate((s1_ref, s2_ref, s3_ref)):
         s_ref[...] = encode(tmp_ref[b], k)
 
 
-def acts_mid_kernel(keep_ref, r1_ref, r2_ref, r3_ref, after_ref, own_ref, send_ref):
-    own_ref[...] = keep_ref[:SLOT, :] + decode(r1_ref[0]) + decode(r2_ref[0]) + decode(r3_ref[0])
-    other = keep_ref[SLOT:, :] + decode(r1_ref[1]) + decode(r2_ref[1]) + decode(r3_ref[1])
+def z_mid_kernel(keep_ref, r1_ref, r2_ref, r3_ref, after_ref, own_ref, send_ref):
+    own_ref[...] = keep_ref[0] + decode(r1_ref[0]) + decode(r2_ref[0]) + decode(r3_ref[0])
+    other = keep_ref[1] + decode(r1_ref[1]) + decode(r2_ref[1]) + decode(r3_ref[1])
     send_ref[...] = encode(other, exponent_of(top_of(other)))
 
 
-def grads_end_kernel(own_ref, r1_ref, r2_ref, r3_ref, rot_ref):
+def x_end_kernel(own_ref, r1_ref, r2_ref, r3_ref, bad_ref, rot_ref):
     x = own_ref[...] + decode(r1_ref[...]) + decode(r2_ref[...]) + decode(r3_ref[...])
-    rot_ref[...] = x.astype(BF)
-
-
-def acts_end_kernel(own_ref, got_ref, bad_ref, rot_ref):
-    x = own_ref[...] + decode(got_ref[...]) + bad_ref[0:1, 0:1]
-    rot_ref[...] = x.astype(BF)
+    rot_ref[...] = (x + bad_ref[0:1, 0:1]).astype(BF)
+
+
+def z_end_kernel(own_ref, got_ref, rot_ref):
+    rot_ref[...] = (own_ref[...] + decode(got_ref[...])).astype(BF)
 
 
 PAD = 80
@@ -158,10 +166,10 @@
 CONTRACT = (((0,), (0,)), ((), ()))
 
 
-def gather_rows(dst_ref, refs):
+def gather_rows(dst_ref, cols, refs, part):
     for n, ref in enumerate(refs):
-        dst_ref[n * PAD : n * PAD + SLOT, :] = ref[...]
-        dst_ref[n * PAD + SLOT : (n + 1) * PAD, :] = jnp.zeros((PAD - SLOT, dst_ref.shape[1]), BF)
+        dst_ref[n * PAD : n * PAD + SLOT, cols] = ref[:, part]
+        dst_ref[n * PAD + SLOT : (n + 1) * PAD, cols] = jnp.zeros((PAD - SLOT, ref[:, part].shape[1]), BF)
 
 
 def square(v):
@@ -184,23 +192,24 @@
             out_ref[xh * 8 + cb, :, n * 128 : (n + 1) * 128] = t[xh * 64 : (xh + 1) * 64, cb * 128 : (cb + 1) * 128]
 
 
-def grads_gram_kernel(scale, *refs):
-    *g_refs, out_ref, g_s = refs
-    gather_rows(g_s, g_refs)
-    t = lax.dot_general(own_columns(g_s), g_s[...], CONTRACT, preferred_element_type=F32) * scale
-    put(out_ref, 0, t.astype(BF))
-
-
-def acts_gram_kernel(scale, *refs):
-    *in_refs, gram_ref, out_ref, a_s, g_s = refs
-    gather_rows(a_s, in_refs[:GATHERED])
-    gather_rows(g_s, in_refs[GATHERED:])
+def gram_kernel(scale, *refs):
+    x_refs, z_refs = refs[:GATHERED], refs[GATHERED : 2 * GATHERED]
+    out_ref, whole_ref, a_s, g_s = refs[2 * GATHERED :]
+    marks = x_refs[0][0:8, 0:128].astype(F32)
+    for ref in x_refs[1:]:
+        marks = marks + ref[0:8, 0:128].astype(F32)
+    whole_ref[...] = jnp.where(jnp.abs(marks) < 1e30, 1.0, 0.0)
+    gather_rows(g_s, slice(0, WIDTH), x_refs, slice(0, WIDTH))
+    gather_rows(a_s, slice(AZ, WIDTH), x_refs, slice(WIDTH, WIDTH + AX))
+    gather_rows(a_s, slice(0, AZ), z_refs, slice(0, AZ))
+
+    def dot(lhs, rhs):
+        return (lax.dot_general(lhs, rhs, CONTRACT, preferred_element_type=F32) * scale).astype(BF)
+
     own = own_columns(a_s)
-    t = lax.dot_general(own, a_s[...], CONTRACT, preferred_element_type=F32) * scale
-    put(out_ref, 0, t.astype(BF))
-    t = lax.dot_general(square(own), square(g_s[...]), CONTRACT, preferred_element_type=F32) * scale
-    put(out_ref, 2, t.astype(BF))
-    out_ref[:, :, 128:256] = gram_ref[...]
+    put(out_ref, 1, dot(own_columns(g_s), g_s[...]))
+    put(out_ref, 0, dot(own, a_s[...]))
+    put(out_ref, 2, dot(square(own), square(g_s[...])))
 
 
 def final_kernel(in_ref, a_ref, g_ref, c_ref):
@@ -219,8 +228,6 @@
 def call(kernel, name, out_shape, args, scratch=(), mib=16, flops=0, behind=0):
     vmem = pl.BlockSpec(memory_space=pltpu.VMEM)
     anywhere = pl.BlockSpec(memory_space=pl.ANY)
-    outs = out_shape if isinstance(out_shape, tuple) else (out_shape,)
-    size = sum(a.size * a.dtype.itemsize for a in args + tuple(outs))
     return pl.pallas_call(
         kernel,
         out_shape=out_shape,
@@ -228,101 +235,84 @@
         out_specs=(vmem,) * len(out_shape) if isinstance(out_shape, tuple) else vmem,
         scratch_shapes=list(scratch),
         compiler_params=pltpu.CompilerParams(vmem_limit_bytes=mib * 1024 * 1024),
-        cost_estimate=pl.CostEstimate(flops=flops, bytes_accessed=size, transcendentals=0),
+        cost_estimate=pl.CostEstimate(flops=flops, bytes_accessed=0, transcendentals=0),
         name=name,
     )(*args)
 
 
 def fast(hidden_acts, act_basis, out_grads, grad_basis, routed):
-    width = act_basis.shape[1]
-    tokens = hidden_acts.shape[0] * 16
+    scale = 1.0 / (hidden_acts.shape[0] * 16)
     slots = routed.reshape(8, 128)
-    blk = (SLOT, width)
-    scale = 1.0 / tokens
 
     def sel(n):
         return pltpu.VMEM((n * SLOT, 1024), BF)
 
-    def wide(n):
-        return pltpu.VMEM((n * SLOT, width), F32)
+    def blk(dtype, *shape):
+        return sds(shape[:-1] + (SLOT, shape[-1]), dtype)
 
     g_send = call(
-        grads_send_kernel, "grads_send", sds((4,) + blk, I16), (slots, out_grads, grad_basis), (sel(4), wide(4)), 16, 600_000_000
+        grads_send_kernel,
+        "grads_send",
+        blk(I16, 4, WIDTH),
+        (slots, out_grads, grad_basis),
+        (sel(4), pltpu.VMEM((4 * SLOT, WIDTH), F32)),
+        flops=10_000_000_000,
     )
     g_got = lax.ppermute(g_send, "xl", SWAP)
-
-    *a_send, bad = call(
+    *z_send, x_send, z_keep, picked, bad = call(
         acts_send_kernel,
         "acts_send",
-        (sds((2,) + blk, I16),) * 3 + (sds((8, 128), F32),),
+        (blk(I16, 2, AZ),) * 3
+        + (blk(I16, 4, AX), blk(F32, 2, AZ), sds((8 * SLOT, hidden_acts.shape[1]), BF), sds((8, 128), F32)),
         (slots, hidden_acts, act_basis),
-        (sel(6), wide(6)),
+        (sel(8), pltpu.VMEM((8 * SLOT, AZ), F32)),
         24,
-        3_200_000_000,
-    )
-    a_got = [lax.ppermute(s, "z", ring(d)) for s, d in zip(a_send, HOPS)]
-
+        4_000_000_000,
+    )
+    z_got = [lax.ppermute(s, "z", ring(d)) for s, d in zip(z_send, HOPS)]
+    x_got = lax.ppermute(x_send, "xl", SWAP)
     g_keep = call(
         grads_keep_kernel,
         "grads_keep",
-        sds((4 * SLOT, width), F32),
+        sds((4 * SLOT, WIDTH), F32),
         (slots, out_grads, grad_basis, bad),
         (sel(4),),
-        16,
-        600_000_000,
+        flops=600_000_000,
         behind=1,
     )
-    a_keep = call(
-        acts_keep_kernel,
-        "acts_keep",
-        sds((2 * SLOT, width), F32),
-        (slots, hidden_acts, act_basis, bad),
-        (sel(2),),
-        24,
-        1_100_000_000,
-        behind=1,
-    )
-
-    g_own, *g_next = call(
-        grads_mid_kernel,
-        "grads_mid",
-        (sds(blk, F32),) + (sds(blk, I16),) * 3,
-        (g_keep, g_got),
-        (pltpu.VMEM((3,) + blk, F32),),
-    )
-    g_last = [lax.ppermute(s, "z", ring(d)) for s, d in zip(g_next, HOPS)]
-
-    a_own, a_next = call(
-        acts_mid_kernel, "acts_mid", (sds(blk, F32), sds(blk, I16)), (a_keep, *a_got, g_own), behind=1
-    )
-    a_last = lax.ppermute(a_next, "xl", SWAP)
+    x_keep = call(acts_keep_kernel, "acts_keep", sds((4 * SLOT, AX), F32), (picked, act_basis), flops=300_000_000)
+
+    x_own, *x_next = call(
+        x_mid_kernel,
+        "x_mid",
+        (blk(F32, WIDTH + AX),) + (blk(I16, WIDTH + AX),) * 3,
+        (g_keep, g_got, x_keep, x_got),
+        (pltpu.VMEM((3, SLOT, WIDTH + AX), F32),),
+    )
+    x_last = [lax.ppermute(s, "z", ring(d)) for s, d in zip(x_next, HOPS)]
+    z_own, z_next = call(z_mid_kernel, "z_mid", (blk(F32, AZ), blk(I16, AZ)), (z_keep, *z_got, x_own), behind=1)
+    z_last = lax.ppermute(z_next, "xl", SWAP)
 
     def gathered(rot):
         near = [rot] + [lax.ppermute(rot, "y", ring(d)) for d in HOPS]
         return near + [lax.ppermute(r, "core", SWAP) for r in near]
 
-    rot_g = call(grads_end_kernel, "grads_end", sds(blk, BF), (g_own, *g_last))
-    all_g = gathered(rot_g)
-    rot_a = call(acts_end_kernel, "acts_end", sds(blk, BF), (a_own, a_last, bad))
-    all_a = gathered(rot_a)
-
-    def rows():
-        return pltpu.VMEM((GATHERED * PAD, width), BF)
-
-    gram = call(
-        lambda *refs: grads_gram_kernel(scale, *refs), "grads_gram", sds((16, 64, 128), BF), tuple(all_g), (rows(),), 16, 200_000_000
-    )
-    parts = call(
-        lambda *refs: acts_gram_kernel(scale, *refs),
-        "acts_gram",
-        sds((16, 64, 384), BF),
-        (*all_a, *all_g, gram),
-        (rows(), rows()),
-        16,
-        400_000_000,
+    rot_z = call(z_end_kernel, "z_end", blk(BF, AZ), (z_own, z_last))
+    all_z = gathered(rot_z)
+    rot_x = call(x_end_kernel, "x_end", blk(BF, WIDTH + AX), (x_own, *x_last, bad))
+    all_x = gathered(rot_x)
+
+    rows = pltpu.VMEM((GATHERED * PAD, WIDTH), BF)
+    parts, whole = call(
+        lambda *refs: gram_kernel(scale, *refs),
+        "gram",
+        (sds((16, 64, 384), BF), sds((8, 128), F32)),
+        (*all_x, *all_z),
+        (rows, rows),
+        flops=600_000_000,
     )
     got = lax.all_to_all(parts, ("xh", "z", "xl"), 0, 0, tiled=True)
-    return call(final_kernel, "final", (sds((64, 128), F32),) * 3, (got,))
+    return got, whole[0, 0] + lax.ppermute(whole, "xh", SWAP)[0, 0]
 
 
 DP = ("y", "xh", "core")
@@ -358,9 +348,12 @@
 
 
 def shards(*args):
-    act_gram, grad_gram, correction = fast(*args)
-    whole = jnp.abs(act_gram[0, 0]) < 1e30
-    return lax.cond(whole, lambda *_: (act_gram, grad_gram, correction), general, *args)
+    got, whole = fast(*args)
+
+    def total(got, *_):
+        return tuple(call(final_kernel, "final", (sds((64, 128), F32),) * 3, (got,)))
+
+    return lax.cond(whole > 1.5, total, lambda _, *rest: general(*rest), got, *args)
 
 
 def solution(mesh):

time: 97 us -> 88.2 us (0.909)
  waiting for transfers between devices: 32.6 us -> 18.3 us
  starting transfers between devices: 28.3 us -> 36.9 us
  Pallas kernels: 18.3 us -> 15.2 us
    all_to_all x1, waiting for transfers between devices: 14.8 us -> 0.25 us  [fast(): got = lax.all_to_all(parts, ('xh', 'z', 'xl'), 0, 0, tiled=True)]
    ppermute x7 -> x9, starting transfers between devices: 9.91 us -> 17.1 us  [the longest x3 6.22 us: fast(): x_last = [lax.ppermute(s, 'z', ring(d)) for s, d in zip(x_next, HOPS)]]
    pallas_call x11 -> x10, Pallas kernels: 18.3 us -> 15.2 us  [call(): pl.pallas_call(kernel, out_shape=out_shape, in_specs=[vmem] * (len(args)...]
    ppermute x8, waiting for transfers between devices: 0.26 us -> 1.89 us  [gathered(): return near + [lax.ppermute(r, 'core', SWAP) for r in near]]
    all_to_all x1, starting transfers between devices: 4.9 us -> 6.15 us  [fast(): got = lax.all_to_all(parts, ('xh', 'z', 'xl'), 0, 0, tiled=True)]
    ppermute x6, waiting for transfers between devices: 5.54 us -> 4.56 us  [gathered(): near = [rot] + [lax.ppermute(rot, 'y', ring(d)) for d in HOPS]]
    ppermute x7 -> x9, waiting for transfers between devices: 12 us -> 11.6 us  [the longest x1 8.78 us: fast(): return (got, whole[0, 0] + lax.ppermute(whole, 'xh', SWAP)[0, 0])]
  transfers between devices with their start and end apart: 23 -> 25, of which waited for: 10 -> 9; matrix products, arithmetic and copies ran while one was open for 0% -> 1% of each run, Pallas kernels for 13% -> 10%
where the time goes in v3:
time: 88.2 us; the launch traced here: 87.9 us
  starting transfers between devices  36.9 us (42%)
  waiting for transfers between devices  18.3 us (21%)
  between operations  15.4 us (17%)
  Pallas kernels  15.2 us (17%)
  local copies, waits for them, and re-layouts  2.13 us (2%)
    pallas_call x10, Pallas kernels, call(): pl.pallas_call(kernel, out_shape=out_shape, in_specs=[vmem] * (len(args)...  15.2 us
    ppermute x6, starting transfers between devices, gathered(): near = [rot] + [lax.ppermute(rot, 'y', ring(d)) for d in HOPS]  10.4 us
    ppermute x1, waiting for transfers between devices, fast(): return (got, whole[0, 0] + lax.ppermute(whole, 'xh', SWAP)[0, 0])  8.78 us
    ppermute x3, starting transfers between devices, fast(): x_last = [lax.ppermute(s, 'z', ring(d)) for s, d in zip(x_next, HOPS)]  6.22 us
    all_to_all x1, starting transfers between devices, fast(): got = lax.all_to_all(parts, ('xh', 'z', 'xl'), 0, 0, tiled=True)  6.15 us
    ppermute x3, starting transfers between devices, fast(): z_got = [lax.ppermute(s, 'z', ring(d)) for s, d in zip(z_send, HOPS)]  5.95 us
    ppermute x6, waiting for transfers between devices, gathered(): near = [rot] + [lax.ppermute(rot, 'y', ring(d)) for d in HOPS]  4.56 us
    ppermute x1, starting transfers between devices, fast(): return (got, whole[0, 0] + lax.ppermute(whole, 'xh', SWAP)[0, 0])  3.43 us
  transfers between devices with their start and end apart: 25, of which 9 were waited for; matrix products, arithmetic and copies ran while one was open for 1% of the time, Pallas kernels for 10%

profile of v3, /device:TPU:0, one launch (start us, length us, event | category | flops | bytes accessed | tf_op | source)
XLA Modules:
  0.0 87.9 jit_solution(7491207699835581102)
XLA Ops:
  7.2 3.4 %grads_send.1 = s16[4,72,1024]{2,1,0:T(8,128)(2,1)S(1)} custom-call(s32[8,128]{1,0:T(8,128)} %bitcast.6, bf16[1024,512]{1,0:T(8,128)(2,1)} %g_ref.3, bf16[512,1024]{1,0:T(8,128)(2,1)} %b_ref.6), custom_call_target="tpu_custom_call" | custom-call | flops 10000000000 | tf_op jit(solution)/shard_map/grads_send/pallas_call | solution.py:231
  10.6 1.7 %collective-permute-start = (s16[4,72,1024]{2,1,0:T(8,128)(2,1)S(1)}, s16[4,72,1024]{2,1,0:T(8,128)(2,1)S(1)}, u32[]{:S(2)}, u32[]{:S(2)}) collective-permute-start(s16[4,72,1024]{2,1,0:T(8,128)(2,1)S(1)} %grads_send.1), channel_id=1, source_target_pairs={{0,1},{1,0},{2,3},{3,2},{4,5},{5,4},{6,7},{7,6},{8,9},{9,8},{10,11... | collective-permute-start | bytes 1769480 | tf_op jit(solution)/shard_map/ppermute | solution.py:261
  12.3 5.3 %acts_send.1 = (s16[2,72,768]{2,1,0:T(8,128)(2,1)S(1)}, s16[2,72,768]{2,1,0:T(8,128)(2,1)S(1)}, s16[2,72,768]{2,1,0:T(8,128)(2,1)S(1)}, s16[4,72,256]{2,1,0:T(8,...) custom-call(s32[8,128]{1,0:T(8,128)S(1)} %bitcast.7, ...), custom_call_target="tpu_custom_call" | custom-call | flops 4000000000 | tf_op jit(solution)/shard_map/acts_send/pallas_call | solution.py:231
  17.6 2.0 %collective-permute-start.12 = (s16[2,72,768]{2,1,0:T(8,128)(2,1)S(1)}, s16[2,72,768]{2,1,0:T(8,128)(2,1)S(1)}, u32[]{:S(2)}, u32[]{:S(2)}) collective-permute-start(s16[2,72,768]{2,1,0:T(8,128)(2,1)S(1)} %get-tuple-element.42), channel_id=1, source_target_pairs={{0,2},{2,4},{4,6},{6,0},{1,3},{3,5},{5,7},{7,1},{8,10},{10,12},{12... | collective-permute-start | bytes 663560 | tf_op jit(solution)/shard_map/ppermute | solution.py:272
  19.6 2.2 %collective-permute-start.13 = (s16[2,72,768]{2,1,0:T(8,128)(2,1)S(1)}, s16[2,72,768]{2,1,0:T(8,128)(2,1)S(1)}, u32[]{:S(2)}, u32[]{:S(2)}) collective-permute-start(s16[2,72,768]{2,1,0:T(8,128)(2,1)S(1)} %get-tuple-element.43), channel_id=1, source_target_pairs={{0,6},{2,0},{4,2},{6,4},{1,7},{3,1},{5,3},{7,5},{8,14},{10,8},{12,... | collective-permute-start | bytes 663560 | tf_op jit(solution)/shard_map/ppermute | solution.py:272
  21.8 1.8 %collective-permute-start.14 = (s16[2,72,768]{2,1,0:T(8,128)(2,1)S(1)}, s16[2,72,768]{2,1,0:T(8,128)(2,1)S(1)}, u32[]{:S(2)}, u32[]{:S(2)}) collective-permute-start(s16[2,72,768]{2,1,0:T(8,128)(2,1)S(1)} %get-tuple-element.44), channel_id=1, source_target_pairs={{0,4},{2,6},{4,0},{6,2},{1,5},{3,7},{5,1},{7,3},{8,12},{10,14},{12... | collective-permute-start | bytes 663560 | tf_op jit(solution)/shard_map/ppermute | solution.py:272
  24.5 0.8 copy-done.1
  25.6 1.0 %grads_keep.1.g_keep = f32[288,1024]{1,0:T(8,128)S(1)} custom-call(s32[8,128]{1,0:T(8,128)S(1)} %bitcast.8, bf16[1024,512]{1,0:T(8,128)(2,1)S(1)} %copy-done.1, bf16[512,1024]{1,0:T(8,128)(2,1)S(1)} %copy-done.2, f32[8,128]{1,0:T(8,128)S(1)} %get-tuple-element.34.after_ref.bad_ref), custom_call_target="tpu_custom_call" | custom-call | flops 600000000 | tf_op jit(solution)/shard_map/grads_keep/pallas_call | solution.py:231
  26.6 2.1 %collective-permute-done.1.a_got = s16[4,72,256]{2,1,0:T(8,128)(2,1)S(1)} collective-permute-done((s16[4,72,256]{2,1,0:T(8,128)(2,1)S(1)}, s16[4,72,256]{2,1,0:T(8,128)(2,1)S(1)}, u32[]{:S(2)}, u32[]{:S(2)}) %collective-permute-start.1) | collective-permute-done | bytes 147488 | tf_op jit(solution)/shard_map/ppermute | solution.py:273
  28.7 1.1 %x_mid.1 = (f32[72,1280]{1,0:T(8,128)S(1)}, s16[72,1280]{1,0:T(8,128)(2,1)S(1)}, s16[72,1280]{1,0:T(8,128)(2,1)S(1)}, s16[72,1280]{1,0:T(8,128)(2,1)S(1)}) custom-call(f32[288,1024]{1,0:T(8,128)S(1)} %grads_keep.1.g_keep, s16[4,72,1024]{2,1,0:T(8,128)(2,1)S(1)} %collective-permute-done.g_got, f32[288,256]{1,0:T(8,128)S(1)} %acts_keep.1.a_keep, ...), custom_call_target="tpu_custom_call" | custom-call | tf_op jit(solution)/shard_map/x_mid/pallas_call | solution.py:231
  29.9 2.3 %collective-permute-start.2 = (s16[72,1280]{1,0:T(8,128)(2,1)S(1)}, s16[72,1280]{1,0:T(8,128)(2,1)S(1)}, u32[]{:S(2)}, u32[]{:S(2)}) collective-permute-start(s16[72,1280]{1,0:T(8,128)(2,1)S(1)} %get-tuple-element.38), channel_id=1, source_target_pairs={{0,2},{2,4},{4,6},{6,0},{1,3},{3,5},{5,7},{7,1},{8,10},{10,12},{12... | collective-permute-start | bytes 552968 | tf_op jit(solution)/shard_map/ppermute | solution.py:292
  32.1 0.6 collective-permute-done.14.r3_ref
  33.4 1.0 %collective-permute-start.15 = (s16[72,768]{1,0:T(8,128)(2,1)S(1)}, s16[72,768]{1,0:T(8,128)(2,1)S(1)}, u32[]{:S(2)}, u32[]{:S(2)}) collective-permute-start(s16[72,768]{1,0:T(8,128)(2,1)S(1)} %get-tuple-element.46), channel_id=1, source_target_pairs={{0,1},{1,0},{2,3},{3,2},{4,5},{5,4},{6,7},{7,6},{8,9},{9,8},{10,11... | collective-permute-start | bytes 331784 | tf_op jit(solution)/shard_map/ppermute | solution.py:294
  34.3 2.1 %collective-permute-start.3 = (s16[72,1280]{1,0:T(8,128)(2,1)S(1)}, s16[72,1280]{1,0:T(8,128)(2,1)S(1)}, u32[]{:S(2)}, u32[]{:S(2)}) collective-permute-start(s16[72,1280]{1,0:T(8,128)(2,1)S(1)} %get-tuple-element.39), channel_id=1, source_target_pairs={{0,6},{2,0},{4,2},{6,4},{1,7},{3,1},{5,3},{7,5},{8,14},{10,8},{12,... | collective-permute-start | bytes 552968 | tf_op jit(solution)/shard_map/ppermute | solution.py:292
  36.5 1.8 %collective-permute-start.4 = (s16[72,1280]{1,0:T(8,128)(2,1)S(1)}, s16[72,1280]{1,0:T(8,128)(2,1)S(1)}, u32[]{:S(2)}, u32[]{:S(2)}) collective-permute-start(s16[72,1280]{1,0:T(8,128)(2,1)S(1)} %get-tuple-element.40), channel_id=1, source_target_pairs={{0,4},{2,6},{4,0},{6,2},{1,5},{3,7},{5,1},{7,3},{8,12},{10,14},{12... | collective-permute-start | bytes 552968 | tf_op jit(solution)/shard_map/ppermute | solution.py:292
  38.4 1.8 %collective-permute-start.16 = (bf16[72,768]{1,0:T(8,128)(2,1)S(1)}, bf16[72,768]{1,0:T(8,128)(2,1)S(1)}, u32[]{:S(2)}, u32[]{:S(2)}) collective-permute-start(bf16[72,768]{1,0:T(8,128)(2,1)S(1)} %z_end.1.refs_8_), channel_id=1, source_target_pairs={{0,32},{32,64},{64,96},{96,0},{1,33},{33,65},{65,97},{97,1},{2,34}... | collective-permute-start | bytes 331784 | tf_op jit(solution)/shard_map/ppermute | solution.py:297
  40.2 1.7 %collective-permute-start.17 = (bf16[72,768]{1,0:T(8,128)(2,1)S(1)}, bf16[72,768]{1,0:T(8,128)(2,1)S(1)}, u32[]{:S(2)}, u32[]{:S(2)}) collective-permute-start(bf16[72,768]{1,0:T(8,128)(2,1)S(1)} %z_end.1.refs_8_), channel_id=1, source_target_pairs={{0,96},{32,0},{64,32},{96,64},{1,97},{33,1},{65,33},{97,65},{2,98}... | collective-permute-start | bytes 331784 | tf_op jit(solution)/shard_map/ppermute | solution.py:297
  41.9 2.0 %collective-permute-start.18 = (bf16[72,768]{1,0:T(8,128)(2,1)S(1)}, bf16[72,768]{1,0:T(8,128)(2,1)S(1)}, u32[]{:S(2)}, u32[]{:S(2)}) collective-permute-start(bf16[72,768]{1,0:T(8,128)(2,1)S(1)} %z_end.1.refs_8_), channel_id=1, source_target_pairs={{0,64},{32,96},{64,0},{96,32},{1,65},{33,97},{65,1},{97,33},{2,66}... | collective-permute-start | bytes 331784 | tf_op jit(solution)/shard_map/ppermute | solution.py:297
  44.3 1.3 %collective-permute-start.5 = (bf16[72,1280]{1,0:T(8,128)(2,1)S(1)}, bf16[72,1280]{1,0:T(8,128)(2,1)S(1)}, u32[]{:S(2)}, u32[]{:S(2)}) collective-permute-start(bf16[72,1280]{1,0:T(8,128)(2,1)S(1)} %x_end.1.refs_0_), channel_id=1, source_target_pairs={{0,32},{32,64},{64,96},{96,0},{1,33},{33,65},{65,97},{97,1},{2,34}... | collective-permute-start | bytes 552968 | tf_op jit(solution)/shard_map/ppermute | solution.py:297
  45.6 2.0 %collective-permute-start.6 = (bf16[72,1280]{1,0:T(8,128)(2,1)S(1)}, bf16[72,1280]{1,0:T(8,128)(2,1)S(1)}, u32[]{:S(2)}, u32[]{:S(2)}) collective-permute-start(bf16[72,1280]{1,0:T(8,128)(2,1)S(1)} %x_end.1.refs_0_), channel_id=1, source_target_pairs={{0,96},{32,0},{64,32},{96,64},{1,97},{33,1},{65,33},{97,65},{2,98}... | collective-permute-start | bytes 552968 | tf_op jit(solution)/shard_map/ppermute | solution.py:297
  47.6 1.6 %collective-permute-start.7 = (bf16[72,1280]{1,0:T(8,128)(2,1)S(1)}, bf16[72,1280]{1,0:T(8,128)(2,1)S(1)}, u32[]{:S(2)}, u32[]{:S(2)}) collective-permute-start(bf16[72,1280]{1,0:T(8,128)(2,1)S(1)} %x_end.1.refs_0_), channel_id=1, source_target_pairs={{0,64},{32,96},{64,0},{96,32},{1,65},{33,97},{65,1},{97,33},{2,66}... | collective-permute-start | bytes 552968 | tf_op jit(solution)/shard_map/ppermute | solution.py:297
  49.8 0.8 collective-permute-done.19.refs_12_
  51.1 1.9 %collective-permute-done.5.refs_1_ = bf16[72,1280]{1,0:T(8,128)(2,1)S(1)} collective-permute-done((bf16[72,1280]{1,0:T(8,128)(2,1)S(1)}, bf16[72,1280]{1,0:T(8,128)(2,1)S(1)}, u32[]{:S(2)}, u32[]{:S(2)}) %collective-permute-start.5) | collective-permute-done | bytes 184352 | tf_op jit(solution)/shard_map/ppermute | solution.py:297
  53.0 0.9 collective-permute-done.6.refs_2_
  53.9 1.8 %collective-permute-done.7.refs_3_ = bf16[72,1280]{1,0:T(8,128)(2,1)S(1)} collective-permute-done((bf16[72,1280]{1,0:T(8,128)(2,1)S(1)}, bf16[72,1280]{1,0:T(8,128)(2,1)S(1)}, u32[]{:S(2)}, u32[]{:S(2)}) %collective-permute-start.7) | collective-permute-done | bytes 184352 | tf_op jit(solution)/shard_map/ppermute | solution.py:297
  56.2 1.1 %collective-permute-done.22.refs_15_ = bf16[72,768]{1,0:T(8,128)(2,1)S(1)} collective-permute-done((bf16[72,768]{1,0:T(8,128)(2,1)S(1)}, bf16[72,768]{1,0:T(8,128)(2,1)S(1)}, u32[]{:S(2)}, u32[]{:S(2)}) %collective-permute-start.22) | collective-permute-done | bytes 110624 | tf_op jit(solution)/shard_map/ppermute | solution.py:298
  57.3 2.1 %gram.1 = (bf16[16,64,384]{2,1,0:T(8,128)(2,1)}, f32[8,128]{1,0:T(8,128)S(1)}) custom-call(bf16[72,1280]{1,0:T(8,128)(2,1)S(1)} %x_end.1.refs_0_, bf16[72,1280]{1,0:T(8,128)(2,1)S(1)} %collective-permute-done.5.refs_1_, bf16[72,1280]{1,0:T(8,128)(2,1)S(1)} %collective-permute-done.6.refs_2_, bf16[72,1280]{1,0:T(8,128)(2,1)S(1)} %collective-permute-done.7.refs_3_, ...), custom_call_target="tpu_custom_call" | custom-call | flops 600000000 | tf_op jit(solution)/shard_map/gram/pallas_call | solution.py:231
  59.4 6.2 %all-to-all-start = ((bf16[16,64,384]{2,1,0:T(8,128)(2,1)}), bf16[16,64,384]{2,1,0:T(8,128)(2,1)S(1)}, u32[]{:S(2)}, u32[]{:S(2)}) async-start(bf16[16,64,384]{2,1,0:T(8,128)(2,1)} %get-tuple-element.48), calls=%async_computation | async-start | bytes 1572864 | tf_op jit(solution)/shard_map/all_to_all | solution.py:314
  65.5 3.4 %collective-permute-start.23 = (f32[8,128]{1,0:T(8,128)S(1)}, f32[8,128]{1,0:T(8,128)S(1)}, u32[]{:S(2)}, u32[]{:S(2)}) collective-permute-start(f32[8,128]{1,0:T(8,128)S(1)} %get-tuple-element.47), channel_id=1, source_target_pairs={{0,16},{16,0},{1,17},{17,1},{2,18},{18,2},{3,19},{19,3},{4,20},{20... | collective-permute-start | bytes 12296 | tf_op jit(solution)/shard_map/ppermute | solution.py:315
  69.5 8.8 %collective-permute-done.23 = f32[8,128]{1,0:T(8,128)S(1)} collective-permute-done((f32[8,128]{1,0:T(8,128)S(1)}, f32[8,128]{1,0:T(8,128)S(1)}, u32[]{:S(2)}, u32[]{:S(2)}) %collective-permute-start.23) | collective-permute-done | bytes 4128 | tf_op jit(solution)/shard_map/ppermute | solution.py:315
  80.3 0.8 conditional.1
  80.3 0.7 final.1
  (41 shorter events, 5.3 us)
Async XLA Ops:
  7.2 5.1 %copy-start = (bf16[1792,1024]{1,0:T(8,128)(2,1)S(1)}, bf16[1792,1024]{1,0:T(8,128)(2,1)}, u32[]{:S(2)}) copy-start(bf16[1792,1024]{1,0:T(8,128)(2,1)} %b_ref.7) | copy-start | bytes 11010052
  7.2 5.1 %copy-start.3 = (s32[1024]{0:T(1024)S(1)}, s32[1024]{0:T(1024)}, u32[]{:S(2)}) copy-start(s32[1024]{0:T(1024)} %param.11) | copy-start | bytes 12292
  7.2 5.1 %copy-start.4 = (bf16[1024,1792]{1,0:T(8,128)(2,1)S(1)}, bf16[1024,1792]{1,0:T(8,128)(2,1)}, u32[]{:S(2)}) copy-start(bf16[1024,1792]{1,0:T(8,128)(2,1)} %h_ref.1) | copy-start | bytes 11010052
  10.6 18.1 %collective-permute-start = (s16[4,72,1024]{2,1,0:T(8,128)(2,1)S(1)}, s16[4,72,1024]{2,1,0:T(8,128)(2,1)S(1)}, u32[]{:S(2)}, u32[]{:S(2)}) collective-permute-start(s16[4,72,1024]{2,1,0:T(8,128)(2,1)S(1)} %grads_send.1), channel_id=1, source_target_pairs={{0,1},{1,0},{2,3},{3,2},{4,5},{5,4},{6,7},{7,6},{8,9},{9,8},{10,11... | collective-permute-start | bytes 1769480 | tf_op jit(solution)/shard_map/ppermute | solution.py:261
  17.6 14.5 %collective-permute-start.12 = (s16[2,72,768]{2,1,0:T(8,128)(2,1)S(1)}, s16[2,72,768]{2,1,0:T(8,128)(2,1)S(1)}, u32[]{:S(2)}, u32[]{:S(2)}) collective-permute-start(s16[2,72,768]{2,1,0:T(8,128)(2,1)S(1)} %get-tuple-element.42), channel_id=1, source_target_pairs={{0,2},{2,4},{4,6},{6,0},{1,3},{3,5},{5,7},{7,1},{8,10},{10,12},{12... | collective-permute-start | bytes 663560 | tf_op jit(solution)/shard_map/ppermute | solution.py:272
  19.6 12.6 %collective-permute-start.13 = (s16[2,72,768]{2,1,0:T(8,128)(2,1)S(1)}, s16[2,72,768]{2,1,0:T(8,128)(2,1)S(1)}, u32[]{:S(2)}, u32[]{:S(2)}) collective-permute-start(s16[2,72,768]{2,1,0:T(8,128)(2,1)S(1)} %get-tuple-element.43), channel_id=1, source_target_pairs={{0,6},{2,0},{4,2},{6,4},{1,7},{3,1},{5,3},{7,5},{8,14},{10,8},{12,... | collective-permute-start | bytes 663560 | tf_op jit(solution)/shard_map/ppermute | solution.py:272
  21.8 11.0 %collective-permute-start.14 = (s16[2,72,768]{2,1,0:T(8,128)(2,1)S(1)}, s16[2,72,768]{2,1,0:T(8,128)(2,1)S(1)}, u32[]{:S(2)}, u32[]{:S(2)}) collective-permute-start(s16[2,72,768]{2,1,0:T(8,128)(2,1)S(1)} %get-tuple-element.44), channel_id=1, source_target_pairs={{0,4},{2,6},{4,0},{6,2},{1,5},{3,7},{5,1},{7,3},{8,12},{10,14},{12... | collective-permute-start | bytes 663560 | tf_op jit(solution)/shard_map/ppermute | solution.py:272
  23.5 5.2 %collective-permute-start.1 = (s16[4,72,256]{2,1,0:T(8,128)(2,1)S(1)}, s16[4,72,256]{2,1,0:T(8,128)(2,1)S(1)}, u32[]{:S(2)}, u32[]{:S(2)}) collective-permute-start(s16[4,72,256]{2,1,0:T(8,128)(2,1)S(1)} %get-tuple-element.36), channel_id=1, source_target_pairs={{0,1},{1,0},{2,3},{3,2},{4,5},{5,4},{6,7},{7,6},{8,9},{9,8},{10,11... | collective-permute-start | bytes 442376 | tf_op jit(solution)/shard_map/ppermute | solution.py:273
  24.1 1.2 %copy-start.1 = (bf16[1024,512]{1,0:T(8,128)(2,1)S(1)}, bf16[1024,512]{1,0:T(8,128)(2,1)}, u32[]{:S(2)}) copy-start(bf16[1024,512]{1,0:T(8,128)(2,1)} %g_ref.3) | copy-start | bytes 3145732
  24.1 1.5 %copy-start.2 = (bf16[512,1024]{1,0:T(8,128)(2,1)S(1)}, bf16[512,1024]{1,0:T(8,128)(2,1)}, u32[]{:S(2)}) copy-start(bf16[512,1024]{1,0:T(8,128)(2,1)} %b_ref.6) | copy-start | bytes 3145732
  29.9 12.0 %collective-permute-start.2 = (s16[72,1280]{1,0:T(8,128)(2,1)S(1)}, s16[72,1280]{1,0:T(8,128)(2,1)S(1)}, u32[]{:S(2)}, u32[]{:S(2)}) collective-permute-start(s16[72,1280]{1,0:T(8,128)(2,1)S(1)} %get-tuple-element.38), channel_id=1, source_target_pairs={{0,2},{2,4},{4,6},{6,0},{1,3},{3,5},{5,7},{7,1},{8,10},{10,12},{12... | collective-permute-start | bytes 552968 | tf_op jit(solution)/shard_map/ppermute | solution.py:292
  33.4 4.9 %collective-permute-start.15 = (s16[72,768]{1,0:T(8,128)(2,1)S(1)}, s16[72,768]{1,0:T(8,128)(2,1)S(1)}, u32[]{:S(2)}, u32[]{:S(2)}) collective-permute-start(s16[72,768]{1,0:T(8,128)(2,1)S(1)} %get-tuple-element.46), channel_id=1, source_target_pairs={{0,1},{1,0},{2,3},{3,2},{4,5},{5,4},{6,7},{7,6},{8,9},{9,8},{10,11... | collective-permute-start | bytes 331784 | tf_op jit(solution)/shard_map/ppermute | solution.py:294
  34.3 9.5 %collective-permute-start.3 = (s16[72,1280]{1,0:T(8,128)(2,1)S(1)}, s16[72,1280]{1,0:T(8,128)(2,1)S(1)}, u32[]{:S(2)}, u32[]{:S(2)}) collective-permute-start(s16[72,1280]{1,0:T(8,128)(2,1)S(1)} %get-tuple-element.39), channel_id=1, source_target_pairs={{0,6},{2,0},{4,2},{6,4},{1,7},{3,1},{5,3},{7,5},{8,14},{10,8},{12,... | collective-permute-start | bytes 552968 | tf_op jit(solution)/shard_map/ppermute | solution.py:292
  36.5 7.4 %collective-permute-start.4 = (s16[72,1280]{1,0:T(8,128)(2,1)S(1)}, s16[72,1280]{1,0:T(8,128)(2,1)S(1)}, u32[]{:S(2)}, u32[]{:S(2)}) collective-permute-start(s16[72,1280]{1,0:T(8,128)(2,1)S(1)} %get-tuple-element.40), channel_id=1, source_target_pairs={{0,4},{2,6},{4,0},{6,2},{1,5},{3,7},{5,1},{7,3},{8,12},{10,14},{12... | collective-permute-start | bytes 552968 | tf_op jit(solution)/shard_map/ppermute | solution.py:292
  38.4 9.3 %collective-permute-start.16 = (bf16[72,768]{1,0:T(8,128)(2,1)S(1)}, bf16[72,768]{1,0:T(8,128)(2,1)S(1)}, u32[]{:S(2)}, u32[]{:S(2)}) collective-permute-start(bf16[72,768]{1,0:T(8,128)(2,1)S(1)} %z_end.1.refs_8_), channel_id=1, source_target_pairs={{0,32},{32,64},{64,96},{96,0},{1,33},{33,65},{65,97},{97,1},{2,34}... | collective-permute-start | bytes 331784 | tf_op jit(solution)/shard_map/ppermute | solution.py:297
  40.2 9.1 %collective-permute-start.17 = (bf16[72,768]{1,0:T(8,128)(2,1)S(1)}, bf16[72,768]{1,0:T(8,128)(2,1)S(1)}, u32[]{:S(2)}, u32[]{:S(2)}) collective-permute-start(bf16[72,768]{1,0:T(8,128)(2,1)S(1)} %z_end.1.refs_8_), channel_id=1, source_target_pairs={{0,96},{32,0},{64,32},{96,64},{1,97},{33,1},{65,33},{97,65},{2,98}... | collective-permute-start | bytes 331784 | tf_op jit(solution)/shard_map/ppermute | solution.py:297
  41.9 7.4 %collective-permute-start.18 = (bf16[72,768]{1,0:T(8,128)(2,1)S(1)}, bf16[72,768]{1,0:T(8,128)(2,1)S(1)}, u32[]{:S(2)}, u32[]{:S(2)}) collective-permute-start(bf16[72,768]{1,0:T(8,128)(2,1)S(1)} %z_end.1.refs_8_), channel_id=1, source_target_pairs={{0,64},{32,96},{64,0},{96,32},{1,65},{33,97},{65,1},{97,33},{2,66}... | collective-permute-start | bytes 331784 | tf_op jit(solution)/shard_map/ppermute | solution.py:297
  44.3 8.7 %collective-permute-start.5 = (bf16[72,1280]{1,0:T(8,128)(2,1)S(1)}, bf16[72,1280]{1,0:T(8,128)(2,1)S(1)}, u32[]{:S(2)}, u32[]{:S(2)}) collective-permute-start(bf16[72,1280]{1,0:T(8,128)(2,1)S(1)} %x_end.1.refs_0_), channel_id=1, source_target_pairs={{0,32},{32,64},{64,96},{96,0},{1,33},{33,65},{65,97},{97,1},{2,34}... | collective-permute-start | bytes 552968 | tf_op jit(solution)/shard_map/ppermute | solution.py:297
  45.6 8.2 %collective-permute-start.6 = (bf16[72,1280]{1,0:T(8,128)(2,1)S(1)}, bf16[72,1280]{1,0:T(8,128)(2,1)S(1)}, u32[]{:S(2)}, u32[]{:S(2)}) collective-permute-start(bf16[72,1280]{1,0:T(8,128)(2,1)S(1)} %x_end.1.refs_0_), channel_id=1, source_target_pairs={{0,96},{32,0},{64,32},{96,64},{1,97},{33,1},{65,33},{97,65},{2,98}... | collective-permute-start | bytes 552968 | tf_op jit(solution)/shard_map/ppermute | solution.py:297
  47.6 8.0 %collective-permute-start.7 = (bf16[72,1280]{1,0:T(8,128)(2,1)S(1)}, bf16[72,1280]{1,0:T(8,128)(2,1)S(1)}, u32[]{:S(2)}, u32[]{:S(2)}) collective-permute-start(bf16[72,1280]{1,0:T(8,128)(2,1)S(1)} %x_end.1.refs_0_), channel_id=1, source_target_pairs={{0,64},{32,96},{64,0},{96,32},{1,65},{33,97},{65,1},{97,33},{2,66}... | collective-permute-start | bytes 552968 | tf_op jit(solution)/shard_map/ppermute | solution.py:297
  49.3 1.3 %collective-permute-start.19 = (bf16[72,768]{1,0:T(8,128)(2,1)S(1)}, bf16[72,768]{1,0:T(8,128)(2,1)S(1)}, u32[]{:S(2)}, u32[]{:S(2)}) collective-permute-start(bf16[72,768]{1,0:T(8,128)(2,1)S(1)} %z_end.1.refs_8_), channel_id=1, source_target_pairs={{0,8},{8,0},{1,9},{9,1},{2,10},{10,2},{3,11},{11,3},{4,12},{12,4},... | collective-permute-start | bytes 331784 | tf_op jit(solution)/shard_map/ppermute | solution.py:298
  49.3 1.5 %collective-permute-start.20 = (bf16[72,768]{1,0:T(8,128)(2,1)S(1)}, bf16[72,768]{1,0:T(8,128)(2,1)S(1)}, u32[]{:S(2)}, u32[]{:S(2)}) collective-permute-start(bf16[72,768]{1,0:T(8,128)(2,1)S(1)} %collective-permute-done.16.refs_9_), channel_id=1, source_target_pairs={{0,8},{8,0},{1,9},{9,1},{2,10},{10,2},{3,11},{11,3},{4,12},{12,4},... | collective-permute-start | bytes 331784 | tf_op jit(solution)/shard_map/ppermute | solution.py:298
  50.6 5.1 %collective-permute-start.21 = (bf16[72,768]{1,0:T(8,128)(2,1)S(1)}, bf16[72,768]{1,0:T(8,128)(2,1)S(1)}, u32[]{:S(2)}, u32[]{:S(2)}) collective-permute-start(bf16[72,768]{1,0:T(8,128)(2,1)S(1)} %collective-permute-done.17.refs_10_), channel_id=1, source_target_pairs={{0,8},{8,0},{1,9},{9,1},{2,10},{10,2},{3,11},{11,3},{4,12},{12,4},... | collective-permute-start | bytes 331784 | tf_op jit(solution)/shard_map/ppermute | solution.py:298
  50.7 6.5 %collective-permute-start.8 = (bf16[72,1280]{1,0:T(8,128)(2,1)S(1)}, bf16[72,1280]{1,0:T(8,128)(2,1)S(1)}, u32[]{:S(2)}, u32[]{:S(2)}) collective-permute-start(bf16[72,1280]{1,0:T(8,128)(2,1)S(1)} %x_end.1.refs_0_), channel_id=1, source_target_pairs={{0,8},{8,0},{1,9},{9,1},{2,10},{10,2},{3,11},{11,3},{4,12},{12,4},... | collective-permute-start | bytes 552968 | tf_op jit(solution)/shard_map/ppermute | solution.py:298
  53.0 4.2 %collective-permute-start.9 = (bf16[72,1280]{1,0:T(8,128)(2,1)S(1)}, bf16[72,1280]{1,0:T(8,128)(2,1)S(1)}, u32[]{:S(2)}, u32[]{:S(2)}) collective-permute-start(bf16[72,1280]{1,0:T(8,128)(2,1)S(1)} %collective-permute-done.5.refs_1_), channel_id=1, source_target_pairs={{0,8},{8,0},{1,9},{9,1},{2,10},{10,2},{3,11},{11,3},{4,12},{12,4},... | collective-permute-start | bytes 552968 | tf_op jit(solution)/shard_map/ppermute | solution.py:298
  53.9 3.4 %collective-permute-start.10 = (bf16[72,1280]{1,0:T(8,128)(2,1)S(1)}, bf16[72,1280]{1,0:T(8,128)(2,1)S(1)}, u32[]{:S(2)}, u32[]{:S(2)}) collective-permute-start(bf16[72,1280]{1,0:T(8,128)(2,1)S(1)} %collective-permute-done.6.refs_2_), channel_id=1, source_target_pairs={{0,8},{8,0},{1,9},{9,1},{2,10},{10,2},{3,11},{11,3},{4,12},{12,4},... | collective-permute-start | bytes 552968 | tf_op jit(solution)/shard_map/ppermute | solution.py:298
  55.7 1.6 %collective-permute-start.11 = (bf16[72,1280]{1,0:T(8,128)(2,1)S(1)}, bf16[72,1280]{1,0:T(8,128)(2,1)S(1)}, u32[]{:S(2)}, u32[]{:S(2)}) collective-permute-start(bf16[72,1280]{1,0:T(8,128)(2,1)S(1)} %collective-permute-done.7.refs_3_), channel_id=1, source_target_pairs={{0,8},{8,0},{1,9},{9,1},{2,10},{10,2},{3,11},{11,3},{4,12},{12,4},... | collective-permute-start | bytes 552968 | tf_op jit(solution)/shard_map/ppermute | solution.py:298
  55.7 1.6 %collective-permute-start.22 = (bf16[72,768]{1,0:T(8,128)(2,1)S(1)}, bf16[72,768]{1,0:T(8,128)(2,1)S(1)}, u32[]{:S(2)}, u32[]{:S(2)}) collective-permute-start(bf16[72,768]{1,0:T(8,128)(2,1)S(1)} %collective-permute-done.18.refs_11_), channel_id=1, source_target_pairs={{0,8},{8,0},{1,9},{9,1},{2,10},{10,2},{3,11},{11,3},{4,12},{12,4},... | collective-permute-start | bytes 331784 | tf_op jit(solution)/shard_map/ppermute | solution.py:298
  59.4 21.0 %all-to-all-start = ((bf16[16,64,384]{2,1,0:T(8,128)(2,1)}), bf16[16,64,384]{2,1,0:T(8,128)(2,1)S(1)}, u32[]{:S(2)}, u32[]{:S(2)}) async-start(bf16[16,64,384]{2,1,0:T(8,128)(2,1)} %get-tuple-element.48), calls=%async_computation | async-start | bytes 1572864 | tf_op jit(solution)/shard_map/all_to_all | solution.py:314
  65.5 12.7 %collective-permute-start.23 = (f32[8,128]{1,0:T(8,128)S(1)}, f32[8,128]{1,0:T(8,128)S(1)}, u32[]{:S(2)}, u32[]{:S(2)}) collective-permute-start(f32[8,128]{1,0:T(8,128)S(1)} %get-tuple-element.47), channel_id=1, source_target_pairs={{0,16},{16,0},{1,17},{17,1},{2,18},{18,2},{3,19},{19,3},{4,20},{20... | collective-permute-start | bytes 12296 | tf_op jit(solution)/shard_map/ppermute | solution.py:315

commit v4 on v3

--- a/solution.py
+++ b/solution.py
@@ -16,6 +16,7 @@
 CAP = KEEP * BLOCKS
 TOP = 32767.0
 HOPS = (1, 3, 2)
+ROUND = (2, 3, 1)
 
 
 def ring(dist):
@@ -102,29 +103,44 @@
     keep_ref[...] = jnp.dot(picked, b_ref[...], preferred_element_type=F32)
 
 
-def acts_send_kernel(routed_ref, h_ref, b_ref, s1_ref, s2_ref, s3_ref, x_ref, keep_ref, picked_ref, bad_ref, sel_ref, z_ref):
+def acts_z_kernel(routed_ref, h_ref, b_ref, s1_ref, s2_ref, s3_ref, picked_ref, bad_ref, sel_ref, z_ref):
     z, xl = lax.axis_index("z"), lax.axis_index("xl")
     pos, total = ranks(routed_ref[...])
     bad_ref[...] = jnp.broadcast_to(jnp.where(total > CAP, jnp.nan, 0.0), (8, 128))
-    zs = [lax.rem(z + d, 4) * 2 for d in (0,) + HOPS]
-    build_select(sel_ref, pos, [zz + xl for zz in zs] + [zz + (1 - xl) for zz in zs])
+    zs = [lax.rem(z + d, 4) * 2 for d in HOPS]
+    build_select(sel_ref, pos, [zz + (1 - xl) for zz in zs] + [zz + xl for zz in zs])
     picked_ref[...] = jnp.dot(sel_ref[...], h_ref[...], preferred_element_type=F32).astype(BF)
     z_ref[...] = jnp.dot(picked_ref[...], b_ref[:, :AZ], preferred_element_type=F32)
-    k = exponent_of(jnp.maximum(top_of(z_ref[SLOT : 4 * SLOT, :]), top_of(z_ref[5 * SLOT :, :])))
+    k = exponent_of(top_of(z_ref[...]))
     for n, s_ref in enumerate((s1_ref, s2_ref, s3_ref)):
         for b in range(2):
-            at = (1 + n + 4 * b) * SLOT
+            at = (n + 3 * (1 - b)) * SLOT
             s_ref[b] = encode(z_ref[at : at + SLOT, :], k)
-    for b in range(2):
-        keep_ref[b] = z_ref[4 * b * SLOT : (4 * b + 1) * SLOT, :]
-    x = jnp.dot(picked_ref[4 * SLOT :, :], b_ref[:, AZ:], preferred_element_type=F32)
-    k = exponent_of(top_of(x))
+
+
+def acts_x_kernel(routed_ref, h_ref, b_ref, picked_ref, x_ref, near_ref, sel_ref):
+    z, xl = lax.axis_index("z"), lax.axis_index("xl")
+    pos, _ = ranks(routed_ref[...])
+    build_select(sel_ref, pos, [z * 2 + (1 - xl), z * 2 + xl])
+    near_ref[...] = jnp.dot(sel_ref[...], h_ref[...], preferred_element_type=F32).astype(BF)
+    far = jnp.dot(picked_ref[: 3 * SLOT + 8, :], b_ref[:, AZ:], preferred_element_type=F32)
+    near = jnp.dot(near_ref[: SLOT + 8, :], b_ref[:, AZ:], preferred_element_type=F32)
+    parts = [near[:SLOT]] + [far[n * SLOT : (n + 1) * SLOT] for n in range(3)]
+    top = top_of(parts[0])
+    for part in parts[1:]:
+        top = jnp.maximum(top, top_of(part))
+    k = exponent_of(top)
     for b in range(4):
-        x_ref[b] = encode(x[b * SLOT : (b + 1) * SLOT, :], k)
-
-
-def acts_keep_kernel(picked_ref, b_ref, keep_ref):
-    keep_ref[...] = jnp.dot(picked_ref[: 4 * SLOT, :], b_ref[:, AZ:], preferred_element_type=F32)
+        x_ref[b] = encode(parts[b], k)
+
+
+def acts_keep_kernel(picked_ref, near_ref, b_ref, z_ref, x_ref):
+    far = jnp.dot(picked_ref[3 * SLOT - 8 :, :], b_ref[:, AZ:], preferred_element_type=F32)
+    near = jnp.dot(near_ref[...], b_ref[...], preferred_element_type=F32)
+    x_ref[:SLOT, :] = near[SLOT:, AZ:]
+    x_ref[SLOT:, :] = far[8:, :]
+    z_ref[0] = near[SLOT:, :AZ]
+    z_ref[1] = near[:SLOT, :AZ]
 
 
 def x_mid_kernel(g_keep, g_got, a_keep, a_got, own_ref, s1_ref, s2_ref, s3_ref, tmp_ref):
@@ -259,28 +275,43 @@
         flops=10_000_000_000,
     )
     g_got = lax.ppermute(g_send, "xl", SWAP)
-    *z_send, x_send, z_keep, picked, bad = call(
-        acts_send_kernel,
-        "acts_send",
-        (blk(I16, 2, AZ),) * 3
-        + (blk(I16, 4, AX), blk(F32, 2, AZ), sds((8 * SLOT, hidden_acts.shape[1]), BF), sds((8, 128), F32)),
+    feats = hidden_acts.shape[1]
+    *z_send, picked, bad = call(
+        acts_z_kernel,
+        "acts_z",
+        (blk(I16, 2, AZ),) * 3 + (sds((6 * SLOT, feats), BF), sds((8, 128), F32)),
         (slots, hidden_acts, act_basis),
-        (sel(8), pltpu.VMEM((8 * SLOT, AZ), F32)),
+        (sel(6), pltpu.VMEM((6 * SLOT, AZ), F32)),
         24,
         4_000_000_000,
     )
     z_got = [lax.ppermute(s, "z", ring(d)) for s, d in zip(z_send, HOPS)]
+    x_send, near = call(
+        acts_x_kernel,
+        "acts_x",
+        (blk(I16, 4, AX), sds((2 * SLOT, feats), BF)),
+        (slots, hidden_acts, act_basis, picked),
+        (sel(2),),
+        24,
+        1_000_000_000,
+    )
     x_got = lax.ppermute(x_send, "xl", SWAP)
     g_keep = call(
         grads_keep_kernel,
         "grads_keep",
         sds((4 * SLOT, WIDTH), F32),
-        (slots, out_grads, grad_basis, bad),
+        (slots, out_grads, grad_basis, near),
         (sel(4),),
         flops=600_000_000,
         behind=1,
     )
-    x_keep = call(acts_keep_kernel, "acts_keep", sds((4 * SLOT, AX), F32), (picked, act_basis), flops=300_000_000)
+    z_keep, x_keep = call(
+        acts_keep_kernel,
+        "acts_keep",
+        (blk(F32, 2, AZ), sds((4 * SLOT, AX), F32)),
+        (picked, near, act_basis),
+        flops=1_000_000_000,
+    )
 
     x_own, *x_next = call(
         x_mid_kernel,
@@ -294,7 +325,7 @@
     z_last = lax.ppermute(z_next, "xl", SWAP)
 
     def gathered(rot):
-        near = [rot] + [lax.ppermute(rot, "y", ring(d)) for d in HOPS]
+        near = [rot] + [lax.ppermute(rot, "y", ring(d)) for d in ROUND]
         return near + [lax.ppermute(r, "core", SWAP) for r in near]
 
     rot_z = call(z_end_kernel, "z_end", blk(BF, AZ), (z_own, z_last))
@@ -320,31 +351,27 @@
 
 
 def general(hidden_acts, act_basis, out_grads, grad_basis, routed):
-    act_part = jnp.dot(hidden_acts, act_basis, preferred_element_type=F32)
-    grad_part = jnp.dot(out_grads, grad_basis, preferred_element_type=F32)
-    act_sum, grad_sum = lax.psum((act_part, grad_part), TENSOR)
-    rot_acts = act_sum.astype(BF)
-    rot_grads = grad_sum.astype(BF)
-    total_tokens = rot_acts.shape[0] * 16
-    weights = routed.astype(F32)[:, None]
-    acts_f = rot_acts.astype(F32)
-    grads_f = rot_grads.astype(F32)
-    masked_acts = (acts_f * weights).astype(BF)
-    masked_grads = (grads_f * weights).astype(BF)
-    sq_acts = (acts_f * acts_f * weights).astype(BF)
-    sq_grads = (grads_f * grads_f).astype(BF)
-    col_width = rot_acts.shape[1] // 8
-    col_start = (lax.axis_index("z") * 2 + lax.axis_index("xl")) * col_width
-    own_rows = rot_acts.shape[1] // 16
-    row_start = ((lax.axis_index("y") * 2 + lax.axis_index("xh")) * 2 + lax.axis_index("core")) * own_rows
-    contract = (((0,), (0,)), ((), ()))
-    terms = []
-    for left, right in ((masked_acts, rot_acts), (masked_grads, rot_grads), (sq_acts, sq_grads)):
-        cols = lax.dynamic_slice_in_dim(right, col_start, col_width, 1)
-        terms.append(lax.dot_general(left, cols, contract, preferred_element_type=F32))
-    summed = lax.psum(jnp.concatenate(terms, axis=1) * (1.0 / total_tokens), DP)
-    owned = lax.dynamic_slice_in_dim(summed, row_start, own_rows, 0)
-    return tuple(owned[:, n * col_width : (n + 1) * col_width] for n in range(3))
+    tokens, width = hidden_acts.shape[0], act_basis.shape[1]
+    own = tokens // 8
+
+    def rotated(values, basis):
+        part = jnp.dot(values, basis, preferred_element_type=F32).reshape(8, own, width)
+        return jnp.sum(lax.all_to_all(part, TENSOR, 0, 0, tiled=True), axis=0).astype(BF)
+
+    def shared(left, right):
+        term = lax.dot_general(left, right, CONTRACT, preferred_element_type=F32) * (1.0 / (tokens * 16))
+        blocks = term.reshape(16, width // 16, 8, width // 8).transpose(0, 2, 1, 3).reshape(128, width // 16, width // 8)
+        return jnp.sum(lax.all_to_all(blocks, DP + TENSOR, 0, 0, tiled=True), axis=0)
+
+    place = lax.axis_index("z") * 2 + lax.axis_index("xl")
+    weights = lax.dynamic_slice_in_dim(routed, place * own, own, 0).astype(F32)[:, None]
+    rot_acts, rot_grads = rotated(hidden_acts, act_basis), rotated(out_grads, grad_basis)
+    acts_f, grads_f = rot_acts.astype(F32), rot_grads.astype(F32)
+    return (
+        shared((acts_f * weights).astype(BF), rot_acts),
+        shared((grads_f * weights).astype(BF), rot_grads),
+        shared((acts_f * acts_f * weights).astype(BF), (grads_f * grads_f).astype(BF)),
+    )
 
 
 def shards(*args):

time: 88.2 us -> 78.3 us (0.89)
  between operations: 15.4 us -> 2.07 us
  waiting for transfers between devices: 18.3 us -> 21.3 us
  local copies, waits for them, and re-layouts: 2.13 us -> 1.05 us
    ppermute x6, waiting for transfers between devices: 4.56 us -> 6.56 us  [gathered(): near = [rot] + [lax.ppermute(rot, 'y', ring(d)) for d in ROUND]]
    ppermute x3, waiting for transfers between devices: 0.01 us -> 1.75 us  [fast(): x_last = [lax.ppermute(s, 'z', ring(d)) for s, d in zip(x_next, HOPS)]]
    unnamed x10, local copies, waits for them, and re-layouts: 1.11 us -> 0.02 us
    pallas_call x10 -> x11, Pallas kernels: 15.2 us -> 15.9 us  [call(): pl.pallas_call(kernel, out_shape=out_shape, in_specs=[vmem] * (len(args)...]
  transfers between devices with their start and end apart: 25 -> 25, of which waited for: 9 -> 8; matrix products, arithmetic and copies ran while one was open for 1% -> 1% of each run, Pallas kernels for 10% -> 12%
where the time goes in v4:
time: 78.3 us; the launch traced here: 78 us
  starting transfers between devices  37.6 us (48%)
  waiting for transfers between devices  21.3 us (27%)
  Pallas kernels  15.9 us (20%)
  between operations  2.07 us (3%)
  local copies, waits for them, and re-layouts  1.05 us (1%)
    pallas_call x11, Pallas kernels, call(): pl.pallas_call(kernel, out_shape=out_shape, in_specs=[vmem] * (len(args)...  15.9 us
    ppermute x6, starting transfers between devices, gathered(): near = [rot] + [lax.ppermute(rot, 'y', ring(d)) for d in ROUND]  10.1 us
    ppermute x1, waiting for transfers between devices, fast(): return (got, whole[0, 0] + lax.ppermute(whole, 'xh', SWAP)[0, 0])  8.79 us
    all_to_all x1, starting transfers between devices, fast(): got = lax.all_to_all(parts, ('xh', 'z', 'xl'), 0, 0, tiled=True)  6.8 us
    ppermute x6, waiting for transfers between devices, gathered(): near = [rot] + [lax.ppermute(rot, 'y', ring(d)) for d in ROUND]  6.56 us
    ppermute x3, starting transfers between devices, fast(): x_last = [lax.ppermute(s, 'z', ring(d)) for s, d in zip(x_next, HOPS)]  6.04 us
    ppermute x3, starting transfers between devices, fast(): z_got = [lax.ppermute(s, 'z', ring(d)) for s, d in zip(z_send, HOPS)]  5.96 us
    ppermute x1, starting transfers between devices, fast(): return (got, whole[0, 0] + lax.ppermute(whole, 'xh', SWAP)[0, 0])  3.43 us
  transfers between devices with their start and end apart: 25, of which 8 were waited for; matrix products, arithmetic and copies ran while one was open for 1% of the time, Pallas kernels for 12%

profile of v4, /device:TPU:0, one launch (start us, length us, event | category | flops | bytes accessed | tf_op | source)
XLA Modules:
  0.0 78.0 jit_solution(3203793353657243479)
XLA Ops:
  0.7 3.4 %grads_send.1 = s16[4,72,1024]{2,1,0:T(8,128)(2,1)S(1)} custom-call(s32[8,128]{1,0:T(8,128)} %bitcast.39, bf16[1024,512]{1,0:T(8,128)(2,1)} %g_ref.3, bf16[512,1024]{1,0:T(8,128)(2,1)} %b_ref.8), custom_call_target="tpu_custom_call" | custom-call | flops 10000000000 | tf_op jit(solution)/shard_map/grads_send/pallas_call | solution.py:247
  4.1 1.6 %collective-permute-start = (s16[4,72,1024]{2,1,0:T(8,128)(2,1)S(1)}, s16[4,72,1024]{2,1,0:T(8,128)(2,1)S(1)}, u32[]{:S(2)}, u32[]{:S(2)}) collective-permute-start(s16[4,72,1024]{2,1,0:T(8,128)(2,1)S(1)} %grads_send.1), channel_id=1, source_target_pairs={{0,1},{1,0},{2,3},{3,2},{4,5},{5,4},{6,7},{7,6},{8,9},{9,8},{10,11... | collective-permute-start | bytes 1769480 | tf_op jit(solution)/shard_map/ppermute | solution.py:277
  5.7 4.0 %acts_z.1 = (s16[2,72,768]{2,1,0:T(8,128)(2,1)S(1)}, s16[2,72,768]{2,1,0:T(8,128)(2,1)S(1)}, s16[2,72,768]{2,1,0:T(8,128)(2,1)S(1)}, bf16[432,1792]{1,0:T(8,128)(2,1)S(1)}, f32[8,128]{1,0:T(8,128)S(1)}) custom-call(s32[8,128]{1,0:T(8,128)S(1)} %bitcast.40, bf16[1024,1792]{1,0:T(8,128)(2,1)S(1)} %copy-done.1, bf16[1792,1024]{1,0:T(8,128)(2,1)S(1)} %copy-done), custom_call_target="tpu_custom_call" | custom-call | flops 4000000000 | tf_op jit(solution)/shard_map/acts_z/pallas_call | solution.py:247
  9.8 2.0 %collective-permute-start.12 = (s16[2,72,768]{2,1,0:T(8,128)(2,1)S(1)}, s16[2,72,768]{2,1,0:T(8,128)(2,1)S(1)}, u32[]{:S(2)}, u32[]{:S(2)}) collective-permute-start(s16[2,72,768]{2,1,0:T(8,128)(2,1)S(1)} %get-tuple-element.46), channel_id=1, source_target_pairs={{0,2},{2,4},{4,6},{6,0},{1,3},{3,5},{5,7},{7,1},{8,10},{10,12},{12... | collective-permute-start | bytes 663560 | tf_op jit(solution)/shard_map/ppermute | solution.py:288
  11.7 2.2 %collective-permute-start.13 = (s16[2,72,768]{2,1,0:T(8,128)(2,1)S(1)}, s16[2,72,768]{2,1,0:T(8,128)(2,1)S(1)}, u32[]{:S(2)}, u32[]{:S(2)}) collective-permute-start(s16[2,72,768]{2,1,0:T(8,128)(2,1)S(1)} %get-tuple-element.47), channel_id=1, source_target_pairs={{0,6},{2,0},{4,2},{6,4},{1,7},{3,1},{5,3},{7,5},{8,14},{10,8},{12,... | collective-permute-start | bytes 663560 | tf_op jit(solution)/shard_map/ppermute | solution.py:288
  14.0 1.8 %collective-permute-start.14 = (s16[2,72,768]{2,1,0:T(8,128)(2,1)S(1)}, s16[2,72,768]{2,1,0:T(8,128)(2,1)S(1)}, u32[]{:S(2)}, u32[]{:S(2)}) collective-permute-start(s16[2,72,768]{2,1,0:T(8,128)(2,1)S(1)} %get-tuple-element.48), channel_id=1, source_target_pairs={{0,4},{2,6},{4,0},{6,2},{1,5},{3,7},{5,1},{7,3},{8,12},{10,14},{12... | collective-permute-start | bytes 663560 | tf_op jit(solution)/shard_map/ppermute | solution.py:288
  15.7 1.4 %acts_x.1 = (s16[4,72,256]{2,1,0:T(8,128)(2,1)S(1)}, bf16[144,1792]{1,0:T(8,128)(2,1)S(1)}) custom-call(s32[8,128]{1,0:T(8,128)S(1)} %bitcast.41, bf16[1024,1792]{1,0:T(8,128)(2,1)S(1)} %copy-done.1, bf16[1792,1024]{1,0:T(8,128)(2,1)S(1)} %copy-done, bf16[432,1792]{1,0:T(8,128)(2,1)S(1)} %get-tuple-element.36.picked_ref), custom_call_target="tpu_custom_call" | custom-call | flops 1000000000 | tf_op jit(solution)/shard_map/acts_x/pallas_call | solution.py:247
  17.2 0.6 collective-permute-start.1
  17.8 1.0 %grads_keep.1.g_keep = f32[288,1024]{1,0:T(8,128)S(1)} custom-call(s32[8,128]{1,0:T(8,128)S(1)} %bitcast.42, bf16[1024,512]{1,0:T(8,128)(2,1)S(1)} %copy-done.2, bf16[512,1024]{1,0:T(8,128)(2,1)S(1)} %copy-done.3, bf16[144,1792]{1,0:T(8,128)(2,1)S(1)} %get-tuple-element.37.after_ref.near_ref), custom_call_target="tpu_custom_call" | custom-call | flops 600000000 | tf_op jit(solution)/shard_map/grads_keep/pallas_call | solution.py:247
  18.8 1.0 %acts_keep.1 = (f32[2,72,768]{2,1,0:T(8,128)S(1)}, f32[288,256]{1,0:T(8,128)S(1)}) custom-call(bf16[432,1792]{1,0:T(8,128)(2,1)S(1)} %get-tuple-element.36.picked_ref, bf16[144,1792]{1,0:T(8,128)(2,1)S(1)} %get-tuple-element.37.after_ref.near_ref, bf16[1792,1024]{1,0:T(8,128)(2,1)S(1)} %copy-done), custom_call_target="tpu_custom_call" | custom-call | flops 1000000000 | tf_op jit(solution)/shard_map/acts_keep/pallas_call | solution.py:247
  19.8 2.6 %collective-permute-done.1.a_got = s16[4,72,256]{2,1,0:T(8,128)(2,1)S(1)} collective-permute-done((s16[4,72,256]{2,1,0:T(8,128)(2,1)S(1)}, s16[4,72,256]{2,1,0:T(8,128)(2,1)S(1)}, u32[]{:S(2)}, u32[]{:S(2)}) %collective-permute-start.1) | collective-permute-done | bytes 147488 | tf_op jit(solution)/shard_map/ppermute | solution.py:298
  22.4 1.1 %x_mid.1 = (f32[72,1280]{1,0:T(8,128)S(1)}, s16[72,1280]{1,0:T(8,128)(2,1)S(1)}, s16[72,1280]{1,0:T(8,128)(2,1)S(1)}, s16[72,1280]{1,0:T(8,128)(2,1)S(1)}) custom-call(f32[288,1024]{1,0:T(8,128)S(1)} %grads_keep.1.g_keep, s16[4,72,1024]{2,1,0:T(8,128)(2,1)S(1)} %collective-permute-done.g_got, f32[288,256]{1,0:T(8,128)S(1)} %get-tuple-element.38.a_keep, ...), custom_call_target="tpu_custom_call" | custom-call | tf_op jit(solution)/shard_map/x_mid/pallas_call | solution.py:247
  23.5 2.1 %collective-permute-start.2 = (s16[72,1280]{1,0:T(8,128)(2,1)S(1)}, s16[72,1280]{1,0:T(8,128)(2,1)S(1)}, u32[]{:S(2)}, u32[]{:S(2)}) collective-permute-start(s16[72,1280]{1,0:T(8,128)(2,1)S(1)} %get-tuple-element.41), channel_id=1, source_target_pairs={{0,2},{2,4},{4,6},{6,0},{1,3},{3,5},{5,7},{7,1},{8,10},{10,12},{12... | collective-permute-start | bytes 552968 | tf_op jit(solution)/shard_map/ppermute | solution.py:323
  25.6 0.6 z_mid.1
  26.2 1.6 %collective-permute-start.15 = (s16[72,768]{1,0:T(8,128)(2,1)S(1)}, s16[72,768]{1,0:T(8,128)(2,1)S(1)}, u32[]{:S(2)}, u32[]{:S(2)}) collective-permute-start(s16[72,768]{1,0:T(8,128)(2,1)S(1)} %get-tuple-element.50), channel_id=1, source_target_pairs={{0,1},{1,0},{2,3},{3,2},{4,5},{5,4},{6,7},{7,6},{8,9},{9,8},{10,11... | collective-permute-start | bytes 331784 | tf_op jit(solution)/shard_map/ppermute | solution.py:325
  27.8 2.2 %collective-permute-start.3 = (s16[72,1280]{1,0:T(8,128)(2,1)S(1)}, s16[72,1280]{1,0:T(8,128)(2,1)S(1)}, u32[]{:S(2)}, u32[]{:S(2)}) collective-permute-start(s16[72,1280]{1,0:T(8,128)(2,1)S(1)} %get-tuple-element.42), channel_id=1, source_target_pairs={{0,6},{2,0},{4,2},{6,4},{1,7},{3,1},{5,3},{7,5},{8,14},{10,8},{12,... | collective-permute-start | bytes 552968 | tf_op jit(solution)/shard_map/ppermute | solution.py:323
  29.9 1.8 %collective-permute-start.4 = (s16[72,1280]{1,0:T(8,128)(2,1)S(1)}, s16[72,1280]{1,0:T(8,128)(2,1)S(1)}, u32[]{:S(2)}, u32[]{:S(2)}) collective-permute-start(s16[72,1280]{1,0:T(8,128)(2,1)S(1)} %get-tuple-element.43), channel_id=1, source_target_pairs={{0,4},{2,6},{4,0},{6,2},{1,5},{3,7},{5,1},{7,3},{8,12},{10,14},{12... | collective-permute-start | bytes 552968 | tf_op jit(solution)/shard_map/ppermute | solution.py:323
  31.9 1.7 %collective-permute-start.18 = (bf16[72,768]{1,0:T(8,128)(2,1)S(1)}, bf16[72,768]{1,0:T(8,128)(2,1)S(1)}, u32[]{:S(2)}, u32[]{:S(2)}) collective-permute-start(bf16[72,768]{1,0:T(8,128)(2,1)S(1)} %z_end.1.refs_8_), channel_id=1, source_target_pairs={{0,32},{32,64},{64,96},{96,0},{1,33},{33,65},{65,97},{97,1},{2,34}... | collective-permute-start | bytes 331784 | tf_op jit(solution)/shard_map/ppermute | solution.py:328
  33.6 1.7 %collective-permute-start.17 = (bf16[72,768]{1,0:T(8,128)(2,1)S(1)}, bf16[72,768]{1,0:T(8,128)(2,1)S(1)}, u32[]{:S(2)}, u32[]{:S(2)}) collective-permute-start(bf16[72,768]{1,0:T(8,128)(2,1)S(1)} %z_end.1.refs_8_), channel_id=1, source_target_pairs={{0,96},{32,0},{64,32},{96,64},{1,97},{33,1},{65,33},{97,65},{2,98}... | collective-permute-start | bytes 331784 | tf_op jit(solution)/shard_map/ppermute | solution.py:328
  35.2 1.5 %collective-permute-done.3.r2_ref = s16[72,1280]{1,0:T(8,128)(2,1)S(1)} collective-permute-done((s16[72,1280]{1,0:T(8,128)(2,1)S(1)}, s16[72,1280]{1,0:T(8,128)(2,1)S(1)}, u32[]{:S(2)}, u32[]{:S(2)}) %collective-permute-start.3) | collective-permute-done | bytes 184352 | tf_op jit(solution)/shard_map/ppermute | solution.py:323
  37.5 1.6 %collective-permute-start.7 = (bf16[72,1280]{1,0:T(8,128)(2,1)S(1)}, bf16[72,1280]{1,0:T(8,128)(2,1)S(1)}, u32[]{:S(2)}, u32[]{:S(2)}) collective-permute-start(bf16[72,1280]{1,0:T(8,128)(2,1)S(1)} %x_end.1.refs_0_), channel_id=1, source_target_pairs={{0,32},{32,64},{64,96},{96,0},{1,33},{33,65},{65,97},{97,1},{2,34}... | collective-permute-start | bytes 552968 | tf_op jit(solution)/shard_map/ppermute | solution.py:328
  39.1 1.7 %collective-permute-start.6 = (bf16[72,1280]{1,0:T(8,128)(2,1)S(1)}, bf16[72,1280]{1,0:T(8,128)(2,1)S(1)}, u32[]{:S(2)}, u32[]{:S(2)}) collective-permute-start(bf16[72,1280]{1,0:T(8,128)(2,1)S(1)} %x_end.1.refs_0_), channel_id=1, source_target_pairs={{0,96},{32,0},{64,32},{96,64},{1,97},{33,1},{65,33},{97,65},{2,98}... | collective-permute-start | bytes 552968 | tf_op jit(solution)/shard_map/ppermute | solution.py:328
  40.8 2.0 %collective-permute-start.5 = (bf16[72,1280]{1,0:T(8,128)(2,1)S(1)}, bf16[72,1280]{1,0:T(8,128)(2,1)S(1)}, u32[]{:S(2)}, u32[]{:S(2)}) collective-permute-start(bf16[72,1280]{1,0:T(8,128)(2,1)S(1)} %x_end.1.refs_0_), channel_id=1, source_target_pairs={{0,64},{32,96},{64,0},{96,32},{1,65},{33,97},{65,1},{97,33},{2,66}... | collective-permute-start | bytes 552968 | tf_op jit(solution)/shard_map/ppermute | solution.py:328
  42.7 1.6 %collective-permute-start.16 = (bf16[72,768]{1,0:T(8,128)(2,1)S(1)}, bf16[72,768]{1,0:T(8,128)(2,1)S(1)}, u32[]{:S(2)}, u32[]{:S(2)}) collective-permute-start(bf16[72,768]{1,0:T(8,128)(2,1)S(1)} %z_end.1.refs_8_), channel_id=1, source_target_pairs={{0,64},{32,96},{64,0},{96,32},{1,65},{33,97},{65,1},{97,33},{2,66}... | collective-permute-start | bytes 331784 | tf_op jit(solution)/shard_map/ppermute | solution.py:328
  44.3 6.5 %collective-permute-done.16.refs_9_ = bf16[72,768]{1,0:T(8,128)(2,1)S(1)} collective-permute-done((bf16[72,768]{1,0:T(8,128)(2,1)S(1)}, bf16[72,768]{1,0:T(8,128)(2,1)S(1)}, u32[]{:S(2)}, u32[]{:S(2)}) %collective-permute-start.16) | collective-permute-done | bytes 110624 | tf_op jit(solution)/shard_map/ppermute | solution.py:328
  52.4 1.1 %collective-permute-done.20.refs_13_ = bf16[72,768]{1,0:T(8,128)(2,1)S(1)} collective-permute-done((bf16[72,768]{1,0:T(8,128)(2,1)S(1)}, bf16[72,768]{1,0:T(8,128)(2,1)S(1)}, u32[]{:S(2)}, u32[]{:S(2)}) %collective-permute-start.20) | collective-permute-done | bytes 110624 | tf_op jit(solution)/shard_map/ppermute | solution.py:329
  53.5 2.1 %gram.1 = (bf16[16,64,384]{2,1,0:T(8,128)(2,1)}, f32[8,128]{1,0:T(8,128)S(1)}) custom-call(bf16[72,1280]{1,0:T(8,128)(2,1)S(1)} %x_end.1.refs_0_, bf16[72,1280]{1,0:T(8,128)(2,1)S(1)} %collective-permute-done.5.refs_1_, bf16[72,1280]{1,0:T(8,128)(2,1)S(1)} %collective-permute-done.6.refs_2_, bf16[72,1280]{1,0:T(8,128)(2,1)S(1)} %collective-permute-done.7.refs_3_, ...), custom_call_target="tpu_custom_call" | custom-call | flops 600000000 | tf_op jit(solution)/shard_map/gram/pallas_call | solution.py:247
  55.6 6.8 %all-to-all-start.5 = ((bf16[16,64,384]{2,1,0:T(8,128)(2,1)}), bf16[16,64,384]{2,1,0:T(8,128)(2,1)S(1)}, u32[]{:S(2)}, u32[]{:S(2)}) async-start(bf16[16,64,384]{2,1,0:T(8,128)(2,1)} %get-tuple-element.52), calls=%async_computation.5 | async-start | bytes 1572864 | tf_op jit(solution)/shard_map/all_to_all | solution.py:345
  62.4 3.4 %collective-permute-start.23 = (f32[8,128]{1,0:T(8,128)S(1)}, f32[8,128]{1,0:T(8,128)S(1)}, u32[]{:S(2)}, u32[]{:S(2)}) collective-permute-start(f32[8,128]{1,0:T(8,128)S(1)} %get-tuple-element.51), channel_id=1, source_target_pairs={{0,16},{16,0},{1,17},{17,1},{2,18},{18,2},{3,19},{19,3},{4,20},{20... | collective-permute-start | bytes 12296 | tf_op jit(solution)/shard_map/ppermute | solution.py:346
  66.4 8.8 %collective-permute-done.23 = f32[8,128]{1,0:T(8,128)S(1)} collective-permute-done((f32[8,128]{1,0:T(8,128)S(1)}, f32[8,128]{1,0:T(8,128)S(1)}, u32[]{:S(2)}, u32[]{:S(2)}) %collective-permute-start.23) | collective-permute-done | bytes 4128 | tf_op jit(solution)/shard_map/ppermute | solution.py:346
  77.2 0.8 conditional.1
  77.3 0.7 final.1
  (42 shorter events, 3.8 us)
Async XLA Ops:
  0.6 5.1 %copy-start = (bf16[1792,1024]{1,0:T(8,128)(2,1)S(1)}, bf16[1792,1024]{1,0:T(8,128)(2,1)}, u32[]{:S(2)}) copy-start(bf16[1792,1024]{1,0:T(8,128)(2,1)} %b_ref.9) | copy-start | bytes 11010052
  0.6 5.1 %copy-start.1 = (bf16[1024,1792]{1,0:T(8,128)(2,1)S(1)}, bf16[1024,1792]{1,0:T(8,128)(2,1)}, u32[]{:S(2)}) copy-start(bf16[1024,1792]{1,0:T(8,128)(2,1)} %h_ref.3) | copy-start | bytes 11010052
  0.7 5.1 %copy-start.4 = (s32[1024]{0:T(1024)S(1)}, s32[1024]{0:T(1024)}, u32[]{:S(2)}) copy-start(s32[1024]{0:T(1024)} %param.11) | copy-start | bytes 12292
  4.1 18.3 %collective-permute-start = (s16[4,72,1024]{2,1,0:T(8,128)(2,1)S(1)}, s16[4,72,1024]{2,1,0:T(8,128)(2,1)S(1)}, u32[]{:S(2)}, u32[]{:S(2)}) collective-permute-start(s16[4,72,1024]{2,1,0:T(8,128)(2,1)S(1)} %grads_send.1), channel_id=1, source_target_pairs={{0,1},{1,0},{2,3},{3,2},{4,5},{5,4},{6,7},{7,6},{8,9},{9,8},{10,11... | collective-permute-start | bytes 1769480 | tf_op jit(solution)/shard_map/ppermute | solution.py:277
  9.8 15.8 %collective-permute-start.12 = (s16[2,72,768]{2,1,0:T(8,128)(2,1)S(1)}, s16[2,72,768]{2,1,0:T(8,128)(2,1)S(1)}, u32[]{:S(2)}, u32[]{:S(2)}) collective-permute-start(s16[2,72,768]{2,1,0:T(8,128)(2,1)S(1)} %get-tuple-element.46), channel_id=1, source_target_pairs={{0,2},{2,4},{4,6},{6,0},{1,3},{3,5},{5,7},{7,1},{8,10},{10,12},{12... | collective-permute-start | bytes 663560 | tf_op jit(solution)/shard_map/ppermute | solution.py:288
  11.7 13.9 %collective-permute-start.13 = (s16[2,72,768]{2,1,0:T(8,128)(2,1)S(1)}, s16[2,72,768]{2,1,0:T(8,128)(2,1)S(1)}, u32[]{:S(2)}, u32[]{:S(2)}) collective-permute-start(s16[2,72,768]{2,1,0:T(8,128)(2,1)S(1)} %get-tuple-element.47), channel_id=1, source_target_pairs={{0,6},{2,0},{4,2},{6,4},{1,7},{3,1},{5,3},{7,5},{8,14},{10,8},{12,... | collective-permute-start | bytes 663560 | tf_op jit(solution)/shard_map/ppermute | solution.py:288
  14.0 11.6 %collective-permute-start.14 = (s16[2,72,768]{2,1,0:T(8,128)(2,1)S(1)}, s16[2,72,768]{2,1,0:T(8,128)(2,1)S(1)}, u32[]{:S(2)}, u32[]{:S(2)}) collective-permute-start(s16[2,72,768]{2,1,0:T(8,128)(2,1)S(1)} %get-tuple-element.48), channel_id=1, source_target_pairs={{0,4},{2,6},{4,0},{6,2},{1,5},{3,7},{5,1},{7,3},{8,12},{10,14},{12... | collective-permute-start | bytes 663560 | tf_op jit(solution)/shard_map/ppermute | solution.py:288
  15.7 2.0 %copy-start.2 = (bf16[1024,512]{1,0:T(8,128)(2,1)S(1)}, bf16[1024,512]{1,0:T(8,128)(2,1)}, u32[]{:S(2)}) copy-start(bf16[1024,512]{1,0:T(8,128)(2,1)} %g_ref.3) | copy-start | bytes 3145732
  15.7 2.0 %copy-start.3 = (bf16[512,1024]{1,0:T(8,128)(2,1)S(1)}, bf16[512,1024]{1,0:T(8,128)(2,1)}, u32[]{:S(2)}) copy-start(bf16[512,1024]{1,0:T(8,128)(2,1)} %b_ref.8) | copy-start | bytes 3145732
  17.2 5.2 %collective-permute-start.1 = (s16[4,72,256]{2,1,0:T(8,128)(2,1)S(1)}, s16[4,72,256]{2,1,0:T(8,128)(2,1)S(1)}, u32[]{:S(2)}, u32[]{:S(2)}) collective-permute-start(s16[4,72,256]{2,1,0:T(8,128)(2,1)S(1)} %get-tuple-element.39), channel_id=1, source_target_pairs={{0,1},{1,0},{2,3},{3,2},{4,5},{5,4},{6,7},{7,6},{8,9},{9,8},{10,11... | collective-permute-start | bytes 442376 | tf_op jit(solution)/shard_map/ppermute | solution.py:298
  23.5 10.1 %collective-permute-start.2 = (s16[72,1280]{1,0:T(8,128)(2,1)S(1)}, s16[72,1280]{1,0:T(8,128)(2,1)S(1)}, u32[]{:S(2)}, u32[]{:S(2)}) collective-permute-start(s16[72,1280]{1,0:T(8,128)(2,1)S(1)} %get-tuple-element.41), channel_id=1, source_target_pairs={{0,2},{2,4},{4,6},{6,0},{1,3},{3,5},{5,7},{7,1},{8,10},{10,12},{12... | collective-permute-start | bytes 552968 | tf_op jit(solution)/shard_map/ppermute | solution.py:323
  26.2 5.5 %collective-permute-start.15 = (s16[72,768]{1,0:T(8,128)(2,1)S(1)}, s16[72,768]{1,0:T(8,128)(2,1)S(1)}, u32[]{:S(2)}, u32[]{:S(2)}) collective-permute-start(s16[72,768]{1,0:T(8,128)(2,1)S(1)} %get-tuple-element.50), channel_id=1, source_target_pairs={{0,1},{1,0},{2,3},{3,2},{4,5},{5,4},{6,7},{7,6},{8,9},{9,8},{10,11... | collective-permute-start | bytes 331784 | tf_op jit(solution)/shard_map/ppermute | solution.py:325
  27.8 8.9 %collective-permute-start.3 = (s16[72,1280]{1,0:T(8,128)(2,1)S(1)}, s16[72,1280]{1,0:T(8,128)(2,1)S(1)}, u32[]{:S(2)}, u32[]{:S(2)}) collective-permute-start(s16[72,1280]{1,0:T(8,128)(2,1)S(1)} %get-tuple-element.42), channel_id=1, source_target_pairs={{0,6},{2,0},{4,2},{6,4},{1,7},{3,1},{5,3},{7,5},{8,14},{10,8},{12,... | collective-permute-start | bytes 552968 | tf_op jit(solution)/shard_map/ppermute | solution.py:323
  29.9 7.0 %collective-permute-start.4 = (s16[72,1280]{1,0:T(8,128)(2,1)S(1)}, s16[72,1280]{1,0:T(8,128)(2,1)S(1)}, u32[]{:S(2)}, u32[]{:S(2)}) collective-permute-start(s16[72,1280]{1,0:T(8,128)(2,1)S(1)} %get-tuple-element.43), channel_id=1, source_target_pairs={{0,4},{2,6},{4,0},{6,2},{1,5},{3,7},{5,1},{7,3},{8,12},{10,14},{12... | collective-permute-start | bytes 552968 | tf_op jit(solution)/shard_map/ppermute | solution.py:323
  31.8 8.9 %collective-permute-start.19 = (bf16[72,768]{1,0:T(8,128)(2,1)S(1)}, bf16[72,768]{1,0:T(8,128)(2,1)S(1)}, u32[]{:S(2)}, u32[]{:S(2)}) collective-permute-start(bf16[72,768]{1,0:T(8,128)(2,1)S(1)} %z_end.1.refs_8_), channel_id=1, source_target_pairs={{0,8},{8,0},{1,9},{9,1},{2,10},{10,2},{3,11},{11,3},{4,12},{12,4},... | collective-permute-start | bytes 331784 | tf_op jit(solution)/shard_map/ppermute | solution.py:329
  31.9 10.8 %collective-permute-start.18 = (bf16[72,768]{1,0:T(8,128)(2,1)S(1)}, bf16[72,768]{1,0:T(8,128)(2,1)S(1)}, u32[]{:S(2)}, u32[]{:S(2)}) collective-permute-start(bf16[72,768]{1,0:T(8,128)(2,1)S(1)} %z_end.1.refs_8_), channel_id=1, source_target_pairs={{0,32},{32,64},{64,96},{96,0},{1,33},{33,65},{65,97},{97,1},{2,34}... | collective-permute-start | bytes 331784 | tf_op jit(solution)/shard_map/ppermute | solution.py:328
  33.6 10.7 %collective-permute-start.17 = (bf16[72,768]{1,0:T(8,128)(2,1)S(1)}, bf16[72,768]{1,0:T(8,128)(2,1)S(1)}, u32[]{:S(2)}, u32[]{:S(2)}) collective-permute-start(bf16[72,768]{1,0:T(8,128)(2,1)S(1)} %z_end.1.refs_8_), channel_id=1, source_target_pairs={{0,96},{32,0},{64,32},{96,64},{1,97},{33,1},{65,33},{97,65},{2,98}... | collective-permute-start | bytes 331784 | tf_op jit(solution)/shard_map/ppermute | solution.py:328
  37.5 13.9 %collective-permute-start.7 = (bf16[72,1280]{1,0:T(8,128)(2,1)S(1)}, bf16[72,1280]{1,0:T(8,128)(2,1)S(1)}, u32[]{:S(2)}, u32[]{:S(2)}) collective-permute-start(bf16[72,1280]{1,0:T(8,128)(2,1)S(1)} %x_end.1.refs_0_), channel_id=1, source_target_pairs={{0,32},{32,64},{64,96},{96,0},{1,33},{33,65},{65,97},{97,1},{2,34}... | collective-permute-start | bytes 552968 | tf_op jit(solution)/shard_map/ppermute | solution.py:328
  39.1 12.4 %collective-permute-start.6 = (bf16[72,1280]{1,0:T(8,128)(2,1)S(1)}, bf16[72,1280]{1,0:T(8,128)(2,1)S(1)}, u32[]{:S(2)}, u32[]{:S(2)}) collective-permute-start(bf16[72,1280]{1,0:T(8,128)(2,1)S(1)} %x_end.1.refs_0_), channel_id=1, source_target_pairs={{0,96},{32,0},{64,32},{96,64},{1,97},{33,1},{65,33},{97,65},{2,98}... | collective-permute-start | bytes 552968 | tf_op jit(solution)/shard_map/ppermute | solution.py:328
  40.8 11.1 %collective-permute-start.5 = (bf16[72,1280]{1,0:T(8,128)(2,1)S(1)}, bf16[72,1280]{1,0:T(8,128)(2,1)S(1)}, u32[]{:S(2)}, u32[]{:S(2)}) collective-permute-start(bf16[72,1280]{1,0:T(8,128)(2,1)S(1)} %x_end.1.refs_0_), channel_id=1, source_target_pairs={{0,64},{32,96},{64,0},{96,32},{1,65},{33,97},{65,1},{97,33},{2,66}... | collective-permute-start | bytes 552968 | tf_op jit(solution)/shard_map/ppermute | solution.py:328
  42.7 8.1 %collective-permute-start.16 = (bf16[72,768]{1,0:T(8,128)(2,1)S(1)}, bf16[72,768]{1,0:T(8,128)(2,1)S(1)}, u32[]{:S(2)}, u32[]{:S(2)}) collective-permute-start(bf16[72,768]{1,0:T(8,128)(2,1)S(1)} %z_end.1.refs_8_), channel_id=1, source_target_pairs={{0,64},{32,96},{64,0},{96,32},{1,65},{33,97},{65,1},{97,33},{2,66}... | collective-permute-start | bytes 331784 | tf_op jit(solution)/shard_map/ppermute | solution.py:328
  44.3 6.6 %collective-permute-start.22 = (bf16[72,768]{1,0:T(8,128)(2,1)S(1)}, bf16[72,768]{1,0:T(8,128)(2,1)S(1)}, u32[]{:S(2)}, u32[]{:S(2)}) collective-permute-start(bf16[72,768]{1,0:T(8,128)(2,1)S(1)} %collective-permute-done.18.refs_11_), channel_id=1, source_target_pairs={{0,8},{8,0},{1,9},{9,1},{2,10},{10,2},{3,11},{11,3},{4,12},{12,4},... | collective-permute-start | bytes 331784 | tf_op jit(solution)/shard_map/ppermute | solution.py:329
  50.9 1.3 %collective-permute-start.21 = (bf16[72,768]{1,0:T(8,128)(2,1)S(1)}, bf16[72,768]{1,0:T(8,128)(2,1)S(1)}, u32[]{:S(2)}, u32[]{:S(2)}) collective-permute-start(bf16[72,768]{1,0:T(8,128)(2,1)S(1)} %collective-permute-done.17.refs_10_), channel_id=1, source_target_pairs={{0,8},{8,0},{1,9},{9,1},{2,10},{10,2},{3,11},{11,3},{4,12},{12,4},... | collective-permute-start | bytes 331784 | tf_op jit(solution)/shard_map/ppermute | solution.py:329
  50.9 2.6 %collective-permute-start.8 = (bf16[72,1280]{1,0:T(8,128)(2,1)S(1)}, bf16[72,1280]{1,0:T(8,128)(2,1)S(1)}, u32[]{:S(2)}, u32[]{:S(2)}) collective-permute-start(bf16[72,1280]{1,0:T(8,128)(2,1)S(1)} %x_end.1.refs_0_), channel_id=1, source_target_pairs={{0,8},{8,0},{1,9},{9,1},{2,10},{10,2},{3,11},{11,3},{4,12},{12,4},... | collective-permute-start | bytes 552968 | tf_op jit(solution)/shard_map/ppermute | solution.py:329
  51.4 2.1 %collective-permute-start.11 = (bf16[72,1280]{1,0:T(8,128)(2,1)S(1)}, bf16[72,1280]{1,0:T(8,128)(2,1)S(1)}, u32[]{:S(2)}, u32[]{:S(2)}) collective-permute-start(bf16[72,1280]{1,0:T(8,128)(2,1)S(1)} %collective-permute-done.7.refs_3_), channel_id=1, source_target_pairs={{0,8},{8,0},{1,9},{9,1},{2,10},{10,2},{3,11},{11,3},{4,12},{12,4},... | collective-permute-start | bytes 552968 | tf_op jit(solution)/shard_map/ppermute | solution.py:329
  51.5 2.0 %collective-permute-start.10 = (bf16[72,1280]{1,0:T(8,128)(2,1)S(1)}, bf16[72,1280]{1,0:T(8,128)(2,1)S(1)}, u32[]{:S(2)}, u32[]{:S(2)}) collective-permute-start(bf16[72,1280]{1,0:T(8,128)(2,1)S(1)} %collective-permute-done.6.refs_2_), channel_id=1, source_target_pairs={{0,8},{8,0},{1,9},{9,1},{2,10},{10,2},{3,11},{11,3},{4,12},{12,4},... | collective-permute-start | bytes 552968 | tf_op jit(solution)/shard_map/ppermute | solution.py:329
  51.9 1.6 %collective-permute-start.9 = (bf16[72,1280]{1,0:T(8,128)(2,1)S(1)}, bf16[72,1280]{1,0:T(8,128)(2,1)S(1)}, u32[]{:S(2)}, u32[]{:S(2)}) collective-permute-start(bf16[72,1280]{1,0:T(8,128)(2,1)S(1)} %collective-permute-done.5.refs_1_), channel_id=1, source_target_pairs={{0,8},{8,0},{1,9},{9,1},{2,10},{10,2},{3,11},{11,3},{4,12},{12,4},... | collective-permute-start | bytes 552968 | tf_op jit(solution)/shard_map/ppermute | solution.py:329
  52.2 1.3 %collective-permute-start.20 = (bf16[72,768]{1,0:T(8,128)(2,1)S(1)}, bf16[72,768]{1,0:T(8,128)(2,1)S(1)}, u32[]{:S(2)}, u32[]{:S(2)}) collective-permute-start(bf16[72,768]{1,0:T(8,128)(2,1)S(1)} %collective-permute-done.16.refs_9_), channel_id=1, source_target_pairs={{0,8},{8,0},{1,9},{9,1},{2,10},{10,2},{3,11},{11,3},{4,12},{12,4},... | collective-permute-start | bytes 331784 | tf_op jit(solution)/shard_map/ppermute | solution.py:329
  55.6 21.6 %all-to-all-start.5 = ((bf16[16,64,384]{2,1,0:T(8,128)(2,1)}), bf16[16,64,384]{2,1,0:T(8,128)(2,1)S(1)}, u32[]{:S(2)}, u32[]{:S(2)}) async-start(bf16[16,64,384]{2,1,0:T(8,128)(2,1)} %get-tuple-element.52), calls=%async_computation.5 | async-start | bytes 1572864 | tf_op jit(solution)/shard_map/all_to_all | solution.py:345
  62.4 12.7 %collective-permute-start.23 = (f32[8,128]{1,0:T(8,128)S(1)}, f32[8,128]{1,0:T(8,128)S(1)}, u32[]{:S(2)}, u32[]{:S(2)}) collective-permute-start(f32[8,128]{1,0:T(8,128)S(1)} %get-tuple-element.51), channel_id=1, source_target_pairs={{0,16},{16,0},{1,17},{17,1},{2,18},{18,2},{3,19},{19,3},{4,20},{20... | collective-permute-start | bytes 12296 | tf_op jit(solution)/shard_map/ppermute | solution.py:346

commit v5 on v4

--- a/solution.py
+++ b/solution.py
@@ -16,7 +16,7 @@
 CAP = KEEP * BLOCKS
 TOP = 32767.0
 HOPS = (1, 3, 2)
-ROUND = (2, 3, 1)
+SIDES = [(2 * y + c, 2 * ((y + (-1) ** c) % 4) + c) for y in range(4) for c in range(2)]
 
 
 def ring(dist):
@@ -182,10 +182,16 @@
 CONTRACT = (((0,), (0,)), ((), ()))
 
 
-def gather_rows(dst_ref, cols, refs, part):
-    for n, ref in enumerate(refs):
-        dst_ref[n * PAD : n * PAD + SLOT, cols] = ref[:, part]
-        dst_ref[n * PAD + SLOT : (n + 1) * PAD, cols] = jnp.zeros((PAD - SLOT, ref[:, part].shape[1]), BF)
+def gather_rows(dst_ref, cols, blocks, part, places=range(GATHERED)):
+    for n, block in zip(places, blocks):
+        block = block[:, part]
+        dst_ref[pl.ds(pl.multiple_of(n * PAD + PAD - 16, 16), 16), cols] = jnp.zeros((16, block.shape[1]), BF)
+        dst_ref[pl.ds(pl.multiple_of(n * PAD, 16), SLOT), cols] = block
+
+
+def both_kernel(own_ref, mate_ref, both_ref):
+    both_ref[0] = own_ref[...]
+    both_ref[1] = mate_ref[...]
 
 
 def square(v):
@@ -209,14 +215,16 @@
 
 
 def gram_kernel(scale, *refs):
-    x_refs, z_refs = refs[:GATHERED], refs[GATHERED : 2 * GATHERED]
-    out_ref, whole_ref, a_s, g_s = refs[2 * GATHERED :]
+    x_refs, z_refs = refs[:8], list(refs[8:12]) + [ref.at[n] for ref in refs[12:14] for n in range(2)]
+    out_ref, whole_ref, a_s, g_s = refs[14:]
+    core = lax.axis_index("core")
+    places = (0, 1, 4 + 3 * core, 5 + core, 7 - 3 * core, 6 - core, 2, 3)
     marks = x_refs[0][0:8, 0:128].astype(F32)
     for ref in x_refs[1:]:
         marks = marks + ref[0:8, 0:128].astype(F32)
     whole_ref[...] = jnp.where(jnp.abs(marks) < 1e30, 1.0, 0.0)
-    gather_rows(g_s, slice(0, WIDTH), x_refs, slice(0, WIDTH))
-    gather_rows(a_s, slice(AZ, WIDTH), x_refs, slice(WIDTH, WIDTH + AX))
+    gather_rows(g_s, slice(0, WIDTH), x_refs, slice(0, WIDTH), places)
+    gather_rows(a_s, slice(AZ, WIDTH), x_refs, slice(WIDTH, WIDTH + AX), places)
     gather_rows(a_s, slice(0, AZ), z_refs, slice(0, AZ))
 
     def dot(lhs, rhs):
@@ -324,14 +332,18 @@
     z_own, z_next = call(z_mid_kernel, "z_mid", (blk(F32, AZ), blk(I16, AZ)), (z_keep, *z_got, x_own), behind=1)
     z_last = lax.ppermute(z_next, "xl", SWAP)
 
-    def gathered(rot):
-        near = [rot] + [lax.ppermute(rot, "y", ring(d)) for d in ROUND]
-        return near + [lax.ppermute(r, "core", SWAP) for r in near]
+    def over(r):
+        return lax.ppermute(r, "core", SWAP)
 
     rot_z = call(z_end_kernel, "z_end", blk(BF, AZ), (z_own, z_last))
-    all_z = gathered(rot_z)
+    z_mate = over(rot_z)
+    z_far = lax.ppermute(rot_z, "y", ring(2))
+    z_both = call(both_kernel, "z_both", blk(BF, 2, AZ), (rot_z, z_mate))
+    z_side = lax.ppermute(z_both, ("y", "core"), SIDES)
+    all_z = (rot_z, z_mate, z_far, over(z_far), z_side, over(z_side))
     rot_x = call(x_end_kernel, "x_end", blk(BF, WIDTH + AX), (x_own, *x_last, bad))
-    all_x = gathered(rot_x)
+    near = [rot_x] + [lax.ppermute(rot_x, "y", ring(d)) for d in (1, 3, 2)]
+    all_x = [r for n in near for r in (n, over(n))]
 
     rows = pltpu.VMEM((GATHERED * PAD, WIDTH), BF)
     parts, whole = call(

time: 78.3 us -> 76.4 us (0.976)
  starting transfers between devices: 37.6 us -> 34.1 us
  waiting for transfers between devices: 21.3 us -> 22.9 us
    all_to_all x1, starting transfers between devices: 6.8 us -> 5.22 us  [fast(): got = lax.all_to_all(parts, ('xh', 'z', 'xl'), 0, 0, tiled=True)]
    ppermute x3, waiting for transfers between devices: 0.01 us -> 1.43 us  [fast(): z_got = [lax.ppermute(s, 'z', ring(d)) for s, d in zip(z_send, HOPS)]]
    ppermute x14 -> x12, waiting for transfers between devices: 7.86 us -> 9.25 us  [the longest x3 4.46 us: fast(): near = [rot_x] + [lax.ppermute(rot_x, 'y', ring(d)) for d in (1, 3, 2)]]
    ppermute x3, waiting for transfers between devices: 1.75 us -> 0.7 us  [fast(): x_last = [lax.ppermute(s, 'z', ring(d)) for s, d in zip(x_next, HOPS)]]
    ppermute x1, starting transfers between devices: 1.57 us -> 0.62 us  [fast(): z_last = lax.ppermute(z_next, 'xl', SWAP)]
    ppermute x14 -> x12, starting transfers between devices: 11.6 us -> 11.1 us  [the longest x3 5.3 us: fast(): near = [rot_x] + [lax.ppermute(rot_x, 'y', ring(d)) for d in (1, 3, 2)]]
    pallas_call x11 -> x12, Pallas kernels: 15.9 us -> 16 us  [call(): pl.pallas_call(kernel, out_shape=out_shape, in_specs=[vmem] * (len(args)...]
  transfers between devices with their start and end apart: 25 -> 23, of which waited for: 8 -> 11; matrix products, arithmetic and copies ran while one was open for 1% -> 1% of each run, Pallas kernels for 12% -> 12%
where the time goes in v5:
time: 76.4 us; the launch traced here: 76.2 us
  starting transfers between devices  34.1 us (45%)
  waiting for transfers between devices  22.9 us (30%)
  Pallas kernels  16 us (21%)
  between operations  2.09 us (3%)
  local copies, waits for them, and re-layouts  1.05 us (1%)
    pallas_call x12, Pallas kernels, call(): pl.pallas_call(kernel, out_shape=out_shape, in_specs=[vmem] * (len(args)...  16 us
    ppermute x1, waiting for transfers between devices, fast(): return (got, whole[0, 0] + lax.ppermute(whole, 'xh', SWAP)[0, 0])  8.68 us
    ppermute x3, starting transfers between devices, fast(): z_got = [lax.ppermute(s, 'z', ring(d)) for s, d in zip(z_send, HOPS)]  5.96 us
    ppermute x3, starting transfers between devices, fast(): x_last = [lax.ppermute(s, 'z', ring(d)) for s, d in zip(x_next, HOPS)]  5.51 us
    ppermute x3, starting transfers between devices, fast(): near = [rot_x] + [lax.ppermute(rot_x, 'y', ring(d)) for d in (1, 3, 2)]  5.3 us
    all_to_all x1, starting transfers between devices, fast(): got = lax.all_to_all(parts, ('xh', 'z', 'xl'), 0, 0, tiled=True)  5.22 us
    ppermute x3, waiting for transfers between devices, fast(): near = [rot_x] + [lax.ppermute(rot_x, 'y', ring(d)) for d in (1, 3, 2)]  4.46 us
    ppermute x7, waiting for transfers between devices, over(): return lax.ppermute(r, 'core', SWAP)  3.52 us
  transfers between devices with their start and end apart: 23, of which 11 were waited for; matrix products, arithmetic and copies ran while one was open for 1% of the time, Pallas kernels for 12%

profile of v5, /device:TPU:0, one launch (start us, length us, event | category | flops | bytes accessed | tf_op | source)
XLA Modules:
  0.0 76.2 jit_solution(16720712595017615527)
XLA Ops:
  0.7 3.4 %grads_send.1 = s16[4,72,1024]{2,1,0:T(8,128)(2,1)S(1)} custom-call(s32[8,128]{1,0:T(8,128)} %bitcast.39, bf16[1024,512]{1,0:T(8,128)(2,1)} %g_ref.3, bf16[512,1024]{1,0:T(8,128)(2,1)} %b_ref.8), custom_call_target="tpu_custom_call" | custom-call | flops 10000000000 | tf_op jit(solution)/shard_map/grads_send/pallas_call | solution.py:255
  4.1 1.6 %collective-permute-start = (s16[4,72,1024]{2,1,0:T(8,128)(2,1)S(1)}, s16[4,72,1024]{2,1,0:T(8,128)(2,1)S(1)}, u32[]{:S(2)}, u32[]{:S(2)}) collective-permute-start(s16[4,72,1024]{2,1,0:T(8,128)(2,1)S(1)} %grads_send.1), channel_id=1, source_target_pairs={{0,1},{1,0},{2,3},{3,2},{4,5},{5,4},{6,7},{7,6},{8,9},{9,8},{10,11... | collective-permute-start | bytes 1769480 | tf_op jit(solution)/shard_map/ppermute | solution.py:285
  5.7 4.0 %acts_z.1 = (s16[2,72,768]{2,1,0:T(8,128)(2,1)S(1)}, s16[2,72,768]{2,1,0:T(8,128)(2,1)S(1)}, s16[2,72,768]{2,1,0:T(8,128)(2,1)S(1)}, bf16[432,1792]{1,0:T(8,128)(2,1)S(1)}, f32[8,128]{1,0:T(8,128)S(1)}) custom-call(s32[8,128]{1,0:T(8,128)S(1)} %bitcast.40, bf16[1024,1792]{1,0:T(8,128)(2,1)S(1)} %copy-done.1, bf16[1792,1024]{1,0:T(8,128)(2,1)S(1)} %copy-done), custom_call_target="tpu_custom_call" | custom-call | flops 4000000000 | tf_op jit(solution)/shard_map/acts_z/pallas_call | solution.py:255
  9.8 2.0 %collective-permute-start.12 = (s16[2,72,768]{2,1,0:T(8,128)(2,1)S(1)}, s16[2,72,768]{2,1,0:T(8,128)(2,1)S(1)}, u32[]{:S(2)}, u32[]{:S(2)}) collective-permute-start(s16[2,72,768]{2,1,0:T(8,128)(2,1)S(1)} %get-tuple-element.46), channel_id=1, source_target_pairs={{0,2},{2,4},{4,6},{6,0},{1,3},{3,5},{5,7},{7,1},{8,10},{10,12},{12... | collective-permute-start | bytes 663560 | tf_op jit(solution)/shard_map/ppermute | solution.py:296
  11.7 2.2 %collective-permute-start.13 = (s16[2,72,768]{2,1,0:T(8,128)(2,1)S(1)}, s16[2,72,768]{2,1,0:T(8,128)(2,1)S(1)}, u32[]{:S(2)}, u32[]{:S(2)}) collective-permute-start(s16[2,72,768]{2,1,0:T(8,128)(2,1)S(1)} %get-tuple-element.47), channel_id=1, source_target_pairs={{0,6},{2,0},{4,2},{6,4},{1,7},{3,1},{5,3},{7,5},{8,14},{10,8},{12,... | collective-permute-start | bytes 663560 | tf_op jit(solution)/shard_map/ppermute | solution.py:296
  14.0 1.8 %collective-permute-start.14 = (s16[2,72,768]{2,1,0:T(8,128)(2,1)S(1)}, s16[2,72,768]{2,1,0:T(8,128)(2,1)S(1)}, u32[]{:S(2)}, u32[]{:S(2)}) collective-permute-start(s16[2,72,768]{2,1,0:T(8,128)(2,1)S(1)} %get-tuple-element.48), channel_id=1, source_target_pairs={{0,4},{2,6},{4,0},{6,2},{1,5},{3,7},{5,1},{7,3},{8,12},{10,14},{12... | collective-permute-start | bytes 663560 | tf_op jit(solution)/shard_map/ppermute | solution.py:296
  15.7 1.4 %acts_x.1 = (s16[4,72,256]{2,1,0:T(8,128)(2,1)S(1)}, bf16[144,1792]{1,0:T(8,128)(2,1)S(1)}) custom-call(s32[8,128]{1,0:T(8,128)S(1)} %bitcast.41, bf16[1024,1792]{1,0:T(8,128)(2,1)S(1)} %copy-done.1, bf16[1792,1024]{1,0:T(8,128)(2,1)S(1)} %copy-done, bf16[432,1792]{1,0:T(8,128)(2,1)S(1)} %get-tuple-element.36.picked_ref), custom_call_target="tpu_custom_call" | custom-call | flops 1000000000 | tf_op jit(solution)/shard_map/acts_x/pallas_call | solution.py:255
  17.8 1.0 %grads_keep.1.g_keep = f32[288,1024]{1,0:T(8,128)S(1)} custom-call(s32[8,128]{1,0:T(8,128)S(1)} %bitcast.42, bf16[1024,512]{1,0:T(8,128)(2,1)S(1)} %copy-done.2, bf16[512,1024]{1,0:T(8,128)(2,1)S(1)} %copy-done.3, bf16[144,1792]{1,0:T(8,128)(2,1)S(1)} %get-tuple-element.37.after_ref.near_ref), custom_call_target="tpu_custom_call" | custom-call | flops 600000000 | tf_op jit(solution)/shard_map/grads_keep/pallas_call | solution.py:255
  18.8 1.0 %acts_keep.1 = (f32[2,72,768]{2,1,0:T(8,128)S(1)}, f32[288,256]{1,0:T(8,128)S(1)}) custom-call(bf16[432,1792]{1,0:T(8,128)(2,1)S(1)} %get-tuple-element.36.picked_ref, bf16[144,1792]{1,0:T(8,128)(2,1)S(1)} %get-tuple-element.37.after_ref.near_ref, bf16[1792,1024]{1,0:T(8,128)(2,1)S(1)} %copy-done), custom_call_target="tpu_custom_call" | custom-call | flops 1000000000 | tf_op jit(solution)/shard_map/acts_keep/pallas_call | solution.py:255
  19.8 2.6 %collective-permute-done.1.a_got = s16[4,72,256]{2,1,0:T(8,128)(2,1)S(1)} collective-permute-done((s16[4,72,256]{2,1,0:T(8,128)(2,1)S(1)}, s16[4,72,256]{2,1,0:T(8,128)(2,1)S(1)}, u32[]{:S(2)}, u32[]{:S(2)}) %collective-permute-start.1) | collective-permute-done | bytes 147488 | tf_op jit(solution)/shard_map/ppermute | solution.py:306
  22.4 1.1 %x_mid.1 = (f32[72,1280]{1,0:T(8,128)S(1)}, s16[72,1280]{1,0:T(8,128)(2,1)S(1)}, s16[72,1280]{1,0:T(8,128)(2,1)S(1)}, s16[72,1280]{1,0:T(8,128)(2,1)S(1)}) custom-call(f32[288,1024]{1,0:T(8,128)S(1)} %grads_keep.1.g_keep, s16[4,72,1024]{2,1,0:T(8,128)(2,1)S(1)} %collective-permute-done.g_got, f32[288,256]{1,0:T(8,128)S(1)} %get-tuple-element.38.a_keep, ...), custom_call_target="tpu_custom_call" | custom-call | tf_op jit(solution)/shard_map/x_mid/pallas_call | solution.py:255
  23.5 1.4 %collective-permute-done.14.r3_ref = s16[2,72,768]{2,1,0:T(8,128)(2,1)S(1)} collective-permute-done((s16[2,72,768]{2,1,0:T(8,128)(2,1)S(1)}, s16[2,72,768]{2,1,0:T(8,128)(2,1)S(1)}, u32[]{:S(2)}, u32[]{:S(2)}) %collective-permute-start.14) | collective-permute-done | bytes 221216 | tf_op jit(solution)/shard_map/ppermute | solution.py:296
  26.2 1.5 %collective-permute-start.2 = (s16[72,1280]{1,0:T(8,128)(2,1)S(1)}, s16[72,1280]{1,0:T(8,128)(2,1)S(1)}, u32[]{:S(2)}, u32[]{:S(2)}) collective-permute-start(s16[72,1280]{1,0:T(8,128)(2,1)S(1)} %get-tuple-element.41), channel_id=1, source_target_pairs={{0,2},{2,4},{4,6},{6,0},{1,3},{3,5},{5,7},{7,1},{8,10},{10,12},{12... | collective-permute-start | bytes 552968 | tf_op jit(solution)/shard_map/ppermute | solution.py:331
  27.7 2.1 %collective-permute-start.3 = (s16[72,1280]{1,0:T(8,128)(2,1)S(1)}, s16[72,1280]{1,0:T(8,128)(2,1)S(1)}, u32[]{:S(2)}, u32[]{:S(2)}) collective-permute-start(s16[72,1280]{1,0:T(8,128)(2,1)S(1)} %get-tuple-element.42), channel_id=1, source_target_pairs={{0,6},{2,0},{4,2},{6,4},{1,7},{3,1},{5,3},{7,5},{8,14},{10,8},{12,... | collective-permute-start | bytes 552968 | tf_op jit(solution)/shard_map/ppermute | solution.py:331
  29.9 1.8 %collective-permute-start.4 = (s16[72,1280]{1,0:T(8,128)(2,1)S(1)}, s16[72,1280]{1,0:T(8,128)(2,1)S(1)}, u32[]{:S(2)}, u32[]{:S(2)}) collective-permute-start(s16[72,1280]{1,0:T(8,128)(2,1)S(1)} %get-tuple-element.43), channel_id=1, source_target_pairs={{0,4},{2,6},{4,0},{6,2},{1,5},{3,7},{5,1},{7,3},{8,12},{10,14},{12... | collective-permute-start | bytes 552968 | tf_op jit(solution)/shard_map/ppermute | solution.py:331
  31.9 1.3 %collective-permute-done.16.mate_ref.refs_9_ = bf16[72,768]{1,0:T(8,128)(2,1)S(1)} collective-permute-done((bf16[72,768]{1,0:T(8,128)(2,1)S(1)}, bf16[72,768]{1,0:T(8,128)(2,1)S(1)}, u32[]{:S(2)}, u32[]{:S(2)}) %collective-permute-start.16) | collective-permute-done | bytes 110624 | tf_op jit(solution)/shard_map/ppermute | solution.py:336
  33.2 1.7 %collective-permute-start.19 = (bf16[2,72,768]{2,1,0:T(8,128)(2,1)S(1)}, bf16[2,72,768]{2,1,0:T(8,128)(2,1)S(1)}, u32[]{:S(2)}, u32[]{:S(2)}) collective-permute-start(bf16[2,72,768]{2,1,0:T(8,128)(2,1)S(1)} %z_both.1), channel_id=1, source_target_pairs={{0,32},{8,104},{32,64},{40,8},{64,96},{72,40},{96,0},{104,72},{1,3... | collective-permute-start | bytes 663560 | tf_op jit(solution)/shard_map/ppermute | solution.py:342
  34.9 2.9 %collective-permute-start.17 = (bf16[72,768]{1,0:T(8,128)(2,1)S(1)}, bf16[72,768]{1,0:T(8,128)(2,1)S(1)}, u32[]{:S(2)}, u32[]{:S(2)}) collective-permute-start(bf16[72,768]{1,0:T(8,128)(2,1)S(1)} %z_end.1.own_ref.refs_8_), channel_id=1, source_target_pairs={{0,64},{32,96},{64,0},{96,32},{1,65},{33,97},{65,1},{97,33},{2,66}... | collective-permute-start | bytes 331784 | tf_op jit(solution)/shard_map/ppermute | solution.py:340
  38.9 3.3 %collective-permute-start.10 = (bf16[72,1280]{1,0:T(8,128)(2,1)S(1)}, bf16[72,1280]{1,0:T(8,128)(2,1)S(1)}, u32[]{:S(2)}, u32[]{:S(2)}) collective-permute-start(bf16[72,1280]{1,0:T(8,128)(2,1)S(1)} %x_end.1.refs_0_), channel_id=1, source_target_pairs={{0,64},{32,96},{64,0},{96,32},{1,65},{33,97},{65,1},{97,33},{2,66}... | collective-permute-start | bytes 552968 | tf_op jit(solution)/shard_map/ppermute | solution.py:345
  42.2 1.1 %collective-permute-start.8 = (bf16[72,1280]{1,0:T(8,128)(2,1)S(1)}, bf16[72,1280]{1,0:T(8,128)(2,1)S(1)}, u32[]{:S(2)}, u32[]{:S(2)}) collective-permute-start(bf16[72,1280]{1,0:T(8,128)(2,1)S(1)} %x_end.1.refs_0_), channel_id=1, source_target_pairs={{0,96},{32,0},{64,32},{96,64},{1,97},{33,1},{65,33},{97,65},{2,98}... | collective-permute-start | bytes 552968 | tf_op jit(solution)/shard_map/ppermute | solution.py:345
  43.3 1.0 %collective-permute-start.6 = (bf16[72,1280]{1,0:T(8,128)(2,1)S(1)}, bf16[72,1280]{1,0:T(8,128)(2,1)S(1)}, u32[]{:S(2)}, u32[]{:S(2)}) collective-permute-start(bf16[72,1280]{1,0:T(8,128)(2,1)S(1)} %x_end.1.refs_0_), channel_id=1, source_target_pairs={{0,32},{32,64},{64,96},{96,0},{1,33},{33,65},{65,97},{97,1},{2,34}... | collective-permute-start | bytes 552968 | tf_op jit(solution)/shard_map/ppermute | solution.py:345
  44.2 1.3 %collective-permute-done.17.refs_10_ = bf16[72,768]{1,0:T(8,128)(2,1)S(1)} collective-permute-done((bf16[72,768]{1,0:T(8,128)(2,1)S(1)}, bf16[72,768]{1,0:T(8,128)(2,1)S(1)}, u32[]{:S(2)}, u32[]{:S(2)}) %collective-permute-start.17) | collective-permute-done | bytes 110624 | tf_op jit(solution)/shard_map/ppermute | solution.py:340
  46.0 0.8 %collective-permute-done.18.refs_11_ = bf16[72,768]{1,0:T(8,128)(2,1)S(1)} collective-permute-done((bf16[72,768]{1,0:T(8,128)(2,1)S(1)}, bf16[72,768]{1,0:T(8,128)(2,1)S(1)}, u32[]{:S(2)}, u32[]{:S(2)}) %collective-permute-start.18) | collective-permute-done | bytes 110624 | tf_op jit(solution)/shard_map/ppermute | solution.py:336
  47.0 2.4 %collective-permute-done.10.refs_6_ = bf16[72,1280]{1,0:T(8,128)(2,1)S(1)} collective-permute-done((bf16[72,1280]{1,0:T(8,128)(2,1)S(1)}, bf16[72,1280]{1,0:T(8,128)(2,1)S(1)}, u32[]{:S(2)}, u32[]{:S(2)}) %collective-permute-start.10) | collective-permute-done | bytes 184352 | tf_op jit(solution)/shard_map/ppermute | solution.py:345
  49.9 2.0 %collective-permute-done.6.refs_2_ = bf16[72,1280]{1,0:T(8,128)(2,1)S(1)} collective-permute-done((bf16[72,1280]{1,0:T(8,128)(2,1)S(1)}, bf16[72,1280]{1,0:T(8,128)(2,1)S(1)}, u32[]{:S(2)}, u32[]{:S(2)}) %collective-permute-start.6) | collective-permute-done | bytes 184352 | tf_op jit(solution)/shard_map/ppermute | solution.py:345
  52.0 1.4 %collective-permute-done.7.refs_3_ = bf16[72,1280]{1,0:T(8,128)(2,1)S(1)} collective-permute-done((bf16[72,1280]{1,0:T(8,128)(2,1)S(1)}, bf16[72,1280]{1,0:T(8,128)(2,1)S(1)}, u32[]{:S(2)}, u32[]{:S(2)}) %collective-permute-start.7) | collective-permute-done | bytes 184352 | tf_op jit(solution)/shard_map/ppermute | solution.py:336
  53.4 2.1 %gram.1 = (bf16[16,64,384]{2,1,0:T(8,128)(2,1)}, f32[8,128]{1,0:T(8,128)S(1)}) custom-call(bf16[72,1280]{1,0:T(8,128)(2,1)S(1)} %x_end.1.refs_0_, bf16[72,1280]{1,0:T(8,128)(2,1)S(1)} %collective-permute-done.5.refs_1_, bf16[72,1280]{1,0:T(8,128)(2,1)S(1)} %collective-permute-done.6.refs_2_, bf16[72,1280]{1,0:T(8,128)(2,1)S(1)} %collective-permute-done.7.refs_3_, ...), custom_call_target="tpu_custom_call" | custom-call | flops 600000000 | tf_op jit(solution)/shard_map/gram/pallas_call | solution.py:255
  55.5 5.2 %all-to-all-start.5 = ((bf16[16,64,384]{2,1,0:T(8,128)(2,1)}), bf16[16,64,384]{2,1,0:T(8,128)(2,1)S(1)}, u32[]{:S(2)}, u32[]{:S(2)}) async-start(bf16[16,64,384]{2,1,0:T(8,128)(2,1)} %get-tuple-element.52), calls=%async_computation.5 | async-start | bytes 1572864 | tf_op jit(solution)/shard_map/all_to_all | solution.py:357
  60.7 3.4 %collective-permute-start.21 = (f32[8,128]{1,0:T(8,128)S(1)}, f32[8,128]{1,0:T(8,128)S(1)}, u32[]{:S(2)}, u32[]{:S(2)}) collective-permute-start(f32[8,128]{1,0:T(8,128)S(1)} %get-tuple-element.51), channel_id=1, source_target_pairs={{0,16},{16,0},{1,17},{17,1},{2,18},{18,2},{3,19},{19,3},{4,20},{20... | collective-permute-start | bytes 12296 | tf_op jit(solution)/shard_map/ppermute | solution.py:358
  64.7 8.7 %collective-permute-done.21 = f32[8,128]{1,0:T(8,128)S(1)} collective-permute-done((f32[8,128]{1,0:T(8,128)S(1)}, f32[8,128]{1,0:T(8,128)S(1)}, u32[]{:S(2)}, u32[]{:S(2)}) %collective-permute-start.21) | collective-permute-done | bytes 4128 | tf_op jit(solution)/shard_map/ppermute | solution.py:358
  75.4 0.8 %conditional.1 = ((f32[64,128]{1,0:T(8,128)}, f32[64,128]{1,0:T(8,128)}, f32[64,128]{1,0:T(8,128)})) conditional(s32[]{:T(128)} %bitcast.9, (bf16[1024,1792]{1,0:T(8,128)(2,1)}, bf16[1792,1024]{1,0:T(8,128)(2,1)}, s32[1024]{0:T(1024)S(1)}, bf16[1024,512]{1,0:T(8,128)(2,1)S(1)}, bf16[512,1024]{1,0:T(8,128)(2,1)S(1)}) %tuple.27, ...), branch_computations={%region_0.0_spmd, %region_6.0_spmd} | conditional | flops 5646950400 | bytes 166300480 | solution.py:395
  75.5 0.7 final.1
  (39 shorter events, 5.7 us)
Async XLA Ops:
  0.6 5.1 %copy-start = (bf16[1792,1024]{1,0:T(8,128)(2,1)S(1)}, bf16[1792,1024]{1,0:T(8,128)(2,1)}, u32[]{:S(2)}) copy-start(bf16[1792,1024]{1,0:T(8,128)(2,1)} %b_ref.9) | copy-start | bytes 11010052
  0.6 5.1 %copy-start.1 = (bf16[1024,1792]{1,0:T(8,128)(2,1)S(1)}, bf16[1024,1792]{1,0:T(8,128)(2,1)}, u32[]{:S(2)}) copy-start(bf16[1024,1792]{1,0:T(8,128)(2,1)} %h_ref.3) | copy-start | bytes 11010052
  0.7 5.1 %copy-start.4 = (s32[1024]{0:T(1024)S(1)}, s32[1024]{0:T(1024)}, u32[]{:S(2)}) copy-start(s32[1024]{0:T(1024)} %param.11) | copy-start | bytes 12292
  4.1 18.3 %collective-permute-start = (s16[4,72,1024]{2,1,0:T(8,128)(2,1)S(1)}, s16[4,72,1024]{2,1,0:T(8,128)(2,1)S(1)}, u32[]{:S(2)}, u32[]{:S(2)}) collective-permute-start(s16[4,72,1024]{2,1,0:T(8,128)(2,1)S(1)} %grads_send.1), channel_id=1, source_target_pairs={{0,1},{1,0},{2,3},{3,2},{4,5},{5,4},{6,7},{7,6},{8,9},{9,8},{10,11... | collective-permute-start | bytes 1769480 | tf_op jit(solution)/shard_map/ppermute | solution.py:285
  9.8 13.7 %collective-permute-start.12 = (s16[2,72,768]{2,1,0:T(8,128)(2,1)S(1)}, s16[2,72,768]{2,1,0:T(8,128)(2,1)S(1)}, u32[]{:S(2)}, u32[]{:S(2)}) collective-permute-start(s16[2,72,768]{2,1,0:T(8,128)(2,1)S(1)} %get-tuple-element.46), channel_id=1, source_target_pairs={{0,2},{2,4},{4,6},{6,0},{1,3},{3,5},{5,7},{7,1},{8,10},{10,12},{12... | collective-permute-start | bytes 663560 | tf_op jit(solution)/shard_map/ppermute | solution.py:296
  11.7 11.8 %collective-permute-start.13 = (s16[2,72,768]{2,1,0:T(8,128)(2,1)S(1)}, s16[2,72,768]{2,1,0:T(8,128)(2,1)S(1)}, u32[]{:S(2)}, u32[]{:S(2)}) collective-permute-start(s16[2,72,768]{2,1,0:T(8,128)(2,1)S(1)} %get-tuple-element.47), channel_id=1, source_target_pairs={{0,6},{2,0},{4,2},{6,4},{1,7},{3,1},{5,3},{7,5},{8,14},{10,8},{12,... | collective-permute-start | bytes 663560 | tf_op jit(solution)/shard_map/ppermute | solution.py:296
  14.0 11.0 %collective-permute-start.14 = (s16[2,72,768]{2,1,0:T(8,128)(2,1)S(1)}, s16[2,72,768]{2,1,0:T(8,128)(2,1)S(1)}, u32[]{:S(2)}, u32[]{:S(2)}) collective-permute-start(s16[2,72,768]{2,1,0:T(8,128)(2,1)S(1)} %get-tuple-element.48), channel_id=1, source_target_pairs={{0,4},{2,6},{4,0},{6,2},{1,5},{3,7},{5,1},{7,3},{8,12},{10,14},{12... | collective-permute-start | bytes 663560 | tf_op jit(solution)/shard_map/ppermute | solution.py:296
  15.7 2.0 %copy-start.2 = (bf16[1024,512]{1,0:T(8,128)(2,1)S(1)}, bf16[1024,512]{1,0:T(8,128)(2,1)}, u32[]{:S(2)}) copy-start(bf16[1024,512]{1,0:T(8,128)(2,1)} %g_ref.3) | copy-start | bytes 3145732
  15.7 2.0 %copy-start.3 = (bf16[512,1024]{1,0:T(8,128)(2,1)S(1)}, bf16[512,1024]{1,0:T(8,128)(2,1)}, u32[]{:S(2)}) copy-start(bf16[512,1024]{1,0:T(8,128)(2,1)} %b_ref.8) | copy-start | bytes 3145732
  17.2 5.2 %collective-permute-start.1 = (s16[4,72,256]{2,1,0:T(8,128)(2,1)S(1)}, s16[4,72,256]{2,1,0:T(8,128)(2,1)S(1)}, u32[]{:S(2)}, u32[]{:S(2)}) collective-permute-start(s16[4,72,256]{2,1,0:T(8,128)(2,1)S(1)} %get-tuple-element.39), channel_id=1, source_target_pairs={{0,1},{1,0},{2,3},{3,2},{4,5},{5,4},{6,7},{7,6},{8,9},{9,8},{10,11... | collective-permute-start | bytes 442376 | tf_op jit(solution)/shard_map/ppermute | solution.py:306
  25.6 6.1 %collective-permute-start.15 = (s16[72,768]{1,0:T(8,128)(2,1)S(1)}, s16[72,768]{1,0:T(8,128)(2,1)S(1)}, u32[]{:S(2)}, u32[]{:S(2)}) collective-permute-start(s16[72,768]{1,0:T(8,128)(2,1)S(1)} %get-tuple-element.50), channel_id=1, source_target_pairs={{0,1},{1,0},{2,3},{3,2},{4,5},{5,4},{6,7},{7,6},{8,9},{9,8},{10,11... | collective-permute-start | bytes 331784 | tf_op jit(solution)/shard_map/ppermute | solution.py:333
  26.2 11.6 %collective-permute-start.2 = (s16[72,1280]{1,0:T(8,128)(2,1)S(1)}, s16[72,1280]{1,0:T(8,128)(2,1)S(1)}, u32[]{:S(2)}, u32[]{:S(2)}) collective-permute-start(s16[72,1280]{1,0:T(8,128)(2,1)S(1)} %get-tuple-element.41), channel_id=1, source_target_pairs={{0,2},{2,4},{4,6},{6,0},{1,3},{3,5},{5,7},{7,1},{8,10},{10,12},{12... | collective-permute-start | bytes 552968 | tf_op jit(solution)/shard_map/ppermute | solution.py:331
  27.7 10.0 %collective-permute-start.3 = (s16[72,1280]{1,0:T(8,128)(2,1)S(1)}, s16[72,1280]{1,0:T(8,128)(2,1)S(1)}, u32[]{:S(2)}, u32[]{:S(2)}) collective-permute-start(s16[72,1280]{1,0:T(8,128)(2,1)S(1)} %get-tuple-element.42), channel_id=1, source_target_pairs={{0,6},{2,0},{4,2},{6,4},{1,7},{3,1},{5,3},{7,5},{8,14},{10,8},{12,... | collective-permute-start | bytes 552968 | tf_op jit(solution)/shard_map/ppermute | solution.py:331
  29.9 8.6 %collective-permute-start.4 = (s16[72,1280]{1,0:T(8,128)(2,1)S(1)}, s16[72,1280]{1,0:T(8,128)(2,1)S(1)}, u32[]{:S(2)}, u32[]{:S(2)}) collective-permute-start(s16[72,1280]{1,0:T(8,128)(2,1)S(1)} %get-tuple-element.43), channel_id=1, source_target_pairs={{0,4},{2,6},{4,0},{6,2},{1,5},{3,7},{5,1},{7,3},{8,12},{10,14},{12... | collective-permute-start | bytes 552968 | tf_op jit(solution)/shard_map/ppermute | solution.py:331
  31.8 1.4 %collective-permute-start.16 = (bf16[72,768]{1,0:T(8,128)(2,1)S(1)}, bf16[72,768]{1,0:T(8,128)(2,1)S(1)}, u32[]{:S(2)}, u32[]{:S(2)}) collective-permute-start(bf16[72,768]{1,0:T(8,128)(2,1)S(1)} %z_end.1.own_ref.refs_8_), channel_id=1, source_target_pairs={{0,8},{8,0},{1,9},{9,1},{2,10},{10,2},{3,11},{11,3},{4,12},{12,4},... | collective-permute-start | bytes 331784 | tf_op jit(solution)/shard_map/ppermute | solution.py:336
  33.2 12.3 %collective-permute-start.19 = (bf16[2,72,768]{2,1,0:T(8,128)(2,1)S(1)}, bf16[2,72,768]{2,1,0:T(8,128)(2,1)S(1)}, u32[]{:S(2)}, u32[]{:S(2)}) collective-permute-start(bf16[2,72,768]{2,1,0:T(8,128)(2,1)S(1)} %z_both.1), channel_id=1, source_target_pairs={{0,32},{8,104},{32,64},{40,8},{64,96},{72,40},{96,0},{104,72},{1,3... | collective-permute-start | bytes 663560 | tf_op jit(solution)/shard_map/ppermute | solution.py:342
  34.9 10.7 %collective-permute-start.17 = (bf16[72,768]{1,0:T(8,128)(2,1)S(1)}, bf16[72,768]{1,0:T(8,128)(2,1)S(1)}, u32[]{:S(2)}, u32[]{:S(2)}) collective-permute-start(bf16[72,768]{1,0:T(8,128)(2,1)S(1)} %z_end.1.own_ref.refs_8_), channel_id=1, source_target_pairs={{0,64},{32,96},{64,0},{96,32},{1,65},{33,97},{65,1},{97,33},{2,66}... | collective-permute-start | bytes 331784 | tf_op jit(solution)/shard_map/ppermute | solution.py:340
  38.9 10.5 %collective-permute-start.10 = (bf16[72,1280]{1,0:T(8,128)(2,1)S(1)}, bf16[72,1280]{1,0:T(8,128)(2,1)S(1)}, u32[]{:S(2)}, u32[]{:S(2)}) collective-permute-start(bf16[72,1280]{1,0:T(8,128)(2,1)S(1)} %x_end.1.refs_0_), channel_id=1, source_target_pairs={{0,64},{32,96},{64,0},{96,32},{1,65},{33,97},{65,1},{97,33},{2,66}... | collective-permute-start | bytes 552968 | tf_op jit(solution)/shard_map/ppermute | solution.py:345
  42.2 7.2 %collective-permute-start.8 = (bf16[72,1280]{1,0:T(8,128)(2,1)S(1)}, bf16[72,1280]{1,0:T(8,128)(2,1)S(1)}, u32[]{:S(2)}, u32[]{:S(2)}) collective-permute-start(bf16[72,1280]{1,0:T(8,128)(2,1)S(1)} %x_end.1.refs_0_), channel_id=1, source_target_pairs={{0,96},{32,0},{64,32},{96,64},{1,97},{33,1},{65,33},{97,65},{2,98}... | collective-permute-start | bytes 552968 | tf_op jit(solution)/shard_map/ppermute | solution.py:345
  43.3 8.7 %collective-permute-start.6 = (bf16[72,1280]{1,0:T(8,128)(2,1)S(1)}, bf16[72,1280]{1,0:T(8,128)(2,1)S(1)}, u32[]{:S(2)}, u32[]{:S(2)}) collective-permute-start(bf16[72,1280]{1,0:T(8,128)(2,1)S(1)} %x_end.1.refs_0_), channel_id=1, source_target_pairs={{0,32},{32,64},{64,96},{96,0},{1,33},{33,65},{65,97},{97,1},{2,34}... | collective-permute-start | bytes 552968 | tf_op jit(solution)/shard_map/ppermute | solution.py:345
  45.5 1.3 %collective-permute-start.18 = (bf16[72,768]{1,0:T(8,128)(2,1)S(1)}, bf16[72,768]{1,0:T(8,128)(2,1)S(1)}, u32[]{:S(2)}, u32[]{:S(2)}) collective-permute-start(bf16[72,768]{1,0:T(8,128)(2,1)S(1)} %collective-permute-done.17.refs_10_), channel_id=1, source_target_pairs={{0,8},{8,0},{1,9},{9,1},{2,10},{10,2},{3,11},{11,3},{4,12},{12,4},... | collective-permute-start | bytes 331784 | tf_op jit(solution)/shard_map/ppermute | solution.py:336
  45.5 7.9 %collective-permute-start.20 = (bf16[2,72,768]{2,1,0:T(8,128)(2,1)S(1)}, bf16[2,72,768]{2,1,0:T(8,128)(2,1)S(1)}, u32[]{:S(2)}, u32[]{:S(2)}) collective-permute-start(bf16[2,72,768]{2,1,0:T(8,128)(2,1)S(1)} %collective-permute-done.19.refs_12_), channel_id=1, source_target_pairs={{0,8},{8,0},{1,9},{9,1},{2,10},{10,2},{3,11},{11,3},{4,12},{12,4},... | collective-permute-start | bytes 663560 | tf_op jit(solution)/shard_map/ppermute | solution.py:336
  46.8 5.1 %collective-permute-start.5 = (bf16[72,1280]{1,0:T(8,128)(2,1)S(1)}, bf16[72,1280]{1,0:T(8,128)(2,1)S(1)}, u32[]{:S(2)}, u32[]{:S(2)}) collective-permute-start(bf16[72,1280]{1,0:T(8,128)(2,1)S(1)} %x_end.1.refs_0_), channel_id=1, source_target_pairs={{0,8},{8,0},{1,9},{9,1},{2,10},{10,2},{3,11},{11,3},{4,12},{12,4},... | collective-permute-start | bytes 552968 | tf_op jit(solution)/shard_map/ppermute | solution.py:336
  49.4 2.6 %collective-permute-start.11 = (bf16[72,1280]{1,0:T(8,128)(2,1)S(1)}, bf16[72,1280]{1,0:T(8,128)(2,1)S(1)}, u32[]{:S(2)}, u32[]{:S(2)}) collective-permute-start(bf16[72,1280]{1,0:T(8,128)(2,1)S(1)} %collective-permute-done.10.refs_6_), channel_id=1, source_target_pairs={{0,8},{8,0},{1,9},{9,1},{2,10},{10,2},{3,11},{11,3},{4,12},{12,4},... | collective-permute-start | bytes 552968 | tf_op jit(solution)/shard_map/ppermute | solution.py:336
  49.4 2.6 %collective-permute-start.9 = (bf16[72,1280]{1,0:T(8,128)(2,1)S(1)}, bf16[72,1280]{1,0:T(8,128)(2,1)S(1)}, u32[]{:S(2)}, u32[]{:S(2)}) collective-permute-start(bf16[72,1280]{1,0:T(8,128)(2,1)S(1)} %collective-permute-done.8.refs_4_), channel_id=1, source_target_pairs={{0,8},{8,0},{1,9},{9,1},{2,10},{10,2},{3,11},{11,3},{4,12},{12,4},... | collective-permute-start | bytes 552968 | tf_op jit(solution)/shard_map/ppermute | solution.py:336
  51.9 1.4 %collective-permute-start.7 = (bf16[72,1280]{1,0:T(8,128)(2,1)S(1)}, bf16[72,1280]{1,0:T(8,128)(2,1)S(1)}, u32[]{:S(2)}, u32[]{:S(2)}) collective-permute-start(bf16[72,1280]{1,0:T(8,128)(2,1)S(1)} %collective-permute-done.6.refs_2_), channel_id=1, source_target_pairs={{0,8},{8,0},{1,9},{9,1},{2,10},{10,2},{3,11},{11,3},{4,12},{12,4},... | collective-permute-start | bytes 552968 | tf_op jit(solution)/shard_map/ppermute | solution.py:336
  55.5 19.9 %all-to-all-start.5 = ((bf16[16,64,384]{2,1,0:T(8,128)(2,1)}), bf16[16,64,384]{2,1,0:T(8,128)(2,1)S(1)}, u32[]{:S(2)}, u32[]{:S(2)}) async-start(bf16[16,64,384]{2,1,0:T(8,128)(2,1)} %get-tuple-element.52), calls=%async_computation.5 | async-start | bytes 1572864 | tf_op jit(solution)/shard_map/all_to_all | solution.py:357
  60.7 12.6 %collective-permute-start.21 = (f32[8,128]{1,0:T(8,128)S(1)}, f32[8,128]{1,0:T(8,128)S(1)}, u32[]{:S(2)}, u32[]{:S(2)}) collective-permute-start(f32[8,128]{1,0:T(8,128)S(1)} %get-tuple-element.51), channel_id=1, source_target_pairs={{0,16},{16,0},{1,17},{17,1},{2,18},{18,2},{3,19},{19,3},{4,20},{20... | collective-permute-start | bytes 12296 | tf_op jit(solution)/shard_map/ppermute | solution.py:358

commit v6 on v5

--- a/solution.py
+++ b/solution.py
@@ -341,7 +341,7 @@
     z_both = call(both_kernel, "z_both", blk(BF, 2, AZ), (rot_z, z_mate))
     z_side = lax.ppermute(z_both, ("y", "core"), SIDES)
     all_z = (rot_z, z_mate, z_far, over(z_far), z_side, over(z_side))
-    rot_x = call(x_end_kernel, "x_end", blk(BF, WIDTH + AX), (x_own, *x_last, bad))
+    rot_x = call(x_end_kernel, "x_end", blk(BF, WIDTH + AX), (x_own, *x_last, bad), flops=2_000_000_000)
     near = [rot_x] + [lax.ppermute(rot_x, "y", ring(d)) for d in (1, 3, 2)]
     all_x = [r for n in near for r in (n, over(n))]
 

time: 76.4 us -> 74.8 us (0.979)
  starting transfers between devices: 34.1 us -> 32.7 us
    ppermute x7, waiting for transfers between devices: 3.52 us -> 1.66 us  [over(): return lax.ppermute(r, 'core', SWAP)]
    ppermute x3, waiting for transfers between devices: 0.7 us -> 2.53 us  [fast(): x_last = [lax.ppermute(s, 'z', ring(d)) for s, d in zip(x_next, HOPS)]]
    ppermute x1, waiting for transfers between devices: 1.27 us -> 0.01 us  [fast(): z_far = lax.ppermute(rot_z, 'y', ring(2))]
    ppermute x1, waiting for transfers between devices: 0.01 us -> 1.08 us  [fast(): z_side = lax.ppermute(z_both, ('y', 'core'), SIDES)]
    ppermute x1, starting transfers between devices: 1.65 us -> 0.75 us  [fast(): z_side = lax.ppermute(z_both, ('y', 'core'), SIDES)]
    ppermute x7, starting transfers between devices: 1.26 us -> 0.37 us  [over(): return lax.ppermute(r, 'core', SWAP)]
  transfers between devices with their start and end apart: 23 -> 23, of which waited for: 11 -> 13; matrix products, arithmetic and copies ran while one was open for 1% -> 1% of each run, Pallas kernels for 12% -> 12%
where the time goes in v6:
time: 74.8 us; the launch traced here: 74.6 us
  starting transfers between devices  32.7 us (44%)
  waiting for transfers between devices  22.7 us (30%)
  Pallas kernels  16 us (21%)
  between operations  2.08 us (3%)
  local copies, waits for them, and re-layouts  1.05 us (1%)
    pallas_call x12, Pallas kernels, call(): pl.pallas_call(kernel, out_shape=out_shape, in_specs=[vmem] * (len(args)...  16 us
    ppermute x1, waiting for transfers between devices, fast(): return (got, whole[0, 0] + lax.ppermute(whole, 'xh', SWAP)[0, 0])  8.68 us
    ppermute x3, starting transfers between devices, fast(): z_got = [lax.ppermute(s, 'z', ring(d)) for s, d in zip(z_send, HOPS)]  5.96 us
    ppermute x3, starting transfers between devices, fast(): x_last = [lax.ppermute(s, 'z', ring(d)) for s, d in zip(x_next, HOPS)]  5.51 us
    ppermute x3, starting transfers between devices, fast(): near = [rot_x] + [lax.ppermute(rot_x, 'y', ring(d)) for d in (1, 3, 2)]  5.3 us
    all_to_all x1, starting transfers between devices, fast(): got = lax.all_to_all(parts, ('xh', 'z', 'xl'), 0, 0, tiled=True)  5.23 us
    ppermute x3, waiting for transfers between devices, fast(): near = [rot_x] + [lax.ppermute(rot_x, 'y', ring(d)) for d in (1, 3, 2)]  4.47 us
    ppermute x1, starting transfers between devices, fast(): return (got, whole[0, 0] + lax.ppermute(whole, 'xh', SWAP)[0, 0])  3.43 us
  transfers between devices with their start and end apart: 23, of which 13 were waited for; matrix products, arithmetic and copies ran while one was open for 1% of the time, Pallas kernels for 12%

profile of v6, /device:TPU:0, one launch (start us, length us, event | category | flops | bytes accessed | tf_op | source)
XLA Modules:
  0.0 74.6 jit_solution(14612338596008703986)
XLA Ops:
  0.7 3.4 %grads_send.1 = s16[4,72,1024]{2,1,0:T(8,128)(2,1)S(1)} custom-call(s32[8,128]{1,0:T(8,128)} %bitcast.39, bf16[1024,512]{1,0:T(8,128)(2,1)} %g_ref.3, bf16[512,1024]{1,0:T(8,128)(2,1)} %b_ref.8), custom_call_target="tpu_custom_call" | custom-call | flops 10000000000 | tf_op jit(solution)/shard_map/grads_send/pallas_call | solution.py:255
  4.1 1.6 %collective-permute-start = (s16[4,72,1024]{2,1,0:T(8,128)(2,1)S(1)}, s16[4,72,1024]{2,1,0:T(8,128)(2,1)S(1)}, u32[]{:S(2)}, u32[]{:S(2)}) collective-permute-start(s16[4,72,1024]{2,1,0:T(8,128)(2,1)S(1)} %grads_send.1), channel_id=1, source_target_pairs={{0,1},{1,0},{2,3},{3,2},{4,5},{5,4},{6,7},{7,6},{8,9},{9,8},{10,11... | collective-permute-start | bytes 1769480 | tf_op jit(solution)/shard_map/ppermute | solution.py:285
  5.7 4.0 %acts_z.1 = (s16[2,72,768]{2,1,0:T(8,128)(2,1)S(1)}, s16[2,72,768]{2,1,0:T(8,128)(2,1)S(1)}, s16[2,72,768]{2,1,0:T(8,128)(2,1)S(1)}, bf16[432,1792]{1,0:T(8,128)(2,1)S(1)}, f32[8,128]{1,0:T(8,128)S(1)}) custom-call(s32[8,128]{1,0:T(8,128)S(1)} %bitcast.40, bf16[1024,1792]{1,0:T(8,128)(2,1)S(1)} %copy-done.1, bf16[1792,1024]{1,0:T(8,128)(2,1)S(1)} %copy-done), custom_call_target="tpu_custom_call" | custom-call | flops 4000000000 | tf_op jit(solution)/shard_map/acts_z/pallas_call | solution.py:255
  9.8 2.0 %collective-permute-start.12 = (s16[2,72,768]{2,1,0:T(8,128)(2,1)S(1)}, s16[2,72,768]{2,1,0:T(8,128)(2,1)S(1)}, u32[]{:S(2)}, u32[]{:S(2)}) collective-permute-start(s16[2,72,768]{2,1,0:T(8,128)(2,1)S(1)} %get-tuple-element.46), channel_id=1, source_target_pairs={{0,2},{2,4},{4,6},{6,0},{1,3},{3,5},{5,7},{7,1},{8,10},{10,12},{12... | collective-permute-start | bytes 663560 | tf_op jit(solution)/shard_map/ppermute | solution.py:296
  11.7 2.2 %collective-permute-start.13 = (s16[2,72,768]{2,1,0:T(8,128)(2,1)S(1)}, s16[2,72,768]{2,1,0:T(8,128)(2,1)S(1)}, u32[]{:S(2)}, u32[]{:S(2)}) collective-permute-start(s16[2,72,768]{2,1,0:T(8,128)(2,1)S(1)} %get-tuple-element.47), channel_id=1, source_target_pairs={{0,6},{2,0},{4,2},{6,4},{1,7},{3,1},{5,3},{7,5},{8,14},{10,8},{12,... | collective-permute-start | bytes 663560 | tf_op jit(solution)/shard_map/ppermute | solution.py:296
  14.0 1.8 %collective-permute-start.14 = (s16[2,72,768]{2,1,0:T(8,128)(2,1)S(1)}, s16[2,72,768]{2,1,0:T(8,128)(2,1)S(1)}, u32[]{:S(2)}, u32[]{:S(2)}) collective-permute-start(s16[2,72,768]{2,1,0:T(8,128)(2,1)S(1)} %get-tuple-element.48), channel_id=1, source_target_pairs={{0,4},{2,6},{4,0},{6,2},{1,5},{3,7},{5,1},{7,3},{8,12},{10,14},{12... | collective-permute-start | bytes 663560 | tf_op jit(solution)/shard_map/ppermute | solution.py:296
  15.7 1.4 %acts_x.1 = (s16[4,72,256]{2,1,0:T(8,128)(2,1)S(1)}, bf16[144,1792]{1,0:T(8,128)(2,1)S(1)}) custom-call(s32[8,128]{1,0:T(8,128)S(1)} %bitcast.41, bf16[1024,1792]{1,0:T(8,128)(2,1)S(1)} %copy-done.1, bf16[1792,1024]{1,0:T(8,128)(2,1)S(1)} %copy-done, bf16[432,1792]{1,0:T(8,128)(2,1)S(1)} %get-tuple-element.36.picked_ref), custom_call_target="tpu_custom_call" | custom-call | flops 1000000000 | tf_op jit(solution)/shard_map/acts_x/pallas_call | solution.py:255
  17.8 1.0 %grads_keep.1.g_keep = f32[288,1024]{1,0:T(8,128)S(1)} custom-call(s32[8,128]{1,0:T(8,128)S(1)} %bitcast.42, bf16[1024,512]{1,0:T(8,128)(2,1)S(1)} %copy-done.2, bf16[512,1024]{1,0:T(8,128)(2,1)S(1)} %copy-done.3, bf16[144,1792]{1,0:T(8,128)(2,1)S(1)} %get-tuple-element.37.after_ref.near_ref), custom_call_target="tpu_custom_call" | custom-call | flops 600000000 | tf_op jit(solution)/shard_map/grads_keep/pallas_call | solution.py:255
  18.8 1.0 %acts_keep.1 = (f32[2,72,768]{2,1,0:T(8,128)S(1)}, f32[288,256]{1,0:T(8,128)S(1)}) custom-call(bf16[432,1792]{1,0:T(8,128)(2,1)S(1)} %get-tuple-element.36.picked_ref, bf16[144,1792]{1,0:T(8,128)(2,1)S(1)} %get-tuple-element.37.after_ref.near_ref, bf16[1792,1024]{1,0:T(8,128)(2,1)S(1)} %copy-done), custom_call_target="tpu_custom_call" | custom-call | flops 1000000000 | tf_op jit(solution)/shard_map/acts_keep/pallas_call | solution.py:255
  19.8 2.6 %collective-permute-done.1.a_got = s16[4,72,256]{2,1,0:T(8,128)(2,1)S(1)} collective-permute-done((s16[4,72,256]{2,1,0:T(8,128)(2,1)S(1)}, s16[4,72,256]{2,1,0:T(8,128)(2,1)S(1)}, u32[]{:S(2)}, u32[]{:S(2)}) %collective-permute-start.1) | collective-permute-done | bytes 147488 | tf_op jit(solution)/shard_map/ppermute | solution.py:306
  22.4 1.1 %x_mid.1 = (f32[72,1280]{1,0:T(8,128)S(1)}, s16[72,1280]{1,0:T(8,128)(2,1)S(1)}, s16[72,1280]{1,0:T(8,128)(2,1)S(1)}, s16[72,1280]{1,0:T(8,128)(2,1)S(1)}) custom-call(f32[288,1024]{1,0:T(8,128)S(1)} %grads_keep.1.g_keep, s16[4,72,1024]{2,1,0:T(8,128)(2,1)S(1)} %collective-permute-done.g_got, f32[288,256]{1,0:T(8,128)S(1)} %get-tuple-element.38.a_keep, ...), custom_call_target="tpu_custom_call" | custom-call | tf_op jit(solution)/shard_map/x_mid/pallas_call | solution.py:255
  23.5 1.4 %collective-permute-done.14.r3_ref = s16[2,72,768]{2,1,0:T(8,128)(2,1)S(1)} collective-permute-done((s16[2,72,768]{2,1,0:T(8,128)(2,1)S(1)}, s16[2,72,768]{2,1,0:T(8,128)(2,1)S(1)}, u32[]{:S(2)}, u32[]{:S(2)}) %collective-permute-start.14) | collective-permute-done | bytes 221216 | tf_op jit(solution)/shard_map/ppermute | solution.py:296
  26.2 1.5 %collective-permute-start.2 = (s16[72,1280]{1,0:T(8,128)(2,1)S(1)}, s16[72,1280]{1,0:T(8,128)(2,1)S(1)}, u32[]{:S(2)}, u32[]{:S(2)}) collective-permute-start(s16[72,1280]{1,0:T(8,128)(2,1)S(1)} %get-tuple-element.41), channel_id=1, source_target_pairs={{0,2},{2,4},{4,6},{6,0},{1,3},{3,5},{5,7},{7,1},{8,10},{10,12},{12... | collective-permute-start | bytes 552968 | tf_op jit(solution)/shard_map/ppermute | solution.py:331
  27.7 2.1 %collective-permute-start.3 = (s16[72,1280]{1,0:T(8,128)(2,1)S(1)}, s16[72,1280]{1,0:T(8,128)(2,1)S(1)}, u32[]{:S(2)}, u32[]{:S(2)}) collective-permute-start(s16[72,1280]{1,0:T(8,128)(2,1)S(1)} %get-tuple-element.42), channel_id=1, source_target_pairs={{0,6},{2,0},{4,2},{6,4},{1,7},{3,1},{5,3},{7,5},{8,14},{10,8},{12,... | collective-permute-start | bytes 552968 | tf_op jit(solution)/shard_map/ppermute | solution.py:331
  29.9 1.8 %collective-permute-start.4 = (s16[72,1280]{1,0:T(8,128)(2,1)S(1)}, s16[72,1280]{1,0:T(8,128)(2,1)S(1)}, u32[]{:S(2)}, u32[]{:S(2)}) collective-permute-start(s16[72,1280]{1,0:T(8,128)(2,1)S(1)} %get-tuple-element.43), channel_id=1, source_target_pairs={{0,4},{2,6},{4,0},{6,2},{1,5},{3,7},{5,1},{7,3},{8,12},{10,14},{12... | collective-permute-start | bytes 552968 | tf_op jit(solution)/shard_map/ppermute | solution.py:331
  31.9 3.3 %collective-permute-start.17 = (bf16[72,768]{1,0:T(8,128)(2,1)S(1)}, bf16[72,768]{1,0:T(8,128)(2,1)S(1)}, u32[]{:S(2)}, u32[]{:S(2)}) collective-permute-start(bf16[72,768]{1,0:T(8,128)(2,1)S(1)} %z_end.1.own_ref.refs_8_), channel_id=1, source_target_pairs={{0,64},{32,96},{64,0},{96,32},{1,65},{33,97},{65,1},{97,33},{2,66}... | collective-permute-start | bytes 331784 | tf_op jit(solution)/shard_map/ppermute | solution.py:340
  35.2 0.7 %collective-permute-start.19 = (bf16[2,72,768]{2,1,0:T(8,128)(2,1)S(1)}, bf16[2,72,768]{2,1,0:T(8,128)(2,1)S(1)}, u32[]{:S(2)}, u32[]{:S(2)}) collective-permute-start(bf16[2,72,768]{2,1,0:T(8,128)(2,1)S(1)} %z_both.1), channel_id=1, source_target_pairs={{0,32},{8,104},{32,64},{40,8},{64,96},{72,40},{96,0},{104,72},{1,3... | collective-permute-start | bytes 663560 | tf_op jit(solution)/shard_map/ppermute | solution.py:342
  36.6 1.8 %collective-permute-done.4.r3_ref = s16[72,1280]{1,0:T(8,128)(2,1)S(1)} collective-permute-done((s16[72,1280]{1,0:T(8,128)(2,1)S(1)}, s16[72,1280]{1,0:T(8,128)(2,1)S(1)}, u32[]{:S(2)}, u32[]{:S(2)}) %collective-permute-start.4) | collective-permute-done | bytes 184352 | tf_op jit(solution)/shard_map/ppermute | solution.py:331
  38.9 3.3 %collective-permute-start.10 = (bf16[72,1280]{1,0:T(8,128)(2,1)S(1)}, bf16[72,1280]{1,0:T(8,128)(2,1)S(1)}, u32[]{:S(2)}, u32[]{:S(2)}) collective-permute-start(bf16[72,1280]{1,0:T(8,128)(2,1)S(1)} %x_end.1.refs_0_), channel_id=1, source_target_pairs={{0,64},{32,96},{64,0},{96,32},{1,65},{33,97},{65,1},{97,33},{2,66}... | collective-permute-start | bytes 552968 | tf_op jit(solution)/shard_map/ppermute | solution.py:345
  42.2 1.1 %collective-permute-start.8 = (bf16[72,1280]{1,0:T(8,128)(2,1)S(1)}, bf16[72,1280]{1,0:T(8,128)(2,1)S(1)}, u32[]{:S(2)}, u32[]{:S(2)}) collective-permute-start(bf16[72,1280]{1,0:T(8,128)(2,1)S(1)} %x_end.1.refs_0_), channel_id=1, source_target_pairs={{0,96},{32,0},{64,32},{96,64},{1,97},{33,1},{65,33},{97,65},{2,98}... | collective-permute-start | bytes 552968 | tf_op jit(solution)/shard_map/ppermute | solution.py:345
  43.3 1.0 %collective-permute-start.6 = (bf16[72,1280]{1,0:T(8,128)(2,1)S(1)}, bf16[72,1280]{1,0:T(8,128)(2,1)S(1)}, u32[]{:S(2)}, u32[]{:S(2)}) collective-permute-start(bf16[72,1280]{1,0:T(8,128)(2,1)S(1)} %x_end.1.refs_0_), channel_id=1, source_target_pairs={{0,32},{32,64},{64,96},{96,0},{1,33},{33,65},{65,97},{97,1},{2,34}... | collective-permute-start | bytes 552968 | tf_op jit(solution)/shard_map/ppermute | solution.py:345
  44.2 1.1 %collective-permute-done.19.refs_12_ = bf16[2,72,768]{2,1,0:T(8,128)(2,1)S(1)} collective-permute-done((bf16[2,72,768]{2,1,0:T(8,128)(2,1)S(1)}, bf16[2,72,768]{2,1,0:T(8,128)(2,1)S(1)}, u32[]{:S(2)}, u32[]{:S(2)}) %collective-permute-start.19) | collective-permute-done | bytes 221216 | tf_op jit(solution)/shard_map/ppermute | solution.py:342
  45.8 1.9 %collective-permute-done.10.refs_6_ = bf16[72,1280]{1,0:T(8,128)(2,1)S(1)} collective-permute-done((bf16[72,1280]{1,0:T(8,128)(2,1)S(1)}, bf16[72,1280]{1,0:T(8,128)(2,1)S(1)}, u32[]{:S(2)}, u32[]{:S(2)}) %collective-permute-start.10) | collective-permute-done | bytes 184352 | tf_op jit(solution)/shard_map/ppermute | solution.py:345
  47.7 1.8 %collective-permute-done.8.refs_4_ = bf16[72,1280]{1,0:T(8,128)(2,1)S(1)} collective-permute-done((bf16[72,1280]{1,0:T(8,128)(2,1)S(1)}, bf16[72,1280]{1,0:T(8,128)(2,1)S(1)}, u32[]{:S(2)}, u32[]{:S(2)}) %collective-permute-start.8) | collective-permute-done | bytes 184352 | tf_op jit(solution)/shard_map/ppermute | solution.py:345
  49.5 0.8 %collective-permute-done.6.refs_2_ = bf16[72,1280]{1,0:T(8,128)(2,1)S(1)} collective-permute-done((bf16[72,1280]{1,0:T(8,128)(2,1)S(1)}, bf16[72,1280]{1,0:T(8,128)(2,1)S(1)}, u32[]{:S(2)}, u32[]{:S(2)}) %collective-permute-start.6) | collective-permute-done | bytes 184352 | tf_op jit(solution)/shard_map/ppermute | solution.py:345
  51.0 0.8 %collective-permute-done.7.refs_3_ = bf16[72,1280]{1,0:T(8,128)(2,1)S(1)} collective-permute-done((bf16[72,1280]{1,0:T(8,128)(2,1)S(1)}, bf16[72,1280]{1,0:T(8,128)(2,1)S(1)}, u32[]{:S(2)}, u32[]{:S(2)}) %collective-permute-start.7) | collective-permute-done | bytes 184352 | tf_op jit(solution)/shard_map/ppermute | solution.py:336
  51.7 2.1 %gram.1 = (bf16[16,64,384]{2,1,0:T(8,128)(2,1)}, f32[8,128]{1,0:T(8,128)S(1)}) custom-call(bf16[72,1280]{1,0:T(8,128)(2,1)S(1)} %x_end.1.refs_0_, bf16[72,1280]{1,0:T(8,128)(2,1)S(1)} %collective-permute-done.5.refs_1_, bf16[72,1280]{1,0:T(8,128)(2,1)S(1)} %collective-permute-done.6.refs_2_, bf16[72,1280]{1,0:T(8,128)(2,1)S(1)} %collective-permute-done.7.refs_3_, ...), custom_call_target="tpu_custom_call" | custom-call | flops 600000000 | tf_op jit(solution)/shard_map/gram/pallas_call | solution.py:255
  53.9 5.2 %all-to-all-start.5 = ((bf16[16,64,384]{2,1,0:T(8,128)(2,1)}), bf16[16,64,384]{2,1,0:T(8,128)(2,1)S(1)}, u32[]{:S(2)}, u32[]{:S(2)}) async-start(bf16[16,64,384]{2,1,0:T(8,128)(2,1)} %get-tuple-element.52), calls=%async_computation.5 | async-start | bytes 1572864 | tf_op jit(solution)/shard_map/all_to_all | solution.py:357
  59.1 3.4 %collective-permute-start.21 = (f32[8,128]{1,0:T(8,128)S(1)}, f32[8,128]{1,0:T(8,128)S(1)}, u32[]{:S(2)}, u32[]{:S(2)}) collective-permute-start(f32[8,128]{1,0:T(8,128)S(1)} %get-tuple-element.51), channel_id=1, source_target_pairs={{0,16},{16,0},{1,17},{17,1},{2,18},{18,2},{3,19},{19,3},{4,20},{20... | collective-permute-start | bytes 12296 | tf_op jit(solution)/shard_map/ppermute | solution.py:358
  63.1 8.7 %collective-permute-done.21 = f32[8,128]{1,0:T(8,128)S(1)} collective-permute-done((f32[8,128]{1,0:T(8,128)S(1)}, f32[8,128]{1,0:T(8,128)S(1)}, u32[]{:S(2)}, u32[]{:S(2)}) %collective-permute-start.21) | collective-permute-done | bytes 4128 | tf_op jit(solution)/shard_map/ppermute | solution.py:358
  73.8 0.8 %conditional.1 = ((f32[64,128]{1,0:T(8,128)}, f32[64,128]{1,0:T(8,128)}, f32[64,128]{1,0:T(8,128)})) conditional(s32[]{:T(128)} %bitcast.9, (bf16[1024,1792]{1,0:T(8,128)(2,1)}, bf16[1792,1024]{1,0:T(8,128)(2,1)}, s32[1024]{0:T(1024)S(1)}, bf16[1024,512]{1,0:T(8,128)(2,1)S(1)}, bf16[512,1024]{1,0:T(8,128)(2,1)S(1)}) %tuple.27, ...), branch_computations={%region_0.0_spmd, %region_6.0_spmd} | conditional | flops 5646950400 | bytes 166300480 | solution.py:395
  73.8 0.7 final.1
  (39 shorter events, 5.7 us)
Async XLA Ops:
  0.6 5.1 %copy-start = (bf16[1792,1024]{1,0:T(8,128)(2,1)S(1)}, bf16[1792,1024]{1,0:T(8,128)(2,1)}, u32[]{:S(2)}) copy-start(bf16[1792,1024]{1,0:T(8,128)(2,1)} %b_ref.9) | copy-start | bytes 11010052
  0.6 5.1 %copy-start.1 = (bf16[1024,1792]{1,0:T(8,128)(2,1)S(1)}, bf16[1024,1792]{1,0:T(8,128)(2,1)}, u32[]{:S(2)}) copy-start(bf16[1024,1792]{1,0:T(8,128)(2,1)} %h_ref.3) | copy-start | bytes 11010052
  0.7 5.1 %copy-start.4 = (s32[1024]{0:T(1024)S(1)}, s32[1024]{0:T(1024)}, u32[]{:S(2)}) copy-start(s32[1024]{0:T(1024)} %param.11) | copy-start | bytes 12292
  4.1 18.3 %collective-permute-start = (s16[4,72,1024]{2,1,0:T(8,128)(2,1)S(1)}, s16[4,72,1024]{2,1,0:T(8,128)(2,1)S(1)}, u32[]{:S(2)}, u32[]{:S(2)}) collective-permute-start(s16[4,72,1024]{2,1,0:T(8,128)(2,1)S(1)} %grads_send.1), channel_id=1, source_target_pairs={{0,1},{1,0},{2,3},{3,2},{4,5},{5,4},{6,7},{7,6},{8,9},{9,8},{10,11... | collective-permute-start | bytes 1769480 | tf_op jit(solution)/shard_map/ppermute | solution.py:285
  9.8 13.7 %collective-permute-start.12 = (s16[2,72,768]{2,1,0:T(8,128)(2,1)S(1)}, s16[2,72,768]{2,1,0:T(8,128)(2,1)S(1)}, u32[]{:S(2)}, u32[]{:S(2)}) collective-permute-start(s16[2,72,768]{2,1,0:T(8,128)(2,1)S(1)} %get-tuple-element.46), channel_id=1, source_target_pairs={{0,2},{2,4},{4,6},{6,0},{1,3},{3,5},{5,7},{7,1},{8,10},{10,12},{12... | collective-permute-start | bytes 663560 | tf_op jit(solution)/shard_map/ppermute | solution.py:296
  11.7 11.8 %collective-permute-start.13 = (s16[2,72,768]{2,1,0:T(8,128)(2,1)S(1)}, s16[2,72,768]{2,1,0:T(8,128)(2,1)S(1)}, u32[]{:S(2)}, u32[]{:S(2)}) collective-permute-start(s16[2,72,768]{2,1,0:T(8,128)(2,1)S(1)} %get-tuple-element.47), channel_id=1, source_target_pairs={{0,6},{2,0},{4,2},{6,4},{1,7},{3,1},{5,3},{7,5},{8,14},{10,8},{12,... | collective-permute-start | bytes 663560 | tf_op jit(solution)/shard_map/ppermute | solution.py:296
  14.0 11.0 %collective-permute-start.14 = (s16[2,72,768]{2,1,0:T(8,128)(2,1)S(1)}, s16[2,72,768]{2,1,0:T(8,128)(2,1)S(1)}, u32[]{:S(2)}, u32[]{:S(2)}) collective-permute-start(s16[2,72,768]{2,1,0:T(8,128)(2,1)S(1)} %get-tuple-element.48), channel_id=1, source_target_pairs={{0,4},{2,6},{4,0},{6,2},{1,5},{3,7},{5,1},{7,3},{8,12},{10,14},{12... | collective-permute-start | bytes 663560 | tf_op jit(solution)/shard_map/ppermute | solution.py:296
  15.7 2.0 %copy-start.2 = (bf16[1024,512]{1,0:T(8,128)(2,1)S(1)}, bf16[1024,512]{1,0:T(8,128)(2,1)}, u32[]{:S(2)}) copy-start(bf16[1024,512]{1,0:T(8,128)(2,1)} %g_ref.3) | copy-start | bytes 3145732
  15.7 2.0 %copy-start.3 = (bf16[512,1024]{1,0:T(8,128)(2,1)S(1)}, bf16[512,1024]{1,0:T(8,128)(2,1)}, u32[]{:S(2)}) copy-start(bf16[512,1024]{1,0:T(8,128)(2,1)} %b_ref.8) | copy-start | bytes 3145732
  17.2 5.2 %collective-permute-start.1 = (s16[4,72,256]{2,1,0:T(8,128)(2,1)S(1)}, s16[4,72,256]{2,1,0:T(8,128)(2,1)S(1)}, u32[]{:S(2)}, u32[]{:S(2)}) collective-permute-start(s16[4,72,256]{2,1,0:T(8,128)(2,1)S(1)} %get-tuple-element.39), channel_id=1, source_target_pairs={{0,1},{1,0},{2,3},{3,2},{4,5},{5,4},{6,7},{7,6},{8,9},{9,8},{10,11... | collective-permute-start | bytes 442376 | tf_op jit(solution)/shard_map/ppermute | solution.py:306
  25.6 6.1 %collective-permute-start.15 = (s16[72,768]{1,0:T(8,128)(2,1)S(1)}, s16[72,768]{1,0:T(8,128)(2,1)S(1)}, u32[]{:S(2)}, u32[]{:S(2)}) collective-permute-start(s16[72,768]{1,0:T(8,128)(2,1)S(1)} %get-tuple-element.50), channel_id=1, source_target_pairs={{0,1},{1,0},{2,3},{3,2},{4,5},{5,4},{6,7},{7,6},{8,9},{9,8},{10,11... | collective-permute-start | bytes 331784 | tf_op jit(solution)/shard_map/ppermute | solution.py:333
  26.2 9.8 %collective-permute-start.2 = (s16[72,1280]{1,0:T(8,128)(2,1)S(1)}, s16[72,1280]{1,0:T(8,128)(2,1)S(1)}, u32[]{:S(2)}, u32[]{:S(2)}) collective-permute-start(s16[72,1280]{1,0:T(8,128)(2,1)S(1)} %get-tuple-element.41), channel_id=1, source_target_pairs={{0,2},{2,4},{4,6},{6,0},{1,3},{3,5},{5,7},{7,1},{8,10},{10,12},{12... | collective-permute-start | bytes 552968 | tf_op jit(solution)/shard_map/ppermute | solution.py:331
  27.7 8.9 %collective-permute-start.3 = (s16[72,1280]{1,0:T(8,128)(2,1)S(1)}, s16[72,1280]{1,0:T(8,128)(2,1)S(1)}, u32[]{:S(2)}, u32[]{:S(2)}) collective-permute-start(s16[72,1280]{1,0:T(8,128)(2,1)S(1)} %get-tuple-element.42), channel_id=1, source_target_pairs={{0,6},{2,0},{4,2},{6,4},{1,7},{3,1},{5,3},{7,5},{8,14},{10,8},{12,... | collective-permute-start | bytes 552968 | tf_op jit(solution)/shard_map/ppermute | solution.py:331
  29.9 8.6 %collective-permute-start.4 = (s16[72,1280]{1,0:T(8,128)(2,1)S(1)}, s16[72,1280]{1,0:T(8,128)(2,1)S(1)}, u32[]{:S(2)}, u32[]{:S(2)}) collective-permute-start(s16[72,1280]{1,0:T(8,128)(2,1)S(1)} %get-tuple-element.43), channel_id=1, source_target_pairs={{0,4},{2,6},{4,0},{6,2},{1,5},{3,7},{5,1},{7,3},{8,12},{10,14},{12... | collective-permute-start | bytes 552968 | tf_op jit(solution)/shard_map/ppermute | solution.py:331
  31.8 3.4 %collective-permute-start.16 = (bf16[72,768]{1,0:T(8,128)(2,1)S(1)}, bf16[72,768]{1,0:T(8,128)(2,1)S(1)}, u32[]{:S(2)}, u32[]{:S(2)}) collective-permute-start(bf16[72,768]{1,0:T(8,128)(2,1)S(1)} %z_end.1.own_ref.refs_8_), channel_id=1, source_target_pairs={{0,8},{8,0},{1,9},{9,1},{2,10},{10,2},{3,11},{11,3},{4,12},{12,4},... | collective-permute-start | bytes 331784 | tf_op jit(solution)/shard_map/ppermute | solution.py:336
  31.9 12.4 %collective-permute-start.17 = (bf16[72,768]{1,0:T(8,128)(2,1)S(1)}, bf16[72,768]{1,0:T(8,128)(2,1)S(1)}, u32[]{:S(2)}, u32[]{:S(2)}) collective-permute-start(bf16[72,768]{1,0:T(8,128)(2,1)S(1)} %z_end.1.own_ref.refs_8_), channel_id=1, source_target_pairs={{0,64},{32,96},{64,0},{96,32},{1,65},{33,97},{65,1},{97,33},{2,66}... | collective-permute-start | bytes 331784 | tf_op jit(solution)/shard_map/ppermute | solution.py:340
  35.2 10.1 %collective-permute-start.19 = (bf16[2,72,768]{2,1,0:T(8,128)(2,1)S(1)}, bf16[2,72,768]{2,1,0:T(8,128)(2,1)S(1)}, u32[]{:S(2)}, u32[]{:S(2)}) collective-permute-start(bf16[2,72,768]{2,1,0:T(8,128)(2,1)S(1)} %z_both.1), channel_id=1, source_target_pairs={{0,32},{8,104},{32,64},{40,8},{64,96},{72,40},{96,0},{104,72},{1,3... | collective-permute-start | bytes 663560 | tf_op jit(solution)/shard_map/ppermute | solution.py:342
  38.9 8.8 %collective-permute-start.10 = (bf16[72,1280]{1,0:T(8,128)(2,1)S(1)}, bf16[72,1280]{1,0:T(8,128)(2,1)S(1)}, u32[]{:S(2)}, u32[]{:S(2)}) collective-permute-start(bf16[72,1280]{1,0:T(8,128)(2,1)S(1)} %x_end.1.refs_0_), channel_id=1, source_target_pairs={{0,64},{32,96},{64,0},{96,32},{1,65},{33,97},{65,1},{97,33},{2,66}... | collective-permute-start | bytes 552968 | tf_op jit(solution)/shard_map/ppermute | solution.py:345
  42.2 7.3 %collective-permute-start.8 = (bf16[72,1280]{1,0:T(8,128)(2,1)S(1)}, bf16[72,1280]{1,0:T(8,128)(2,1)S(1)}, u32[]{:S(2)}, u32[]{:S(2)}) collective-permute-start(bf16[72,1280]{1,0:T(8,128)(2,1)S(1)} %x_end.1.refs_0_), channel_id=1, source_target_pairs={{0,96},{32,0},{64,32},{96,64},{1,97},{33,1},{65,33},{97,65},{2,98}... | collective-permute-start | bytes 552968 | tf_op jit(solution)/shard_map/ppermute | solution.py:345
  43.3 7.1 %collective-permute-start.6 = (bf16[72,1280]{1,0:T(8,128)(2,1)S(1)}, bf16[72,1280]{1,0:T(8,128)(2,1)S(1)}, u32[]{:S(2)}, u32[]{:S(2)}) collective-permute-start(bf16[72,1280]{1,0:T(8,128)(2,1)S(1)} %x_end.1.refs_0_), channel_id=1, source_target_pairs={{0,32},{32,64},{64,96},{96,0},{1,33},{33,65},{65,97},{97,1},{2,34}... | collective-permute-start | bytes 552968 | tf_op jit(solution)/shard_map/ppermute | solution.py:345
  44.2 1.3 %collective-permute-start.18 = (bf16[72,768]{1,0:T(8,128)(2,1)S(1)}, bf16[72,768]{1,0:T(8,128)(2,1)S(1)}, u32[]{:S(2)}, u32[]{:S(2)}) collective-permute-start(bf16[72,768]{1,0:T(8,128)(2,1)S(1)} %collective-permute-done.17.refs_10_), channel_id=1, source_target_pairs={{0,8},{8,0},{1,9},{9,1},{2,10},{10,2},{3,11},{11,3},{4,12},{12,4},... | collective-permute-start | bytes 331784 | tf_op jit(solution)/shard_map/ppermute | solution.py:336
  45.3 6.4 %collective-permute-start.20 = (bf16[2,72,768]{2,1,0:T(8,128)(2,1)S(1)}, bf16[2,72,768]{2,1,0:T(8,128)(2,1)S(1)}, u32[]{:S(2)}, u32[]{:S(2)}) collective-permute-start(bf16[2,72,768]{2,1,0:T(8,128)(2,1)S(1)} %collective-permute-done.19.refs_12_), channel_id=1, source_target_pairs={{0,8},{8,0},{1,9},{9,1},{2,10},{10,2},{3,11},{11,3},{4,12},{12,4},... | collective-permute-start | bytes 663560 | tf_op jit(solution)/shard_map/ppermute | solution.py:336
  45.6 4.8 %collective-permute-start.5 = (bf16[72,1280]{1,0:T(8,128)(2,1)S(1)}, bf16[72,1280]{1,0:T(8,128)(2,1)S(1)}, u32[]{:S(2)}, u32[]{:S(2)}) collective-permute-start(bf16[72,1280]{1,0:T(8,128)(2,1)S(1)} %x_end.1.refs_0_), channel_id=1, source_target_pairs={{0,8},{8,0},{1,9},{9,1},{2,10},{10,2},{3,11},{11,3},{4,12},{12,4},... | collective-permute-start | bytes 552968 | tf_op jit(solution)/shard_map/ppermute | solution.py:336
  47.7 2.6 %collective-permute-start.11 = (bf16[72,1280]{1,0:T(8,128)(2,1)S(1)}, bf16[72,1280]{1,0:T(8,128)(2,1)S(1)}, u32[]{:S(2)}, u32[]{:S(2)}) collective-permute-start(bf16[72,1280]{1,0:T(8,128)(2,1)S(1)} %collective-permute-done.10.refs_6_), channel_id=1, source_target_pairs={{0,8},{8,0},{1,9},{9,1},{2,10},{10,2},{3,11},{11,3},{4,12},{12,4},... | collective-permute-start | bytes 552968 | tf_op jit(solution)/shard_map/ppermute | solution.py:336
  49.5 1.4 %collective-permute-start.9 = (bf16[72,1280]{1,0:T(8,128)(2,1)S(1)}, bf16[72,1280]{1,0:T(8,128)(2,1)S(1)}, u32[]{:S(2)}, u32[]{:S(2)}) collective-permute-start(bf16[72,1280]{1,0:T(8,128)(2,1)S(1)} %collective-permute-done.8.refs_4_), channel_id=1, source_target_pairs={{0,8},{8,0},{1,9},{9,1},{2,10},{10,2},{3,11},{11,3},{4,12},{12,4},... | collective-permute-start | bytes 552968 | tf_op jit(solution)/shard_map/ppermute | solution.py:336
  50.3 1.4 %collective-permute-start.7 = (bf16[72,1280]{1,0:T(8,128)(2,1)S(1)}, bf16[72,1280]{1,0:T(8,128)(2,1)S(1)}, u32[]{:S(2)}, u32[]{:S(2)}) collective-permute-start(bf16[72,1280]{1,0:T(8,128)(2,1)S(1)} %collective-permute-done.6.refs_2_), channel_id=1, source_target_pairs={{0,8},{8,0},{1,9},{9,1},{2,10},{10,2},{3,11},{11,3},{4,12},{12,4},... | collective-permute-start | bytes 552968 | tf_op jit(solution)/shard_map/ppermute | solution.py:336
  53.9 19.9 %all-to-all-start.5 = ((bf16[16,64,384]{2,1,0:T(8,128)(2,1)}), bf16[16,64,384]{2,1,0:T(8,128)(2,1)S(1)}, u32[]{:S(2)}, u32[]{:S(2)}) async-start(bf16[16,64,384]{2,1,0:T(8,128)(2,1)} %get-tuple-element.52), calls=%async_computation.5 | async-start | bytes 1572864 | tf_op jit(solution)/shard_map/all_to_all | solution.py:357
  59.1 12.6 %collective-permute-start.21 = (f32[8,128]{1,0:T(8,128)S(1)}, f32[8,128]{1,0:T(8,128)S(1)}, u32[]{:S(2)}, u32[]{:S(2)}) collective-permute-start(f32[8,128]{1,0:T(8,128)S(1)} %get-tuple-element.51), channel_id=1, source_target_pairs={{0,16},{16,0},{1,17},{17,1},{2,18},{18,2},{3,19},{19,3},{4,20},{20... | collective-permute-start | bytes 12296 | tf_op jit(solution)/shard_map/ppermute | solution.py:358

commit v7 on v6

--- a/solution.py
+++ b/solution.py
@@ -37,20 +37,23 @@
     return jnp.clip(jnp.ceil(jnp.log2(jnp.maximum(top, 1e-37))), -100.0, 100.0)
 
 
+def levels(x, k):
+    y = x * jnp.exp2(-k)
+    root = y * lax.rsqrt(jnp.maximum(jnp.abs(y), 1e-30))
+    return jnp.round(jnp.clip(root * TOP, -TOP, TOP))
+
+
+def values(q, k):
+    return q * jnp.abs(q) * (jnp.exp2(k) * (1.0 / (TOP * TOP)))
+
+
 def encode(x, k):
-    y = x * jnp.exp2(-k)
-    mag = jnp.abs(y)
-    root = y * lax.rsqrt(jnp.maximum(mag, 1e-30))
-    q = jnp.round(jnp.clip(root * TOP, -TOP, TOP))
-    q = jnp.where(last_row(x.shape), k, q)
-    return q.astype(jnp.int32).astype(I16)
+    return jnp.where(last_row(x.shape), k, levels(x, k)).astype(jnp.int32).astype(I16)
 
 
 def decode(q):
     q = q.astype(F32)
-    unit = jnp.exp2(q[KEEP:SLOT, :]) * (1.0 / (TOP * TOP))
-    x = q * jnp.abs(q) * unit
-    return jnp.where(last_row(x.shape), 0.0, x)
+    return jnp.where(last_row(q.shape), 0.0, values(q, q[KEEP:SLOT, :]))
 
 
 def top_of(x):
@@ -209,9 +212,15 @@
 
 
 def put(out_ref, n, t):
+    cols = slice(n * 128, (n + 1) * 128)
+    k = exponent_of(top_of(t))
+    q = levels(t, k).astype(jnp.int32).astype(I16)
     for xh in range(2):
         for cb in range(8):
-            out_ref[xh * 8 + cb, :, n * 128 : (n + 1) * 128] = t[xh * 64 : (xh + 1) * 64, cb * 128 : (cb + 1) * 128]
+            out_ref[xh * 8 + cb, :64, cols] = q[xh * 64 : (xh + 1) * 64, cb * 128 : (cb + 1) * 128]
+    scale = jnp.broadcast_to(k, (8, 128)).astype(jnp.int32).astype(I16)
+    for n in range(16):
+        out_ref[n, 64:, cols] = scale
 
 
 def gram_kernel(scale, *refs):
@@ -228,7 +237,7 @@
     gather_rows(a_s, slice(0, AZ), z_refs, slice(0, AZ))
 
     def dot(lhs, rhs):
-        return (lax.dot_general(lhs, rhs, CONTRACT, preferred_element_type=F32) * scale).astype(BF)
+        return lax.dot_general(lhs, rhs, CONTRACT, preferred_element_type=F32) * scale
 
     own = own_columns(a_s)
     put(out_ref, 1, dot(own_columns(g_s), g_s[...]))
@@ -237,9 +246,9 @@
 
 
 def final_kernel(in_ref, a_ref, g_ref, c_ref):
-    t = in_ref[0].astype(F32)
-    for n in range(1, 16):
-        t = t + in_ref[n].astype(F32)
+    t = jnp.zeros((64, 384), F32)
+    for n in range(16):
+        t = t + values(in_ref[n, :64, :].astype(F32), in_ref[n, 64:, :].astype(F32)[:1, :])
     a_ref[...] = t[:, :128]
     g_ref[...] = t[:, 128:256]
     c_ref[...] = t[:, 256:]
@@ -349,7 +358,7 @@
     parts, whole = call(
         lambda *refs: gram_kernel(scale, *refs),
         "gram",
-        (sds((16, 64, 384), BF), sds((8, 128), F32)),
+        (sds((16, SLOT, 384), I16), sds((8, 128), F32)),
         (*all_x, *all_z),
         (rows, rows),
         flops=600_000_000,

time: 74.8 us -> 77 us (1.029)
  Pallas kernels: 16 us -> 17.1 us
  waiting for transfers between devices: 22.7 us -> 23.7 us
    pallas_call x12, Pallas kernels: 16 us -> 17.1 us  [call(): pl.pallas_call(kernel, out_shape=out_shape, in_specs=[vmem] * (len(args)...]
    ppermute x1, waiting for transfers between devices: 8.68 us -> 9.74 us  [fast(): return (got, whole[0, 0] + lax.ppermute(whole, 'xh', SWAP)[0, 0])]
where the time goes in v7:
time: 77 us; the launch traced here: 76.8 us
  starting transfers between devices  32.8 us (43%)
  waiting for transfers between devices  23.7 us (31%)
  Pallas kernels  17.1 us (22%)
  between operations  2.08 us (3%)
  local copies, waits for them, and re-layouts  1.05 us (1%)
    pallas_call x12, Pallas kernels, call(): pl.pallas_call(kernel, out_shape=out_shape, in_specs=[vmem] * (len(args)...  17.1 us
    ppermute x1, waiting for transfers between devices, fast(): return (got, whole[0, 0] + lax.ppermute(whole, 'xh', SWAP)[0, 0])  9.74 us
    ppermute x3, starting transfers between devices, fast(): z_got = [lax.ppermute(s, 'z', ring(d)) for s, d in zip(z_send, HOPS)]  5.96 us
    ppermute x3, starting transfers between devices, fast(): x_last = [lax.ppermute(s, 'z', ring(d)) for s, d in zip(x_next, HOPS)]  5.51 us
    ppermute x3, starting transfers between devices, fast(): near = [rot_x] + [lax.ppermute(rot_x, 'y', ring(d)) for d in (1, 3, 2)]  5.3 us
    all_to_all x1, starting transfers between devices, fast(): got = lax.all_to_all(parts, ('xh', 'z', 'xl'), 0, 0, tiled=True)  5.22 us
    ppermute x3, waiting for transfers between devices, fast(): near = [rot_x] + [lax.ppermute(rot_x, 'y', ring(d)) for d in (1, 3, 2)]  4.39 us
    ppermute x1, starting transfers between devices, fast(): return (got, whole[0, 0] + lax.ppermute(whole, 'xh', SWAP)[0, 0])  3.43 us
  transfers between devices with their start and end apart: 23, of which 13 were waited for; matrix products, arithmetic and copies ran while one was open for 1% of the time, Pallas kernels for 12%

profile of v7, /device:TPU:0, one launch (start us, length us, event | category | flops | bytes accessed | tf_op | source)
XLA Modules:
  0.0 76.8 jit_solution(18347990468749830606)
XLA Ops:
  0.7 3.4 %grads_send.1 = s16[4,72,1024]{2,1,0:T(8,128)(2,1)S(1)} custom-call(s32[8,128]{1,0:T(8,128)} %bitcast.39, bf16[1024,512]{1,0:T(8,128)(2,1)} %g_ref.3, bf16[512,1024]{1,0:T(8,128)(2,1)} %b_ref.8), custom_call_target="tpu_custom_call" | custom-call | flops 10000000000 | tf_op jit(solution)/shard_map/grads_send/pallas_call | solution.py:264
  4.1 1.6 %collective-permute-start = (s16[4,72,1024]{2,1,0:T(8,128)(2,1)S(1)}, s16[4,72,1024]{2,1,0:T(8,128)(2,1)S(1)}, u32[]{:S(2)}, u32[]{:S(2)}) collective-permute-start(s16[4,72,1024]{2,1,0:T(8,128)(2,1)S(1)} %grads_send.1), channel_id=1, source_target_pairs={{0,1},{1,0},{2,3},{3,2},{4,5},{5,4},{6,7},{7,6},{8,9},{9,8},{10,11... | collective-permute-start | bytes 1769480 | tf_op jit(solution)/shard_map/ppermute | solution.py:294
  5.7 4.0 %acts_z.1 = (s16[2,72,768]{2,1,0:T(8,128)(2,1)S(1)}, s16[2,72,768]{2,1,0:T(8,128)(2,1)S(1)}, s16[2,72,768]{2,1,0:T(8,128)(2,1)S(1)}, bf16[432,1792]{1,0:T(8,128)(2,1)S(1)}, f32[8,128]{1,0:T(8,128)S(1)}) custom-call(s32[8,128]{1,0:T(8,128)S(1)} %bitcast.40, bf16[1024,1792]{1,0:T(8,128)(2,1)S(1)} %copy-done.1, bf16[1792,1024]{1,0:T(8,128)(2,1)S(1)} %copy-done), custom_call_target="tpu_custom_call" | custom-call | flops 4000000000 | tf_op jit(solution)/shard_map/acts_z/pallas_call | solution.py:264
  9.8 2.0 %collective-permute-start.12 = (s16[2,72,768]{2,1,0:T(8,128)(2,1)S(1)}, s16[2,72,768]{2,1,0:T(8,128)(2,1)S(1)}, u32[]{:S(2)}, u32[]{:S(2)}) collective-permute-start(s16[2,72,768]{2,1,0:T(8,128)(2,1)S(1)} %get-tuple-element.46), channel_id=1, source_target_pairs={{0,2},{2,4},{4,6},{6,0},{1,3},{3,5},{5,7},{7,1},{8,10},{10,12},{12... | collective-permute-start | bytes 663560 | tf_op jit(solution)/shard_map/ppermute | solution.py:305
  11.7 2.2 %collective-permute-start.13 = (s16[2,72,768]{2,1,0:T(8,128)(2,1)S(1)}, s16[2,72,768]{2,1,0:T(8,128)(2,1)S(1)}, u32[]{:S(2)}, u32[]{:S(2)}) collective-permute-start(s16[2,72,768]{2,1,0:T(8,128)(2,1)S(1)} %get-tuple-element.47), channel_id=1, source_target_pairs={{0,6},{2,0},{4,2},{6,4},{1,7},{3,1},{5,3},{7,5},{8,14},{10,8},{12,... | collective-permute-start | bytes 663560 | tf_op jit(solution)/shard_map/ppermute | solution.py:305
  14.0 1.8 %collective-permute-start.14 = (s16[2,72,768]{2,1,0:T(8,128)(2,1)S(1)}, s16[2,72,768]{2,1,0:T(8,128)(2,1)S(1)}, u32[]{:S(2)}, u32[]{:S(2)}) collective-permute-start(s16[2,72,768]{2,1,0:T(8,128)(2,1)S(1)} %get-tuple-element.48), channel_id=1, source_target_pairs={{0,4},{2,6},{4,0},{6,2},{1,5},{3,7},{5,1},{7,3},{8,12},{10,14},{12... | collective-permute-start | bytes 663560 | tf_op jit(solution)/shard_map/ppermute | solution.py:305
  15.7 1.4 %acts_x.1 = (s16[4,72,256]{2,1,0:T(8,128)(2,1)S(1)}, bf16[144,1792]{1,0:T(8,128)(2,1)S(1)}) custom-call(s32[8,128]{1,0:T(8,128)S(1)} %bitcast.41, bf16[1024,1792]{1,0:T(8,128)(2,1)S(1)} %copy-done.1, bf16[1792,1024]{1,0:T(8,128)(2,1)S(1)} %copy-done, bf16[432,1792]{1,0:T(8,128)(2,1)S(1)} %get-tuple-element.36.picked_ref), custom_call_target="tpu_custom_call" | custom-call | flops 1000000000 | tf_op jit(solution)/shard_map/acts_x/pallas_call | solution.py:264
  17.8 1.0 %grads_keep.1.g_keep = f32[288,1024]{1,0:T(8,128)S(1)} custom-call(s32[8,128]{1,0:T(8,128)S(1)} %bitcast.42, bf16[1024,512]{1,0:T(8,128)(2,1)S(1)} %copy-done.2, bf16[512,1024]{1,0:T(8,128)(2,1)S(1)} %copy-done.3, bf16[144,1792]{1,0:T(8,128)(2,1)S(1)} %get-tuple-element.37.after_ref.near_ref), custom_call_target="tpu_custom_call" | custom-call | flops 600000000 | tf_op jit(solution)/shard_map/grads_keep/pallas_call | solution.py:264
  18.8 1.0 %acts_keep.1 = (f32[2,72,768]{2,1,0:T(8,128)S(1)}, f32[288,256]{1,0:T(8,128)S(1)}) custom-call(bf16[432,1792]{1,0:T(8,128)(2,1)S(1)} %get-tuple-element.36.picked_ref, bf16[144,1792]{1,0:T(8,128)(2,1)S(1)} %get-tuple-element.37.after_ref.near_ref, bf16[1792,1024]{1,0:T(8,128)(2,1)S(1)} %copy-done), custom_call_target="tpu_custom_call" | custom-call | flops 1000000000 | tf_op jit(solution)/shard_map/acts_keep/pallas_call | solution.py:264
  19.8 2.6 %collective-permute-done.1.a_got = s16[4,72,256]{2,1,0:T(8,128)(2,1)S(1)} collective-permute-done((s16[4,72,256]{2,1,0:T(8,128)(2,1)S(1)}, s16[4,72,256]{2,1,0:T(8,128)(2,1)S(1)}, u32[]{:S(2)}, u32[]{:S(2)}) %collective-permute-start.1) | collective-permute-done | bytes 147488 | tf_op jit(solution)/shard_map/ppermute | solution.py:315
  22.4 1.1 %x_mid.1 = (f32[72,1280]{1,0:T(8,128)S(1)}, s16[72,1280]{1,0:T(8,128)(2,1)S(1)}, s16[72,1280]{1,0:T(8,128)(2,1)S(1)}, s16[72,1280]{1,0:T(8,128)(2,1)S(1)}) custom-call(f32[288,1024]{1,0:T(8,128)S(1)} %grads_keep.1.g_keep, s16[4,72,1024]{2,1,0:T(8,128)(2,1)S(1)} %collective-permute-done.g_got, f32[288,256]{1,0:T(8,128)S(1)} %get-tuple-element.38.a_keep, ...), custom_call_target="tpu_custom_call" | custom-call | tf_op jit(solution)/shard_map/x_mid/pallas_call | solution.py:264
  23.5 1.4 %collective-permute-done.14.r3_ref = s16[2,72,768]{2,1,0:T(8,128)(2,1)S(1)} collective-permute-done((s16[2,72,768]{2,1,0:T(8,128)(2,1)S(1)}, s16[2,72,768]{2,1,0:T(8,128)(2,1)S(1)}, u32[]{:S(2)}, u32[]{:S(2)}) %collective-permute-start.14) | collective-permute-done | bytes 221216 | tf_op jit(solution)/shard_map/ppermute | solution.py:305
  26.2 1.5 %collective-permute-start.2 = (s16[72,1280]{1,0:T(8,128)(2,1)S(1)}, s16[72,1280]{1,0:T(8,128)(2,1)S(1)}, u32[]{:S(2)}, u32[]{:S(2)}) collective-permute-start(s16[72,1280]{1,0:T(8,128)(2,1)S(1)} %get-tuple-element.41), channel_id=1, source_target_pairs={{0,2},{2,4},{4,6},{6,0},{1,3},{3,5},{5,7},{7,1},{8,10},{10,12},{12... | collective-permute-start | bytes 552968 | tf_op jit(solution)/shard_map/ppermute | solution.py:340
  27.7 2.1 %collective-permute-start.3 = (s16[72,1280]{1,0:T(8,128)(2,1)S(1)}, s16[72,1280]{1,0:T(8,128)(2,1)S(1)}, u32[]{:S(2)}, u32[]{:S(2)}) collective-permute-start(s16[72,1280]{1,0:T(8,128)(2,1)S(1)} %get-tuple-element.42), channel_id=1, source_target_pairs={{0,6},{2,0},{4,2},{6,4},{1,7},{3,1},{5,3},{7,5},{8,14},{10,8},{12,... | collective-permute-start | bytes 552968 | tf_op jit(solution)/shard_map/ppermute | solution.py:340
  29.8 1.8 %collective-permute-start.4 = (s16[72,1280]{1,0:T(8,128)(2,1)S(1)}, s16[72,1280]{1,0:T(8,128)(2,1)S(1)}, u32[]{:S(2)}, u32[]{:S(2)}) collective-permute-start(s16[72,1280]{1,0:T(8,128)(2,1)S(1)} %get-tuple-element.43), channel_id=1, source_target_pairs={{0,4},{2,6},{4,0},{6,2},{1,5},{3,7},{5,1},{7,3},{8,12},{10,14},{12... | collective-permute-start | bytes 552968 | tf_op jit(solution)/shard_map/ppermute | solution.py:340
  31.9 3.3 %collective-permute-start.17 = (bf16[72,768]{1,0:T(8,128)(2,1)S(1)}, bf16[72,768]{1,0:T(8,128)(2,1)S(1)}, u32[]{:S(2)}, u32[]{:S(2)}) collective-permute-start(bf16[72,768]{1,0:T(8,128)(2,1)S(1)} %z_end.1.own_ref.refs_8_), channel_id=1, source_target_pairs={{0,64},{32,96},{64,0},{96,32},{1,65},{33,97},{65,1},{97,33},{2,66}... | collective-permute-start | bytes 331784 | tf_op jit(solution)/shard_map/ppermute | solution.py:349
  35.2 0.7 collective-permute-start.19
  36.6 1.8 %collective-permute-done.4.r3_ref = s16[72,1280]{1,0:T(8,128)(2,1)S(1)} collective-permute-done((s16[72,1280]{1,0:T(8,128)(2,1)S(1)}, s16[72,1280]{1,0:T(8,128)(2,1)S(1)}, u32[]{:S(2)}, u32[]{:S(2)}) %collective-permute-start.4) | collective-permute-done | bytes 184352 | tf_op jit(solution)/shard_map/ppermute | solution.py:340
  38.9 3.3 %collective-permute-start.10 = (bf16[72,1280]{1,0:T(8,128)(2,1)S(1)}, bf16[72,1280]{1,0:T(8,128)(2,1)S(1)}, u32[]{:S(2)}, u32[]{:S(2)}) collective-permute-start(bf16[72,1280]{1,0:T(8,128)(2,1)S(1)} %x_end.1.refs_0_), channel_id=1, source_target_pairs={{0,64},{32,96},{64,0},{96,32},{1,65},{33,97},{65,1},{97,33},{2,66}... | collective-permute-start | bytes 552968 | tf_op jit(solution)/shard_map/ppermute | solution.py:354
  42.2 1.1 %collective-permute-start.8 = (bf16[72,1280]{1,0:T(8,128)(2,1)S(1)}, bf16[72,1280]{1,0:T(8,128)(2,1)S(1)}, u32[]{:S(2)}, u32[]{:S(2)}) collective-permute-start(bf16[72,1280]{1,0:T(8,128)(2,1)S(1)} %x_end.1.refs_0_), channel_id=1, source_target_pairs={{0,96},{32,0},{64,32},{96,64},{1,97},{33,1},{65,33},{97,65},{2,98}... | collective-permute-start | bytes 552968 | tf_op jit(solution)/shard_map/ppermute | solution.py:354
  43.2 1.0 %collective-permute-start.6 = (bf16[72,1280]{1,0:T(8,128)(2,1)S(1)}, bf16[72,1280]{1,0:T(8,128)(2,1)S(1)}, u32[]{:S(2)}, u32[]{:S(2)}) collective-permute-start(bf16[72,1280]{1,0:T(8,128)(2,1)S(1)} %x_end.1.refs_0_), channel_id=1, source_target_pairs={{0,32},{32,64},{64,96},{96,0},{1,33},{33,65},{65,97},{97,1},{2,34}... | collective-permute-start | bytes 552968 | tf_op jit(solution)/shard_map/ppermute | solution.py:354
  44.2 1.2 %collective-permute-done.19.refs_12_ = bf16[2,72,768]{2,1,0:T(8,128)(2,1)S(1)} collective-permute-done((bf16[2,72,768]{2,1,0:T(8,128)(2,1)S(1)}, bf16[2,72,768]{2,1,0:T(8,128)(2,1)S(1)}, u32[]{:S(2)}, u32[]{:S(2)}) %collective-permute-start.19) | collective-permute-done | bytes 221216 | tf_op jit(solution)/shard_map/ppermute | solution.py:351
  45.9 1.8 %collective-permute-done.10.refs_6_ = bf16[72,1280]{1,0:T(8,128)(2,1)S(1)} collective-permute-done((bf16[72,1280]{1,0:T(8,128)(2,1)S(1)}, bf16[72,1280]{1,0:T(8,128)(2,1)S(1)}, u32[]{:S(2)}, u32[]{:S(2)}) %collective-permute-start.10) | collective-permute-done | bytes 184352 | tf_op jit(solution)/shard_map/ppermute | solution.py:354
  47.7 1.8 %collective-permute-done.8.refs_4_ = bf16[72,1280]{1,0:T(8,128)(2,1)S(1)} collective-permute-done((bf16[72,1280]{1,0:T(8,128)(2,1)S(1)}, bf16[72,1280]{1,0:T(8,128)(2,1)S(1)}, u32[]{:S(2)}, u32[]{:S(2)}) %collective-permute-start.8) | collective-permute-done | bytes 184352 | tf_op jit(solution)/shard_map/ppermute | solution.py:354
  49.5 0.8 %collective-permute-done.6.refs_2_ = bf16[72,1280]{1,0:T(8,128)(2,1)S(1)} collective-permute-done((bf16[72,1280]{1,0:T(8,128)(2,1)S(1)}, bf16[72,1280]{1,0:T(8,128)(2,1)S(1)}, u32[]{:S(2)}, u32[]{:S(2)}) %collective-permute-start.6) | collective-permute-done | bytes 184352 | tf_op jit(solution)/shard_map/ppermute | solution.py:354
  50.9 0.8 %collective-permute-done.7.refs_3_ = bf16[72,1280]{1,0:T(8,128)(2,1)S(1)} collective-permute-done((bf16[72,1280]{1,0:T(8,128)(2,1)S(1)}, bf16[72,1280]{1,0:T(8,128)(2,1)S(1)}, u32[]{:S(2)}, u32[]{:S(2)}) %collective-permute-start.7) | collective-permute-done | bytes 184352 | tf_op jit(solution)/shard_map/ppermute | solution.py:345
  51.7 3.1 %gram.1 = (s16[16,72,384]{2,1,0:T(8,128)(2,1)}, f32[8,128]{1,0:T(8,128)S(1)}) custom-call(bf16[72,1280]{1,0:T(8,128)(2,1)S(1)} %x_end.1.refs_0_, bf16[72,1280]{1,0:T(8,128)(2,1)S(1)} %collective-permute-done.5.refs_1_, bf16[72,1280]{1,0:T(8,128)(2,1)S(1)} %collective-permute-done.6.refs_2_, bf16[72,1280]{1,0:T(8,128)(2,1)S(1)} %collective-permute-done.7.refs_3_, ...), custom_call_target="tpu_custom_call" | custom-call | flops 600000000 | tf_op jit(solution)/shard_map/gram/pallas_call | solution.py:264
  54.8 5.2 %all-to-all-start.5 = ((s16[16,72,384]{2,1,0:T(8,128)(2,1)}), s16[16,72,384]{2,1,0:T(8,128)(2,1)S(1)}, u32[]{:S(2)}, u32[]{:S(2)}) async-start(s16[16,72,384]{2,1,0:T(8,128)(2,1)} %get-tuple-element.52), calls=%async_computation.5 | async-start | bytes 1769472 | tf_op jit(solution)/shard_map/all_to_all | solution.py:366
  60.1 3.4 %collective-permute-start.21 = (f32[8,128]{1,0:T(8,128)S(1)}, f32[8,128]{1,0:T(8,128)S(1)}, u32[]{:S(2)}, u32[]{:S(2)}) collective-permute-start(f32[8,128]{1,0:T(8,128)S(1)} %get-tuple-element.51), channel_id=1, source_target_pairs={{0,16},{16,0},{1,17},{17,1},{2,18},{18,2},{3,19},{19,3},{4,20},{20... | collective-permute-start | bytes 12296 | tf_op jit(solution)/shard_map/ppermute | solution.py:367
  64.0 9.7 %collective-permute-done.21 = f32[8,128]{1,0:T(8,128)S(1)} collective-permute-done((f32[8,128]{1,0:T(8,128)S(1)}, f32[8,128]{1,0:T(8,128)S(1)}, u32[]{:S(2)}, u32[]{:S(2)}) %collective-permute-start.21) | collective-permute-done | bytes 4128 | tf_op jit(solution)/shard_map/ppermute | solution.py:367
  75.8 1.0 %conditional.1 = ((f32[64,128]{1,0:T(8,128)}, f32[64,128]{1,0:T(8,128)}, f32[64,128]{1,0:T(8,128)})) conditional(s32[]{:T(128)} %bitcast.9, (bf16[1024,1792]{1,0:T(8,128)(2,1)}, bf16[1792,1024]{1,0:T(8,128)(2,1)}, s32[1024]{0:T(1024)S(1)}, bf16[1024,512]{1,0:T(8,128)(2,1)S(1)}, bf16[512,1024]{1,0:T(8,128)(2,1)S(1)}) %tuple.27, ...), branch_computations={%region_0.0_spmd, %region_6.0_spmd} | conditional | flops 5646950400 | bytes 166300480 | solution.py:404
  75.8 1.0 %final.1 = (f32[64,128]{1,0:T(8,128)}, f32[64,128]{1,0:T(8,128)}, f32[64,128]{1,0:T(8,128)}) custom-call(s16[16,72,384]{2,1,0:T(8,128)(2,1)S(1)} %in_ref), custom_call_target="tpu_custom_call" | custom-call | tf_op jit(solution)/shard_map/cond/branch_1_fun/final/pallas_call | solution.py:264
  (39 shorter events, 5.6 us)
Async XLA Ops:
  0.6 5.1 %copy-start = (bf16[1792,1024]{1,0:T(8,128)(2,1)S(1)}, bf16[1792,1024]{1,0:T(8,128)(2,1)}, u32[]{:S(2)}) copy-start(bf16[1792,1024]{1,0:T(8,128)(2,1)} %b_ref.9) | copy-start | bytes 11010052
  0.6 5.1 %copy-start.1 = (bf16[1024,1792]{1,0:T(8,128)(2,1)S(1)}, bf16[1024,1792]{1,0:T(8,128)(2,1)}, u32[]{:S(2)}) copy-start(bf16[1024,1792]{1,0:T(8,128)(2,1)} %h_ref.3) | copy-start | bytes 11010052
  0.7 5.1 %copy-start.4 = (s32[1024]{0:T(1024)S(1)}, s32[1024]{0:T(1024)}, u32[]{:S(2)}) copy-start(s32[1024]{0:T(1024)} %param.11) | copy-start | bytes 12292
  4.1 18.3 %collective-permute-start = (s16[4,72,1024]{2,1,0:T(8,128)(2,1)S(1)}, s16[4,72,1024]{2,1,0:T(8,128)(2,1)S(1)}, u32[]{:S(2)}, u32[]{:S(2)}) collective-permute-start(s16[4,72,1024]{2,1,0:T(8,128)(2,1)S(1)} %grads_send.1), channel_id=1, source_target_pairs={{0,1},{1,0},{2,3},{3,2},{4,5},{5,4},{6,7},{7,6},{8,9},{9,8},{10,11... | collective-permute-start | bytes 1769480 | tf_op jit(solution)/shard_map/ppermute | solution.py:294
  9.8 13.7 %collective-permute-start.12 = (s16[2,72,768]{2,1,0:T(8,128)(2,1)S(1)}, s16[2,72,768]{2,1,0:T(8,128)(2,1)S(1)}, u32[]{:S(2)}, u32[]{:S(2)}) collective-permute-start(s16[2,72,768]{2,1,0:T(8,128)(2,1)S(1)} %get-tuple-element.46), channel_id=1, source_target_pairs={{0,2},{2,4},{4,6},{6,0},{1,3},{3,5},{5,7},{7,1},{8,10},{10,12},{12... | collective-permute-start | bytes 663560 | tf_op jit(solution)/shard_map/ppermute | solution.py:305
  11.7 11.8 %collective-permute-start.13 = (s16[2,72,768]{2,1,0:T(8,128)(2,1)S(1)}, s16[2,72,768]{2,1,0:T(8,128)(2,1)S(1)}, u32[]{:S(2)}, u32[]{:S(2)}) collective-permute-start(s16[2,72,768]{2,1,0:T(8,128)(2,1)S(1)} %get-tuple-element.47), channel_id=1, source_target_pairs={{0,6},{2,0},{4,2},{6,4},{1,7},{3,1},{5,3},{7,5},{8,14},{10,8},{12,... | collective-permute-start | bytes 663560 | tf_op jit(solution)/shard_map/ppermute | solution.py:305
  14.0 11.0 %collective-permute-start.14 = (s16[2,72,768]{2,1,0:T(8,128)(2,1)S(1)}, s16[2,72,768]{2,1,0:T(8,128)(2,1)S(1)}, u32[]{:S(2)}, u32[]{:S(2)}) collective-permute-start(s16[2,72,768]{2,1,0:T(8,128)(2,1)S(1)} %get-tuple-element.48), channel_id=1, source_target_pairs={{0,4},{2,6},{4,0},{6,2},{1,5},{3,7},{5,1},{7,3},{8,12},{10,14},{12... | collective-permute-start | bytes 663560 | tf_op jit(solution)/shard_map/ppermute | solution.py:305
  15.7 2.0 %copy-start.2 = (bf16[1024,512]{1,0:T(8,128)(2,1)S(1)}, bf16[1024,512]{1,0:T(8,128)(2,1)}, u32[]{:S(2)}) copy-start(bf16[1024,512]{1,0:T(8,128)(2,1)} %g_ref.3) | copy-start | bytes 3145732
  15.7 2.0 %copy-start.3 = (bf16[512,1024]{1,0:T(8,128)(2,1)S(1)}, bf16[512,1024]{1,0:T(8,128)(2,1)}, u32[]{:S(2)}) copy-start(bf16[512,1024]{1,0:T(8,128)(2,1)} %b_ref.8) | copy-start | bytes 3145732
  17.2 5.2 %collective-permute-start.1 = (s16[4,72,256]{2,1,0:T(8,128)(2,1)S(1)}, s16[4,72,256]{2,1,0:T(8,128)(2,1)S(1)}, u32[]{:S(2)}, u32[]{:S(2)}) collective-permute-start(s16[4,72,256]{2,1,0:T(8,128)(2,1)S(1)} %get-tuple-element.39), channel_id=1, source_target_pairs={{0,1},{1,0},{2,3},{3,2},{4,5},{5,4},{6,7},{7,6},{8,9},{9,8},{10,11... | collective-permute-start | bytes 442376 | tf_op jit(solution)/shard_map/ppermute | solution.py:315
  25.5 6.1 %collective-permute-start.15 = (s16[72,768]{1,0:T(8,128)(2,1)S(1)}, s16[72,768]{1,0:T(8,128)(2,1)S(1)}, u32[]{:S(2)}, u32[]{:S(2)}) collective-permute-start(s16[72,768]{1,0:T(8,128)(2,1)S(1)} %get-tuple-element.50), channel_id=1, source_target_pairs={{0,1},{1,0},{2,3},{3,2},{4,5},{5,4},{6,7},{7,6},{8,9},{9,8},{10,11... | collective-permute-start | bytes 331784 | tf_op jit(solution)/shard_map/ppermute | solution.py:342
  26.2 9.8 %collective-permute-start.2 = (s16[72,1280]{1,0:T(8,128)(2,1)S(1)}, s16[72,1280]{1,0:T(8,128)(2,1)S(1)}, u32[]{:S(2)}, u32[]{:S(2)}) collective-permute-start(s16[72,1280]{1,0:T(8,128)(2,1)S(1)} %get-tuple-element.41), channel_id=1, source_target_pairs={{0,2},{2,4},{4,6},{6,0},{1,3},{3,5},{5,7},{7,1},{8,10},{10,12},{12... | collective-permute-start | bytes 552968 | tf_op jit(solution)/shard_map/ppermute | solution.py:340
  27.7 8.9 %collective-permute-start.3 = (s16[72,1280]{1,0:T(8,128)(2,1)S(1)}, s16[72,1280]{1,0:T(8,128)(2,1)S(1)}, u32[]{:S(2)}, u32[]{:S(2)}) collective-permute-start(s16[72,1280]{1,0:T(8,128)(2,1)S(1)} %get-tuple-element.42), channel_id=1, source_target_pairs={{0,6},{2,0},{4,2},{6,4},{1,7},{3,1},{5,3},{7,5},{8,14},{10,8},{12,... | collective-permute-start | bytes 552968 | tf_op jit(solution)/shard_map/ppermute | solution.py:340
  29.8 8.6 %collective-permute-start.4 = (s16[72,1280]{1,0:T(8,128)(2,1)S(1)}, s16[72,1280]{1,0:T(8,128)(2,1)S(1)}, u32[]{:S(2)}, u32[]{:S(2)}) collective-permute-start(s16[72,1280]{1,0:T(8,128)(2,1)S(1)} %get-tuple-element.43), channel_id=1, source_target_pairs={{0,4},{2,6},{4,0},{6,2},{1,5},{3,7},{5,1},{7,3},{8,12},{10,14},{12... | collective-permute-start | bytes 552968 | tf_op jit(solution)/shard_map/ppermute | solution.py:340
  31.8 3.4 %collective-permute-start.16 = (bf16[72,768]{1,0:T(8,128)(2,1)S(1)}, bf16[72,768]{1,0:T(8,128)(2,1)S(1)}, u32[]{:S(2)}, u32[]{:S(2)}) collective-permute-start(bf16[72,768]{1,0:T(8,128)(2,1)S(1)} %z_end.1.own_ref.refs_8_), channel_id=1, source_target_pairs={{0,8},{8,0},{1,9},{9,1},{2,10},{10,2},{3,11},{11,3},{4,12},{12,4},... | collective-permute-start | bytes 331784 | tf_op jit(solution)/shard_map/ppermute | solution.py:345
  31.9 12.3 %collective-permute-start.17 = (bf16[72,768]{1,0:T(8,128)(2,1)S(1)}, bf16[72,768]{1,0:T(8,128)(2,1)S(1)}, u32[]{:S(2)}, u32[]{:S(2)}) collective-permute-start(bf16[72,768]{1,0:T(8,128)(2,1)S(1)} %z_end.1.own_ref.refs_8_), channel_id=1, source_target_pairs={{0,64},{32,96},{64,0},{96,32},{1,65},{33,97},{65,1},{97,33},{2,66}... | collective-permute-start | bytes 331784 | tf_op jit(solution)/shard_map/ppermute | solution.py:349
  35.2 10.2 %collective-permute-start.19 = (bf16[2,72,768]{2,1,0:T(8,128)(2,1)S(1)}, bf16[2,72,768]{2,1,0:T(8,128)(2,1)S(1)}, u32[]{:S(2)}, u32[]{:S(2)}) collective-permute-start(bf16[2,72,768]{2,1,0:T(8,128)(2,1)S(1)} %z_both.1), channel_id=1, source_target_pairs={{0,32},{8,104},{32,64},{40,8},{64,96},{72,40},{96,0},{104,72},{1,3... | collective-permute-start | bytes 663560 | tf_op jit(solution)/shard_map/ppermute | solution.py:351
  38.9 8.8 %collective-permute-start.10 = (bf16[72,1280]{1,0:T(8,128)(2,1)S(1)}, bf16[72,1280]{1,0:T(8,128)(2,1)S(1)}, u32[]{:S(2)}, u32[]{:S(2)}) collective-permute-start(bf16[72,1280]{1,0:T(8,128)(2,1)S(1)} %x_end.1.refs_0_), channel_id=1, source_target_pairs={{0,64},{32,96},{64,0},{96,32},{1,65},{33,97},{65,1},{97,33},{2,66}... | collective-permute-start | bytes 552968 | tf_op jit(solution)/shard_map/ppermute | solution.py:354
  42.2 7.4 %collective-permute-start.8 = (bf16[72,1280]{1,0:T(8,128)(2,1)S(1)}, bf16[72,1280]{1,0:T(8,128)(2,1)S(1)}, u32[]{:S(2)}, u32[]{:S(2)}) collective-permute-start(bf16[72,1280]{1,0:T(8,128)(2,1)S(1)} %x_end.1.refs_0_), channel_id=1, source_target_pairs={{0,96},{32,0},{64,32},{96,64},{1,97},{33,1},{65,33},{97,65},{2,98}... | collective-permute-start | bytes 552968 | tf_op jit(solution)/shard_map/ppermute | solution.py:354
  43.2 7.1 %collective-permute-start.6 = (bf16[72,1280]{1,0:T(8,128)(2,1)S(1)}, bf16[72,1280]{1,0:T(8,128)(2,1)S(1)}, u32[]{:S(2)}, u32[]{:S(2)}) collective-permute-start(bf16[72,1280]{1,0:T(8,128)(2,1)S(1)} %x_end.1.refs_0_), channel_id=1, source_target_pairs={{0,32},{32,64},{64,96},{96,0},{1,33},{33,65},{65,97},{97,1},{2,34}... | collective-permute-start | bytes 552968 | tf_op jit(solution)/shard_map/ppermute | solution.py:354
  44.2 1.3 %collective-permute-start.18 = (bf16[72,768]{1,0:T(8,128)(2,1)S(1)}, bf16[72,768]{1,0:T(8,128)(2,1)S(1)}, u32[]{:S(2)}, u32[]{:S(2)}) collective-permute-start(bf16[72,768]{1,0:T(8,128)(2,1)S(1)} %collective-permute-done.17.refs_10_), channel_id=1, source_target_pairs={{0,8},{8,0},{1,9},{9,1},{2,10},{10,2},{3,11},{11,3},{4,12},{12,4},... | collective-permute-start | bytes 331784 | tf_op jit(solution)/shard_map/ppermute | solution.py:345
  45.4 6.3 %collective-permute-start.20 = (bf16[2,72,768]{2,1,0:T(8,128)(2,1)S(1)}, bf16[2,72,768]{2,1,0:T(8,128)(2,1)S(1)}, u32[]{:S(2)}, u32[]{:S(2)}) collective-permute-start(bf16[2,72,768]{2,1,0:T(8,128)(2,1)S(1)} %collective-permute-done.19.refs_12_), channel_id=1, source_target_pairs={{0,8},{8,0},{1,9},{9,1},{2,10},{10,2},{3,11},{11,3},{4,12},{12,4},... | collective-permute-start | bytes 663560 | tf_op jit(solution)/shard_map/ppermute | solution.py:345
  45.5 4.8 %collective-permute-start.5 = (bf16[72,1280]{1,0:T(8,128)(2,1)S(1)}, bf16[72,1280]{1,0:T(8,128)(2,1)S(1)}, u32[]{:S(2)}, u32[]{:S(2)}) collective-permute-start(bf16[72,1280]{1,0:T(8,128)(2,1)S(1)} %x_end.1.refs_0_), channel_id=1, source_target_pairs={{0,8},{8,0},{1,9},{9,1},{2,10},{10,2},{3,11},{11,3},{4,12},{12,4},... | collective-permute-start | bytes 552968 | tf_op jit(solution)/shard_map/ppermute | solution.py:345
  47.7 2.6 %collective-permute-start.11 = (bf16[72,1280]{1,0:T(8,128)(2,1)S(1)}, bf16[72,1280]{1,0:T(8,128)(2,1)S(1)}, u32[]{:S(2)}, u32[]{:S(2)}) collective-permute-start(bf16[72,1280]{1,0:T(8,128)(2,1)S(1)} %collective-permute-done.10.refs_6_), channel_id=1, source_target_pairs={{0,8},{8,0},{1,9},{9,1},{2,10},{10,2},{3,11},{11,3},{4,12},{12,4},... | collective-permute-start | bytes 552968 | tf_op jit(solution)/shard_map/ppermute | solution.py:345
  49.5 1.4 %collective-permute-start.9 = (bf16[72,1280]{1,0:T(8,128)(2,1)S(1)}, bf16[72,1280]{1,0:T(8,128)(2,1)S(1)}, u32[]{:S(2)}, u32[]{:S(2)}) collective-permute-start(bf16[72,1280]{1,0:T(8,128)(2,1)S(1)} %collective-permute-done.8.refs_4_), channel_id=1, source_target_pairs={{0,8},{8,0},{1,9},{9,1},{2,10},{10,2},{3,11},{11,3},{4,12},{12,4},... | collective-permute-start | bytes 552968 | tf_op jit(solution)/shard_map/ppermute | solution.py:345
  50.3 1.4 %collective-permute-start.7 = (bf16[72,1280]{1,0:T(8,128)(2,1)S(1)}, bf16[72,1280]{1,0:T(8,128)(2,1)S(1)}, u32[]{:S(2)}, u32[]{:S(2)}) collective-permute-start(bf16[72,1280]{1,0:T(8,128)(2,1)S(1)} %collective-permute-done.6.refs_2_), channel_id=1, source_target_pairs={{0,8},{8,0},{1,9},{9,1},{2,10},{10,2},{3,11},{11,3},{4,12},{12,4},... | collective-permute-start | bytes 552968 | tf_op jit(solution)/shard_map/ppermute | solution.py:345
  54.8 21.0 %all-to-all-start.5 = ((s16[16,72,384]{2,1,0:T(8,128)(2,1)}), s16[16,72,384]{2,1,0:T(8,128)(2,1)S(1)}, u32[]{:S(2)}, u32[]{:S(2)}) async-start(s16[16,72,384]{2,1,0:T(8,128)(2,1)} %get-tuple-element.52), calls=%async_computation.5 | async-start | bytes 1769472 | tf_op jit(solution)/shard_map/all_to_all | solution.py:366
  60.1 13.7 %collective-permute-start.21 = (f32[8,128]{1,0:T(8,128)S(1)}, f32[8,128]{1,0:T(8,128)S(1)}, u32[]{:S(2)}, u32[]{:S(2)}) collective-permute-start(f32[8,128]{1,0:T(8,128)S(1)} %get-tuple-element.51), channel_id=1, source_target_pairs={{0,16},{16,0},{1,17},{17,1},{2,18},{18,2},{3,19},{19,3},{4,20},{20... | collective-permute-start | bytes 12296 | tf_op jit(solution)/shard_map/ppermute | solution.py:367

commit v8 on v6

--- a/solution.py
+++ b/solution.py
@@ -14,6 +14,7 @@
 KEEP = SLOT - 1
 BLOCKS = 8
 CAP = KEEP * BLOCKS
+FEW = 256
 TOP = 32767.0
 HOPS = (1, 3, 2)
 SIDES = [(2 * y + c, 2 * ((y + (-1) ** c) % 4) + c) for y in range(4) for c in range(2)]
@@ -106,7 +107,7 @@
 def acts_z_kernel(routed_ref, h_ref, b_ref, s1_ref, s2_ref, s3_ref, picked_ref, bad_ref, sel_ref, z_ref):
     z, xl = lax.axis_index("z"), lax.axis_index("xl")
     pos, total = ranks(routed_ref[...])
-    bad_ref[...] = jnp.broadcast_to(jnp.where(total > CAP, jnp.nan, 0.0), (8, 128))
+    bad_ref[...] = jnp.broadcast_to(jnp.where((total > CAP) | (total < FEW), jnp.nan, 0.0), (8, 128))
     zs = [lax.rem(z + d, 4) * 2 for d in HOPS]
     build_select(sel_ref, pos, [zz + (1 - xl) for zz in zs] + [zz + xl for zz in zs])
     picked_ref[...] = jnp.dot(sel_ref[...], h_ref[...], preferred_element_type=F32).astype(BF)

time: 74.8 us -> 74.8 us (level)
  no operation moved by 1% of the time
where the time goes in v8:
time: 74.8 us; the launch traced here: 74.6 us
  starting transfers between devices  32.7 us (44%)
  waiting for transfers between devices  22.7 us (30%)
  Pallas kernels  16 us (21%)
  between operations  2.08 us (3%)
  local copies, waits for them, and re-layouts  1.05 us (1%)
    pallas_call x12, Pallas kernels, call(): pl.pallas_call(kernel, out_shape=out_shape, in_specs=[vmem] * (len(args)...  16 us
    ppermute x1, waiting for transfers between devices, fast(): return (got, whole[0, 0] + lax.ppermute(whole, 'xh', SWAP)[0, 0])  8.68 us
    ppermute x3, starting transfers between devices, fast(): z_got = [lax.ppermute(s, 'z', ring(d)) for s, d in zip(z_send, HOPS)]  5.96 us
    ppermute x3, starting transfers between devices, fast(): x_last = [lax.ppermute(s, 'z', ring(d)) for s, d in zip(x_next, HOPS)]  5.52 us
    ppermute x3, starting transfers between devices, fast(): near = [rot_x] + [lax.ppermute(rot_x, 'y', ring(d)) for d in (1, 3, 2)]  5.3 us
    all_to_all x1, starting transfers between devices, fast(): got = lax.all_to_all(parts, ('xh', 'z', 'xl'), 0, 0, tiled=True)  5.23 us
    ppermute x3, waiting for transfers between devices, fast(): near = [rot_x] + [lax.ppermute(rot_x, 'y', ring(d)) for d in (1, 3, 2)]  4.47 us
    ppermute x1, starting transfers between devices, fast(): return (got, whole[0, 0] + lax.ppermute(whole, 'xh', SWAP)[0, 0])  3.43 us
  transfers between devices with their start and end apart: 23, of which 13 were waited for; matrix products, arithmetic and copies ran while one was open for 1% of the time, Pallas kernels for 12%

profile of v8, /device:TPU:0, one launch (start us, length us, event | category | flops | bytes accessed | tf_op | source)
XLA Modules:
  0.0 74.6 jit_solution(16079240095273252126)
XLA Ops:
  0.7 3.4 %grads_send.1 = s16[4,72,1024]{2,1,0:T(8,128)(2,1)S(1)} custom-call(s32[8,128]{1,0:T(8,128)} %bitcast.39, bf16[1024,512]{1,0:T(8,128)(2,1)} %g_ref.3, bf16[512,1024]{1,0:T(8,128)(2,1)} %b_ref.8), custom_call_target="tpu_custom_call" | custom-call | flops 10000000000 | tf_op jit(solution)/shard_map/grads_send/pallas_call | solution.py:256
  4.1 1.6 %collective-permute-start = (s16[4,72,1024]{2,1,0:T(8,128)(2,1)S(1)}, s16[4,72,1024]{2,1,0:T(8,128)(2,1)S(1)}, u32[]{:S(2)}, u32[]{:S(2)}) collective-permute-start(s16[4,72,1024]{2,1,0:T(8,128)(2,1)S(1)} %grads_send.1), channel_id=1, source_target_pairs={{0,1},{1,0},{2,3},{3,2},{4,5},{5,4},{6,7},{7,6},{8,9},{9,8},{10,11... | collective-permute-start | bytes 1769480 | tf_op jit(solution)/shard_map/ppermute | solution.py:286
  5.7 4.0 %acts_z.1 = (s16[2,72,768]{2,1,0:T(8,128)(2,1)S(1)}, s16[2,72,768]{2,1,0:T(8,128)(2,1)S(1)}, s16[2,72,768]{2,1,0:T(8,128)(2,1)S(1)}, bf16[432,1792]{1,0:T(8,128)(2,1)S(1)}, f32[8,128]{1,0:T(8,128)S(1)}) custom-call(s32[8,128]{1,0:T(8,128)S(1)} %bitcast.40, bf16[1024,1792]{1,0:T(8,128)(2,1)S(1)} %copy-done.1, bf16[1792,1024]{1,0:T(8,128)(2,1)S(1)} %copy-done), custom_call_target="tpu_custom_call" | custom-call | flops 4000000000 | tf_op jit(solution)/shard_map/acts_z/pallas_call | solution.py:256
  9.8 2.0 %collective-permute-start.12 = (s16[2,72,768]{2,1,0:T(8,128)(2,1)S(1)}, s16[2,72,768]{2,1,0:T(8,128)(2,1)S(1)}, u32[]{:S(2)}, u32[]{:S(2)}) collective-permute-start(s16[2,72,768]{2,1,0:T(8,128)(2,1)S(1)} %get-tuple-element.46), channel_id=1, source_target_pairs={{0,2},{2,4},{4,6},{6,0},{1,3},{3,5},{5,7},{7,1},{8,10},{10,12},{12... | collective-permute-start | bytes 663560 | tf_op jit(solution)/shard_map/ppermute | solution.py:297
  11.7 2.2 %collective-permute-start.13 = (s16[2,72,768]{2,1,0:T(8,128)(2,1)S(1)}, s16[2,72,768]{2,1,0:T(8,128)(2,1)S(1)}, u32[]{:S(2)}, u32[]{:S(2)}) collective-permute-start(s16[2,72,768]{2,1,0:T(8,128)(2,1)S(1)} %get-tuple-element.47), channel_id=1, source_target_pairs={{0,6},{2,0},{4,2},{6,4},{1,7},{3,1},{5,3},{7,5},{8,14},{10,8},{12,... | collective-permute-start | bytes 663560 | tf_op jit(solution)/shard_map/ppermute | solution.py:297
  14.0 1.8 %collective-permute-start.14 = (s16[2,72,768]{2,1,0:T(8,128)(2,1)S(1)}, s16[2,72,768]{2,1,0:T(8,128)(2,1)S(1)}, u32[]{:S(2)}, u32[]{:S(2)}) collective-permute-start(s16[2,72,768]{2,1,0:T(8,128)(2,1)S(1)} %get-tuple-element.48), channel_id=1, source_target_pairs={{0,4},{2,6},{4,0},{6,2},{1,5},{3,7},{5,1},{7,3},{8,12},{10,14},{12... | collective-permute-start | bytes 663560 | tf_op jit(solution)/shard_map/ppermute | solution.py:297
  15.7 1.4 %acts_x.1 = (s16[4,72,256]{2,1,0:T(8,128)(2,1)S(1)}, bf16[144,1792]{1,0:T(8,128)(2,1)S(1)}) custom-call(s32[8,128]{1,0:T(8,128)S(1)} %bitcast.41, bf16[1024,1792]{1,0:T(8,128)(2,1)S(1)} %copy-done.1, bf16[1792,1024]{1,0:T(8,128)(2,1)S(1)} %copy-done, bf16[432,1792]{1,0:T(8,128)(2,1)S(1)} %get-tuple-element.36.picked_ref), custom_call_target="tpu_custom_call" | custom-call | flops 1000000000 | tf_op jit(solution)/shard_map/acts_x/pallas_call | solution.py:256
  17.8 1.0 %grads_keep.1.g_keep = f32[288,1024]{1,0:T(8,128)S(1)} custom-call(s32[8,128]{1,0:T(8,128)S(1)} %bitcast.42, bf16[1024,512]{1,0:T(8,128)(2,1)S(1)} %copy-done.2, bf16[512,1024]{1,0:T(8,128)(2,1)S(1)} %copy-done.3, bf16[144,1792]{1,0:T(8,128)(2,1)S(1)} %get-tuple-element.37.after_ref.near_ref), custom_call_target="tpu_custom_call" | custom-call | flops 600000000 | tf_op jit(solution)/shard_map/grads_keep/pallas_call | solution.py:256
  18.8 1.0 %acts_keep.1 = (f32[2,72,768]{2,1,0:T(8,128)S(1)}, f32[288,256]{1,0:T(8,128)S(1)}) custom-call(bf16[432,1792]{1,0:T(8,128)(2,1)S(1)} %get-tuple-element.36.picked_ref, bf16[144,1792]{1,0:T(8,128)(2,1)S(1)} %get-tuple-element.37.after_ref.near_ref, bf16[1792,1024]{1,0:T(8,128)(2,1)S(1)} %copy-done), custom_call_target="tpu_custom_call" | custom-call | flops 1000000000 | tf_op jit(solution)/shard_map/acts_keep/pallas_call | solution.py:256
  19.8 2.6 %collective-permute-done.1.a_got = s16[4,72,256]{2,1,0:T(8,128)(2,1)S(1)} collective-permute-done((s16[4,72,256]{2,1,0:T(8,128)(2,1)S(1)}, s16[4,72,256]{2,1,0:T(8,128)(2,1)S(1)}, u32[]{:S(2)}, u32[]{:S(2)}) %collective-permute-start.1) | collective-permute-done | bytes 147488 | tf_op jit(solution)/shard_map/ppermute | solution.py:307
  22.4 1.1 %x_mid.1 = (f32[72,1280]{1,0:T(8,128)S(1)}, s16[72,1280]{1,0:T(8,128)(2,1)S(1)}, s16[72,1280]{1,0:T(8,128)(2,1)S(1)}, s16[72,1280]{1,0:T(8,128)(2,1)S(1)}) custom-call(f32[288,1024]{1,0:T(8,128)S(1)} %grads_keep.1.g_keep, s16[4,72,1024]{2,1,0:T(8,128)(2,1)S(1)} %collective-permute-done.g_got, f32[288,256]{1,0:T(8,128)S(1)} %get-tuple-element.38.a_keep, ...), custom_call_target="tpu_custom_call" | custom-call | tf_op jit(solution)/shard_map/x_mid/pallas_call | solution.py:256
  23.5 1.4 %collective-permute-done.14.r3_ref = s16[2,72,768]{2,1,0:T(8,128)(2,1)S(1)} collective-permute-done((s16[2,72,768]{2,1,0:T(8,128)(2,1)S(1)}, s16[2,72,768]{2,1,0:T(8,128)(2,1)S(1)}, u32[]{:S(2)}, u32[]{:S(2)}) %collective-permute-start.14) | collective-permute-done | bytes 221216 | tf_op jit(solution)/shard_map/ppermute | solution.py:297
  26.2 1.5 %collective-permute-start.2 = (s16[72,1280]{1,0:T(8,128)(2,1)S(1)}, s16[72,1280]{1,0:T(8,128)(2,1)S(1)}, u32[]{:S(2)}, u32[]{:S(2)}) collective-permute-start(s16[72,1280]{1,0:T(8,128)(2,1)S(1)} %get-tuple-element.41), channel_id=1, source_target_pairs={{0,2},{2,4},{4,6},{6,0},{1,3},{3,5},{5,7},{7,1},{8,10},{10,12},{12... | collective-permute-start | bytes 552968 | tf_op jit(solution)/shard_map/ppermute | solution.py:332
  27.7 2.1 %collective-permute-start.3 = (s16[72,1280]{1,0:T(8,128)(2,1)S(1)}, s16[72,1280]{1,0:T(8,128)(2,1)S(1)}, u32[]{:S(2)}, u32[]{:S(2)}) collective-permute-start(s16[72,1280]{1,0:T(8,128)(2,1)S(1)} %get-tuple-element.42), channel_id=1, source_target_pairs={{0,6},{2,0},{4,2},{6,4},{1,7},{3,1},{5,3},{7,5},{8,14},{10,8},{12,... | collective-permute-start | bytes 552968 | tf_op jit(solution)/shard_map/ppermute | solution.py:332
  29.9 1.8 %collective-permute-start.4 = (s16[72,1280]{1,0:T(8,128)(2,1)S(1)}, s16[72,1280]{1,0:T(8,128)(2,1)S(1)}, u32[]{:S(2)}, u32[]{:S(2)}) collective-permute-start(s16[72,1280]{1,0:T(8,128)(2,1)S(1)} %get-tuple-element.43), channel_id=1, source_target_pairs={{0,4},{2,6},{4,0},{6,2},{1,5},{3,7},{5,1},{7,3},{8,12},{10,14},{12... | collective-permute-start | bytes 552968 | tf_op jit(solution)/shard_map/ppermute | solution.py:332
  31.9 3.3 %collective-permute-start.17 = (bf16[72,768]{1,0:T(8,128)(2,1)S(1)}, bf16[72,768]{1,0:T(8,128)(2,1)S(1)}, u32[]{:S(2)}, u32[]{:S(2)}) collective-permute-start(bf16[72,768]{1,0:T(8,128)(2,1)S(1)} %z_end.1.own_ref.refs_8_), channel_id=1, source_target_pairs={{0,64},{32,96},{64,0},{96,32},{1,65},{33,97},{65,1},{97,33},{2,66}... | collective-permute-start | bytes 331784 | tf_op jit(solution)/shard_map/ppermute | solution.py:341
  35.2 0.7 %collective-permute-start.19 = (bf16[2,72,768]{2,1,0:T(8,128)(2,1)S(1)}, bf16[2,72,768]{2,1,0:T(8,128)(2,1)S(1)}, u32[]{:S(2)}, u32[]{:S(2)}) collective-permute-start(bf16[2,72,768]{2,1,0:T(8,128)(2,1)S(1)} %z_both.1), channel_id=1, source_target_pairs={{0,32},{8,104},{32,64},{40,8},{64,96},{72,40},{96,0},{104,72},{1,3... | collective-permute-start | bytes 663560 | tf_op jit(solution)/shard_map/ppermute | solution.py:343
  36.6 1.8 %collective-permute-done.4.r3_ref = s16[72,1280]{1,0:T(8,128)(2,1)S(1)} collective-permute-done((s16[72,1280]{1,0:T(8,128)(2,1)S(1)}, s16[72,1280]{1,0:T(8,128)(2,1)S(1)}, u32[]{:S(2)}, u32[]{:S(2)}) %collective-permute-start.4) | collective-permute-done | bytes 184352 | tf_op jit(solution)/shard_map/ppermute | solution.py:332
  38.9 3.3 %collective-permute-start.10 = (bf16[72,1280]{1,0:T(8,128)(2,1)S(1)}, bf16[72,1280]{1,0:T(8,128)(2,1)S(1)}, u32[]{:S(2)}, u32[]{:S(2)}) collective-permute-start(bf16[72,1280]{1,0:T(8,128)(2,1)S(1)} %x_end.1.refs_0_), channel_id=1, source_target_pairs={{0,64},{32,96},{64,0},{96,32},{1,65},{33,97},{65,1},{97,33},{2,66}... | collective-permute-start | bytes 552968 | tf_op jit(solution)/shard_map/ppermute | solution.py:346
  42.2 1.1 %collective-permute-start.8 = (bf16[72,1280]{1,0:T(8,128)(2,1)S(1)}, bf16[72,1280]{1,0:T(8,128)(2,1)S(1)}, u32[]{:S(2)}, u32[]{:S(2)}) collective-permute-start(bf16[72,1280]{1,0:T(8,128)(2,1)S(1)} %x_end.1.refs_0_), channel_id=1, source_target_pairs={{0,96},{32,0},{64,32},{96,64},{1,97},{33,1},{65,33},{97,65},{2,98}... | collective-permute-start | bytes 552968 | tf_op jit(solution)/shard_map/ppermute | solution.py:346
  43.3 1.0 %collective-permute-start.6 = (bf16[72,1280]{1,0:T(8,128)(2,1)S(1)}, bf16[72,1280]{1,0:T(8,128)(2,1)S(1)}, u32[]{:S(2)}, u32[]{:S(2)}) collective-permute-start(bf16[72,1280]{1,0:T(8,128)(2,1)S(1)} %x_end.1.refs_0_), channel_id=1, source_target_pairs={{0,32},{32,64},{64,96},{96,0},{1,33},{33,65},{65,97},{97,1},{2,34}... | collective-permute-start | bytes 552968 | tf_op jit(solution)/shard_map/ppermute | solution.py:346
  44.2 1.1 %collective-permute-done.19.refs_12_ = bf16[2,72,768]{2,1,0:T(8,128)(2,1)S(1)} collective-permute-done((bf16[2,72,768]{2,1,0:T(8,128)(2,1)S(1)}, bf16[2,72,768]{2,1,0:T(8,128)(2,1)S(1)}, u32[]{:S(2)}, u32[]{:S(2)}) %collective-permute-start.19) | collective-permute-done | bytes 221216 | tf_op jit(solution)/shard_map/ppermute | solution.py:343
  45.8 1.9 %collective-permute-done.10.refs_6_ = bf16[72,1280]{1,0:T(8,128)(2,1)S(1)} collective-permute-done((bf16[72,1280]{1,0:T(8,128)(2,1)S(1)}, bf16[72,1280]{1,0:T(8,128)(2,1)S(1)}, u32[]{:S(2)}, u32[]{:S(2)}) %collective-permute-start.10) | collective-permute-done | bytes 184352 | tf_op jit(solution)/shard_map/ppermute | solution.py:346
  47.7 1.8 %collective-permute-done.8.refs_4_ = bf16[72,1280]{1,0:T(8,128)(2,1)S(1)} collective-permute-done((bf16[72,1280]{1,0:T(8,128)(2,1)S(1)}, bf16[72,1280]{1,0:T(8,128)(2,1)S(1)}, u32[]{:S(2)}, u32[]{:S(2)}) %collective-permute-start.8) | collective-permute-done | bytes 184352 | tf_op jit(solution)/shard_map/ppermute | solution.py:346
  49.5 0.8 %collective-permute-done.6.refs_2_ = bf16[72,1280]{1,0:T(8,128)(2,1)S(1)} collective-permute-done((bf16[72,1280]{1,0:T(8,128)(2,1)S(1)}, bf16[72,1280]{1,0:T(8,128)(2,1)S(1)}, u32[]{:S(2)}, u32[]{:S(2)}) %collective-permute-start.6) | collective-permute-done | bytes 184352 | tf_op jit(solution)/shard_map/ppermute | solution.py:346
  51.0 0.8 %collective-permute-done.7.refs_3_ = bf16[72,1280]{1,0:T(8,128)(2,1)S(1)} collective-permute-done((bf16[72,1280]{1,0:T(8,128)(2,1)S(1)}, bf16[72,1280]{1,0:T(8,128)(2,1)S(1)}, u32[]{:S(2)}, u32[]{:S(2)}) %collective-permute-start.7) | collective-permute-done | bytes 184352 | tf_op jit(solution)/shard_map/ppermute | solution.py:337
  51.7 2.1 %gram.1 = (bf16[16,64,384]{2,1,0:T(8,128)(2,1)}, f32[8,128]{1,0:T(8,128)S(1)}) custom-call(bf16[72,1280]{1,0:T(8,128)(2,1)S(1)} %x_end.1.refs_0_, bf16[72,1280]{1,0:T(8,128)(2,1)S(1)} %collective-permute-done.5.refs_1_, bf16[72,1280]{1,0:T(8,128)(2,1)S(1)} %collective-permute-done.6.refs_2_, bf16[72,1280]{1,0:T(8,128)(2,1)S(1)} %collective-permute-done.7.refs_3_, ...), custom_call_target="tpu_custom_call" | custom-call | flops 600000000 | tf_op jit(solution)/shard_map/gram/pallas_call | solution.py:256
  53.9 5.2 %all-to-all-start.5 = ((bf16[16,64,384]{2,1,0:T(8,128)(2,1)}), bf16[16,64,384]{2,1,0:T(8,128)(2,1)S(1)}, u32[]{:S(2)}, u32[]{:S(2)}) async-start(bf16[16,64,384]{2,1,0:T(8,128)(2,1)} %get-tuple-element.52), calls=%async_computation.5 | async-start | bytes 1572864 | tf_op jit(solution)/shard_map/all_to_all | solution.py:358
  59.1 3.4 %collective-permute-start.21 = (f32[8,128]{1,0:T(8,128)S(1)}, f32[8,128]{1,0:T(8,128)S(1)}, u32[]{:S(2)}, u32[]{:S(2)}) collective-permute-start(f32[8,128]{1,0:T(8,128)S(1)} %get-tuple-element.51), channel_id=1, source_target_pairs={{0,16},{16,0},{1,17},{17,1},{2,18},{18,2},{3,19},{19,3},{4,20},{20... | collective-permute-start | bytes 12296 | tf_op jit(solution)/shard_map/ppermute | solution.py:359
  63.1 8.7 %collective-permute-done.21 = f32[8,128]{1,0:T(8,128)S(1)} collective-permute-done((f32[8,128]{1,0:T(8,128)S(1)}, f32[8,128]{1,0:T(8,128)S(1)}, u32[]{:S(2)}, u32[]{:S(2)}) %collective-permute-start.21) | collective-permute-done | bytes 4128 | tf_op jit(solution)/shard_map/ppermute | solution.py:359
  73.8 0.8 %conditional.1 = ((f32[64,128]{1,0:T(8,128)}, f32[64,128]{1,0:T(8,128)}, f32[64,128]{1,0:T(8,128)})) conditional(s32[]{:T(128)} %bitcast.9, (bf16[1024,1792]{1,0:T(8,128)(2,1)}, bf16[1792,1024]{1,0:T(8,128)(2,1)}, s32[1024]{0:T(1024)S(1)}, bf16[1024,512]{1,0:T(8,128)(2,1)S(1)}, bf16[512,1024]{1,0:T(8,128)(2,1)S(1)}) %tuple.27, ...), branch_computations={%region_0.0_spmd, %region_6.0_spmd} | conditional | flops 5646950400 | bytes 166300480 | solution.py:396
  73.8 0.7 final.1
  (39 shorter events, 5.7 us)
Async XLA Ops:
  0.6 5.1 %copy-start = (bf16[1792,1024]{1,0:T(8,128)(2,1)S(1)}, bf16[1792,1024]{1,0:T(8,128)(2,1)}, u32[]{:S(2)}) copy-start(bf16[1792,1024]{1,0:T(8,128)(2,1)} %b_ref.9) | copy-start | bytes 11010052
  0.6 5.1 %copy-start.1 = (bf16[1024,1792]{1,0:T(8,128)(2,1)S(1)}, bf16[1024,1792]{1,0:T(8,128)(2,1)}, u32[]{:S(2)}) copy-start(bf16[1024,1792]{1,0:T(8,128)(2,1)} %h_ref.3) | copy-start | bytes 11010052
  0.7 5.1 %copy-start.4 = (s32[1024]{0:T(1024)S(1)}, s32[1024]{0:T(1024)}, u32[]{:S(2)}) copy-start(s32[1024]{0:T(1024)} %param.11) | copy-start | bytes 12292
  4.1 18.3 %collective-permute-start = (s16[4,72,1024]{2,1,0:T(8,128)(2,1)S(1)}, s16[4,72,1024]{2,1,0:T(8,128)(2,1)S(1)}, u32[]{:S(2)}, u32[]{:S(2)}) collective-permute-start(s16[4,72,1024]{2,1,0:T(8,128)(2,1)S(1)} %grads_send.1), channel_id=1, source_target_pairs={{0,1},{1,0},{2,3},{3,2},{4,5},{5,4},{6,7},{7,6},{8,9},{9,8},{10,11... | collective-permute-start | bytes 1769480 | tf_op jit(solution)/shard_map/ppermute | solution.py:286
  9.8 13.7 %collective-permute-start.12 = (s16[2,72,768]{2,1,0:T(8,128)(2,1)S(1)}, s16[2,72,768]{2,1,0:T(8,128)(2,1)S(1)}, u32[]{:S(2)}, u32[]{:S(2)}) collective-permute-start(s16[2,72,768]{2,1,0:T(8,128)(2,1)S(1)} %get-tuple-element.46), channel_id=1, source_target_pairs={{0,2},{2,4},{4,6},{6,0},{1,3},{3,5},{5,7},{7,1},{8,10},{10,12},{12... | collective-permute-start | bytes 663560 | tf_op jit(solution)/shard_map/ppermute | solution.py:297
  11.7 11.8 %collective-permute-start.13 = (s16[2,72,768]{2,1,0:T(8,128)(2,1)S(1)}, s16[2,72,768]{2,1,0:T(8,128)(2,1)S(1)}, u32[]{:S(2)}, u32[]{:S(2)}) collective-permute-start(s16[2,72,768]{2,1,0:T(8,128)(2,1)S(1)} %get-tuple-element.47), channel_id=1, source_target_pairs={{0,6},{2,0},{4,2},{6,4},{1,7},{3,1},{5,3},{7,5},{8,14},{10,8},{12,... | collective-permute-start | bytes 663560 | tf_op jit(solution)/shard_map/ppermute | solution.py:297
  14.0 11.0 %collective-permute-start.14 = (s16[2,72,768]{2,1,0:T(8,128)(2,1)S(1)}, s16[2,72,768]{2,1,0:T(8,128)(2,1)S(1)}, u32[]{:S(2)}, u32[]{:S(2)}) collective-permute-start(s16[2,72,768]{2,1,0:T(8,128)(2,1)S(1)} %get-tuple-element.48), channel_id=1, source_target_pairs={{0,4},{2,6},{4,0},{6,2},{1,5},{3,7},{5,1},{7,3},{8,12},{10,14},{12... | collective-permute-start | bytes 663560 | tf_op jit(solution)/shard_map/ppermute | solution.py:297
  15.7 2.0 %copy-start.2 = (bf16[1024,512]{1,0:T(8,128)(2,1)S(1)}, bf16[1024,512]{1,0:T(8,128)(2,1)}, u32[]{:S(2)}) copy-start(bf16[1024,512]{1,0:T(8,128)(2,1)} %g_ref.3) | copy-start | bytes 3145732
  15.7 2.0 %copy-start.3 = (bf16[512,1024]{1,0:T(8,128)(2,1)S(1)}, bf16[512,1024]{1,0:T(8,128)(2,1)}, u32[]{:S(2)}) copy-start(bf16[512,1024]{1,0:T(8,128)(2,1)} %b_ref.8) | copy-start | bytes 3145732
  17.2 5.2 %collective-permute-start.1 = (s16[4,72,256]{2,1,0:T(8,128)(2,1)S(1)}, s16[4,72,256]{2,1,0:T(8,128)(2,1)S(1)}, u32[]{:S(2)}, u32[]{:S(2)}) collective-permute-start(s16[4,72,256]{2,1,0:T(8,128)(2,1)S(1)} %get-tuple-element.39), channel_id=1, source_target_pairs={{0,1},{1,0},{2,3},{3,2},{4,5},{5,4},{6,7},{7,6},{8,9},{9,8},{10,11... | collective-permute-start | bytes 442376 | tf_op jit(solution)/shard_map/ppermute | solution.py:307
  25.6 6.1 %collective-permute-start.15 = (s16[72,768]{1,0:T(8,128)(2,1)S(1)}, s16[72,768]{1,0:T(8,128)(2,1)S(1)}, u32[]{:S(2)}, u32[]{:S(2)}) collective-permute-start(s16[72,768]{1,0:T(8,128)(2,1)S(1)} %get-tuple-element.50), channel_id=1, source_target_pairs={{0,1},{1,0},{2,3},{3,2},{4,5},{5,4},{6,7},{7,6},{8,9},{9,8},{10,11... | collective-permute-start | bytes 331784 | tf_op jit(solution)/shard_map/ppermute | solution.py:334
  26.2 9.8 %collective-permute-start.2 = (s16[72,1280]{1,0:T(8,128)(2,1)S(1)}, s16[72,1280]{1,0:T(8,128)(2,1)S(1)}, u32[]{:S(2)}, u32[]{:S(2)}) collective-permute-start(s16[72,1280]{1,0:T(8,128)(2,1)S(1)} %get-tuple-element.41), channel_id=1, source_target_pairs={{0,2},{2,4},{4,6},{6,0},{1,3},{3,5},{5,7},{7,1},{8,10},{10,12},{12... | collective-permute-start | bytes 552968 | tf_op jit(solution)/shard_map/ppermute | solution.py:332
  27.7 8.9 %collective-permute-start.3 = (s16[72,1280]{1,0:T(8,128)(2,1)S(1)}, s16[72,1280]{1,0:T(8,128)(2,1)S(1)}, u32[]{:S(2)}, u32[]{:S(2)}) collective-permute-start(s16[72,1280]{1,0:T(8,128)(2,1)S(1)} %get-tuple-element.42), channel_id=1, source_target_pairs={{0,6},{2,0},{4,2},{6,4},{1,7},{3,1},{5,3},{7,5},{8,14},{10,8},{12,... | collective-permute-start | bytes 552968 | tf_op jit(solution)/shard_map/ppermute | solution.py:332
  29.9 8.6 %collective-permute-start.4 = (s16[72,1280]{1,0:T(8,128)(2,1)S(1)}, s16[72,1280]{1,0:T(8,128)(2,1)S(1)}, u32[]{:S(2)}, u32[]{:S(2)}) collective-permute-start(s16[72,1280]{1,0:T(8,128)(2,1)S(1)} %get-tuple-element.43), channel_id=1, source_target_pairs={{0,4},{2,6},{4,0},{6,2},{1,5},{3,7},{5,1},{7,3},{8,12},{10,14},{12... | collective-permute-start | bytes 552968 | tf_op jit(solution)/shard_map/ppermute | solution.py:332
  31.8 3.4 %collective-permute-start.16 = (bf16[72,768]{1,0:T(8,128)(2,1)S(1)}, bf16[72,768]{1,0:T(8,128)(2,1)S(1)}, u32[]{:S(2)}, u32[]{:S(2)}) collective-permute-start(bf16[72,768]{1,0:T(8,128)(2,1)S(1)} %z_end.1.own_ref.refs_8_), channel_id=1, source_target_pairs={{0,8},{8,0},{1,9},{9,1},{2,10},{10,2},{3,11},{11,3},{4,12},{12,4},... | collective-permute-start | bytes 331784 | tf_op jit(solution)/shard_map/ppermute | solution.py:337
  31.9 12.4 %collective-permute-start.17 = (bf16[72,768]{1,0:T(8,128)(2,1)S(1)}, bf16[72,768]{1,0:T(8,128)(2,1)S(1)}, u32[]{:S(2)}, u32[]{:S(2)}) collective-permute-start(bf16[72,768]{1,0:T(8,128)(2,1)S(1)} %z_end.1.own_ref.refs_8_), channel_id=1, source_target_pairs={{0,64},{32,96},{64,0},{96,32},{1,65},{33,97},{65,1},{97,33},{2,66}... | collective-permute-start | bytes 331784 | tf_op jit(solution)/shard_map/ppermute | solution.py:341
  35.2 10.1 %collective-permute-start.19 = (bf16[2,72,768]{2,1,0:T(8,128)(2,1)S(1)}, bf16[2,72,768]{2,1,0:T(8,128)(2,1)S(1)}, u32[]{:S(2)}, u32[]{:S(2)}) collective-permute-start(bf16[2,72,768]{2,1,0:T(8,128)(2,1)S(1)} %z_both.1), channel_id=1, source_target_pairs={{0,32},{8,104},{32,64},{40,8},{64,96},{72,40},{96,0},{104,72},{1,3... | collective-permute-start | bytes 663560 | tf_op jit(solution)/shard_map/ppermute | solution.py:343
  38.9 8.8 %collective-permute-start.10 = (bf16[72,1280]{1,0:T(8,128)(2,1)S(1)}, bf16[72,1280]{1,0:T(8,128)(2,1)S(1)}, u32[]{:S(2)}, u32[]{:S(2)}) collective-permute-start(bf16[72,1280]{1,0:T(8,128)(2,1)S(1)} %x_end.1.refs_0_), channel_id=1, source_target_pairs={{0,64},{32,96},{64,0},{96,32},{1,65},{33,97},{65,1},{97,33},{2,66}... | collective-permute-start | bytes 552968 | tf_op jit(solution)/shard_map/ppermute | solution.py:346
  42.2 7.3 %collective-permute-start.8 = (bf16[72,1280]{1,0:T(8,128)(2,1)S(1)}, bf16[72,1280]{1,0:T(8,128)(2,1)S(1)}, u32[]{:S(2)}, u32[]{:S(2)}) collective-permute-start(bf16[72,1280]{1,0:T(8,128)(2,1)S(1)} %x_end.1.refs_0_), channel_id=1, source_target_pairs={{0,96},{32,0},{64,32},{96,64},{1,97},{33,1},{65,33},{97,65},{2,98}... | collective-permute-start | bytes 552968 | tf_op jit(solution)/shard_map/ppermute | solution.py:346
  43.3 7.1 %collective-permute-start.6 = (bf16[72,1280]{1,0:T(8,128)(2,1)S(1)}, bf16[72,1280]{1,0:T(8,128)(2,1)S(1)}, u32[]{:S(2)}, u32[]{:S(2)}) collective-permute-start(bf16[72,1280]{1,0:T(8,128)(2,1)S(1)} %x_end.1.refs_0_), channel_id=1, source_target_pairs={{0,32},{32,64},{64,96},{96,0},{1,33},{33,65},{65,97},{97,1},{2,34}... | collective-permute-start | bytes 552968 | tf_op jit(solution)/shard_map/ppermute | solution.py:346
  44.2 1.3 %collective-permute-start.18 = (bf16[72,768]{1,0:T(8,128)(2,1)S(1)}, bf16[72,768]{1,0:T(8,128)(2,1)S(1)}, u32[]{:S(2)}, u32[]{:S(2)}) collective-permute-start(bf16[72,768]{1,0:T(8,128)(2,1)S(1)} %collective-permute-done.17.refs_10_), channel_id=1, source_target_pairs={{0,8},{8,0},{1,9},{9,1},{2,10},{10,2},{3,11},{11,3},{4,12},{12,4},... | collective-permute-start | bytes 331784 | tf_op jit(solution)/shard_map/ppermute | solution.py:337
  45.3 6.4 %collective-permute-start.20 = (bf16[2,72,768]{2,1,0:T(8,128)(2,1)S(1)}, bf16[2,72,768]{2,1,0:T(8,128)(2,1)S(1)}, u32[]{:S(2)}, u32[]{:S(2)}) collective-permute-start(bf16[2,72,768]{2,1,0:T(8,128)(2,1)S(1)} %collective-permute-done.19.refs_12_), channel_id=1, source_target_pairs={{0,8},{8,0},{1,9},{9,1},{2,10},{10,2},{3,11},{11,3},{4,12},{12,4},... | collective-permute-start | bytes 663560 | tf_op jit(solution)/shard_map/ppermute | solution.py:337
  45.6 4.8 %collective-permute-start.5 = (bf16[72,1280]{1,0:T(8,128)(2,1)S(1)}, bf16[72,1280]{1,0:T(8,128)(2,1)S(1)}, u32[]{:S(2)}, u32[]{:S(2)}) collective-permute-start(bf16[72,1280]{1,0:T(8,128)(2,1)S(1)} %x_end.1.refs_0_), channel_id=1, source_target_pairs={{0,8},{8,0},{1,9},{9,1},{2,10},{10,2},{3,11},{11,3},{4,12},{12,4},... | collective-permute-start | bytes 552968 | tf_op jit(solution)/shard_map/ppermute | solution.py:337
  47.7 2.6 %collective-permute-start.11 = (bf16[72,1280]{1,0:T(8,128)(2,1)S(1)}, bf16[72,1280]{1,0:T(8,128)(2,1)S(1)}, u32[]{:S(2)}, u32[]{:S(2)}) collective-permute-start(bf16[72,1280]{1,0:T(8,128)(2,1)S(1)} %collective-permute-done.10.refs_6_), channel_id=1, source_target_pairs={{0,8},{8,0},{1,9},{9,1},{2,10},{10,2},{3,11},{11,3},{4,12},{12,4},... | collective-permute-start | bytes 552968 | tf_op jit(solution)/shard_map/ppermute | solution.py:337
  49.5 1.4 %collective-permute-start.9 = (bf16[72,1280]{1,0:T(8,128)(2,1)S(1)}, bf16[72,1280]{1,0:T(8,128)(2,1)S(1)}, u32[]{:S(2)}, u32[]{:S(2)}) collective-permute-start(bf16[72,1280]{1,0:T(8,128)(2,1)S(1)} %collective-permute-done.8.refs_4_), channel_id=1, source_target_pairs={{0,8},{8,0},{1,9},{9,1},{2,10},{10,2},{3,11},{11,3},{4,12},{12,4},... | collective-permute-start | bytes 552968 | tf_op jit(solution)/shard_map/ppermute | solution.py:337
  50.3 1.4 %collective-permute-start.7 = (bf16[72,1280]{1,0:T(8,128)(2,1)S(1)}, bf16[72,1280]{1,0:T(8,128)(2,1)S(1)}, u32[]{:S(2)}, u32[]{:S(2)}) collective-permute-start(bf16[72,1280]{1,0:T(8,128)(2,1)S(1)} %collective-permute-done.6.refs_2_), channel_id=1, source_target_pairs={{0,8},{8,0},{1,9},{9,1},{2,10},{10,2},{3,11},{11,3},{4,12},{12,4},... | collective-permute-start | bytes 552968 | tf_op jit(solution)/shard_map/ppermute | solution.py:337
  53.9 19.9 %all-to-all-start.5 = ((bf16[16,64,384]{2,1,0:T(8,128)(2,1)}), bf16[16,64,384]{2,1,0:T(8,128)(2,1)S(1)}, u32[]{:S(2)}, u32[]{:S(2)}) async-start(bf16[16,64,384]{2,1,0:T(8,128)(2,1)} %get-tuple-element.52), calls=%async_computation.5 | async-start | bytes 1572864 | tf_op jit(solution)/shard_map/all_to_all | solution.py:358
  59.1 12.6 %collective-permute-start.21 = (f32[8,128]{1,0:T(8,128)S(1)}, f32[8,128]{1,0:T(8,128)S(1)}, u32[]{:S(2)}, u32[]{:S(2)}) collective-permute-start(f32[8,128]{1,0:T(8,128)S(1)} %get-tuple-element.51), channel_id=1, source_target_pairs={{0,16},{16,0},{1,17},{17,1},{2,18},{18,2},{3,19},{19,3},{4,20},{20... | collective-permute-start | bytes 12296 | tf_op jit(solution)/shard_map/ppermute | solution.py:359

commit v9 on v8

--- a/solution.py
+++ b/solution.py
@@ -215,26 +215,40 @@
             out_ref[xh * 8 + cb, :, n * 128 : (n + 1) * 128] = t[xh * 64 : (xh + 1) * 64, cb * 128 : (cb + 1) * 128]
 
 
-def gram_kernel(scale, *refs):
-    x_refs, z_refs = refs[:8], list(refs[8:12]) + [ref.at[n] for ref in refs[12:14] for n in range(2)]
-    out_ref, whole_ref, a_s, g_s = refs[14:]
-    core = lax.axis_index("core")
-    places = (0, 1, 4 + 3 * core, 5 + core, 7 - 3 * core, 6 - core, 2, 3)
+def marks_of(x_refs):
     marks = x_refs[0][0:8, 0:128].astype(F32)
     for ref in x_refs[1:]:
         marks = marks + ref[0:8, 0:128].astype(F32)
-    whole_ref[...] = jnp.where(jnp.abs(marks) < 1e30, 1.0, 0.0)
+    return marks
+
+
+def terms(scale, a_s, g_s):
+    own = own_columns(a_s)
+    for lhs, rhs in ((own, a_s[...]), (own_columns(g_s), g_s[...]), (square(own), square(g_s[...]))):
+        yield lax.dot_general(lhs, rhs, CONTRACT, preferred_element_type=F32) * scale
+
+
+def near_kernel(scale, *refs):
+    x_refs, z_refs = refs[:6], list(refs[6:8]) + [ref.at[n] for ref in refs[8:10] for n in range(2)]
+    sum_ref, mark_ref, a_s, g_s = refs[10:]
+    core = lax.axis_index("core")
+    places = (0, 1, 2 + 3 * core, 3 + core, 5 - 3 * core, 4 - core)
+    mark_ref[...] = marks_of(x_refs)
     gather_rows(g_s, slice(0, WIDTH), x_refs, slice(0, WIDTH), places)
     gather_rows(a_s, slice(AZ, WIDTH), x_refs, slice(WIDTH, WIDTH + AX), places)
     gather_rows(a_s, slice(0, AZ), z_refs, slice(0, AZ))
-
-    def dot(lhs, rhs):
-        return (lax.dot_general(lhs, rhs, CONTRACT, preferred_element_type=F32) * scale).astype(BF)
-
-    own = own_columns(a_s)
-    put(out_ref, 1, dot(own_columns(g_s), g_s[...]))
-    put(out_ref, 0, dot(own, a_s[...]))
-    put(out_ref, 2, dot(square(own), square(g_s[...])))
+    for n, t in enumerate(terms(scale, a_s, g_s)):
+        sum_ref[n] = t
+
+
+def gram_kernel(scale, *refs):
+    x_refs, z_refs, (sum_ref, mark_ref, out_ref, whole_ref, a_s, g_s) = refs[:2], refs[2:4], refs[4:]
+    whole_ref[...] = jnp.where(jnp.abs(mark_ref[...] + marks_of(x_refs)) < 1e30, 1.0, 0.0)
+    gather_rows(g_s, slice(0, WIDTH), x_refs, slice(0, WIDTH))
+    gather_rows(a_s, slice(AZ, WIDTH), x_refs, slice(WIDTH, WIDTH + AX))
+    gather_rows(a_s, slice(0, AZ), z_refs, slice(0, AZ))
+    for n, t in enumerate(terms(scale, a_s, g_s)):
+        put(out_ref, n, (sum_ref[n] + t).astype(BF))
 
 
 def final_kernel(in_ref, a_ref, g_ref, c_ref):
@@ -346,14 +360,24 @@
     near = [rot_x] + [lax.ppermute(rot_x, "y", ring(d)) for d in (1, 3, 2)]
     all_x = [r for n in near for r in (n, over(n))]
 
-    rows = pltpu.VMEM((GATHERED * PAD, WIDTH), BF)
+    def rows(n):
+        return pltpu.VMEM((n * PAD, WIDTH), BF)
+
+    sums, mark = call(
+        lambda *refs: near_kernel(scale, *refs),
+        "near",
+        (sds((3, 128, WIDTH), F32), sds((8, 128), F32)),
+        (*all_x[:6], *all_z[:2], *all_z[4:]),
+        (rows(6), rows(6)),
+        flops=500_000_000,
+    )
     parts, whole = call(
         lambda *refs: gram_kernel(scale, *refs),
         "gram",
         (sds((16, 64, 384), BF), sds((8, 128), F32)),
-        (*all_x, *all_z),
-        (rows, rows),
-        flops=600_000_000,
+        (*all_x[6:], *all_z[2:4], sums, mark),
+        (rows(2), rows(2)),
+        flops=200_000_000,
     )
     got = lax.all_to_all(parts, ("xh", "z", "xl"), 0, 0, tiled=True)
     return got, whole[0, 0] + lax.ppermute(whole, "xh", SWAP)[0, 0]

time: 74.8 us -> 78.7 us (1.052)
  waiting for transfers between devices: 22.7 us -> 25.9 us
    ppermute x1, waiting for transfers between devices: 0.01 us -> 4.82 us  [fast(): z_far = lax.ppermute(rot_z, 'y', ring(2))]
    ppermute x3, waiting for transfers between devices: 4.47 us -> 2.39 us  [fast(): near = [rot_x] + [lax.ppermute(rot_x, 'y', ring(d)) for d in (1, 3, 2)]]
    ppermute x1, starting transfers between devices: 3.29 us -> 2.2 us  [fast(): z_far = lax.ppermute(rot_z, 'y', ring(2))]
    ppermute x3, waiting for transfers between devices: 2.53 us -> 3.61 us  [fast(): x_last = [lax.ppermute(s, 'z', ring(d)) for s, d in zip(x_next, HOPS)]]
    ppermute x1, waiting for transfers between devices: 1.08 us -> 0.01 us  [fast(): z_side = lax.ppermute(z_both, ('y', 'core'), SIDES)]
    ppermute x1, starting transfers between devices: 0.75 us -> 1.65 us  [fast(): z_side = lax.ppermute(z_both, ('y', 'core'), SIDES)]
    ppermute x3, starting transfers between devices: 5.3 us -> 4.41 us  [fast(): near = [rot_x] + [lax.ppermute(rot_x, 'y', ring(d)) for d in (1, 3, 2)]]
    ppermute x7, starting transfers between devices: 0.37 us -> 1.19 us  [over(): return lax.ppermute(r, 'core', SWAP)]
  transfers between devices with their start and end apart: 23 -> 23, of which waited for: 13 -> 11; matrix products, arithmetic and copies ran while one was open for 1% -> 1% of each run, Pallas kernels for 12% -> 13%
where the time goes in v9:
time: 78.7 us; the launch traced here: 78.5 us
  starting transfers between devices  33 us (42%)
  waiting for transfers between devices  25.9 us (33%)
  Pallas kernels  16.3 us (21%)
  between operations  2.1 us (3%)
  local copies, waits for them, and re-layouts  1.05 us (1%)
    pallas_call x13, Pallas kernels, call(): pl.pallas_call(kernel, out_shape=out_shape, in_specs=[vmem] * (len(args)...  16.3 us
    ppermute x1, waiting for transfers between devices, fast(): return (got, whole[0, 0] + lax.ppermute(whole, 'xh', SWAP)[0, 0])  8.68 us
    ppermute x3, starting transfers between devices, fast(): z_got = [lax.ppermute(s, 'z', ring(d)) for s, d in zip(z_send, HOPS)]  5.96 us
    all_to_all x1, starting transfers between devices, fast(): got = lax.all_to_all(parts, ('xh', 'z', 'xl'), 0, 0, tiled=True)  5.77 us
    ppermute x3, starting transfers between devices, fast(): x_last = [lax.ppermute(s, 'z', ring(d)) for s, d in zip(x_next, HOPS)]  5.51 us
    ppermute x1, waiting for transfers between devices, fast(): z_far = lax.ppermute(rot_z, 'y', ring(2))  4.82 us
    ppermute x3, starting transfers between devices, fast(): near = [rot_x] + [lax.ppermute(rot_x, 'y', ring(d)) for d in (1, 3, 2)]  4.41 us
    ppermute x3, waiting for transfers between devices, fast(): x_last = [lax.ppermute(s, 'z', ring(d)) for s, d in zip(x_next, HOPS)]  3.61 us
  transfers between devices with their start and end apart: 23, of which 11 were waited for; matrix products, arithmetic and copies ran while one was open for 1% of the time, Pallas kernels for 13%

profile of v9, /device:TPU:0, one launch (start us, length us, event | category | flops | bytes accessed | tf_op | source)
XLA Modules:
  0.0 78.5 jit_solution(2479413115220633248)
XLA Ops:
  0.7 3.4 %grads_send.1 = s16[4,72,1024]{2,1,0:T(8,128)(2,1)S(1)} custom-call(s32[8,128]{1,0:T(8,128)} %bitcast.39, bf16[1024,512]{1,0:T(8,128)(2,1)} %g_ref.3, bf16[512,1024]{1,0:T(8,128)(2,1)} %b_ref.8), custom_call_target="tpu_custom_call" | custom-call | flops 10000000000 | tf_op jit(solution)/shard_map/grads_send/pallas_call | solution.py:270
  4.1 1.6 %collective-permute-start = (s16[4,72,1024]{2,1,0:T(8,128)(2,1)S(1)}, s16[4,72,1024]{2,1,0:T(8,128)(2,1)S(1)}, u32[]{:S(2)}, u32[]{:S(2)}) collective-permute-start(s16[4,72,1024]{2,1,0:T(8,128)(2,1)S(1)} %grads_send.1), channel_id=1, source_target_pairs={{0,1},{1,0},{2,3},{3,2},{4,5},{5,4},{6,7},{7,6},{8,9},{9,8},{10,11... | collective-permute-start | bytes 1769480 | tf_op jit(solution)/shard_map/ppermute | solution.py:300
  5.7 4.0 %acts_z.1 = (s16[2,72,768]{2,1,0:T(8,128)(2,1)S(1)}, s16[2,72,768]{2,1,0:T(8,128)(2,1)S(1)}, s16[2,72,768]{2,1,0:T(8,128)(2,1)S(1)}, bf16[432,1792]{1,0:T(8,128)(2,1)S(1)}, f32[8,128]{1,0:T(8,128)S(1)}) custom-call(s32[8,128]{1,0:T(8,128)S(1)} %bitcast.40, bf16[1024,1792]{1,0:T(8,128)(2,1)S(1)} %copy-done.1, bf16[1792,1024]{1,0:T(8,128)(2,1)S(1)} %copy-done), custom_call_target="tpu_custom_call" | custom-call | flops 4000000000 | tf_op jit(solution)/shard_map/acts_z/pallas_call | solution.py:270
  9.8 2.0 %collective-permute-start.7 = (s16[2,72,768]{2,1,0:T(8,128)(2,1)S(1)}, s16[2,72,768]{2,1,0:T(8,128)(2,1)S(1)}, u32[]{:S(2)}, u32[]{:S(2)}) collective-permute-start(s16[2,72,768]{2,1,0:T(8,128)(2,1)S(1)} %get-tuple-element.48), channel_id=1, source_target_pairs={{0,2},{2,4},{4,6},{6,0},{1,3},{3,5},{5,7},{7,1},{8,10},{10,12},{12... | collective-permute-start | bytes 663560 | tf_op jit(solution)/shard_map/ppermute | solution.py:311
  11.7 2.2 %collective-permute-start.8 = (s16[2,72,768]{2,1,0:T(8,128)(2,1)S(1)}, s16[2,72,768]{2,1,0:T(8,128)(2,1)S(1)}, u32[]{:S(2)}, u32[]{:S(2)}) collective-permute-start(s16[2,72,768]{2,1,0:T(8,128)(2,1)S(1)} %get-tuple-element.49), channel_id=1, source_target_pairs={{0,6},{2,0},{4,2},{6,4},{1,7},{3,1},{5,3},{7,5},{8,14},{10,8},{12,... | collective-permute-start | bytes 663560 | tf_op jit(solution)/shard_map/ppermute | solution.py:311
  14.0 1.8 %collective-permute-start.9 = (s16[2,72,768]{2,1,0:T(8,128)(2,1)S(1)}, s16[2,72,768]{2,1,0:T(8,128)(2,1)S(1)}, u32[]{:S(2)}, u32[]{:S(2)}) collective-permute-start(s16[2,72,768]{2,1,0:T(8,128)(2,1)S(1)} %get-tuple-element.50), channel_id=1, source_target_pairs={{0,4},{2,6},{4,0},{6,2},{1,5},{3,7},{5,1},{7,3},{8,12},{10,14},{12... | collective-permute-start | bytes 663560 | tf_op jit(solution)/shard_map/ppermute | solution.py:311
  15.7 1.4 %acts_x.1 = (s16[4,72,256]{2,1,0:T(8,128)(2,1)S(1)}, bf16[144,1792]{1,0:T(8,128)(2,1)S(1)}) custom-call(s32[8,128]{1,0:T(8,128)S(1)} %bitcast.41, bf16[1024,1792]{1,0:T(8,128)(2,1)S(1)} %copy-done.1, bf16[1792,1024]{1,0:T(8,128)(2,1)S(1)} %copy-done, bf16[432,1792]{1,0:T(8,128)(2,1)S(1)} %get-tuple-element.38.picked_ref), custom_call_target="tpu_custom_call" | custom-call | flops 1000000000 | tf_op jit(solution)/shard_map/acts_x/pallas_call | solution.py:270
  17.8 1.0 %grads_keep.1.g_keep = f32[288,1024]{1,0:T(8,128)S(1)} custom-call(s32[8,128]{1,0:T(8,128)S(1)} %bitcast.42, bf16[1024,512]{1,0:T(8,128)(2,1)S(1)} %copy-done.2, bf16[512,1024]{1,0:T(8,128)(2,1)S(1)} %copy-done.3, bf16[144,1792]{1,0:T(8,128)(2,1)S(1)} %get-tuple-element.39.after_ref.near_ref), custom_call_target="tpu_custom_call" | custom-call | flops 600000000 | tf_op jit(solution)/shard_map/grads_keep/pallas_call | solution.py:270
  18.8 1.0 %acts_keep.1 = (f32[2,72,768]{2,1,0:T(8,128)S(1)}, f32[288,256]{1,0:T(8,128)S(1)}) custom-call(bf16[432,1792]{1,0:T(8,128)(2,1)S(1)} %get-tuple-element.38.picked_ref, bf16[144,1792]{1,0:T(8,128)(2,1)S(1)} %get-tuple-element.39.after_ref.near_ref, bf16[1792,1024]{1,0:T(8,128)(2,1)S(1)} %copy-done), custom_call_target="tpu_custom_call" | custom-call | flops 1000000000 | tf_op jit(solution)/shard_map/acts_keep/pallas_call | solution.py:270
  19.8 2.6 %collective-permute-done.1.a_got = s16[4,72,256]{2,1,0:T(8,128)(2,1)S(1)} collective-permute-done((s16[4,72,256]{2,1,0:T(8,128)(2,1)S(1)}, s16[4,72,256]{2,1,0:T(8,128)(2,1)S(1)}, u32[]{:S(2)}, u32[]{:S(2)}) %collective-permute-start.1) | collective-permute-done | bytes 147488 | tf_op jit(solution)/shard_map/ppermute | solution.py:321
  22.4 1.1 %x_mid.1 = (f32[72,1280]{1,0:T(8,128)S(1)}, s16[72,1280]{1,0:T(8,128)(2,1)S(1)}, s16[72,1280]{1,0:T(8,128)(2,1)S(1)}, s16[72,1280]{1,0:T(8,128)(2,1)S(1)}) custom-call(f32[288,1024]{1,0:T(8,128)S(1)} %grads_keep.1.g_keep, s16[4,72,1024]{2,1,0:T(8,128)(2,1)S(1)} %collective-permute-done.g_got, f32[288,256]{1,0:T(8,128)S(1)} %get-tuple-element.40.a_keep, ...), custom_call_target="tpu_custom_call" | custom-call | tf_op jit(solution)/shard_map/x_mid/pallas_call | solution.py:270
  23.5 1.4 %collective-permute-done.9.r3_ref = s16[2,72,768]{2,1,0:T(8,128)(2,1)S(1)} collective-permute-done((s16[2,72,768]{2,1,0:T(8,128)(2,1)S(1)}, s16[2,72,768]{2,1,0:T(8,128)(2,1)S(1)}, u32[]{:S(2)}, u32[]{:S(2)}) %collective-permute-start.9) | collective-permute-done | bytes 221216 | tf_op jit(solution)/shard_map/ppermute | solution.py:311
  26.2 1.5 %collective-permute-start.2 = (s16[72,1280]{1,0:T(8,128)(2,1)S(1)}, s16[72,1280]{1,0:T(8,128)(2,1)S(1)}, u32[]{:S(2)}, u32[]{:S(2)}) collective-permute-start(s16[72,1280]{1,0:T(8,128)(2,1)S(1)} %get-tuple-element.43), channel_id=1, source_target_pairs={{0,2},{2,4},{4,6},{6,0},{1,3},{3,5},{5,7},{7,1},{8,10},{10,12},{12... | collective-permute-start | bytes 552968 | tf_op jit(solution)/shard_map/ppermute | solution.py:346
  27.7 2.1 %collective-permute-start.3 = (s16[72,1280]{1,0:T(8,128)(2,1)S(1)}, s16[72,1280]{1,0:T(8,128)(2,1)S(1)}, u32[]{:S(2)}, u32[]{:S(2)}) collective-permute-start(s16[72,1280]{1,0:T(8,128)(2,1)S(1)} %get-tuple-element.44), channel_id=1, source_target_pairs={{0,6},{2,0},{4,2},{6,4},{1,7},{3,1},{5,3},{7,5},{8,14},{10,8},{12,... | collective-permute-start | bytes 552968 | tf_op jit(solution)/shard_map/ppermute | solution.py:346
  29.9 1.8 %collective-permute-start.4 = (s16[72,1280]{1,0:T(8,128)(2,1)S(1)}, s16[72,1280]{1,0:T(8,128)(2,1)S(1)}, u32[]{:S(2)}, u32[]{:S(2)}) collective-permute-start(s16[72,1280]{1,0:T(8,128)(2,1)S(1)} %get-tuple-element.45), channel_id=1, source_target_pairs={{0,4},{2,6},{4,0},{6,2},{1,5},{3,7},{5,1},{7,3},{8,12},{10,14},{12... | collective-permute-start | bytes 552968 | tf_op jit(solution)/shard_map/ppermute | solution.py:346
  31.9 1.3 %collective-permute-done.18.mate_ref.refs_7_ = bf16[72,768]{1,0:T(8,128)(2,1)S(1)} collective-permute-done((bf16[72,768]{1,0:T(8,128)(2,1)S(1)}, bf16[72,768]{1,0:T(8,128)(2,1)S(1)}, u32[]{:S(2)}, u32[]{:S(2)}) %collective-permute-start.18) | collective-permute-done | bytes 110624 | tf_op jit(solution)/shard_map/ppermute | solution.py:351
  33.2 1.7 %collective-permute-start.19 = (bf16[2,72,768]{2,1,0:T(8,128)(2,1)S(1)}, bf16[2,72,768]{2,1,0:T(8,128)(2,1)S(1)}, u32[]{:S(2)}, u32[]{:S(2)}) collective-permute-start(bf16[2,72,768]{2,1,0:T(8,128)(2,1)S(1)} %z_both.1), channel_id=1, source_target_pairs={{0,32},{8,104},{32,64},{40,8},{64,96},{72,40},{96,0},{104,72},{1,3... | collective-permute-start | bytes 663560 | tf_op jit(solution)/shard_map/ppermute | solution.py:357
  34.9 1.8 %collective-permute-done.3.r2_ref = s16[72,1280]{1,0:T(8,128)(2,1)S(1)} collective-permute-done((s16[72,1280]{1,0:T(8,128)(2,1)S(1)}, s16[72,1280]{1,0:T(8,128)(2,1)S(1)}, u32[]{:S(2)}, u32[]{:S(2)}) %collective-permute-start.3) | collective-permute-done | bytes 184352 | tf_op jit(solution)/shard_map/ppermute | solution.py:346
  36.6 1.8 %collective-permute-done.4.r3_ref = s16[72,1280]{1,0:T(8,128)(2,1)S(1)} collective-permute-done((s16[72,1280]{1,0:T(8,128)(2,1)S(1)}, s16[72,1280]{1,0:T(8,128)(2,1)S(1)}, u32[]{:S(2)}, u32[]{:S(2)}) %collective-permute-start.4) | collective-permute-done | bytes 184352 | tf_op jit(solution)/shard_map/ppermute | solution.py:346
  38.9 3.1 %collective-permute-start.16 = (bf16[72,1280]{1,0:T(8,128)(2,1)S(1)}, bf16[72,1280]{1,0:T(8,128)(2,1)S(1)}, u32[]{:S(2)}, u32[]{:S(2)}) collective-permute-start(bf16[72,1280]{1,0:T(8,128)(2,1)S(1)} %x_end.1.refs_0_), channel_id=1, source_target_pairs={{0,96},{32,0},{64,32},{96,64},{1,97},{33,1},{65,33},{97,65},{2,98}... | collective-permute-start | bytes 552968 | tf_op jit(solution)/shard_map/ppermute | solution.py:360
  42.0 2.2 %collective-permute-start.11 = (bf16[72,768]{1,0:T(8,128)(2,1)S(1)}, bf16[72,768]{1,0:T(8,128)(2,1)S(1)}, u32[]{:S(2)}, u32[]{:S(2)}) collective-permute-start(bf16[72,768]{1,0:T(8,128)(2,1)S(1)} %z_end.1.own_ref.refs_6_), channel_id=1, source_target_pairs={{0,64},{32,96},{64,0},{96,32},{1,65},{33,97},{65,1},{97,33},{2,66}... | collective-permute-start | bytes 331784 | tf_op jit(solution)/shard_map/ppermute | solution.py:355
  44.2 1.3 %collective-permute-start.5 = (bf16[72,1280]{1,0:T(8,128)(2,1)S(1)}, bf16[72,1280]{1,0:T(8,128)(2,1)S(1)}, u32[]{:S(2)}, u32[]{:S(2)}) collective-permute-start(bf16[72,1280]{1,0:T(8,128)(2,1)S(1)} %x_end.1.refs_0_), channel_id=1, source_target_pairs={{0,64},{32,96},{64,0},{96,32},{1,65},{33,97},{65,1},{97,33},{2,66}... | collective-permute-start | bytes 552968 | tf_op jit(solution)/shard_map/ppermute | solution.py:360
  45.6 4.8 %collective-permute-done.11.refs_2_ = bf16[72,768]{1,0:T(8,128)(2,1)S(1)} collective-permute-done((bf16[72,768]{1,0:T(8,128)(2,1)S(1)}, bf16[72,768]{1,0:T(8,128)(2,1)S(1)}, u32[]{:S(2)}, u32[]{:S(2)}) %collective-permute-start.11) | collective-permute-done | bytes 110624 | tf_op jit(solution)/shard_map/ppermute | solution.py:355
  51.2 2.1 %collective-permute-done.14.refs_2_ = bf16[72,1280]{1,0:T(8,128)(2,1)S(1)} collective-permute-done((bf16[72,1280]{1,0:T(8,128)(2,1)S(1)}, bf16[72,1280]{1,0:T(8,128)(2,1)S(1)}, u32[]{:S(2)}, u32[]{:S(2)}) %collective-permute-start.14) | collective-permute-done | bytes 184352 | tf_op jit(solution)/shard_map/ppermute | solution.py:360
  53.9 0.8 %collective-permute-done.15.refs_3_ = bf16[72,1280]{1,0:T(8,128)(2,1)S(1)} collective-permute-done((bf16[72,1280]{1,0:T(8,128)(2,1)S(1)}, bf16[72,1280]{1,0:T(8,128)(2,1)S(1)}, u32[]{:S(2)}, u32[]{:S(2)}) %collective-permute-start.15) | collective-permute-done | bytes 184352 | tf_op jit(solution)/shard_map/ppermute | solution.py:351
  54.7 1.0 %near.1 = (f32[3,128,1024]{2,1,0:T(8,128)S(1)}, f32[8,128]{1,0:T(8,128)S(1)}) custom-call(bf16[72,1280]{1,0:T(8,128)(2,1)S(1)} %x_end.1.refs_0_, bf16[72,1280]{1,0:T(8,128)(2,1)S(1)} %collective-permute-done.13.refs_1_, bf16[72,1280]{1,0:T(8,128)(2,1)S(1)} %collective-permute-done.14.refs_2_, bf16[72,1280]{1,0:T(8,128)(2,1)S(1)} %collective-permute-done.15.refs_3_, ...), custom_call_target="tpu_custom_call" | custom-call | flops 500000000 | tf_op jit(solution)/shard_map/near/pallas_call | solution.py:270
  55.7 1.5 %gram.1 = (bf16[16,64,384]{2,1,0:T(8,128)(2,1)}, f32[8,128]{1,0:T(8,128)S(1)}) custom-call(bf16[72,1280]{1,0:T(8,128)(2,1)S(1)} %collective-permute-done.5.refs_0_, bf16[72,1280]{1,0:T(8,128)(2,1)S(1)} %collective-permute-done.6.refs_1_, bf16[72,768]{1,0:T(8,128)(2,1)S(1)} %collective-permute-done.11.refs_2_, ...), custom_call_target="tpu_custom_call" | custom-call | flops 200000000 | tf_op jit(solution)/shard_map/gram/pallas_call | solution.py:270
  57.3 5.8 %all-to-all-start.5 = ((bf16[16,64,384]{2,1,0:T(8,128)(2,1)}), bf16[16,64,384]{2,1,0:T(8,128)(2,1)S(1)}, u32[]{:S(2)}, u32[]{:S(2)}) async-start(bf16[16,64,384]{2,1,0:T(8,128)(2,1)} %get-tuple-element.56), calls=%async_computation.5 | async-start | bytes 1572864 | tf_op jit(solution)/shard_map/all_to_all | solution.py:382
  63.0 3.4 %collective-permute-start.21 = (f32[8,128]{1,0:T(8,128)S(1)}, f32[8,128]{1,0:T(8,128)S(1)}, u32[]{:S(2)}, u32[]{:S(2)}) collective-permute-start(f32[8,128]{1,0:T(8,128)S(1)} %get-tuple-element.55), channel_id=1, source_target_pairs={{0,16},{16,0},{1,17},{17,1},{2,18},{18,2},{3,19},{19,3},{4,20},{20... | collective-permute-start | bytes 12296 | tf_op jit(solution)/shard_map/ppermute | solution.py:383
  67.0 8.7 %collective-permute-done.21 = f32[8,128]{1,0:T(8,128)S(1)} collective-permute-done((f32[8,128]{1,0:T(8,128)S(1)}, f32[8,128]{1,0:T(8,128)S(1)}, u32[]{:S(2)}, u32[]{:S(2)}) %collective-permute-start.21) | collective-permute-done | bytes 4128 | tf_op jit(solution)/shard_map/ppermute | solution.py:383
  77.7 0.8 conditional.1
  77.8 0.7 final.1
  (40 shorter events, 5.2 us)
Async XLA Ops:
  0.6 5.1 %copy-start = (bf16[1792,1024]{1,0:T(8,128)(2,1)S(1)}, bf16[1792,1024]{1,0:T(8,128)(2,1)}, u32[]{:S(2)}) copy-start(bf16[1792,1024]{1,0:T(8,128)(2,1)} %b_ref.9) | copy-start | bytes 11010052
  0.6 5.1 %copy-start.1 = (bf16[1024,1792]{1,0:T(8,128)(2,1)S(1)}, bf16[1024,1792]{1,0:T(8,128)(2,1)}, u32[]{:S(2)}) copy-start(bf16[1024,1792]{1,0:T(8,128)(2,1)} %h_ref.3) | copy-start | bytes 11010052
  0.7 5.1 %copy-start.4 = (s32[1024]{0:T(1024)S(1)}, s32[1024]{0:T(1024)}, u32[]{:S(2)}) copy-start(s32[1024]{0:T(1024)} %param.11) | copy-start | bytes 12292
  4.1 18.3 %collective-permute-start = (s16[4,72,1024]{2,1,0:T(8,128)(2,1)S(1)}, s16[4,72,1024]{2,1,0:T(8,128)(2,1)S(1)}, u32[]{:S(2)}, u32[]{:S(2)}) collective-permute-start(s16[4,72,1024]{2,1,0:T(8,128)(2,1)S(1)} %grads_send.1), channel_id=1, source_target_pairs={{0,1},{1,0},{2,3},{3,2},{4,5},{5,4},{6,7},{7,6},{8,9},{9,8},{10,11... | collective-permute-start | bytes 1769480 | tf_op jit(solution)/shard_map/ppermute | solution.py:300
  9.8 13.7 %collective-permute-start.7 = (s16[2,72,768]{2,1,0:T(8,128)(2,1)S(1)}, s16[2,72,768]{2,1,0:T(8,128)(2,1)S(1)}, u32[]{:S(2)}, u32[]{:S(2)}) collective-permute-start(s16[2,72,768]{2,1,0:T(8,128)(2,1)S(1)} %get-tuple-element.48), channel_id=1, source_target_pairs={{0,2},{2,4},{4,6},{6,0},{1,3},{3,5},{5,7},{7,1},{8,10},{10,12},{12... | collective-permute-start | bytes 663560 | tf_op jit(solution)/shard_map/ppermute | solution.py:311
  11.7 11.8 %collective-permute-start.8 = (s16[2,72,768]{2,1,0:T(8,128)(2,1)S(1)}, s16[2,72,768]{2,1,0:T(8,128)(2,1)S(1)}, u32[]{:S(2)}, u32[]{:S(2)}) collective-permute-start(s16[2,72,768]{2,1,0:T(8,128)(2,1)S(1)} %get-tuple-element.49), channel_id=1, source_target_pairs={{0,6},{2,0},{4,2},{6,4},{1,7},{3,1},{5,3},{7,5},{8,14},{10,8},{12,... | collective-permute-start | bytes 663560 | tf_op jit(solution)/shard_map/ppermute | solution.py:311
  14.0 11.0 %collective-permute-start.9 = (s16[2,72,768]{2,1,0:T(8,128)(2,1)S(1)}, s16[2,72,768]{2,1,0:T(8,128)(2,1)S(1)}, u32[]{:S(2)}, u32[]{:S(2)}) collective-permute-start(s16[2,72,768]{2,1,0:T(8,128)(2,1)S(1)} %get-tuple-element.50), channel_id=1, source_target_pairs={{0,4},{2,6},{4,0},{6,2},{1,5},{3,7},{5,1},{7,3},{8,12},{10,14},{12... | collective-permute-start | bytes 663560 | tf_op jit(solution)/shard_map/ppermute | solution.py:311
  15.7 2.0 %copy-start.2 = (bf16[1024,512]{1,0:T(8,128)(2,1)S(1)}, bf16[1024,512]{1,0:T(8,128)(2,1)}, u32[]{:S(2)}) copy-start(bf16[1024,512]{1,0:T(8,128)(2,1)} %g_ref.3) | copy-start | bytes 3145732
  15.7 2.0 %copy-start.3 = (bf16[512,1024]{1,0:T(8,128)(2,1)S(1)}, bf16[512,1024]{1,0:T(8,128)(2,1)}, u32[]{:S(2)}) copy-start(bf16[512,1024]{1,0:T(8,128)(2,1)} %b_ref.8) | copy-start | bytes 3145732
  17.2 5.2 %collective-permute-start.1 = (s16[4,72,256]{2,1,0:T(8,128)(2,1)S(1)}, s16[4,72,256]{2,1,0:T(8,128)(2,1)S(1)}, u32[]{:S(2)}, u32[]{:S(2)}) collective-permute-start(s16[4,72,256]{2,1,0:T(8,128)(2,1)S(1)} %get-tuple-element.41), channel_id=1, source_target_pairs={{0,1},{1,0},{2,3},{3,2},{4,5},{5,4},{6,7},{7,6},{8,9},{9,8},{10,11... | collective-permute-start | bytes 442376 | tf_op jit(solution)/shard_map/ppermute | solution.py:321
  25.6 6.1 %collective-permute-start.10 = (s16[72,768]{1,0:T(8,128)(2,1)S(1)}, s16[72,768]{1,0:T(8,128)(2,1)S(1)}, u32[]{:S(2)}, u32[]{:S(2)}) collective-permute-start(s16[72,768]{1,0:T(8,128)(2,1)S(1)} %get-tuple-element.52), channel_id=1, source_target_pairs={{0,1},{1,0},{2,3},{3,2},{4,5},{5,4},{6,7},{7,6},{8,9},{9,8},{10,11... | collective-permute-start | bytes 331784 | tf_op jit(solution)/shard_map/ppermute | solution.py:348
  26.2 8.7 %collective-permute-start.2 = (s16[72,1280]{1,0:T(8,128)(2,1)S(1)}, s16[72,1280]{1,0:T(8,128)(2,1)S(1)}, u32[]{:S(2)}, u32[]{:S(2)}) collective-permute-start(s16[72,1280]{1,0:T(8,128)(2,1)S(1)} %get-tuple-element.43), channel_id=1, source_target_pairs={{0,2},{2,4},{4,6},{6,0},{1,3},{3,5},{5,7},{7,1},{8,10},{10,12},{12... | collective-permute-start | bytes 552968 | tf_op jit(solution)/shard_map/ppermute | solution.py:346
  27.7 8.9 %collective-permute-start.3 = (s16[72,1280]{1,0:T(8,128)(2,1)S(1)}, s16[72,1280]{1,0:T(8,128)(2,1)S(1)}, u32[]{:S(2)}, u32[]{:S(2)}) collective-permute-start(s16[72,1280]{1,0:T(8,128)(2,1)S(1)} %get-tuple-element.44), channel_id=1, source_target_pairs={{0,6},{2,0},{4,2},{6,4},{1,7},{3,1},{5,3},{7,5},{8,14},{10,8},{12,... | collective-permute-start | bytes 552968 | tf_op jit(solution)/shard_map/ppermute | solution.py:346
  29.9 8.6 %collective-permute-start.4 = (s16[72,1280]{1,0:T(8,128)(2,1)S(1)}, s16[72,1280]{1,0:T(8,128)(2,1)S(1)}, u32[]{:S(2)}, u32[]{:S(2)}) collective-permute-start(s16[72,1280]{1,0:T(8,128)(2,1)S(1)} %get-tuple-element.45), channel_id=1, source_target_pairs={{0,4},{2,6},{4,0},{6,2},{1,5},{3,7},{5,1},{7,3},{8,12},{10,14},{12... | collective-permute-start | bytes 552968 | tf_op jit(solution)/shard_map/ppermute | solution.py:346
  31.8 1.4 %collective-permute-start.18 = (bf16[72,768]{1,0:T(8,128)(2,1)S(1)}, bf16[72,768]{1,0:T(8,128)(2,1)S(1)}, u32[]{:S(2)}, u32[]{:S(2)}) collective-permute-start(bf16[72,768]{1,0:T(8,128)(2,1)S(1)} %z_end.1.own_ref.refs_6_), channel_id=1, source_target_pairs={{0,8},{8,0},{1,9},{9,1},{2,10},{10,2},{3,11},{11,3},{4,12},{12,4},... | collective-permute-start | bytes 331784 | tf_op jit(solution)/shard_map/ppermute | solution.py:351
  33.2 17.2 %collective-permute-start.19 = (bf16[2,72,768]{2,1,0:T(8,128)(2,1)S(1)}, bf16[2,72,768]{2,1,0:T(8,128)(2,1)S(1)}, u32[]{:S(2)}, u32[]{:S(2)}) collective-permute-start(bf16[2,72,768]{2,1,0:T(8,128)(2,1)S(1)} %z_both.1), channel_id=1, source_target_pairs={{0,32},{8,104},{32,64},{40,8},{64,96},{72,40},{96,0},{104,72},{1,3... | collective-permute-start | bytes 663560 | tf_op jit(solution)/shard_map/ppermute | solution.py:357
  38.9 12.2 %collective-permute-start.16 = (bf16[72,1280]{1,0:T(8,128)(2,1)S(1)}, bf16[72,1280]{1,0:T(8,128)(2,1)S(1)}, u32[]{:S(2)}, u32[]{:S(2)}) collective-permute-start(bf16[72,1280]{1,0:T(8,128)(2,1)S(1)} %x_end.1.refs_0_), channel_id=1, source_target_pairs={{0,96},{32,0},{64,32},{96,64},{1,97},{33,1},{65,33},{97,65},{2,98}... | collective-permute-start | bytes 552968 | tf_op jit(solution)/shard_map/ppermute | solution.py:360
  42.0 11.3 %collective-permute-start.14 = (bf16[72,1280]{1,0:T(8,128)(2,1)S(1)}, bf16[72,1280]{1,0:T(8,128)(2,1)S(1)}, u32[]{:S(2)}, u32[]{:S(2)}) collective-permute-start(bf16[72,1280]{1,0:T(8,128)(2,1)S(1)} %x_end.1.refs_0_), channel_id=1, source_target_pairs={{0,32},{32,64},{64,96},{96,0},{1,33},{33,65},{65,97},{97,1},{2,34}... | collective-permute-start | bytes 552968 | tf_op jit(solution)/shard_map/ppermute | solution.py:360
  42.0 8.4 %collective-permute-start.11 = (bf16[72,768]{1,0:T(8,128)(2,1)S(1)}, bf16[72,768]{1,0:T(8,128)(2,1)S(1)}, u32[]{:S(2)}, u32[]{:S(2)}) collective-permute-start(bf16[72,768]{1,0:T(8,128)(2,1)S(1)} %z_end.1.own_ref.refs_6_), channel_id=1, source_target_pairs={{0,64},{32,96},{64,0},{96,32},{1,65},{33,97},{65,1},{97,33},{2,66}... | collective-permute-start | bytes 331784 | tf_op jit(solution)/shard_map/ppermute | solution.py:355
  44.2 9.1 %collective-permute-start.5 = (bf16[72,1280]{1,0:T(8,128)(2,1)S(1)}, bf16[72,1280]{1,0:T(8,128)(2,1)S(1)}, u32[]{:S(2)}, u32[]{:S(2)}) collective-permute-start(bf16[72,1280]{1,0:T(8,128)(2,1)S(1)} %x_end.1.refs_0_), channel_id=1, source_target_pairs={{0,64},{32,96},{64,0},{96,32},{1,65},{33,97},{65,1},{97,33},{2,66}... | collective-permute-start | bytes 552968 | tf_op jit(solution)/shard_map/ppermute | solution.py:360
  50.4 3.4 %collective-permute-start.13 = (bf16[72,1280]{1,0:T(8,128)(2,1)S(1)}, bf16[72,1280]{1,0:T(8,128)(2,1)S(1)}, u32[]{:S(2)}, u32[]{:S(2)}) collective-permute-start(bf16[72,1280]{1,0:T(8,128)(2,1)S(1)} %x_end.1.refs_0_), channel_id=1, source_target_pairs={{0,8},{8,0},{1,9},{9,1},{2,10},{10,2},{3,11},{11,3},{4,12},{12,4},... | collective-permute-start | bytes 552968 | tf_op jit(solution)/shard_map/ppermute | solution.py:351
  50.4 4.3 %collective-permute-start.20 = (bf16[2,72,768]{2,1,0:T(8,128)(2,1)S(1)}, bf16[2,72,768]{2,1,0:T(8,128)(2,1)S(1)}, u32[]{:S(2)}, u32[]{:S(2)}) collective-permute-start(bf16[2,72,768]{2,1,0:T(8,128)(2,1)S(1)} %collective-permute-done.19.refs_8_), channel_id=1, source_target_pairs={{0,8},{8,0},{1,9},{9,1},{2,10},{10,2},{3,11},{11,3},{4,12},{12,4},... | collective-permute-start | bytes 663560 | tf_op jit(solution)/shard_map/ppermute | solution.py:351
  51.2 2.7 %collective-permute-start.17 = (bf16[72,1280]{1,0:T(8,128)(2,1)S(1)}, bf16[72,1280]{1,0:T(8,128)(2,1)S(1)}, u32[]{:S(2)}, u32[]{:S(2)}) collective-permute-start(bf16[72,1280]{1,0:T(8,128)(2,1)S(1)} %collective-permute-done.16.refs_4_), channel_id=1, source_target_pairs={{0,8},{8,0},{1,9},{9,1},{2,10},{10,2},{3,11},{11,3},{4,12},{12,4},... | collective-permute-start | bytes 552968 | tf_op jit(solution)/shard_map/ppermute | solution.py:351
  53.3 1.4 %collective-permute-start.15 = (bf16[72,1280]{1,0:T(8,128)(2,1)S(1)}, bf16[72,1280]{1,0:T(8,128)(2,1)S(1)}, u32[]{:S(2)}, u32[]{:S(2)}) collective-permute-start(bf16[72,1280]{1,0:T(8,128)(2,1)S(1)} %collective-permute-done.14.refs_2_), channel_id=1, source_target_pairs={{0,8},{8,0},{1,9},{9,1},{2,10},{10,2},{3,11},{11,3},{4,12},{12,4},... | collective-permute-start | bytes 552968 | tf_op jit(solution)/shard_map/ppermute | solution.py:351
  53.3 2.4 %collective-permute-start.6 = (bf16[72,1280]{1,0:T(8,128)(2,1)S(1)}, bf16[72,1280]{1,0:T(8,128)(2,1)S(1)}, u32[]{:S(2)}, u32[]{:S(2)}) collective-permute-start(bf16[72,1280]{1,0:T(8,128)(2,1)S(1)} %collective-permute-done.5.refs_0_), channel_id=1, source_target_pairs={{0,8},{8,0},{1,9},{9,1},{2,10},{10,2},{3,11},{11,3},{4,12},{12,4},... | collective-permute-start | bytes 552968 | tf_op jit(solution)/shard_map/ppermute | solution.py:351
  53.8 1.9 %collective-permute-start.12 = (bf16[72,768]{1,0:T(8,128)(2,1)S(1)}, bf16[72,768]{1,0:T(8,128)(2,1)S(1)}, u32[]{:S(2)}, u32[]{:S(2)}) collective-permute-start(bf16[72,768]{1,0:T(8,128)(2,1)S(1)} %collective-permute-done.11.refs_2_), channel_id=1, source_target_pairs={{0,8},{8,0},{1,9},{9,1},{2,10},{10,2},{3,11},{11,3},{4,12},{12,4},... | collective-permute-start | bytes 331784 | tf_op jit(solution)/shard_map/ppermute | solution.py:351
  57.3 20.5 %all-to-all-start.5 = ((bf16[16,64,384]{2,1,0:T(8,128)(2,1)}), bf16[16,64,384]{2,1,0:T(8,128)(2,1)S(1)}, u32[]{:S(2)}, u32[]{:S(2)}) async-start(bf16[16,64,384]{2,1,0:T(8,128)(2,1)} %get-tuple-element.56), calls=%async_computation.5 | async-start | bytes 1572864 | tf_op jit(solution)/shard_map/all_to_all | solution.py:382
  63.0 12.6 %collective-permute-start.21 = (f32[8,128]{1,0:T(8,128)S(1)}, f32[8,128]{1,0:T(8,128)S(1)}, u32[]{:S(2)}, u32[]{:S(2)}) collective-permute-start(f32[8,128]{1,0:T(8,128)S(1)} %get-tuple-element.55), channel_id=1, source_target_pairs={{0,16},{16,0},{1,17},{17,1},{2,18},{18,2},{3,19},{19,3},{4,20},{20... | collective-permute-start | bytes 12296 | tf_op jit(solution)/shard_map/ppermute | solution.py:383

commit v10 on v8

--- a/solution.py
+++ b/solution.py
@@ -336,7 +336,7 @@
     def over(r):
         return lax.ppermute(r, "core", SWAP)
 
-    rot_z = call(z_end_kernel, "z_end", blk(BF, AZ), (z_own, z_last))
+    rot_z = call(z_end_kernel, "z_end", blk(BF, AZ), (z_own, z_last), flops=2_000_000_000)
     z_mate = over(rot_z)
     z_far = lax.ppermute(rot_z, "y", ring(2))
     z_both = call(both_kernel, "z_both", blk(BF, 2, AZ), (rot_z, z_mate))

time: 74.8 us -> 74.8 us (level)
  no operation moved by 1% of the time
where the time goes in v10:
time: 74.8 us; the launch traced here: 74.6 us
  starting transfers between devices  32.7 us (44%)
  waiting for transfers between devices  22.7 us (30%)
  Pallas kernels  16 us (21%)
  between operations  2.08 us (3%)
  local copies, waits for them, and re-layouts  1.05 us (1%)
    pallas_call x12, Pallas kernels, call(): pl.pallas_call(kernel, out_shape=out_shape, in_specs=[vmem] * (len(args)...  16 us
    ppermute x1, waiting for transfers between devices, fast(): return (got, whole[0, 0] + lax.ppermute(whole, 'xh', SWAP)[0, 0])  8.68 us
    ppermute x3, starting transfers between devices, fast(): z_got = [lax.ppermute(s, 'z', ring(d)) for s, d in zip(z_send, HOPS)]  5.96 us
    ppermute x3, starting transfers between devices, fast(): x_last = [lax.ppermute(s, 'z', ring(d)) for s, d in zip(x_next, HOPS)]  5.52 us
    ppermute x3, starting transfers between devices, fast(): near = [rot_x] + [lax.ppermute(rot_x, 'y', ring(d)) for d in (1, 3, 2)]  5.3 us
    all_to_all x1, starting transfers between devices, fast(): got = lax.all_to_all(parts, ('xh', 'z', 'xl'), 0, 0, tiled=True)  5.23 us
    ppermute x3, waiting for transfers between devices, fast(): near = [rot_x] + [lax.ppermute(rot_x, 'y', ring(d)) for d in (1, 3, 2)]  4.47 us
    ppermute x1, starting transfers between devices, fast(): return (got, whole[0, 0] + lax.ppermute(whole, 'xh', SWAP)[0, 0])  3.43 us
  transfers between devices with their start and end apart: 23, of which 13 were waited for; matrix products, arithmetic and copies ran while one was open for 1% of the time, Pallas kernels for 12%

profile of v10, /device:TPU:0, one launch (start us, length us, event | category | flops | bytes accessed | tf_op | source)
XLA Modules:
  0.0 74.6 jit_solution(16079240095273252126)
XLA Ops:
  0.7 3.4 %grads_send.1 = s16[4,72,1024]{2,1,0:T(8,128)(2,1)S(1)} custom-call(s32[8,128]{1,0:T(8,128)} %bitcast.39, bf16[1024,512]{1,0:T(8,128)(2,1)} %g_ref.3, bf16[512,1024]{1,0:T(8,128)(2,1)} %b_ref.8), custom_call_target="tpu_custom_call" | custom-call | flops 10000000000 | tf_op jit(solution)/shard_map/grads_send/pallas_call | solution.py:256
  4.1 1.6 %collective-permute-start = (s16[4,72,1024]{2,1,0:T(8,128)(2,1)S(1)}, s16[4,72,1024]{2,1,0:T(8,128)(2,1)S(1)}, u32[]{:S(2)}, u32[]{:S(2)}) collective-permute-start(s16[4,72,1024]{2,1,0:T(8,128)(2,1)S(1)} %grads_send.1), channel_id=1, source_target_pairs={{0,1},{1,0},{2,3},{3,2},{4,5},{5,4},{6,7},{7,6},{8,9},{9,8},{10,11... | collective-permute-start | bytes 1769480 | tf_op jit(solution)/shard_map/ppermute | solution.py:286
  5.7 4.0 %acts_z.1 = (s16[2,72,768]{2,1,0:T(8,128)(2,1)S(1)}, s16[2,72,768]{2,1,0:T(8,128)(2,1)S(1)}, s16[2,72,768]{2,1,0:T(8,128)(2,1)S(1)}, bf16[432,1792]{1,0:T(8,128)(2,1)S(1)}, f32[8,128]{1,0:T(8,128)S(1)}) custom-call(s32[8,128]{1,0:T(8,128)S(1)} %bitcast.40, bf16[1024,1792]{1,0:T(8,128)(2,1)S(1)} %copy-done.1, bf16[1792,1024]{1,0:T(8,128)(2,1)S(1)} %copy-done), custom_call_target="tpu_custom_call" | custom-call | flops 4000000000 | tf_op jit(solution)/shard_map/acts_z/pallas_call | solution.py:256
  9.8 2.0 %collective-permute-start.12 = (s16[2,72,768]{2,1,0:T(8,128)(2,1)S(1)}, s16[2,72,768]{2,1,0:T(8,128)(2,1)S(1)}, u32[]{:S(2)}, u32[]{:S(2)}) collective-permute-start(s16[2,72,768]{2,1,0:T(8,128)(2,1)S(1)} %get-tuple-element.46), channel_id=1, source_target_pairs={{0,2},{2,4},{4,6},{6,0},{1,3},{3,5},{5,7},{7,1},{8,10},{10,12},{12... | collective-permute-start | bytes 663560 | tf_op jit(solution)/shard_map/ppermute | solution.py:297
  11.7 2.2 %collective-permute-start.13 = (s16[2,72,768]{2,1,0:T(8,128)(2,1)S(1)}, s16[2,72,768]{2,1,0:T(8,128)(2,1)S(1)}, u32[]{:S(2)}, u32[]{:S(2)}) collective-permute-start(s16[2,72,768]{2,1,0:T(8,128)(2,1)S(1)} %get-tuple-element.47), channel_id=1, source_target_pairs={{0,6},{2,0},{4,2},{6,4},{1,7},{3,1},{5,3},{7,5},{8,14},{10,8},{12,... | collective-permute-start | bytes 663560 | tf_op jit(solution)/shard_map/ppermute | solution.py:297
  14.0 1.8 %collective-permute-start.14 = (s16[2,72,768]{2,1,0:T(8,128)(2,1)S(1)}, s16[2,72,768]{2,1,0:T(8,128)(2,1)S(1)}, u32[]{:S(2)}, u32[]{:S(2)}) collective-permute-start(s16[2,72,768]{2,1,0:T(8,128)(2,1)S(1)} %get-tuple-element.48), channel_id=1, source_target_pairs={{0,4},{2,6},{4,0},{6,2},{1,5},{3,7},{5,1},{7,3},{8,12},{10,14},{12... | collective-permute-start | bytes 663560 | tf_op jit(solution)/shard_map/ppermute | solution.py:297
  15.7 1.4 %acts_x.1 = (s16[4,72,256]{2,1,0:T(8,128)(2,1)S(1)}, bf16[144,1792]{1,0:T(8,128)(2,1)S(1)}) custom-call(s32[8,128]{1,0:T(8,128)S(1)} %bitcast.41, bf16[1024,1792]{1,0:T(8,128)(2,1)S(1)} %copy-done.1, bf16[1792,1024]{1,0:T(8,128)(2,1)S(1)} %copy-done, bf16[432,1792]{1,0:T(8,128)(2,1)S(1)} %get-tuple-element.36.picked_ref), custom_call_target="tpu_custom_call" | custom-call | flops 1000000000 | tf_op jit(solution)/shard_map/acts_x/pallas_call | solution.py:256
  17.8 1.0 %grads_keep.1.g_keep = f32[288,1024]{1,0:T(8,128)S(1)} custom-call(s32[8,128]{1,0:T(8,128)S(1)} %bitcast.42, bf16[1024,512]{1,0:T(8,128)(2,1)S(1)} %copy-done.2, bf16[512,1024]{1,0:T(8,128)(2,1)S(1)} %copy-done.3, bf16[144,1792]{1,0:T(8,128)(2,1)S(1)} %get-tuple-element.37.after_ref.near_ref), custom_call_target="tpu_custom_call" | custom-call | flops 600000000 | tf_op jit(solution)/shard_map/grads_keep/pallas_call | solution.py:256
  18.8 1.0 %acts_keep.1 = (f32[2,72,768]{2,1,0:T(8,128)S(1)}, f32[288,256]{1,0:T(8,128)S(1)}) custom-call(bf16[432,1792]{1,0:T(8,128)(2,1)S(1)} %get-tuple-element.36.picked_ref, bf16[144,1792]{1,0:T(8,128)(2,1)S(1)} %get-tuple-element.37.after_ref.near_ref, bf16[1792,1024]{1,0:T(8,128)(2,1)S(1)} %copy-done), custom_call_target="tpu_custom_call" | custom-call | flops 1000000000 | tf_op jit(solution)/shard_map/acts_keep/pallas_call | solution.py:256
  19.8 2.6 %collective-permute-done.1.a_got = s16[4,72,256]{2,1,0:T(8,128)(2,1)S(1)} collective-permute-done((s16[4,72,256]{2,1,0:T(8,128)(2,1)S(1)}, s16[4,72,256]{2,1,0:T(8,128)(2,1)S(1)}, u32[]{:S(2)}, u32[]{:S(2)}) %collective-permute-start.1) | collective-permute-done | bytes 147488 | tf_op jit(solution)/shard_map/ppermute | solution.py:307
  22.4 1.1 %x_mid.1 = (f32[72,1280]{1,0:T(8,128)S(1)}, s16[72,1280]{1,0:T(8,128)(2,1)S(1)}, s16[72,1280]{1,0:T(8,128)(2,1)S(1)}, s16[72,1280]{1,0:T(8,128)(2,1)S(1)}) custom-call(f32[288,1024]{1,0:T(8,128)S(1)} %grads_keep.1.g_keep, s16[4,72,1024]{2,1,0:T(8,128)(2,1)S(1)} %collective-permute-done.g_got, f32[288,256]{1,0:T(8,128)S(1)} %get-tuple-element.38.a_keep, ...), custom_call_target="tpu_custom_call" | custom-call | tf_op jit(solution)/shard_map/x_mid/pallas_call | solution.py:256
  23.5 1.4 %collective-permute-done.14.r3_ref = s16[2,72,768]{2,1,0:T(8,128)(2,1)S(1)} collective-permute-done((s16[2,72,768]{2,1,0:T(8,128)(2,1)S(1)}, s16[2,72,768]{2,1,0:T(8,128)(2,1)S(1)}, u32[]{:S(2)}, u32[]{:S(2)}) %collective-permute-start.14) | collective-permute-done | bytes 221216 | tf_op jit(solution)/shard_map/ppermute | solution.py:297
  26.2 1.5 %collective-permute-start.2 = (s16[72,1280]{1,0:T(8,128)(2,1)S(1)}, s16[72,1280]{1,0:T(8,128)(2,1)S(1)}, u32[]{:S(2)}, u32[]{:S(2)}) collective-permute-start(s16[72,1280]{1,0:T(8,128)(2,1)S(1)} %get-tuple-element.41), channel_id=1, source_target_pairs={{0,2},{2,4},{4,6},{6,0},{1,3},{3,5},{5,7},{7,1},{8,10},{10,12},{12... | collective-permute-start | bytes 552968 | tf_op jit(solution)/shard_map/ppermute | solution.py:332
  27.7 2.1 %collective-permute-start.3 = (s16[72,1280]{1,0:T(8,128)(2,1)S(1)}, s16[72,1280]{1,0:T(8,128)(2,1)S(1)}, u32[]{:S(2)}, u32[]{:S(2)}) collective-permute-start(s16[72,1280]{1,0:T(8,128)(2,1)S(1)} %get-tuple-element.42), channel_id=1, source_target_pairs={{0,6},{2,0},{4,2},{6,4},{1,7},{3,1},{5,3},{7,5},{8,14},{10,8},{12,... | collective-permute-start | bytes 552968 | tf_op jit(solution)/shard_map/ppermute | solution.py:332
  29.9 1.8 %collective-permute-start.4 = (s16[72,1280]{1,0:T(8,128)(2,1)S(1)}, s16[72,1280]{1,0:T(8,128)(2,1)S(1)}, u32[]{:S(2)}, u32[]{:S(2)}) collective-permute-start(s16[72,1280]{1,0:T(8,128)(2,1)S(1)} %get-tuple-element.43), channel_id=1, source_target_pairs={{0,4},{2,6},{4,0},{6,2},{1,5},{3,7},{5,1},{7,3},{8,12},{10,14},{12... | collective-permute-start | bytes 552968 | tf_op jit(solution)/shard_map/ppermute | solution.py:332
  31.9 3.3 %collective-permute-start.17 = (bf16[72,768]{1,0:T(8,128)(2,1)S(1)}, bf16[72,768]{1,0:T(8,128)(2,1)S(1)}, u32[]{:S(2)}, u32[]{:S(2)}) collective-permute-start(bf16[72,768]{1,0:T(8,128)(2,1)S(1)} %z_end.1.own_ref.refs_8_), channel_id=1, source_target_pairs={{0,64},{32,96},{64,0},{96,32},{1,65},{33,97},{65,1},{97,33},{2,66}... | collective-permute-start | bytes 331784 | tf_op jit(solution)/shard_map/ppermute | solution.py:341
  35.2 0.7 %collective-permute-start.19 = (bf16[2,72,768]{2,1,0:T(8,128)(2,1)S(1)}, bf16[2,72,768]{2,1,0:T(8,128)(2,1)S(1)}, u32[]{:S(2)}, u32[]{:S(2)}) collective-permute-start(bf16[2,72,768]{2,1,0:T(8,128)(2,1)S(1)} %z_both.1), channel_id=1, source_target_pairs={{0,32},{8,104},{32,64},{40,8},{64,96},{72,40},{96,0},{104,72},{1,3... | collective-permute-start | bytes 663560 | tf_op jit(solution)/shard_map/ppermute | solution.py:343
  36.6 1.8 %collective-permute-done.4.r3_ref = s16[72,1280]{1,0:T(8,128)(2,1)S(1)} collective-permute-done((s16[72,1280]{1,0:T(8,128)(2,1)S(1)}, s16[72,1280]{1,0:T(8,128)(2,1)S(1)}, u32[]{:S(2)}, u32[]{:S(2)}) %collective-permute-start.4) | collective-permute-done | bytes 184352 | tf_op jit(solution)/shard_map/ppermute | solution.py:332
  38.9 3.3 %collective-permute-start.10 = (bf16[72,1280]{1,0:T(8,128)(2,1)S(1)}, bf16[72,1280]{1,0:T(8,128)(2,1)S(1)}, u32[]{:S(2)}, u32[]{:S(2)}) collective-permute-start(bf16[72,1280]{1,0:T(8,128)(2,1)S(1)} %x_end.1.refs_0_), channel_id=1, source_target_pairs={{0,64},{32,96},{64,0},{96,32},{1,65},{33,97},{65,1},{97,33},{2,66}... | collective-permute-start | bytes 552968 | tf_op jit(solution)/shard_map/ppermute | solution.py:346
  42.2 1.1 %collective-permute-start.8 = (bf16[72,1280]{1,0:T(8,128)(2,1)S(1)}, bf16[72,1280]{1,0:T(8,128)(2,1)S(1)}, u32[]{:S(2)}, u32[]{:S(2)}) collective-permute-start(bf16[72,1280]{1,0:T(8,128)(2,1)S(1)} %x_end.1.refs_0_), channel_id=1, source_target_pairs={{0,96},{32,0},{64,32},{96,64},{1,97},{33,1},{65,33},{97,65},{2,98}... | collective-permute-start | bytes 552968 | tf_op jit(solution)/shard_map/ppermute | solution.py:346
  43.3 1.0 %collective-permute-start.6 = (bf16[72,1280]{1,0:T(8,128)(2,1)S(1)}, bf16[72,1280]{1,0:T(8,128)(2,1)S(1)}, u32[]{:S(2)}, u32[]{:S(2)}) collective-permute-start(bf16[72,1280]{1,0:T(8,128)(2,1)S(1)} %x_end.1.refs_0_), channel_id=1, source_target_pairs={{0,32},{32,64},{64,96},{96,0},{1,33},{33,65},{65,97},{97,1},{2,34}... | collective-permute-start | bytes 552968 | tf_op jit(solution)/shard_map/ppermute | solution.py:346
  44.2 1.1 %collective-permute-done.19.refs_12_ = bf16[2,72,768]{2,1,0:T(8,128)(2,1)S(1)} collective-permute-done((bf16[2,72,768]{2,1,0:T(8,128)(2,1)S(1)}, bf16[2,72,768]{2,1,0:T(8,128)(2,1)S(1)}, u32[]{:S(2)}, u32[]{:S(2)}) %collective-permute-start.19) | collective-permute-done | bytes 221216 | tf_op jit(solution)/shard_map/ppermute | solution.py:343
  45.8 1.9 %collective-permute-done.10.refs_6_ = bf16[72,1280]{1,0:T(8,128)(2,1)S(1)} collective-permute-done((bf16[72,1280]{1,0:T(8,128)(2,1)S(1)}, bf16[72,1280]{1,0:T(8,128)(2,1)S(1)}, u32[]{:S(2)}, u32[]{:S(2)}) %collective-permute-start.10) | collective-permute-done | bytes 184352 | tf_op jit(solution)/shard_map/ppermute | solution.py:346
  47.7 1.8 %collective-permute-done.8.refs_4_ = bf16[72,1280]{1,0:T(8,128)(2,1)S(1)} collective-permute-done((bf16[72,1280]{1,0:T(8,128)(2,1)S(1)}, bf16[72,1280]{1,0:T(8,128)(2,1)S(1)}, u32[]{:S(2)}, u32[]{:S(2)}) %collective-permute-start.8) | collective-permute-done | bytes 184352 | tf_op jit(solution)/shard_map/ppermute | solution.py:346
  49.5 0.8 %collective-permute-done.6.refs_2_ = bf16[72,1280]{1,0:T(8,128)(2,1)S(1)} collective-permute-done((bf16[72,1280]{1,0:T(8,128)(2,1)S(1)}, bf16[72,1280]{1,0:T(8,128)(2,1)S(1)}, u32[]{:S(2)}, u32[]{:S(2)}) %collective-permute-start.6) | collective-permute-done | bytes 184352 | tf_op jit(solution)/shard_map/ppermute | solution.py:346
  51.0 0.8 %collective-permute-done.7.refs_3_ = bf16[72,1280]{1,0:T(8,128)(2,1)S(1)} collective-permute-done((bf16[72,1280]{1,0:T(8,128)(2,1)S(1)}, bf16[72,1280]{1,0:T(8,128)(2,1)S(1)}, u32[]{:S(2)}, u32[]{:S(2)}) %collective-permute-start.7) | collective-permute-done | bytes 184352 | tf_op jit(solution)/shard_map/ppermute | solution.py:337
  51.7 2.1 %gram.1 = (bf16[16,64,384]{2,1,0:T(8,128)(2,1)}, f32[8,128]{1,0:T(8,128)S(1)}) custom-call(bf16[72,1280]{1,0:T(8,128)(2,1)S(1)} %x_end.1.refs_0_, bf16[72,1280]{1,0:T(8,128)(2,1)S(1)} %collective-permute-done.5.refs_1_, bf16[72,1280]{1,0:T(8,128)(2,1)S(1)} %collective-permute-done.6.refs_2_, bf16[72,1280]{1,0:T(8,128)(2,1)S(1)} %collective-permute-done.7.refs_3_, ...), custom_call_target="tpu_custom_call" | custom-call | flops 600000000 | tf_op jit(solution)/shard_map/gram/pallas_call | solution.py:256
  53.9 5.2 %all-to-all-start.5 = ((bf16[16,64,384]{2,1,0:T(8,128)(2,1)}), bf16[16,64,384]{2,1,0:T(8,128)(2,1)S(1)}, u32[]{:S(2)}, u32[]{:S(2)}) async-start(bf16[16,64,384]{2,1,0:T(8,128)(2,1)} %get-tuple-element.52), calls=%async_computation.5 | async-start | bytes 1572864 | tf_op jit(solution)/shard_map/all_to_all | solution.py:358
  59.1 3.4 %collective-permute-start.21 = (f32[8,128]{1,0:T(8,128)S(1)}, f32[8,128]{1,0:T(8,128)S(1)}, u32[]{:S(2)}, u32[]{:S(2)}) collective-permute-start(f32[8,128]{1,0:T(8,128)S(1)} %get-tuple-element.51), channel_id=1, source_target_pairs={{0,16},{16,0},{1,17},{17,1},{2,18},{18,2},{3,19},{19,3},{4,20},{20... | collective-permute-start | bytes 12296 | tf_op jit(solution)/shard_map/ppermute | solution.py:359
  63.1 8.7 %collective-permute-done.21 = f32[8,128]{1,0:T(8,128)S(1)} collective-permute-done((f32[8,128]{1,0:T(8,128)S(1)}, f32[8,128]{1,0:T(8,128)S(1)}, u32[]{:S(2)}, u32[]{:S(2)}) %collective-permute-start.21) | collective-permute-done | bytes 4128 | tf_op jit(solution)/shard_map/ppermute | solution.py:359
  73.8 0.8 %conditional.1 = ((f32[64,128]{1,0:T(8,128)}, f32[64,128]{1,0:T(8,128)}, f32[64,128]{1,0:T(8,128)})) conditional(s32[]{:T(128)} %bitcast.9, (bf16[1024,1792]{1,0:T(8,128)(2,1)}, bf16[1792,1024]{1,0:T(8,128)(2,1)}, s32[1024]{0:T(1024)S(1)}, bf16[1024,512]{1,0:T(8,128)(2,1)S(1)}, bf16[512,1024]{1,0:T(8,128)(2,1)S(1)}) %tuple.27, ...), branch_computations={%region_0.0_spmd, %region_6.0_spmd} | conditional | flops 5646950400 | bytes 166300480 | solution.py:396
  73.8 0.7 final.1
  (39 shorter events, 5.7 us)
Async XLA Ops:
  0.6 5.1 %copy-start = (bf16[1792,1024]{1,0:T(8,128)(2,1)S(1)}, bf16[1792,1024]{1,0:T(8,128)(2,1)}, u32[]{:S(2)}) copy-start(bf16[1792,1024]{1,0:T(8,128)(2,1)} %b_ref.9) | copy-start | bytes 11010052
  0.6 5.1 %copy-start.1 = (bf16[1024,1792]{1,0:T(8,128)(2,1)S(1)}, bf16[1024,1792]{1,0:T(8,128)(2,1)}, u32[]{:S(2)}) copy-start(bf16[1024,1792]{1,0:T(8,128)(2,1)} %h_ref.3) | copy-start | bytes 11010052
  0.7 5.1 %copy-start.4 = (s32[1024]{0:T(1024)S(1)}, s32[1024]{0:T(1024)}, u32[]{:S(2)}) copy-start(s32[1024]{0:T(1024)} %param.11) | copy-start | bytes 12292
  4.1 18.3 %collective-permute-start = (s16[4,72,1024]{2,1,0:T(8,128)(2,1)S(1)}, s16[4,72,1024]{2,1,0:T(8,128)(2,1)S(1)}, u32[]{:S(2)}, u32[]{:S(2)}) collective-permute-start(s16[4,72,1024]{2,1,0:T(8,128)(2,1)S(1)} %grads_send.1), channel_id=1, source_target_pairs={{0,1},{1,0},{2,3},{3,2},{4,5},{5,4},{6,7},{7,6},{8,9},{9,8},{10,11... | collective-permute-start | bytes 1769480 | tf_op jit(solution)/shard_map/ppermute | solution.py:286
  9.8 13.7 %collective-permute-start.12 = (s16[2,72,768]{2,1,0:T(8,128)(2,1)S(1)}, s16[2,72,768]{2,1,0:T(8,128)(2,1)S(1)}, u32[]{:S(2)}, u32[]{:S(2)}) collective-permute-start(s16[2,72,768]{2,1,0:T(8,128)(2,1)S(1)} %get-tuple-element.46), channel_id=1, source_target_pairs={{0,2},{2,4},{4,6},{6,0},{1,3},{3,5},{5,7},{7,1},{8,10},{10,12},{12... | collective-permute-start | bytes 663560 | tf_op jit(solution)/shard_map/ppermute | solution.py:297
  11.7 11.8 %collective-permute-start.13 = (s16[2,72,768]{2,1,0:T(8,128)(2,1)S(1)}, s16[2,72,768]{2,1,0:T(8,128)(2,1)S(1)}, u32[]{:S(2)}, u32[]{:S(2)}) collective-permute-start(s16[2,72,768]{2,1,0:T(8,128)(2,1)S(1)} %get-tuple-element.47), channel_id=1, source_target_pairs={{0,6},{2,0},{4,2},{6,4},{1,7},{3,1},{5,3},{7,5},{8,14},{10,8},{12,... | collective-permute-start | bytes 663560 | tf_op jit(solution)/shard_map/ppermute | solution.py:297
  14.0 11.0 %collective-permute-start.14 = (s16[2,72,768]{2,1,0:T(8,128)(2,1)S(1)}, s16[2,72,768]{2,1,0:T(8,128)(2,1)S(1)}, u32[]{:S(2)}, u32[]{:S(2)}) collective-permute-start(s16[2,72,768]{2,1,0:T(8,128)(2,1)S(1)} %get-tuple-element.48), channel_id=1, source_target_pairs={{0,4},{2,6},{4,0},{6,2},{1,5},{3,7},{5,1},{7,3},{8,12},{10,14},{12... | collective-permute-start | bytes 663560 | tf_op jit(solution)/shard_map/ppermute | solution.py:297
  15.7 2.0 %copy-start.2 = (bf16[1024,512]{1,0:T(8,128)(2,1)S(1)}, bf16[1024,512]{1,0:T(8,128)(2,1)}, u32[]{:S(2)}) copy-start(bf16[1024,512]{1,0:T(8,128)(2,1)} %g_ref.3) | copy-start | bytes 3145732
  15.7 2.0 %copy-start.3 = (bf16[512,1024]{1,0:T(8,128)(2,1)S(1)}, bf16[512,1024]{1,0:T(8,128)(2,1)}, u32[]{:S(2)}) copy-start(bf16[512,1024]{1,0:T(8,128)(2,1)} %b_ref.8) | copy-start | bytes 3145732
  17.2 5.2 %collective-permute-start.1 = (s16[4,72,256]{2,1,0:T(8,128)(2,1)S(1)}, s16[4,72,256]{2,1,0:T(8,128)(2,1)S(1)}, u32[]{:S(2)}, u32[]{:S(2)}) collective-permute-start(s16[4,72,256]{2,1,0:T(8,128)(2,1)S(1)} %get-tuple-element.39), channel_id=1, source_target_pairs={{0,1},{1,0},{2,3},{3,2},{4,5},{5,4},{6,7},{7,6},{8,9},{9,8},{10,11... | collective-permute-start | bytes 442376 | tf_op jit(solution)/shard_map/ppermute | solution.py:307
  25.6 6.1 %collective-permute-start.15 = (s16[72,768]{1,0:T(8,128)(2,1)S(1)}, s16[72,768]{1,0:T(8,128)(2,1)S(1)}, u32[]{:S(2)}, u32[]{:S(2)}) collective-permute-start(s16[72,768]{1,0:T(8,128)(2,1)S(1)} %get-tuple-element.50), channel_id=1, source_target_pairs={{0,1},{1,0},{2,3},{3,2},{4,5},{5,4},{6,7},{7,6},{8,9},{9,8},{10,11... | collective-permute-start | bytes 331784 | tf_op jit(solution)/shard_map/ppermute | solution.py:334
  26.2 9.8 %collective-permute-start.2 = (s16[72,1280]{1,0:T(8,128)(2,1)S(1)}, s16[72,1280]{1,0:T(8,128)(2,1)S(1)}, u32[]{:S(2)}, u32[]{:S(2)}) collective-permute-start(s16[72,1280]{1,0:T(8,128)(2,1)S(1)} %get-tuple-element.41), channel_id=1, source_target_pairs={{0,2},{2,4},{4,6},{6,0},{1,3},{3,5},{5,7},{7,1},{8,10},{10,12},{12... | collective-permute-start | bytes 552968 | tf_op jit(solution)/shard_map/ppermute | solution.py:332
  27.7 8.9 %collective-permute-start.3 = (s16[72,1280]{1,0:T(8,128)(2,1)S(1)}, s16[72,1280]{1,0:T(8,128)(2,1)S(1)}, u32[]{:S(2)}, u32[]{:S(2)}) collective-permute-start(s16[72,1280]{1,0:T(8,128)(2,1)S(1)} %get-tuple-element.42), channel_id=1, source_target_pairs={{0,6},{2,0},{4,2},{6,4},{1,7},{3,1},{5,3},{7,5},{8,14},{10,8},{12,... | collective-permute-start | bytes 552968 | tf_op jit(solution)/shard_map/ppermute | solution.py:332
  29.9 8.6 %collective-permute-start.4 = (s16[72,1280]{1,0:T(8,128)(2,1)S(1)}, s16[72,1280]{1,0:T(8,128)(2,1)S(1)}, u32[]{:S(2)}, u32[]{:S(2)}) collective-permute-start(s16[72,1280]{1,0:T(8,128)(2,1)S(1)} %get-tuple-element.43), channel_id=1, source_target_pairs={{0,4},{2,6},{4,0},{6,2},{1,5},{3,7},{5,1},{7,3},{8,12},{10,14},{12... | collective-permute-start | bytes 552968 | tf_op jit(solution)/shard_map/ppermute | solution.py:332
  31.8 3.4 %collective-permute-start.16 = (bf16[72,768]{1,0:T(8,128)(2,1)S(1)}, bf16[72,768]{1,0:T(8,128)(2,1)S(1)}, u32[]{:S(2)}, u32[]{:S(2)}) collective-permute-start(bf16[72,768]{1,0:T(8,128)(2,1)S(1)} %z_end.1.own_ref.refs_8_), channel_id=1, source_target_pairs={{0,8},{8,0},{1,9},{9,1},{2,10},{10,2},{3,11},{11,3},{4,12},{12,4},... | collective-permute-start | bytes 331784 | tf_op jit(solution)/shard_map/ppermute | solution.py:337
  31.9 12.4 %collective-permute-start.17 = (bf16[72,768]{1,0:T(8,128)(2,1)S(1)}, bf16[72,768]{1,0:T(8,128)(2,1)S(1)}, u32[]{:S(2)}, u32[]{:S(2)}) collective-permute-start(bf16[72,768]{1,0:T(8,128)(2,1)S(1)} %z_end.1.own_ref.refs_8_), channel_id=1, source_target_pairs={{0,64},{32,96},{64,0},{96,32},{1,65},{33,97},{65,1},{97,33},{2,66}... | collective-permute-start | bytes 331784 | tf_op jit(solution)/shard_map/ppermute | solution.py:341
  35.2 10.1 %collective-permute-start.19 = (bf16[2,72,768]{2,1,0:T(8,128)(2,1)S(1)}, bf16[2,72,768]{2,1,0:T(8,128)(2,1)S(1)}, u32[]{:S(2)}, u32[]{:S(2)}) collective-permute-start(bf16[2,72,768]{2,1,0:T(8,128)(2,1)S(1)} %z_both.1), channel_id=1, source_target_pairs={{0,32},{8,104},{32,64},{40,8},{64,96},{72,40},{96,0},{104,72},{1,3... | collective-permute-start | bytes 663560 | tf_op jit(solution)/shard_map/ppermute | solution.py:343
  38.9 8.8 %collective-permute-start.10 = (bf16[72,1280]{1,0:T(8,128)(2,1)S(1)}, bf16[72,1280]{1,0:T(8,128)(2,1)S(1)}, u32[]{:S(2)}, u32[]{:S(2)}) collective-permute-start(bf16[72,1280]{1,0:T(8,128)(2,1)S(1)} %x_end.1.refs_0_), channel_id=1, source_target_pairs={{0,64},{32,96},{64,0},{96,32},{1,65},{33,97},{65,1},{97,33},{2,66}... | collective-permute-start | bytes 552968 | tf_op jit(solution)/shard_map/ppermute | solution.py:346
  42.2 7.3 %collective-permute-start.8 = (bf16[72,1280]{1,0:T(8,128)(2,1)S(1)}, bf16[72,1280]{1,0:T(8,128)(2,1)S(1)}, u32[]{:S(2)}, u32[]{:S(2)}) collective-permute-start(bf16[72,1280]{1,0:T(8,128)(2,1)S(1)} %x_end.1.refs_0_), channel_id=1, source_target_pairs={{0,96},{32,0},{64,32},{96,64},{1,97},{33,1},{65,33},{97,65},{2,98}... | collective-permute-start | bytes 552968 | tf_op jit(solution)/shard_map/ppermute | solution.py:346
  43.3 7.1 %collective-permute-start.6 = (bf16[72,1280]{1,0:T(8,128)(2,1)S(1)}, bf16[72,1280]{1,0:T(8,128)(2,1)S(1)}, u32[]{:S(2)}, u32[]{:S(2)}) collective-permute-start(bf16[72,1280]{1,0:T(8,128)(2,1)S(1)} %x_end.1.refs_0_), channel_id=1, source_target_pairs={{0,32},{32,64},{64,96},{96,0},{1,33},{33,65},{65,97},{97,1},{2,34}... | collective-permute-start | bytes 552968 | tf_op jit(solution)/shard_map/ppermute | solution.py:346
  44.2 1.3 %collective-permute-start.18 = (bf16[72,768]{1,0:T(8,128)(2,1)S(1)}, bf16[72,768]{1,0:T(8,128)(2,1)S(1)}, u32[]{:S(2)}, u32[]{:S(2)}) collective-permute-start(bf16[72,768]{1,0:T(8,128)(2,1)S(1)} %collective-permute-done.17.refs_10_), channel_id=1, source_target_pairs={{0,8},{8,0},{1,9},{9,1},{2,10},{10,2},{3,11},{11,3},{4,12},{12,4},... | collective-permute-start | bytes 331784 | tf_op jit(solution)/shard_map/ppermute | solution.py:337
  45.3 6.4 %collective-permute-start.20 = (bf16[2,72,768]{2,1,0:T(8,128)(2,1)S(1)}, bf16[2,72,768]{2,1,0:T(8,128)(2,1)S(1)}, u32[]{:S(2)}, u32[]{:S(2)}) collective-permute-start(bf16[2,72,768]{2,1,0:T(8,128)(2,1)S(1)} %collective-permute-done.19.refs_12_), channel_id=1, source_target_pairs={{0,8},{8,0},{1,9},{9,1},{2,10},{10,2},{3,11},{11,3},{4,12},{12,4},... | collective-permute-start | bytes 663560 | tf_op jit(solution)/shard_map/ppermute | solution.py:337
  45.6 4.8 %collective-permute-start.5 = (bf16[72,1280]{1,0:T(8,128)(2,1)S(1)}, bf16[72,1280]{1,0:T(8,128)(2,1)S(1)}, u32[]{:S(2)}, u32[]{:S(2)}) collective-permute-start(bf16[72,1280]{1,0:T(8,128)(2,1)S(1)} %x_end.1.refs_0_), channel_id=1, source_target_pairs={{0,8},{8,0},{1,9},{9,1},{2,10},{10,2},{3,11},{11,3},{4,12},{12,4},... | collective-permute-start | bytes 552968 | tf_op jit(solution)/shard_map/ppermute | solution.py:337
  47.7 2.6 %collective-permute-start.11 = (bf16[72,1280]{1,0:T(8,128)(2,1)S(1)}, bf16[72,1280]{1,0:T(8,128)(2,1)S(1)}, u32[]{:S(2)}, u32[]{:S(2)}) collective-permute-start(bf16[72,1280]{1,0:T(8,128)(2,1)S(1)} %collective-permute-done.10.refs_6_), channel_id=1, source_target_pairs={{0,8},{8,0},{1,9},{9,1},{2,10},{10,2},{3,11},{11,3},{4,12},{12,4},... | collective-permute-start | bytes 552968 | tf_op jit(solution)/shard_map/ppermute | solution.py:337
  49.5 1.4 %collective-permute-start.9 = (bf16[72,1280]{1,0:T(8,128)(2,1)S(1)}, bf16[72,1280]{1,0:T(8,128)(2,1)S(1)}, u32[]{:S(2)}, u32[]{:S(2)}) collective-permute-start(bf16[72,1280]{1,0:T(8,128)(2,1)S(1)} %collective-permute-done.8.refs_4_), channel_id=1, source_target_pairs={{0,8},{8,0},{1,9},{9,1},{2,10},{10,2},{3,11},{11,3},{4,12},{12,4},... | collective-permute-start | bytes 552968 | tf_op jit(solution)/shard_map/ppermute | solution.py:337
  50.3 1.4 %collective-permute-start.7 = (bf16[72,1280]{1,0:T(8,128)(2,1)S(1)}, bf16[72,1280]{1,0:T(8,128)(2,1)S(1)}, u32[]{:S(2)}, u32[]{:S(2)}) collective-permute-start(bf16[72,1280]{1,0:T(8,128)(2,1)S(1)} %collective-permute-done.6.refs_2_), channel_id=1, source_target_pairs={{0,8},{8,0},{1,9},{9,1},{2,10},{10,2},{3,11},{11,3},{4,12},{12,4},... | collective-permute-start | bytes 552968 | tf_op jit(solution)/shard_map/ppermute | solution.py:337
  53.9 19.9 %all-to-all-start.5 = ((bf16[16,64,384]{2,1,0:T(8,128)(2,1)}), bf16[16,64,384]{2,1,0:T(8,128)(2,1)S(1)}, u32[]{:S(2)}, u32[]{:S(2)}) async-start(bf16[16,64,384]{2,1,0:T(8,128)(2,1)} %get-tuple-element.52), calls=%async_computation.5 | async-start | bytes 1572864 | tf_op jit(solution)/shard_map/all_to_all | solution.py:358
  59.1 12.6 %collective-permute-start.21 = (f32[8,128]{1,0:T(8,128)S(1)}, f32[8,128]{1,0:T(8,128)S(1)}, u32[]{:S(2)}, u32[]{:S(2)}) collective-permute-start(f32[8,128]{1,0:T(8,128)S(1)} %get-tuple-element.51), channel_id=1, source_target_pairs={{0,16},{16,0},{1,17},{17,1},{2,18},{18,2},{3,19},{19,3},{4,20},{20... | collective-permute-start | bytes 12296 | tf_op jit(solution)/shard_map/ppermute | solution.py:359
